TPU v7x, 32 devices: a whole 2x2x4 slice. The times are simulated.
32 devices in a mesh: pat: 8 (over z, x), obj: 4 (over y, core).
Axes of the slice: x: 2, y: 2, z: 4, core: 2. Of those that a mesh axis runs over, the one named last changes fastest.
Arguments:
- object_image: bfloat16 [2, 2048, 3072], P(None, 'obj'), may hold values from -4 to 4
- probe: float32 [2, 512, 512], replicated, may hold values from -4 to 4
- amplitudes: bfloat16 [64, 512, 512], P(('pat', 'obj')), may hold values from 0.19921875 to 3
- pos_tile: int32 [64, 2], P(('pat', 'obj')), may hold values from 0 to 9, as said below
- pos_offset: int32 [64, 2], P(('pat', 'obj')), may hold values from 0 to 255
Outputs:
- object_next: bfloat16 [2, 2048, 3072], P(None, 'obj')
- probe_next: float32 [2, 512, 512], replicated
Inputs may be any that keep to these rules, and one draw needn't show every extreme that they name: On each device (aligned blocks of 2 rows) the tile rows pos_tile[:, 0] of its positions differ by at most one, and so do the tile columns pos_tile[:, 1]; every patch lies inside the object: pos_tile[:, 0] <= 5 and pos_tile[:, 1] <= 9.
All inputs are finite; a program needn't handle non-finite values.
Results may differ from a plain program's by a relative error of at most 0.01.
The roundings to bfloat16 on the way count: a program that leaves them out, or rounds other values in their place, can miss the bound.
Values may be sent and summed in bfloat16 or wider, within the bound.
No kernel may reach another device: no remote copies, remote signals or barrier semaphores. Data moves between devices by JAX's collectives and lax.ppermute only.
A program may use at most 128 MiB of HBM per device.

v0:
```python
import math

import jax
import jax.numpy as jnp
from jax import lax
from jax.sharding import PartitionSpec as P

PATCH = 512
TILE = 256


OBJECT_RATE = 0.1
PROBE_RATE = 0.05
MAGNITUDE_FLOOR = 0.5


def dft_tables(length):
    counter = jnp.arange(length, dtype=jnp.int32)
    phase_angle = (counter[:, None] * counter[None, :] % length).astype(jnp.float32) * (
        2.0 * math.pi / length
    )
    factor = 1.0 / math.sqrt(length)
    cosine = (jnp.cos(phase_angle) * factor).astype(jnp.bfloat16)
    sine_part = (-jnp.sin(phase_angle) * factor).astype(jnp.bfloat16)
    return (cosine, sine_part)


def operator_pair(cosine, sine_part):
    left_side = jnp.stack([jnp.stack([cosine, -sine_part]), jnp.stack([sine_part, cosine])])
    right_side = jnp.stack([jnp.stack([cosine, sine_part]), jnp.stack([-sine_part, cosine])])
    return (left_side, right_side)


def transform(wave_field, left_side, right_side):
    half_done = jnp.einsum(
        "ocjk,bckn->bojn", left_side, wave_field, preferred_element_type=jnp.float32
    ).astype(jnp.bfloat16)
    return jnp.einsum("bcjk,cokn->bojn", half_done, right_side, preferred_element_type=jnp.float32)


def shards(object_image, probe, amplitudes, pos_tile, pos_offset):
    owners = lax.axis_size("obj")
    my_index = lax.axis_index("obj")
    zero_index = jnp.zeros((), jnp.int32)
    band_height = object_image.shape[1]
    width_all = object_image.shape[2]
    tile_count = width_all // TILE
    top_row = jnp.minimum(jnp.min(pos_tile[:, 0]), 2 * owners - 4)
    left_col = jnp.minimum(jnp.min(pos_tile[:, 1]), tile_count - 4)
    corner = jnp.stack([top_row, left_col])[None, :]
    corners = lax.all_gather(corner, "obj", axis=0, tiled=True)
    band_tiles = 2 * my_index + jnp.arange(2, dtype=jnp.int32)

    def cut_piece(request):
        column_strip = lax.dynamic_slice(
            object_image, (zero_index, zero_index, request[1] * TILE), (2, band_height, 4 * TILE)
        )
        inside = (band_tiles >= request[0]) & (band_tiles < request[0] + 4)
        row_mask = jnp.repeat(inside, TILE)
        return jnp.where(row_mask[None, :, None], column_strip, jnp.zeros_like(column_strip))

    outgoing = jax.vmap(cut_piece, out_axes=1)(corners).reshape(2, owners * band_height, 4 * TILE)
    incoming = lax.all_to_all(outgoing, "obj", split_axis=1, concat_axis=1, tiled=True)
    window = lax.dynamic_slice(
        incoming, (zero_index, top_row * TILE, zero_index), (2, 4 * TILE, 4 * TILE)
    )
    row_starts = (pos_tile[:, 0] - top_row) * TILE + pos_offset[:, 0]
    col_starts = (pos_tile[:, 1] - left_col) * TILE + pos_offset[:, 1]

    def slice_patch(row_at, col_at):
        return lax.dynamic_slice(window, (zero_index, row_at, col_at), (2, PATCH, PATCH))

    patches = jax.vmap(slice_patch)(row_starts, col_starts)
    cosine, sine_part = dft_tables(PATCH)
    forward_left, forward_right = operator_pair(cosine, sine_part)
    inverse_left, inverse_right = operator_pair(cosine, -sine_part)
    probe_real = probe[0]
    probe_imag = probe[1]
    patch_real = patches[:, 0].astype(jnp.float32)
    patch_imag = patches[:, 1].astype(jnp.float32)
    exit_wave = jnp.stack(
        [
            probe_real * patch_real - probe_imag * patch_imag,
            probe_real * patch_imag + probe_imag * patch_real,
        ],
        1,
    ).astype(jnp.bfloat16)
    far_field = transform(exit_wave, forward_left, forward_right)
    modulus = jnp.sqrt(far_field[:, 0] * far_field[:, 0] + far_field[:, 1] * far_field[:, 1])
    keep_share = 1.0 - amplitudes.astype(jnp.float32) / jnp.maximum(modulus, MAGNITUDE_FLOOR)
    residual = (far_field * keep_share[:, None]).astype(jnp.bfloat16)
    back_field = transform(residual, inverse_left, inverse_right)
    back_real = back_field[:, 0]
    back_imag = back_field[:, 1]
    patch_grad = jnp.stack(
        [
            probe_real * back_real + probe_imag * back_imag,
            probe_real * back_imag - probe_imag * back_real,
        ],
        1,
    )
    probe_term = jnp.stack(
        [
            jnp.sum(patch_real * back_real + patch_imag * back_imag, 0),
            jnp.sum(patch_real * back_imag - patch_imag * back_real, 0),
        ]
    )
    probe_total = lax.psum(probe_term, ("pat", "obj"))

    def place(item_index, accumulated):
        corner_at = (zero_index, row_starts[item_index], col_starts[item_index])
        current = lax.dynamic_slice(accumulated, corner_at, (2, PATCH, PATCH))
        return lax.dynamic_update_slice(accumulated, current + patch_grad[item_index], corner_at)

    window_grad = lax.fori_loop(
        0, patches.shape[0], place, jnp.zeros((2, 4 * TILE, 4 * TILE), jnp.float32)
    ).astype(jnp.bfloat16)
    returning = lax.dynamic_update_slice(
        jnp.zeros((2, owners * band_height, 4 * TILE), jnp.bfloat16),
        window_grad,
        (zero_index, top_row * TILE, zero_index),
    )
    returned = lax.all_to_all(returning, "obj", split_axis=1, concat_axis=1, tiled=True)
    band_grad = jnp.zeros((2, band_height, width_all), jnp.float32)
    for sender in range(owners):
        sender_piece = returned[:, sender * band_height : (sender + 1) * band_height, :].astype(
            jnp.float32
        )
        column_at = corners[sender, 1] * TILE
        current = lax.dynamic_slice(
            band_grad, (zero_index, zero_index, column_at), (2, band_height, 4 * TILE)
        )
        band_grad = lax.dynamic_update_slice(
            band_grad, current + sender_piece, (zero_index, zero_index, column_at)
        )
    summed = lax.psum(band_grad.astype(jnp.bfloat16), "pat").astype(jnp.float32)
    object_next = (object_image.astype(jnp.float32) - OBJECT_RATE * summed).astype(jnp.bfloat16)
    probe_next = probe - PROBE_RATE * probe_total
    return (object_next, probe_next)


def solution(mesh):
    return jax.shard_map(
        shards,
        mesh=mesh,
        in_specs=(
            P(None, "obj", None),
            P(),
            P(("pat", "obj"), None, None),
            P(("pat", "obj"), None),
            P(("pat", "obj"), None),
        ),
        out_specs=(P(None, "obj", None), P()),
        check_vma=False,
    )
```

profile of v0, /device:TPU:0, one launch (start us, length us, event | category | flops | bytes accessed | tf_op | source)
XLA Modules:
  0.0 855.6 jit_solution(10759894042603056275)
XLA Ops:
  12.0 6.4 all-reduce.1
  18.7 20.8 %while.19 = (s32[]{:T(128)}, bf16[2,512,3072]{2,1,0:T(8,128)(2,1)}, s32[4,3]{1,0:T(4,128)S(1)}, bf16[4,2,512,1024]{3,2,1,0:T(8,128)(2,1)}) while((s32[]{:T(128)}, bf16[2,512,3072]{2,1,0:T(8,128)(2,1)}, s32[4,3]{1,0:T(4,128)S(1)}, bf16[4,2,512,1024]{3,2,1,0:T(8,128)(2,1)}) %tuple.91), condition=%wide.while_cond.clone, body=%wide.while_body.sunk.clone | while | flops 2 | bytes 4195417 | solution.py:55
  19.3 4.6 bitcast_dynamic-update-slice_fusion.6
  24.5 4.6 bitcast_dynamic-update-slice_fusion.6
  29.7 4.7 bitcast_dynamic-update-slice_fusion.6
  35.0 4.6 bitcast_dynamic-update-slice_fusion.6
  39.7 7.3 select_bitcast_fusion
  47.0 16.4 %copy.27 = bf16[2,4,512,1024]{3,0,2,1:T(2,128)(2,1)} copy(bf16[2,4,512,1024]{3,2,0,1:T(8,128)(2,1)} %select_bitcast_fusion) | data formatting | bytes 16777216 | tf_op jit(solution)/shard_map/vmap(jit(_where))/select_n | solution.py:60
  63.4 6.3 all-to-all-start
  80.0 4.4 multiply_convert_fusion.1
  86.5 76.4 %all-to-all-done = bf16[2,2048,1024]{2,0,1:T(2,128)(2,1)} async-done(((bf16[2,2048,1024]{2,0,1:T(2,128)(2,1)}), bf16[2,2048,1024]{2,0,1:T(2,128)(2,1)}, u32[]{:S(2)}, u32[]{:S(2)}) %all-to-all-start) | async-done | bytes 8388640 | tf_op jit(solution)/shard_map/all_to_all | solution.py:63
  162.9 7.1 constant_dynamic-slice_fusion.5
  170.0 15.6 %while.20 = (s32[]{:T(128)}, bf16[2,1024,1024]{2,0,1:T(2,128)(2,1)}, s32[2,3]{1,0:T(2,128)S(1)}, bf16[2,2,512,512]{2,3,1,0:T(8,128)(2,1)}) while((s32[]{:T(128)}, bf16[2,1024,1024]{2,0,1:T(2,128)(2,1)}, s32[2,3]{1,0:T(2,128)S(1)}, bf16[2,2,512,512]{2,3,1,0:T(8,128)(2,1)}) %tuple.94), condition=%wide.while_cond.1.clone, body=%wide.while_body.1.sunk.clone | while | flops 2 | bytes 6292073 | solution.py:71
  170.6 4.6 constant_dynamic-slice_fusion.20
  178.3 4.6 constant_dynamic-slice_fusion.20
  189.4 9.1 %convolution_bitcast_fusion.1 = f32[2,2,512,512]{2,3,0,1:T(8,128)} fusion(bf16[2,1,512,512]{2,3,1,0:T(8,128)(2,1)} %get-tuple-element.175, bf16[2,1,512,512]{2,3,1,0:T(8,128)(2,1)} %get-tuple-element.174, bf16[1,2,512,512]{3,2,1,0:T(8,128)(2,1)} %get-tuple-element.179, bf16[1,2,512,512]{3,2,1,0:T(8,128)(2,1)} %get-tuple-element.182, ...), kind=kOutput, calls=%fused_computation.28 | convolution fusion | flops 4305453056 | bytes 10485760 | tf_op jit(solution)/shard_map/bcjk,cokn->bojn/dot_general | solution.py:38
  198.6 4.6 fusion.16
  203.2 10.3 %convolution_bitcast_fusion = f32[2,2,512,512]{2,3,1,0:T(8,128)} fusion(bf16[1,2,512,512]{3,2,1,0:T(8,128)(2,1)} %get-tuple-element.179, bf16[1,2,512,512]{3,2,1,0:T(8,128)(2,1)} %get-tuple-element.182, bf16[1,2,512,512]{3,2,1,0:T(8,128)(2,1)} %get-tuple-element.183, bf16[1,2,512,512]{3,2,1,0:T(8,128)(2,1)S(1)} %copy-done.7, ...), kind=kOutput, calls=%fused_computation.27 | convolution fusion | flops 4306501632 | bytes 14680064 | tf_op jit(solution)/shard_map/bcjk,cokn->bojn/dot_general | solution.py:38
  218.9 5.8 broadcast_in_dim.41.clone
  224.7 227.2 %while.18 = (s32[]{:T(128)}, f32[2,1024,1024]{2,0,1:T(2,128)}, s32[2]{0:T(128)S(1)}, s32[2]{0:T(128)S(1)}, f32[2,2,512,512]{2,3,1,0:T(8,128)}) while((s32[]{:T(128)}, f32[2,1024,1024]{2,0,1:T(2,128)}, s32[2]{0:T(128)S(1)}, s32[2]{0:T(128)S(1)}, f32[2,2,512,512]{2,3,1,0:T(8,128)}) %tuple.97), condition=%wide.region_3.4_spmd.clone, body=%wide.region_2.3_spmd.sunk.clone | while | flops 524296 | bytes 44040388 | solution.py:115
  241.5 96.7 %dynamic_update_slice.34 = f32[2,1024,1024]{2,0,1:T(2,128)} dynamic-update-slice(f32[2,1024,1024]{2,0,1:T(2,128)} %get-tuple-element.344, f32[2,512,512]{2,0,1:T(2,128)S(1)} %copy.96, s32[]{:T(128)} %constant.45.clone.1..sunk.1, s32[]{:T(128)S(6)} %select_n.129, s32[]{:T(128)S(6)} %select_n.130) | dynamic-update-slice | bytes 4194308 | tf_op jit(solution)/shard_map/while/body/eval_jaxpr/dynamic_update_slice | solution.py:113
  355.1 96.7 %dynamic_update_slice.34 = f32[2,1024,1024]{2,0,1:T(2,128)} dynamic-update-slice(f32[2,1024,1024]{2,0,1:T(2,128)} %get-tuple-element.344, f32[2,512,512]{2,0,1:T(2,128)S(1)} %copy.96, s32[]{:T(128)} %constant.45.clone.1..sunk.1, s32[]{:T(128)S(6)} %select_n.129, s32[]{:T(128)S(6)} %select_n.130) | dynamic-update-slice | bytes 4194308 | tf_op jit(solution)/shard_map/while/body/eval_jaxpr/dynamic_update_slice | solution.py:113
  451.8 5.4 broadcast_in_dim.40
  457.2 8.3 convert_dynamic-update-slice_fusion.1
  465.5 5.8 all-to-all-start.1
  479.4 92.1 %all-to-all-done.1 = bf16[2,2048,1024]{2,0,1:T(2,128)(2,1)} async-done(((bf16[2,2048,1024]{2,0,1:T(2,128)(2,1)}), bf16[2,2048,1024]{2,0,1:T(2,128)(2,1)}, u32[]{:S(2)}, u32[]{:S(2)}) %all-to-all-start.1) | async-done | bytes 8388640 | tf_op jit(solution)/shard_map/all_to_all | solution.py:123
  586.8 4.2 add_dynamic-update-slice_fusion
  591.0 5.4 convert_element_type.145
  598.4 17.6 %all-reduce.7.cloned.1.call-done = f32[2,512,512]{1,2,0:T(8,128)} async-done(((f32[2,512,512]{1,2,0:T(8,128)}), f32[2,512,512]{1,2,0:T(8,128)}) %all-reduce.7.cloned.1.call-update) | async-done | bytes 2097168 | tf_op jit(solution)/shard_map/psum | solution.py:108
  622.3 208.7 %all-reduce.5.cloned.1.call-done = bf16[2,512,3072]{2,0,1:T(2,128)(2,1)} async-done(((bf16[2,512,3072]{2,0,1:T(2,128)(2,1)}), bf16[2,512,3072]{2,0,1:T(2,128)(2,1)}) %all-reduce.5.cloned.1.call-update) | async-done | bytes 6291472 | tf_op jit(solution)/shard_map/psum | solution.py:136
  831.0 13.0 %subtract_convert_fusion = bf16[2,512,3072]{2,0,1:T(2,128)(2,1)S(1)} fusion(bf16[2,512,3072]{2,0,1:T(2,128)(2,1)} %all-reduce.5.cloned.1.call-done, bf16[2,512,3072]{2,1,0:T(8,128)(2,1)} %get-tuple-element.355), kind=kLoop, calls=%fused_computation.8 | loop fusion | flops 15728640 | bytes 18874368 | tf_op jit(solution)/shard_map/convert_element_type | solution.py:137
  844.0 4.6 copy.44
  (92 shorter events, 89.5 us)
Async XLA Ops:
  63.4 6.3 copy-start.2
  63.4 99.4 %all-to-all-start = ((bf16[2,2048,1024]{2,0,1:T(2,128)(2,1)}), bf16[2,2048,1024]{2,0,1:T(2,128)(2,1)}, u32[]{:S(2)}, u32[]{:S(2)}) async-start(bf16[2,2048,1024]{2,0,1:T(2,128)(2,1)} %bitcast.144), calls=%async_computation | async-start | bytes 16777216 | tf_op jit(solution)/shard_map/all_to_all | solution.py:63
  71.2 1.7 copy-start.5
  71.2 3.1 copy-start.6
  73.0 2.6 copy-start.8
  73.0 2.6 copy-start.9
  185.5 3.9 copy-start.7
  189.4 9.1 %copy-start.4 = (bf16[2,512,512]{1,2,0:T(8,128)(2,1)S(1)}, bf16[2,512,512]{1,2,0:T(8,128)(2,1)}, u32[]{:S(2)}) copy-start(bf16[2,512,512]{1,2,0:T(8,128)(2,1)} %copy.34) | copy-start | bytes 3145732
  203.2 10.3 %copy-start.1 = (f32[512,512]{0,1:T(8,128)S(1)}, f32[512,512]{0,1:T(8,128)}, u32[]{:S(2)}) copy-start(f32[512,512]{0,1:T(8,128)} %copy.30) | copy-start | bytes 3145732
  229.2 4.1 copy-start
  342.8 4.1 copy-start
  465.5 9.0 %copy-start.3 = (bf16[2,2,512,512]{2,3,1,0:T(8,128)(2,1)S(1)}, bf16[2,2,512,512]{2,3,1,0:T(8,128)(2,1)}, u32[]{:S(2)}) copy-start(bf16[2,2,512,512]{2,3,1,0:T(8,128)(2,1)} %get-tuple-element.112) | copy-start | bytes 6291460
  465.5 106.0 %all-to-all-start.1 = ((bf16[2,2048,1024]{2,0,1:T(2,128)(2,1)}), bf16[2,2048,1024]{2,0,1:T(2,128)(2,1)}, u32[]{:S(2)}, u32[]{:S(2)}) async-start(bf16[2,2048,1024]{2,0,1:T(2,128)(2,1)} %convert_dynamic-update-slice_fusion.1), calls=%async_computation.1 | async-start | bytes 16777216 | tf_op jit(solution)/shard_map/all_to_all | solution.py:123
  471.3 144.7 %all-reduce.7.cloned.1.call-start = ((), (), s32[]{:S(2)}) async-start(), calls=%async_computation.3 | async-start | bytes 4194304 | tf_op jit(solution)/shard_map/psum | solution.py:108
  479.3 351.7 %all-reduce.5.cloned.1.call-start = ((), (), s32[]{:S(2)}) async-start(), calls=%async_computation.2 | async-start | bytes 12582912 | tf_op jit(solution)/shard_map/psum | solution.py:136
Sparse Core Ops, SparseCore 0:
  479.4 136.5 all-reduce.6
  620.8 210.1 all-reduce.4
where the time goes:
time: 863 us; the launch traced here: 856 us
  waiting for transfers between devices  395 us (46%)
  local copies, waits for them, and re-layouts  308 us (36%)
  other arithmetic  88.9 us (10%)
  matrix products  19.4 us (2%)
  between operations  18.9 us (2%)
  starting transfers between devices  12.1 us (1%)
    psum x1, waiting for transfers between devices, shards(): summed = lax.psum(band_grad.astype(jnp.bfloat16), 'pat').astype(jnp.float32)  209 us
    dynamic_update_slice x4, local copies, waits for them, and re-layouts, place(): lax.dynamic_update_slice(accumulated, current + patch_grad[item_index], c...  197 us
    all_to_all x1, waiting for transfers between devices, shards(): lax.all_to_all(returning, 'obj', split_axis=1, concat_axis=1, tiled=True)  92.1 us
    all_to_all x1, waiting for transfers between devices, shards(): lax.all_to_all(outgoing, 'obj', split_axis=1, concat_axis=1, tiled=True)  76.4 us
    gather x22, local copies, waits for them, and re-layouts  36.2 us
    dot_general x2, matrix products, transform(): jnp.einsum('bcjk,cokn->bojn', half_done, right_side, preferred_element_ty...  19.4 us
    psum x1, waiting for transfers between devices, shards(): probe_total = lax.psum(probe_term, ('pat', 'obj'))  17.6 us
  transfers between devices with their start and end apart: 4, of which 4 were waited for; matrix products, arithmetic and copies ran while one was open for 6% of the time, Pallas kernels for 0%

commit v1 on v0

v1 whole, which is shorter than its diff:
```python
import functools
import math

import jax
import jax.numpy as jnp
from jax import lax
from jax.experimental import pallas as pl
from jax.experimental.pallas import tpu as pltpu
from jax.sharding import PartitionSpec as P

PATCH = 512
TILE = 256
LANES = 128
WIDE = PATCH + LANES

OBJECT_RATE = 0.1
PROBE_RATE = 0.05
MAGNITUDE_FLOOR = 0.5
VMEM_LIMIT = 56 * 1024 * 1024


def dft_matrices(length):
    counter = jnp.arange(length, dtype=jnp.int32)
    phase_angle = (counter[:, None] * counter[None, :] % length).astype(jnp.float32) * (
        2.0 * math.pi / length
    )
    factor = 1.0 / math.sqrt(length)
    cosine = (jnp.cos(phase_angle) * factor).astype(jnp.bfloat16)
    sine_part = (-jnp.sin(phase_angle) * factor).astype(jnp.bfloat16)
    top = jnp.concatenate([cosine, -sine_part], 1)
    bottom = jnp.concatenate([sine_part, cosine], 1)
    left = jnp.concatenate([top, bottom], 0)
    top = jnp.concatenate([cosine, sine_part], 1)
    bottom = jnp.concatenate([-sine_part, cosine], 1)
    right = jnp.concatenate([top, bottom], 0)
    return left, right


def first_row(pos, index):
    return pos[index, 0] * TILE + pos[index, 2]


def first_col(pos, index):
    return pos[index, 1] * TILE + pos[index, 3]


def shifted_left(wide, amount):
    return pltpu.roll(wide, lax.rem(WIDE - amount, WIDE), axis=1)[:, :PATCH]


def band_of_rows(row_at, start, count):
    rows = lax.broadcasted_iota(jnp.int32, (count, PATCH), 0) + start
    return row_at // PATCH + (rows < lax.rem(row_at, PATCH)).astype(jnp.int32)


CHUNK = 64
SUBLANES = 8


def rows_from(ref, plane, start, count):
    aligned = pl.multiple_of(start // SUBLANES * SUBLANES, SUBLANES)
    tall = count + SUBLANES
    data = ref[plane, pl.ds(aligned, tall), :]
    return pltpu.roll(data, lax.rem(tall - lax.rem(start, SUBLANES), tall), axis=0)[:count]


def cut_kernel(flips, pos, me, *refs):
    step = pl.program_id(0)
    blocks, out = refs[:-1], refs[-1]
    target = lax.bitwise_xor(me[0], flips[0])
    for k in range(1, len(flips)):
        target = jnp.where(step // 2 == k, lax.bitwise_xor(me[0], flips[k]), target)
    amount = lax.rem(first_col(pos, 2 * target + lax.rem(step, 2)), LANES)

    def body(i, carry):
        rows = pl.ds(pl.multiple_of(i * CHUNK, CHUNK), CHUNK)
        for plane in range(2):
            wide = jnp.concatenate([b[plane, rows, :] for b in blocks], 1)
            out[0, plane, rows, :] = shifted_left(wide.astype(jnp.float32), amount).astype(
                jnp.bfloat16
            )
        return carry

    lax.fori_loop(0, PATCH // CHUNK, body, 0)


def cut(band, pos, me, flips):
    def block(k):
        def index(i, pos, me):
            target = lax.bitwise_xor(me[0], flips[0])
            for j in range(1, len(flips)):
                target = jnp.where(i // 2 == j, lax.bitwise_xor(me[0], flips[j]), target)
            return (0, 0, first_col(pos, 2 * target + lax.rem(i, 2)) // LANES + k)

        return pl.BlockSpec((2, PATCH, LANES), index)

    count = 2 * len(flips)
    return pl.pallas_call(
        functools.partial(cut_kernel, flips),
        grid_spec=pltpu.PrefetchScalarGridSpec(
            num_scalar_prefetch=2,
            grid=(count,),
            in_specs=[block(k) for k in range(WIDE // LANES)],
            out_specs=pl.BlockSpec((1, 2, PATCH, PATCH), lambda i, pos, me: (i, 0, 0, 0)),
        ),
        out_shape=jax.ShapeDtypeStruct((count, 2, PATCH, PATCH), jnp.bfloat16),
        compiler_params=pltpu.CompilerParams(vmem_limit_bytes=VMEM_LIMIT),
        cost_estimate=pl.CostEstimate(
            flops=count * 2 * PATCH * WIDE, bytes_accessed=count * 2300000, transcendentals=0
        ),
    )(pos, me, *([band] * (WIDE // LANES)))


def merge_kernel(which, pos, me, *refs):
    blocks, sibling, out = refs[:-2], refs[-2], refs[-1]
    index = 2 * lax.bitwise_xor(me[0], 2) + which
    amount = lax.rem(first_col(pos, index), LANES)
    row_at = first_row(pos, index)

    def body(i, carry):
        rows = pl.ds(pl.multiple_of(i * CHUNK, CHUNK), CHUNK)
        mine = band_of_rows(row_at, i * CHUNK, CHUNK) == me[0]
        for plane in range(2):
            wide = jnp.concatenate([b[plane, rows, :] for b in blocks], 1)
            own = shifted_left(wide.astype(jnp.float32), amount)
            other = sibling[0, plane, rows, :].astype(jnp.float32)
            out[plane, rows, :] = jnp.where(mine, own, other).astype(jnp.bfloat16)
        return carry

    lax.fori_loop(0, PATCH // CHUNK, body, 0)


def cut_and_merge(band, sibling, pos, me, which):
    def block(k):
        def index(i, pos, me):
            return (0, 0, first_col(pos, 2 * lax.bitwise_xor(me[0], 2) + which) // LANES + k)

        return pl.BlockSpec((2, PATCH, LANES), index)

    return pl.pallas_call(
        functools.partial(merge_kernel, which),
        grid_spec=pltpu.PrefetchScalarGridSpec(
            num_scalar_prefetch=2,
            grid=(1,),
            in_specs=[block(k) for k in range(WIDE // LANES)]
            + [pl.BlockSpec((1, 2, PATCH, PATCH), lambda i, pos, me: (which, 0, 0, 0))],
            out_specs=pl.BlockSpec((2, PATCH, PATCH), lambda i, pos, me: (0, 0, 0)),
        ),
        out_shape=jax.ShapeDtypeStruct((2, PATCH, PATCH), jnp.bfloat16),
        compiler_params=pltpu.CompilerParams(vmem_limit_bytes=VMEM_LIMIT),
        cost_estimate=pl.CostEstimate(
            flops=2 * PATCH * WIDE, bytes_accessed=3300000, transcendentals=0
        ),
    )(pos, me, *([band] * (WIDE // LANES)), sibling)


def wave_kernel(which, has_term, pos, me, band, sibling, across, probe, amplitudes, left, right, *refs):
    if has_term:
        term_in, grad, term, *scratch = refs
    else:
        grad, term, *scratch = refs
    window, sib_v, far_v, probe_v, amp_v, left_v, right_v, term_v, patch_v, twice, field, half, sems = scratch
    index = 2 * me[0] + which
    col_at = first_col(pos, index)
    row_at = first_row(pos, index)
    start = pl.multiple_of(col_at // LANES * LANES, LANES)
    pairs = [
        (band.at[:, :, pl.ds(start, WIDE)], window),
        (sibling.at[which], sib_v),
        (across, far_v),
        (probe, probe_v),
        (left, left_v),
        (right, right_v),
        (amplitudes.at[which], amp_v),
    ]
    if has_term:
        pairs.append((term_in, term_v))
    copies = [pltpu.make_async_copy(a, b, sems.at[k]) for k, (a, b) in enumerate(pairs)]
    for copy in copies:
        copy.start()
    for copy in copies[:3]:
        copy.wait()
    amount = lax.rem(col_at, LANES)
    down = lax.rem(row_at, PATCH)

    def assemble(i, carry):
        at = pl.multiple_of(i * CHUNK, CHUNK)
        rows = pl.ds(at, CHUNK)
        owner = band_of_rows(row_at, at, CHUNK)
        mine = owner == me[0]
        near = owner == lax.bitwise_xor(me[0], 1)
        for plane in range(2):
            own = shifted_left(window[plane, rows, :].astype(jnp.float32), amount)
            beside = sib_v[plane, rows, :].astype(jnp.float32)
            beyond = far_v[plane, rows, :].astype(jnp.float32)
            patch = jnp.where(mine, own, jnp.where(near, beside, beyond))
            twice[plane, rows, :] = patch
            twice[plane, pl.ds(pl.multiple_of(at + PATCH, CHUNK), CHUNK), :] = patch
        return carry

    lax.fori_loop(0, PATCH // CHUNK, assemble, 0)
    copies[3].wait()

    def illuminate(i, carry):
        at = pl.multiple_of(i * CHUNK, CHUNK)
        rows = pl.ds(at, CHUNK)
        patch_real = rows_from(twice, 0, at + down, CHUNK)
        patch_imag = rows_from(twice, 1, at + down, CHUNK)
        patch_v[0, rows, :] = patch_real.astype(jnp.bfloat16)
        patch_v[1, rows, :] = patch_imag.astype(jnp.bfloat16)
        probe_real = probe_v[0, rows, :]
        probe_imag = probe_v[1, rows, :]
        field[rows, :] = (probe_real * patch_real - probe_imag * patch_imag).astype(jnp.bfloat16)
        field[pl.ds(pl.multiple_of(at + PATCH, CHUNK), CHUNK), :] = (
            probe_real * patch_imag + probe_imag * patch_real
        ).astype(jnp.bfloat16)
        return carry

    lax.fori_loop(0, PATCH // CHUNK, illuminate, 0)
    copies[4].wait()

    def over_rows(table):
        for k in range(4):
            part = jnp.dot(
                table[256 * k : 256 * (k + 1), :], field[...], preferred_element_type=jnp.float32
            ).astype(jnp.bfloat16)
            half[256 * (k % 2) : 256 * (k % 2 + 1), PATCH * (k // 2) : PATCH * (k // 2 + 1)] = part

    over_rows(left_v)
    copies[5].wait()
    copies[6].wait()
    for k in range(2):
        rows = slice(256 * k, 256 * (k + 1))
        far = jnp.dot(half[rows, :], right_v[...], preferred_element_type=jnp.float32)
        far_real = far[:, :PATCH]
        far_imag = far[:, PATCH:]
        power = far_real * far_real + far_imag * far_imag
        keep = 1.0 - amp_v[rows, :].astype(jnp.float32) * lax.rsqrt(
            jnp.maximum(power, MAGNITUDE_FLOOR * MAGNITUDE_FLOOR)
        )
        field[rows, :] = (far_real * keep).astype(jnp.bfloat16)
        field[PATCH + 256 * k : PATCH + 256 * (k + 1), :] = (far_imag * keep).astype(jnp.bfloat16)
    over_rows(right_v)
    if has_term:
        copies[7].wait()
    for k in range(2):
        rows = slice(256 * k, 256 * (k + 1))
        back = jnp.dot(half[rows, :], left_v[...], preferred_element_type=jnp.float32)
        back_real = back[:, :PATCH]
        back_imag = back[:, PATCH:]
        patch_real = patch_v[0, rows, :].astype(jnp.float32)
        patch_imag = patch_v[1, rows, :].astype(jnp.float32)
        term_real = patch_real * back_real + patch_imag * back_imag
        term_imag = patch_real * back_imag - patch_imag * back_real
        if has_term:
            term_real = term_real + term_v[0, rows, :]
            term_imag = term_imag + term_v[1, rows, :]
        term[0, rows, :] = term_real
        term[1, rows, :] = term_imag
        term_v[0, rows, :] = back_real
        term_v[1, rows, :] = back_imag

    def weigh(i, carry):
        at = pl.multiple_of(i * CHUNK, CHUNK)
        rows = pl.ds(at, CHUNK)
        again = pl.ds(pl.multiple_of(at + PATCH, CHUNK), CHUNK)
        probe_real = probe_v[0, rows, :]
        probe_imag = probe_v[1, rows, :]
        back_real = term_v[0, rows, :]
        back_imag = term_v[1, rows, :]
        grad_real = probe_real * back_real + probe_imag * back_imag
        grad_imag = probe_real * back_imag - probe_imag * back_real
        twice[0, rows, :] = grad_real
        twice[0, again, :] = grad_real
        twice[1, rows, :] = grad_imag
        twice[1, again, :] = grad_imag
        return carry

    lax.fori_loop(0, PATCH // CHUNK, weigh, 0)
    classes, height = grad.shape[0], grad.shape[2]

    def spread(k, carry):
        for plane in range(2):
            grad[k, plane] = rows_from(twice, plane, PATCH - down + k * height, height).astype(
                jnp.bfloat16
            )
        return carry

    lax.fori_loop(0, classes, spread, 0)


def wave(which, classes, pos, me, band, sibling, across, probe, amplitudes, left, right, term):
    has_term = term is not None
    operands = [band, sibling, across, probe, amplitudes, left, right] + ([term] if has_term else [])
    smem = pl.BlockSpec(memory_space=pltpu.SMEM)
    hbm = pl.BlockSpec(memory_space=pl.ANY)
    vmem = pl.BlockSpec(memory_space=pltpu.VMEM)
    planes = (2, PATCH, PATCH)
    return pl.pallas_call(
        functools.partial(wave_kernel, which, has_term),
        in_specs=[smem, smem] + [hbm] * len(operands),
        out_specs=[vmem, vmem],
        out_shape=[
            jax.ShapeDtypeStruct((classes, 2, PATCH // classes, PATCH), jnp.bfloat16),
            jax.ShapeDtypeStruct(planes, jnp.float32),
        ],
        scratch_shapes=[
            pltpu.VMEM((2, PATCH, WIDE), jnp.bfloat16),
            pltpu.VMEM(planes, jnp.bfloat16),
            pltpu.VMEM(planes, jnp.bfloat16),
            pltpu.VMEM(planes, jnp.float32),
            pltpu.VMEM((PATCH, PATCH), jnp.bfloat16),
            pltpu.VMEM((2 * PATCH, 2 * PATCH), jnp.bfloat16),
            pltpu.VMEM((2 * PATCH, 2 * PATCH), jnp.bfloat16),
            pltpu.VMEM(planes, jnp.float32),
            pltpu.VMEM(planes, jnp.bfloat16),
            pltpu.VMEM((2, 2 * PATCH + SUBLANES, PATCH), jnp.float32),
            pltpu.VMEM((2 * PATCH, PATCH), jnp.bfloat16),
            pltpu.VMEM((PATCH, 2 * PATCH), jnp.bfloat16),
            pltpu.SemaphoreType.DMA((8,)),
        ],
        compiler_params=pltpu.CompilerParams(vmem_limit_bytes=VMEM_LIMIT),
        cost_estimate=pl.CostEstimate(
            flops=32 * PATCH**3, bytes_accessed=14000000, transcendentals=PATCH * PATCH
        ),
    )(pos, me, *operands)


def sum_kernel(pos, me, first, second, own, away, canvas):
    classes, height = first.shape[0], first.shape[2]
    start = me[1] * height
    canvas[...] = jnp.zeros_like(canvas)
    rows = lax.broadcasted_iota(jnp.int32, (2 * height, WIDE), 0)
    rows = start + jnp.where(rows >= height, rows - height, rows)

    def piece(k, source, which):
        index = 2 * k + which
        row_at = first_row(pos, index)
        col_at = first_col(pos, index)
        down = lax.rem(row_at, PATCH)
        at = pl.ds(pl.multiple_of(col_at // LANES * LANES, LANES), WIDE)
        data = source[k].astype(jnp.float32).reshape(2 * height, PATCH)
        data = jnp.concatenate([data, jnp.zeros((2 * height, LANES), jnp.float32)], 1)
        data = pltpu.roll(data, lax.rem(col_at, LANES), axis=1)

        @pl.when(down < start + height)
        def _():
            canvas[row_at // PATCH, :, at] += jnp.where(rows >= down, data, 0.0)

        @pl.when(down > start)
        def _():
            canvas[row_at // PATCH + 1, :, at] += jnp.where(rows < down, data, 0.0)

    def body(k, carry):
        piece(k, first, 0)
        piece(k, second, 1)
        return carry

    lax.fori_loop(0, classes, body, 0)
    shape = own.shape[1:]
    for k in range(2):
        keep = lax.bitwise_xor(me[0], 2 - 2 * k)
        give = lax.bitwise_xor(me[0], 3 - 2 * k)
        own[k] = canvas[keep].reshape(shape)
        away[k] = canvas[give].reshape(shape).astype(jnp.bfloat16)


def sum_pieces(pos, me, first, second, bands, width):
    height = first.shape[2]
    smem = pl.BlockSpec(memory_space=pltpu.SMEM)
    vmem = pl.BlockSpec(memory_space=pltpu.VMEM)
    shape = (2, 2, height, width)
    return pl.pallas_call(
        sum_kernel,
        in_specs=[smem, smem, vmem, vmem],
        out_specs=[vmem, vmem],
        out_shape=[
            jax.ShapeDtypeStruct(shape, jnp.float32),
            jax.ShapeDtypeStruct(shape, jnp.bfloat16),
        ],
        scratch_shapes=[pltpu.VMEM((bands, 2 * height, width), jnp.float32)],
        compiler_params=pltpu.CompilerParams(vmem_limit_bytes=VMEM_LIMIT),
        cost_estimate=pl.CostEstimate(
            flops=8 * first.size, bytes_accessed=4 * first.size + 6 * math.prod(shape), transcendentals=0
        ),
    )(pos, me, first, second)


def shards(object_image, probe, amplitudes, pos_tile, pos_offset):
    owners = lax.axis_size("obj")
    classes = lax.axis_size("pat")
    my_owner = lax.axis_index("obj").astype(jnp.int32)
    my_class = lax.axis_index("pat").astype(jnp.int32)
    me = jnp.stack([my_owner, my_class])
    height = PATCH // classes
    width = object_image.shape[2]
    assert owners == 4 and object_image.shape[1] == PATCH and pos_tile.shape[0] == 2

    def flip(value, bit):
        return lax.ppermute(value, "obj", [(k, k ^ bit) for k in range(owners)])

    own_pos = jnp.concatenate([pos_tile, pos_offset], 1)
    pos = lax.all_gather(own_pos, "obj", axis=0, tiled=True)
    pos_pat = lax.all_gather(own_pos, "pat", axis=0, tiled=True)

    relay = flip(cut(object_image, pos, me, (3,)), 1)
    across = [flip(cut_and_merge(object_image, relay, pos, me, k), 2) for k in range(2)]
    sibling = flip(cut(object_image, pos, me, (1,)), 1)

    left, right = dft_matrices(PATCH)
    grad_0, term = wave(
        0, classes, pos, me, object_image, sibling, across[0], probe, amplitudes, left, right, None
    )
    part_0 = lax.all_to_all(grad_0, "pat", split_axis=0, concat_axis=0, tiled=True)
    grad_1, term = wave(
        1, classes, pos, me, object_image, sibling, across[1], probe, amplitudes, left, right, term
    )
    part_1 = lax.all_to_all(grad_1, "pat", split_axis=0, concat_axis=0, tiled=True)

    own, away = sum_pieces(pos_pat, me, part_0, part_1, owners, width)
    from_sibling_far = flip(away[0], 1)
    from_sibling = flip(away[1], 1)
    from_across = flip(
        (own[0] + from_sibling_far.astype(jnp.float32)).astype(jnp.bfloat16), 2
    )
    total = own[1] + from_sibling.astype(jnp.float32) + from_across.astype(jnp.float32)
    mine = lax.dynamic_slice_in_dim(object_image, my_class * height, height, 1)
    updated = (mine.astype(jnp.float32) - OBJECT_RATE * total).astype(jnp.bfloat16)
    object_next = lax.all_gather(updated, "pat", axis=1, tiled=True)

    core = my_owner % 2
    line = my_owner // 2
    plane = lax.dynamic_index_in_dim(term, core, 0, False) + flip(
        lax.dynamic_index_in_dim(term, 1 - core, 0, False), 1
    )
    rows = plane.shape[0] // 2
    quarter = lax.dynamic_slice_in_dim(plane, line * rows, rows, 0) + flip(
        lax.dynamic_slice_in_dim(plane, (1 - line) * rows, rows, 0), 2
    )
    quarter = lax.psum(quarter, "pat")
    quarters = lax.all_gather(quarter, "obj", axis=0)
    probe_total = quarters.reshape(2, 2, rows, PATCH).transpose(1, 0, 2, 3).reshape(2, PATCH, PATCH)
    probe_next = probe - PROBE_RATE * probe_total
    return (object_next, probe_next)


def solution(mesh):
    return jax.shard_map(
        shards,
        mesh=mesh,
        in_specs=(
            P(None, "obj", None),
            P(),
            P(("pat", "obj"), None, None),
            P(("pat", "obj"), None),
            P(("pat", "obj"), None),
        ),
        out_specs=(P(None, "obj", None), P()),
        check_vma=False,
    )
```

time: 863 us -> 375 us (0.43)
  local copies, waits for them, and re-layouts: 308 us -> 16.1 us
  waiting for transfers between devices: 395 us -> 215 us
  other arithmetic: 88.9 us -> 30.2 us
  Pallas kernels: 0 us -> 55.7 us
  blocking collectives: 6.38 us -> 27.5 us
  matrix products: 19.4 us -> 0 us
    dynamic_update_slice x4 -> x0, local copies, waits for them, and re-layouts: 197 us -> none  [place(): lax.dynamic_update_slice(accumulated, current + patch_grad[item_index], c...]
    psum x2 -> x1, waiting for transfers between devices: 226 us -> 43.8 us  [shards(): quarter = lax.psum(quarter, 'pat')]
    all_to_all x2, waiting for transfers between devices: 168 us -> 24.6 us  [the longest x1 24.6 us: shards(): lax.all_to_all(grad_1, 'pat', split_axis=0, concat_axis=0, tiled=True)]
    all_gather x0 -> x2, waiting for transfers between devices: none -> 93.2 us  [the longest x1 93.2 us: shards(): object_next = lax.all_gather(updated, 'pat', axis=1, tiled=True)]
    pallas_call x0 -> x7, Pallas kernels: none -> 55.7 us  [the longest x2 27.4 us: wave(): pl.pallas_call(functools.partial(wave_kernel, which, has_term), in_specs=...]
    ppermute x0 -> x9, waiting for transfers between devices: none -> 53.2 us  [flip(): return lax.ppermute(value, 'obj', [(k, k ^ bit) for k in range(owners)])]
    gather x22 -> x0, local copies, waits for them, and re-layouts: 36.2 us -> none
    all_gather x0 -> x2, blocking collectives: none -> 27.5 us  [the longest x1 21.1 us: shards(): pos_pat = lax.all_gather(own_pos, 'pat', axis=0, tiled=True)]
  transfers between devices with their start and end apart: 4 -> 14, of which waited for: 4 -> 8; matrix products, arithmetic and copies ran while one was open for 6% -> 9% of each run, Pallas kernels for 0% -> 10%
where the time goes in v1:
time: 375 us; the launch traced here: 374 us
  waiting for transfers between devices  215 us (57%)
  Pallas kernels  55.7 us (15%)
  other arithmetic  30.2 us (8%)
  blocking collectives  27.5 us (7%)
  starting transfers between devices  16.1 us (4%)
  local copies, waits for them, and re-layouts  16.1 us (4%)
  between operations  13.9 us (4%)
    all_gather x1, waiting for transfers between devices, shards(): object_next = lax.all_gather(updated, 'pat', axis=1, tiled=True)  93.2 us
    ppermute x9, waiting for transfers between devices, flip(): return lax.ppermute(value, 'obj', [(k, k ^ bit) for k in range(owners)])  53.2 us
    psum x1, waiting for transfers between devices, shards(): quarter = lax.psum(quarter, 'pat')  43.8 us
    pallas_call x2, Pallas kernels, wave(): pl.pallas_call(functools.partial(wave_kernel, which, has_term), in_specs=...  27.4 us
    all_to_all x1, waiting for transfers between devices, shards(): lax.all_to_all(grad_1, 'pat', split_axis=0, concat_axis=0, tiled=True)  24.6 us
    all_gather x1, blocking collectives, shards(): pos_pat = lax.all_gather(own_pos, 'pat', axis=0, tiled=True)  21.1 us
    unnamed x19, local copies, waits for them, and re-layouts  11.7 us
    pallas_call x2, Pallas kernels, cut(): pl.pallas_call(functools.partial(cut_kernel, flips), grid_spec=pltpu.Pref...  11.2 us
  transfers between devices with their start and end apart: 14, of which 8 were waited for; matrix products, arithmetic and copies ran while one was open for 9% of the time, Pallas kernels for 10%

profile of v1, /device:TPU:0, one launch (start us, length us, event | category | flops | bytes accessed | tf_op | source)
XLA Modules:
  0.0 374.3 jit_solution(368438173534523135)
XLA Ops:
  7.9 6.4 %all-gather.1 = s32[4,2,4]{2,1,0:T(2,128)} all-gather(s32[1,2,4]{2,1,0:T(2,128)S(1)} %add_bitcast_fusion.1), channel_id=1, replica_groups=mesh['pat'=8,'obj'=4] {'obj'}, dimensions={0}, use_global_device_ids=true | all-gather | bytes 160 | tf_op jit(solution)/shard_map/all_gather | solution.py:403
  15.0 5.6 %shard_map.69 = bf16[2,2,512,512]{3,2,1,0:T(8,128)(2,1)} custom-call(s32[8,4]{1,0:T(8,128)} %bitcast.36, s32[2]{0:T(128)} %pad_add_fusion.me, bf16[2,512,3072]{2,1,0:T(8,128)(2,1)} %band.3, bf16[2,512,3072]{2,1,0:T(8,128)(2,1)} %band.3, bf16[2,512,3072]{2,1,0:T(8,128)(2,1)} %band.3, bf16[2,512,3072]{2,1,0:T(8,128)(2,1)} %band.3, bf16[2,512,3072]{2,1,0:T(8,128)(2,1)} %band.3), custom_call_target="tpu_custom_call" | custom-call | flops 1310720 | bytes 4600000 | tf_op jit(solution)/shard_map/pallas_call | solution.py:98
  21.0 5.6 %shard_map.68 = bf16[2,2,512,512]{3,2,1,0:T(8,128)(2,1)} custom-call(s32[8,4]{1,0:T(8,128)} %bitcast.37, s32[2]{0:T(128)} %pad_add_fusion.me, bf16[2,512,3072]{2,1,0:T(8,128)(2,1)} %band.3, bf16[2,512,3072]{2,1,0:T(8,128)(2,1)} %band.3, bf16[2,512,3072]{2,1,0:T(8,128)(2,1)} %band.3, bf16[2,512,3072]{2,1,0:T(8,128)(2,1)} %band.3, bf16[2,512,3072]{2,1,0:T(8,128)(2,1)} %band.3), custom_call_target="tpu_custom_call" | custom-call | flops 1310720 | bytes 4600000 | tf_op jit(solution)/shard_map/pallas_call | solution.py:98
  26.8 1.3 copy-done.1
  28.1 4.7 %shard_map.70 = bf16[2,512,512]{2,1,0:T(8,128)(2,1)} custom-call(s32[8,4]{1,0:T(8,128)} %bitcast.38, s32[2]{0:T(128)} %pad_add_fusion.me, bf16[2,512,3072]{2,1,0:T(8,128)(2,1)} %band.3, bf16[2,512,3072]{2,1,0:T(8,128)(2,1)} %band.3, bf16[2,512,3072]{2,1,0:T(8,128)(2,1)} %band.3, bf16[2,512,3072]{2,1,0:T(8,128)(2,1)} %band.3, bf16[2,512,3072]{2,1,0:T(8,128)(2,1)} %band.3, ...), custom_call_target="tpu_custom_call" | custom-call | flops 655360 | bytes 3300000 | tf_op jit(solution)/shard_map/pallas_call | solution.py:140
  32.8 2.0 collective-permute-start.2
  34.8 4.7 %shard_map.72 = bf16[2,512,512]{2,1,0:T(8,128)(2,1)} custom-call(s32[8,4]{1,0:T(8,128)} %bitcast.39, s32[2]{0:T(128)} %pad_add_fusion.me, bf16[2,512,3072]{2,1,0:T(8,128)(2,1)} %band.3, bf16[2,512,3072]{2,1,0:T(8,128)(2,1)} %band.3, bf16[2,512,3072]{2,1,0:T(8,128)(2,1)} %band.3, bf16[2,512,3072]{2,1,0:T(8,128)(2,1)} %band.3, bf16[2,512,3072]{2,1,0:T(8,128)(2,1)} %band.3, ...), custom_call_target="tpu_custom_call" | custom-call | flops 655360 | bytes 3300000 | tf_op jit(solution)/shard_map/pallas_call | solution.py:140
  39.5 4.0 %fusion.13 = bf16[512,512]{1,0:T(8,128)(2,1)S(1)} fusion(), kind=kLoop, calls=%fused_computation.31 | loop fusion | flops 5242880 | bytes 524288 | tf_op jit(solution)/shard_map/neg | solution.py:30
  43.5 4.4 %multiply_convert_fusion = (bf16[512,512]{1,0:T(8,128)(2,1)S(1)}, bf16[512,512]{1,0:T(8,128)(2,1)S(1)}) fusion(), kind=kLoop, calls=%fused_computation.23 | loop fusion | flops 4980736 | bytes 1048576 | tf_op jit(solution)/shard_map/convert_element_type | solution.py:29
  47.9 10.1 %fusion.1 = (bf16[1024,1024]{1,0:T(8,128)(2,1)}, bf16[1024,1024]{1,0:T(8,128)(2,1)}) fusion(bf16[512,512]{1,0:T(8,128)(2,1)S(1)} %get-tuple-element.19, bf16[512,512]{1,0:T(8,128)(2,1)S(1)} %fusion.13, bf16[512,512]{1,0:T(8,128)(2,1)S(1)} %get-tuple-element.18), kind=kLoop, calls=%fused_computation.5 | loop fusion | flops 14680064 | bytes 5767168 | tf_op jit(solution)/shard_map/concatenate | solution.py:35
  59.9 13.5 %shard_map.71 = (bf16[8,2,64,512]{3,2,1,0:T(8,128)(2,1)}, f32[2,512,512]{2,1,0:T(8,128)}) custom-call(s32[8,4]{1,0:T(8,128)} %bitcast.40, s32[2]{0:T(128)} %pad_add_fusion.me, bf16[2,512,3072]{2,1,0:T(8,128)(2,1)} %band.3, bf16[2,2,512,512]{3,2,1,0:T(8,128)(2,1)} %copy-done.2, bf16[2,512,512]{2,1,0:T(8,128)(2,1)} %copy-done.8, f32[2,512,512]{2,1,0:T(8,128)} %probe.3, ...), custom_call_target="tpu_custom_call" | custom-call | flops 4294967296 | bytes 14000000 | tf_op jit(solution)/shard_map/pallas_call | solution.py:299
  73.5 7.6 %collective-permute-done.3.across = bf16[2,512,512]{2,1,0:T(8,128)(2,1)S(1)} collective-permute-done((bf16[2,512,512]{2,1,0:T(8,128)(2,1)}, bf16[2,512,512]{2,1,0:T(8,128)(2,1)S(1)}, u32[]{:S(2)}, u32[]{:S(2)}) %collective-permute-start.3) | collective-permute-done | bytes 1048608 | tf_op jit(solution)/shard_map/ppermute | solution.py:400
  82.1 13.8 %shard_map.73 = (bf16[8,2,64,512]{3,2,1,0:T(8,128)(2,1)}, f32[2,512,512]{2,1,0:T(8,128)}) custom-call(s32[8,4]{1,0:T(8,128)} %bitcast.41, s32[2]{0:T(128)} %pad_add_fusion.me, bf16[2,512,3072]{2,1,0:T(8,128)(2,1)} %band.3, bf16[2,2,512,512]{3,2,1,0:T(8,128)(2,1)} %copy-done.2, bf16[2,512,512]{2,1,0:T(8,128)(2,1)} %copy-done.7, f32[2,512,512]{2,1,0:T(8,128)} %probe.3, ...), custom_call_target="tpu_custom_call" | custom-call | flops 4294967296 | bytes 14000000 | tf_op jit(solution)/shard_map/pallas_call | solution.py:299
  96.0 6.2 %all-to-all-start.1 = ((bf16[8,2,64,512]{3,2,1,0:T(8,128)(2,1)}), bf16[8,2,64,512]{3,2,1,0:T(8,128)(2,1)S(1)}, u32[]{:S(2)}, u32[]{:S(2)}) async-start(bf16[8,2,64,512]{3,2,1,0:T(8,128)(2,1)} %get-tuple-element.10), calls=%async_computation.1 | async-start | bytes 2097152 | tf_op jit(solution)/shard_map/all_to_all | solution.py:418
  103.2 24.6 %all-to-all-done.1.second = bf16[8,2,64,512]{3,2,1,0:T(8,128)(2,1)S(1)} async-done(((bf16[8,2,64,512]{3,2,1,0:T(8,128)(2,1)}), bf16[8,2,64,512]{3,2,1,0:T(8,128)(2,1)S(1)}, u32[]{:S(2)}, u32[]{:S(2)}) %all-to-all-start.1) | async-done | bytes 1048608 | tf_op jit(solution)/shard_map/all_to_all | solution.py:418
  127.8 3.6 all-to-all-start
  131.4 1.8 bitcast_add_fusion.2
  134.0 1.5 collective-permute-start.8
  135.6 12.1 %collective-permute-done.8 = f32[256,512]{1,0:T(8,128)S(1)} collective-permute-done((f32[256,512]{1,0:T(8,128)}, f32[256,512]{1,0:T(8,128)S(1)}, u32[]{:S(2)}, u32[]{:S(2)}) %collective-permute-start.8) | collective-permute-done | bytes 524320 | tf_op jit(solution)/shard_map/ppermute | solution.py:400
  148.7 21.1 %all-gather = s32[8,2,4]{2,1,0:T(2,128)} all-gather(s32[1,2,4]{2,1,0:T(2,128)S(1)} %add_bitcast_fusion.1), channel_id=1, replica_groups=mesh['pat'=8,'obj'=4] {'pat'}, dimensions={0}, use_global_device_ids=true | all-gather | bytes 288 | tf_op jit(solution)/shard_map/all_gather | solution.py:404
  170.7 7.7 %shard_map.74 = (f32[2,2,64,3072]{3,2,1,0:T(8,128)}, bf16[2,2,64,3072]{3,2,1,0:T(8,128)(2,1)}) custom-call(s32[16,4]{1,0:T(8,128)} %bitcast.42, s32[2]{0:T(128)} %pad_add_fusion.me, bf16[8,2,64,512]{3,2,1,0:T(8,128)(2,1)} %copy-done.4, bf16[8,2,64,512]{3,2,1,0:T(8,128)(2,1)} %copy-done.3), custom_call_target="tpu_custom_call" | custom-call | flops 4194304 | bytes 6815744 | tf_op jit(solution)/shard_map/pallas_call | solution.py:373
  178.4 43.8 %all-reduce.2.cloned.1.call-done = f32[1,256,512]{2,1,0:T(8,128)} async-done(((f32[1,256,512]{2,1,0:T(8,128)}), f32[1,256,512]{2,1,0:T(8,128)}) %all-reduce.2.cloned.1.call-update) | async-done | bytes 524304 | tf_op jit(solution)/shard_map/psum | solution.py:440
  222.5 2.4 slice_bitcast_fusion.1
  225.4 2.9 collective-permute-done.5
  229.3 1.5 collective-permute-start.6
  230.8 29.7 %collective-permute-done.6 = bf16[2,64,3072]{2,1,0:T(8,128)(2,1)} collective-permute-done((bf16[2,64,3072]{2,1,0:T(8,128)(2,1)}, bf16[2,64,3072]{2,1,0:T(8,128)(2,1)}, u32[]{:S(2)}, u32[]{:S(2)}) %collective-permute-start.6) | collective-permute-done | bytes 786464 | tf_op jit(solution)/shard_map/ppermute | solution.py:400
  260.5 2.9 fusion.6
  263.4 1.8 broadcast_multiply_fusion
  265.5 1.4 copy-done
  266.9 1.8 bitcast_subtract_fusion
  268.7 93.2 %all-gather.5.cloned.1.call-done = bf16[2,512,3072]{2,1,0:T(8,128)(2,1)} async-done(((bf16[2,64,3072]{2,1,0:T(8,128)(2,1)}), bf16[2,512,3072]{2,1,0:T(8,128)(2,1)}) %all-gather.5.cloned.1.call-update) | async-done | bytes 6291472 | tf_op jit(solution)/shard_map/all_gather | solution.py:429
  361.9 5.9 %copy.11 = bf16[2,512,3072]{2,1,0:T(8,128)(2,1)} copy(bf16[2,512,3072]{2,1,0:T(8,128)(2,1)} %all-gather.5.cloned.1.call-done) | data formatting | bytes 12582912
  (42 shorter events, 10.8 us)
Async XLA Ops:
  20.6 6.1 %collective-permute-start.1 = (bf16[2,2,512,512]{3,2,1,0:T(8,128)(2,1)}, bf16[2,2,512,512]{3,2,1,0:T(8,128)(2,1)S(1)}, u32[]{:S(2)}, u32[]{:S(2)}) collective-permute-start(bf16[2,2,512,512]{3,2,1,0:T(8,128)(2,1)} %shard_map.69), channel_id=1, source_target_pairs={{0,1},{1,0},{2,3},{3,2},{4,5},{5,4},{6,7},{7,6},{8,9},{9,8},{10,11... | collective-permute-start | bytes 6291464 | tf_op jit(solution)/shard_map/ppermute | solution.py:400
  26.6 31.4 %collective-permute-start = (bf16[2,2,512,512]{3,2,1,0:T(8,128)(2,1)}, bf16[2,2,512,512]{3,2,1,0:T(8,128)(2,1)S(1)}, u32[]{:S(2)}, u32[]{:S(2)}) collective-permute-start(bf16[2,2,512,512]{3,2,1,0:T(8,128)(2,1)} %shard_map.68), channel_id=1, source_target_pairs={{0,1},{1,0},{2,3},{3,2},{4,5},{5,4},{6,7},{7,6},{8,9},{9,8},{10,11... | collective-permute-start | bytes 6291464 | tf_op jit(solution)/shard_map/ppermute | solution.py:400
  26.8 1.3 copy-start.1
  32.8 26.2 %collective-permute-start.2 = (bf16[2,512,512]{2,1,0:T(8,128)(2,1)}, bf16[2,512,512]{2,1,0:T(8,128)(2,1)S(1)}, u32[]{:S(2)}, u32[]{:S(2)}) collective-permute-start(bf16[2,512,512]{2,1,0:T(8,128)(2,1)} %shard_map.70), channel_id=1, source_target_pairs={{0,2},{1,3},{2,0},{3,1},{4,6},{5,7},{6,4},{7,5},{8,10},{9,11},{10,... | collective-permute-start | bytes 3145736 | tf_op jit(solution)/shard_map/ppermute | solution.py:400
  39.5 41.6 %collective-permute-start.3 = (bf16[2,512,512]{2,1,0:T(8,128)(2,1)}, bf16[2,512,512]{2,1,0:T(8,128)(2,1)S(1)}, u32[]{:S(2)}, u32[]{:S(2)}) collective-permute-start(bf16[2,512,512]{2,1,0:T(8,128)(2,1)} %shard_map.72), channel_id=1, source_target_pairs={{0,2},{1,3},{2,0},{3,1},{4,6},{5,7},{6,4},{7,5},{8,10},{9,11},{10,... | collective-permute-start | bytes 3145736 | tf_op jit(solution)/shard_map/ppermute | solution.py:400
  58.0 1.3 copy-start.2
  58.9 1.0 copy-start.8
  81.1 1.0 copy-start.7
  96.0 6.2 %copy-start.6 = (f32[2,512,512]{2,1,0:T(8,128)S(1)}, f32[2,512,512]{2,1,0:T(8,128)}, u32[]{:S(2)}) copy-start(f32[2,512,512]{2,1,0:T(8,128)} %get-tuple-element.13) | copy-start | bytes 6291460
  96.0 31.8 %all-to-all-start.1 = ((bf16[8,2,64,512]{3,2,1,0:T(8,128)(2,1)}), bf16[8,2,64,512]{3,2,1,0:T(8,128)(2,1)S(1)}, u32[]{:S(2)}, u32[]{:S(2)}) async-start(bf16[8,2,64,512]{3,2,1,0:T(8,128)(2,1)} %get-tuple-element.10), calls=%async_computation.1 | async-start | bytes 2097152 | tf_op jit(solution)/shard_map/all_to_all | solution.py:418
  103.2 28.2 %collective-permute-start.7 = (f32[512,512]{1,0:T(8,128)}, f32[512,512]{1,0:T(8,128)}, u32[]{:S(2)}, u32[]{:S(2)}) collective-permute-start(f32[512,512]{1,0:T(8,128)} %dynamic-slice_bitcast_fusion), channel_id=1, source_target_pairs={{0,1},{1,0},{2,3},{3,2},{4,5},{5,4},{6,7},{7,6},{8,9},{9,8},{10,11... | collective-permute-start | bytes 3145736 | tf_op jit(solution)/shard_map/ppermute | solution.py:400
  127.8 5.4 %copy-start.3 = (bf16[8,2,64,512]{3,2,1,0:T(8,128)(2,1)}, bf16[8,2,64,512]{3,2,1,0:T(8,128)(2,1)S(1)}, u32[]{:S(2)}) copy-start(bf16[8,2,64,512]{3,2,1,0:T(8,128)(2,1)S(1)} %all-to-all-done.1.second) | copy-start | bytes 3145732
  127.8 41.9 %all-to-all-start = ((bf16[8,2,64,512]{3,2,1,0:T(8,128)(2,1)}), bf16[8,2,64,512]{3,2,1,0:T(8,128)(2,1)S(1)}, u32[]{:S(2)}, u32[]{:S(2)}) async-start(bf16[8,2,64,512]{3,2,1,0:T(8,128)(2,1)} %get-tuple-element.8), calls=%async_computation | async-start | bytes 2097152 | tf_op jit(solution)/shard_map/all_to_all | solution.py:414
  131.3 90.8 %all-reduce.2.cloned.1.call-start = ((), (), s32[]{:S(2)}) async-start(), calls=%async_computation.3 | async-start | bytes 1048576 | tf_op jit(solution)/shard_map/psum | solution.py:440
  134.0 13.6 %collective-permute-start.8 = (f32[256,512]{1,0:T(8,128)}, f32[256,512]{1,0:T(8,128)S(1)}, u32[]{:S(2)}, u32[]{:S(2)}) collective-permute-start(f32[256,512]{1,0:T(8,128)} %constant_dynamic-slice_fusion), channel_id=1, source_target_pairs={{0,2},{1,3},{2,0},{3,1},{4,6},{5,7},{6,4},{7,5},{8,10},{9,11},{10,... | collective-permute-start | bytes 1572872 | tf_op jit(solution)/shard_map/ppermute | solution.py:400
  148.6 114.8 %all-gather.7.cloned.1.call-start = ((), (), s32[]{:S(2)}) async-start(), calls=%async_computation.4 | async-start | bytes 2621440 | tf_op jit(solution)/shard_map/all_gather | solution.py:441
  169.7 1.0 copy-start.4
  178.4 49.8 %copy-start.5 = (f32[2,2,64,3072]{3,2,1,0:T(8,128)S(1)}, f32[2,2,64,3072]{3,2,1,0:T(8,128)}, u32[]{:S(2)}) copy-start(f32[2,2,64,3072]{3,2,1,0:T(8,128)} %get-tuple-element.11) | copy-start | bytes 9437188
  222.2 139.6 %all-gather.5.cloned.1.call-start = ((), (), s32[]{:S(2)}) async-start(), calls=%async_computation.2 | async-start | bytes 7077888 | tf_op jit(solution)/shard_map/all_gather | solution.py:429
  224.9 3.4 collective-permute-start.5
  224.9 5.9 %collective-permute-start.4 = (bf16[2,64,3072]{2,1,0:T(8,128)(2,1)}, bf16[2,64,3072]{2,1,0:T(8,128)(2,1)}, u32[]{:S(2)}, u32[]{:S(2)}) collective-permute-start(bf16[2,64,3072]{2,1,0:T(8,128)(2,1)} %get-tuple-element.14), channel_id=1, source_target_pairs={{0,1},{1,0},{2,3},{3,2},{4,5},{5,4},{6,7},{7,6},{8,9},{9,8},{10,11... | collective-permute-start | bytes 2359304 | tf_op jit(solution)/shard_map/ppermute | solution.py:400
  229.3 31.1 %collective-permute-start.6 = (bf16[2,64,3072]{2,1,0:T(8,128)(2,1)}, bf16[2,64,3072]{2,1,0:T(8,128)(2,1)}, u32[]{:S(2)}, u32[]{:S(2)}) collective-permute-start(bf16[2,64,3072]{2,1,0:T(8,128)(2,1)} %fusion.2), channel_id=1, source_target_pairs={{0,2},{1,3},{2,0},{3,1},{4,6},{5,7},{6,4},{7,5},{8,10},{9,11},{10,... | collective-permute-start | bytes 2359304 | tf_op jit(solution)/shard_map/ppermute | solution.py:400
  265.3 1.6 copy-start
Sparse Core Ops, SparseCore 0:
  148.7 73.4 all-reduce.1
  223.8 33.0 all-gather.6
  263.5 98.2 all-gather.4

commit v2 on v1

--- a/solution.py
+++ b/solution.py
@@ -16,10 +16,12 @@
 OBJECT_RATE = 0.1
 PROBE_RATE = 0.05
 MAGNITUDE_FLOOR = 0.5
-VMEM_LIMIT = 56 * 1024 * 1024
-
-
-def dft_matrices(length):
+CUT_VMEM = 14 * 1024 * 1024
+WAVE_VMEM = 32 * 1024 * 1024
+SUM_VMEM = 24 * 1024 * 1024
+
+
+def dft_tables(length):
     counter = jnp.arange(length, dtype=jnp.int32)
     phase_angle = (counter[:, None] * counter[None, :] % length).astype(jnp.float32) * (
         2.0 * math.pi / length
@@ -27,13 +29,7 @@
     factor = 1.0 / math.sqrt(length)
     cosine = (jnp.cos(phase_angle) * factor).astype(jnp.bfloat16)
     sine_part = (-jnp.sin(phase_angle) * factor).astype(jnp.bfloat16)
-    top = jnp.concatenate([cosine, -sine_part], 1)
-    bottom = jnp.concatenate([sine_part, cosine], 1)
-    left = jnp.concatenate([top, bottom], 0)
-    top = jnp.concatenate([cosine, sine_part], 1)
-    bottom = jnp.concatenate([-sine_part, cosine], 1)
-    right = jnp.concatenate([top, bottom], 0)
-    return left, right
+    return cosine, sine_part, -sine_part
 
 
 def first_row(pos, index):
@@ -44,8 +40,21 @@
     return pos[index, 1] * TILE + pos[index, 3]
 
 
-def shifted_left(wide, amount):
-    return pltpu.roll(wide, lax.rem(WIDE - amount, WIDE), axis=1)[:, :PATCH]
+def shifted_left(blocks, amount):
+    turned = [pltpu.roll(b, lax.rem(LANES - amount, LANES), axis=1) for b in blocks]
+    lane = lax.broadcasted_iota(jnp.int32, turned[0].shape, 1)
+    stay = lane < LANES - amount
+    return jnp.concatenate([jnp.where(stay, a, b) for a, b in zip(turned, turned[1:])], 1)
+
+
+def shifted_right(data, amount):
+    count = data.shape[1] // LANES
+    turned = [pltpu.roll(data[:, LANES * k : LANES * (k + 1)], amount, axis=1) for k in range(count)]
+    lane = lax.broadcasted_iota(jnp.int32, turned[0].shape, 1)
+    stay = lane >= amount
+    before = [jnp.zeros_like(turned[0])] + turned
+    after = turned + [jnp.zeros_like(turned[0])]
+    return jnp.concatenate([jnp.where(stay, a, b) for a, b in zip(after, before)], 1)
 
 
 def band_of_rows(row_at, start, count):
@@ -59,44 +68,42 @@
 
 def rows_from(ref, plane, start, count):
     aligned = pl.multiple_of(start // SUBLANES * SUBLANES, SUBLANES)
-    tall = count + SUBLANES
-    data = ref[plane, pl.ds(aligned, tall), :]
-    return pltpu.roll(data, lax.rem(tall - lax.rem(start, SUBLANES), tall), axis=0)[:count]
-
-
-def cut_kernel(flips, pos, me, *refs):
-    step = pl.program_id(0)
+    amount = lax.rem(start, SUBLANES)
+    data = ref[plane, pl.ds(aligned, count + SUBLANES), :]
+    data = data.reshape(count // SUBLANES + 1, SUBLANES, data.shape[1])
+    turned = pltpu.roll(data, lax.rem(SUBLANES - amount, SUBLANES), axis=1)
+    row = lax.broadcasted_iota(jnp.int32, turned[1:].shape, 1)
+    data = jnp.where(row < SUBLANES - amount, turned[:-1], turned[1:])
+    return data.reshape(count, data.shape[2])
+
+
+def cut_rows(blocks, plane, rows, amount):
+    return shifted_left([b[plane, rows, :].astype(jnp.float32) for b in blocks], amount)
+
+
+def cut_kernel(flip, first, pos, me, *refs):
     blocks, out = refs[:-1], refs[-1]
-    target = lax.bitwise_xor(me[0], flips[0])
-    for k in range(1, len(flips)):
-        target = jnp.where(step // 2 == k, lax.bitwise_xor(me[0], flips[k]), target)
-    amount = lax.rem(first_col(pos, 2 * target + lax.rem(step, 2)), LANES)
+    target = lax.bitwise_xor(me[0], flip)
+    amount = lax.rem(first_col(pos, 2 * target + first + pl.program_id(0)), LANES)
 
     def body(i, carry):
         rows = pl.ds(pl.multiple_of(i * CHUNK, CHUNK), CHUNK)
         for plane in range(2):
-            wide = jnp.concatenate([b[plane, rows, :] for b in blocks], 1)
-            out[0, plane, rows, :] = shifted_left(wide.astype(jnp.float32), amount).astype(
-                jnp.bfloat16
-            )
+            out[0, plane, rows, :] = cut_rows(blocks, plane, rows, amount).astype(jnp.bfloat16)
         return carry
 
     lax.fori_loop(0, PATCH // CHUNK, body, 0)
 
 
-def cut(band, pos, me, flips):
+def cut(band, pos, me, flip, first, count):
     def block(k):
         def index(i, pos, me):
-            target = lax.bitwise_xor(me[0], flips[0])
-            for j in range(1, len(flips)):
-                target = jnp.where(i // 2 == j, lax.bitwise_xor(me[0], flips[j]), target)
-            return (0, 0, first_col(pos, 2 * target + lax.rem(i, 2)) // LANES + k)
+            return (0, 0, first_col(pos, 2 * lax.bitwise_xor(me[0], flip) + first + i) // LANES + k)
 
         return pl.BlockSpec((2, PATCH, LANES), index)
 
-    count = 2 * len(flips)
     return pl.pallas_call(
-        functools.partial(cut_kernel, flips),
+        functools.partial(cut_kernel, flip, first),
         grid_spec=pltpu.PrefetchScalarGridSpec(
             num_scalar_prefetch=2,
             grid=(count,),
@@ -104,7 +111,7 @@
             out_specs=pl.BlockSpec((1, 2, PATCH, PATCH), lambda i, pos, me: (i, 0, 0, 0)),
         ),
         out_shape=jax.ShapeDtypeStruct((count, 2, PATCH, PATCH), jnp.bfloat16),
-        compiler_params=pltpu.CompilerParams(vmem_limit_bytes=VMEM_LIMIT),
+        compiler_params=pltpu.CompilerParams(vmem_limit_bytes=CUT_VMEM),
         cost_estimate=pl.CostEstimate(
             flops=count * 2 * PATCH * WIDE, bytes_accessed=count * 2300000, transcendentals=0
         ),
@@ -121,8 +128,7 @@
         rows = pl.ds(pl.multiple_of(i * CHUNK, CHUNK), CHUNK)
         mine = band_of_rows(row_at, i * CHUNK, CHUNK) == me[0]
         for plane in range(2):
-            wide = jnp.concatenate([b[plane, rows, :] for b in blocks], 1)
-            own = shifted_left(wide.astype(jnp.float32), amount)
+            own = cut_rows(blocks, plane, rows, amount)
             other = sibling[0, plane, rows, :].astype(jnp.float32)
             out[plane, rows, :] = jnp.where(mine, own, other).astype(jnp.bfloat16)
         return carry
@@ -143,22 +149,24 @@
             num_scalar_prefetch=2,
             grid=(1,),
             in_specs=[block(k) for k in range(WIDE // LANES)]
-            + [pl.BlockSpec((1, 2, PATCH, PATCH), lambda i, pos, me: (which, 0, 0, 0))],
+            + [pl.BlockSpec((1, 2, PATCH, PATCH), lambda i, pos, me: (0, 0, 0, 0))],
             out_specs=pl.BlockSpec((2, PATCH, PATCH), lambda i, pos, me: (0, 0, 0)),
         ),
         out_shape=jax.ShapeDtypeStruct((2, PATCH, PATCH), jnp.bfloat16),
-        compiler_params=pltpu.CompilerParams(vmem_limit_bytes=VMEM_LIMIT),
+        compiler_params=pltpu.CompilerParams(vmem_limit_bytes=CUT_VMEM),
         cost_estimate=pl.CostEstimate(
             flops=2 * PATCH * WIDE, bytes_accessed=3300000, transcendentals=0
         ),
     )(pos, me, *([band] * (WIDE // LANES)), sibling)
 
 
-def wave_kernel(which, has_term, pos, me, band, sibling, across, probe, amplitudes, left, right, *refs):
-    if has_term:
-        term_in, grad, term, *scratch = refs
+def wave_kernel(which, pos, me, spare, band, sibling, across, probe, amplitudes, *refs):
+    tables, refs = refs[:3], refs[3:]
+    last = which == 1
+    if last:
+        term_in, grad, keep_term, give_term, *scratch = refs
     else:
-        grad, term, *scratch = refs
+        grad, term_out, *scratch = refs
     window, sib_v, far_v, probe_v, amp_v, left_v, right_v, term_v, patch_v, twice, field, half, sems = scratch
     index = 2 * me[0] + which
     col_at = first_col(pos, index)
@@ -169,11 +177,14 @@
         (sibling.at[which], sib_v),
         (across, far_v),
         (probe, probe_v),
-        (left, left_v),
-        (right, right_v),
-        (amplitudes.at[which], amp_v),
     ]
-    if has_term:
+    cosine, sine, minus = tables
+    quarters = [(slice(0, PATCH), slice(0, PATCH)), (slice(0, PATCH), slice(PATCH, 2 * PATCH))]
+    quarters += [(slice(PATCH, 2 * PATCH), slice(0, PATCH)), (slice(PATCH, 2 * PATCH), slice(PATCH, 2 * PATCH))]
+    pairs += [(t, left_v.at[q]) for t, q in zip((cosine, minus, sine, cosine), quarters)]
+    pairs.append((amplitudes.at[which], amp_v))
+    pairs += [(t, right_v.at[q]) for t, q in zip((cosine, sine, minus, cosine), quarters)]
+    if last:
         pairs.append((term_in, term_v))
     copies = [pltpu.make_async_copy(a, b, sems.at[k]) for k, (a, b) in enumerate(pairs)]
     for copy in copies:
@@ -182,6 +193,7 @@
         copy.wait()
     amount = lax.rem(col_at, LANES)
     down = lax.rem(row_at, PATCH)
+    views = [window.at[:, :, LANES * k : LANES * (k + 1)] for k in range(WIDE // LANES)]
 
     def assemble(i, carry):
         at = pl.multiple_of(i * CHUNK, CHUNK)
@@ -190,7 +202,7 @@
         mine = owner == me[0]
         near = owner == lax.bitwise_xor(me[0], 1)
         for plane in range(2):
-            own = shifted_left(window[plane, rows, :].astype(jnp.float32), amount)
+            own = cut_rows(views, plane, rows, amount)
             beside = sib_v[plane, rows, :].astype(jnp.float32)
             beyond = far_v[plane, rows, :].astype(jnp.float32)
             patch = jnp.where(mine, own, jnp.where(near, beside, beyond))
@@ -217,7 +229,8 @@
         return carry
 
     lax.fori_loop(0, PATCH // CHUNK, illuminate, 0)
-    copies[4].wait()
+    for copy in copies[4:8]:
+        copy.wait()
 
     def over_rows(table):
         for k in range(4):
@@ -227,8 +240,8 @@
             half[256 * (k % 2) : 256 * (k % 2 + 1), PATCH * (k // 2) : PATCH * (k // 2 + 1)] = part
 
     over_rows(left_v)
-    copies[5].wait()
-    copies[6].wait()
+    for copy in copies[8:13]:
+        copy.wait()
     for k in range(2):
         rows = slice(256 * k, 256 * (k + 1))
         far = jnp.dot(half[rows, :], right_v[...], preferred_element_type=jnp.float32)
@@ -241,8 +254,9 @@
         field[rows, :] = (far_real * keep).astype(jnp.bfloat16)
         field[PATCH + 256 * k : PATCH + 256 * (k + 1), :] = (far_imag * keep).astype(jnp.bfloat16)
     over_rows(right_v)
-    if has_term:
-        copies[7].wait()
+    if last:
+        copies[13].wait()
+        core = lax.rem(me[0], 2)
     for k in range(2):
         rows = slice(256 * k, 256 * (k + 1))
         back = jnp.dot(half[rows, :], left_v[...], preferred_element_type=jnp.float32)
@@ -252,11 +266,14 @@
         patch_imag = patch_v[1, rows, :].astype(jnp.float32)
         term_real = patch_real * back_real + patch_imag * back_imag
         term_imag = patch_real * back_imag - patch_imag * back_real
-        if has_term:
+        if last:
             term_real = term_real + term_v[0, rows, :]
             term_imag = term_imag + term_v[1, rows, :]
-        term[0, rows, :] = term_real
-        term[1, rows, :] = term_imag
+            keep_term[rows, :] = jnp.where(core == 0, term_real, term_imag)
+            give_term[rows, :] = jnp.where(core == 0, term_imag, term_real)
+        else:
+            term_out[0, rows, :] = term_real
+            term_out[1, rows, :] = term_imag
         term_v[0, rows, :] = back_real
         term_v[1, rows, :] = back_imag
 
@@ -289,20 +306,25 @@
     lax.fori_loop(0, classes, spread, 0)
 
 
-def wave(which, classes, pos, me, band, sibling, across, probe, amplitudes, left, right, term):
-    has_term = term is not None
-    operands = [band, sibling, across, probe, amplitudes, left, right] + ([term] if has_term else [])
+def wave(which, classes, pos, me, spare, band, sibling, across, probe, amplitudes, tables, term):
+    operands = [band, sibling, across, probe, amplitudes, *tables]
     smem = pl.BlockSpec(memory_space=pltpu.SMEM)
     hbm = pl.BlockSpec(memory_space=pl.ANY)
     vmem = pl.BlockSpec(memory_space=pltpu.VMEM)
     planes = (2, PATCH, PATCH)
+    plane = jax.ShapeDtypeStruct((PATCH, PATCH), jnp.float32)
+    if term is None:
+        terms = [jax.ShapeDtypeStruct(planes, jnp.float32)]
+    else:
+        operands.append(term)
+        terms = [plane, plane]
     return pl.pallas_call(
-        functools.partial(wave_kernel, which, has_term),
-        in_specs=[smem, smem] + [hbm] * len(operands),
-        out_specs=[vmem, vmem],
+        functools.partial(wave_kernel, which),
+        in_specs=[smem, smem, smem] + [hbm] * len(operands),
+        out_specs=[vmem] * (1 + len(terms)),
         out_shape=[
             jax.ShapeDtypeStruct((classes, 2, PATCH // classes, PATCH), jnp.bfloat16),
-            jax.ShapeDtypeStruct(planes, jnp.float32),
+            *terms,
         ],
         scratch_shapes=[
             pltpu.VMEM((2, PATCH, WIDE), jnp.bfloat16),
@@ -317,13 +339,13 @@
             pltpu.VMEM((2, 2 * PATCH + SUBLANES, PATCH), jnp.float32),
             pltpu.VMEM((2 * PATCH, PATCH), jnp.bfloat16),
             pltpu.VMEM((PATCH, 2 * PATCH), jnp.bfloat16),
-            pltpu.SemaphoreType.DMA((8,)),
+            pltpu.SemaphoreType.DMA((14,)),
         ],
-        compiler_params=pltpu.CompilerParams(vmem_limit_bytes=VMEM_LIMIT),
+        compiler_params=pltpu.CompilerParams(vmem_limit_bytes=WAVE_VMEM),
         cost_estimate=pl.CostEstimate(
             flops=32 * PATCH**3, bytes_accessed=14000000, transcendentals=PATCH * PATCH
         ),
-    )(pos, me, *operands)
+    )(pos, me, spare, *operands)
 
 
 def sum_kernel(pos, me, first, second, own, away, canvas):
@@ -340,8 +362,7 @@
         down = lax.rem(row_at, PATCH)
         at = pl.ds(pl.multiple_of(col_at // LANES * LANES, LANES), WIDE)
         data = source[k].astype(jnp.float32).reshape(2 * height, PATCH)
-        data = jnp.concatenate([data, jnp.zeros((2 * height, LANES), jnp.float32)], 1)
-        data = pltpu.roll(data, lax.rem(col_at, LANES), axis=1)
+        data = shifted_right(data, lax.rem(col_at, LANES))
 
         @pl.when(down < start + height)
         def _():
@@ -379,7 +400,7 @@
             jax.ShapeDtypeStruct(shape, jnp.bfloat16),
         ],
         scratch_shapes=[pltpu.VMEM((bands, 2 * height, width), jnp.float32)],
-        compiler_params=pltpu.CompilerParams(vmem_limit_bytes=VMEM_LIMIT),
+        compiler_params=pltpu.CompilerParams(vmem_limit_bytes=SUM_VMEM),
         cost_estimate=pl.CostEstimate(
             flops=8 * first.size, bytes_accessed=4 * first.size + 6 * math.prod(shape), transcendentals=0
         ),
@@ -403,18 +424,20 @@
     pos = lax.all_gather(own_pos, "obj", axis=0, tiled=True)
     pos_pat = lax.all_gather(own_pos, "pat", axis=0, tiled=True)
 
-    relay = flip(cut(object_image, pos, me, (3,)), 1)
-    across = [flip(cut_and_merge(object_image, relay, pos, me, k), 2) for k in range(2)]
-    sibling = flip(cut(object_image, pos, me, (1,)), 1)
-
-    left, right = dft_matrices(PATCH)
+    relay = [flip(cut(object_image, pos, me, 3, k, 1), 1) for k in range(2)]
+    across = [flip(cut_and_merge(object_image, relay[k], pos, me, k), 2) for k in range(2)]
+    sibling = flip(cut(object_image, pos, me, 1, 0, 2), 1)
+
+    tables = dft_tables(PATCH)
+    operands = (probe, amplitudes, tables)
     grad_0, term = wave(
-        0, classes, pos, me, object_image, sibling, across[0], probe, amplitudes, left, right, None
+        0, classes, pos, me, pos_pat, object_image, sibling, across[0], *operands, None
     )
     part_0 = lax.all_to_all(grad_0, "pat", split_axis=0, concat_axis=0, tiled=True)
-    grad_1, term = wave(
-        1, classes, pos, me, object_image, sibling, across[1], probe, amplitudes, left, right, term
+    grad_1, keep_term, give_term = wave(
+        1, classes, pos, me, pos_pat, object_image, sibling, across[1], *operands, term
     )
+    grad_1, part_0 = lax.optimization_barrier((grad_1, part_0))
     part_1 = lax.all_to_all(grad_1, "pat", split_axis=0, concat_axis=0, tiled=True)
 
     own, away = sum_pieces(pos_pat, me, part_0, part_1, owners, width)
@@ -430,16 +453,28 @@
 
     core = my_owner % 2
     line = my_owner // 2
-    plane = lax.dynamic_index_in_dim(term, core, 0, False) + flip(
-        lax.dynamic_index_in_dim(term, 1 - core, 0, False), 1
-    )
-    rows = plane.shape[0] // 2
-    quarter = lax.dynamic_slice_in_dim(plane, line * rows, rows, 0) + flip(
-        lax.dynamic_slice_in_dim(plane, (1 - line) * rows, rows, 0), 2
-    )
-    quarter = lax.psum(quarter, "pat")
-    quarters = lax.all_gather(quarter, "obj", axis=0)
-    probe_total = quarters.reshape(2, 2, rows, PATCH).transpose(1, 0, 2, 3).reshape(2, PATCH, PATCH)
+    part = keep_term + flip(give_term, 1)
+
+    def halved(part, bit, other):
+        rows = part.shape[0] // 2
+        give = lax.dynamic_slice_in_dim(part, (1 - bit) * rows, rows, 0)
+        return lax.dynamic_slice_in_dim(part, bit * rows, rows, 0) + other(give)
+
+    def doubled(part, bit, other):
+        got = other(part)
+        return jnp.where(bit == 0, jnp.concatenate([part, got]), jnp.concatenate([got, part]))
+
+    def pat_flip(bit):
+        return lambda value: lax.ppermute(value, "pat", [(k, k ^ bit) for k in range(classes)])
+
+    part = halved(part, line, lambda value: flip(value, 2))
+    bits = [1 << k for k in range(classes.bit_length() - 1)]
+    for bit in bits:
+        part = halved(part, my_class // bit % 2, pat_flip(bit))
+    for bit in reversed(bits):
+        part = doubled(part, my_class // bit % 2, pat_flip(bit))
+    part = doubled(part, line, lambda value: flip(value, 2))
+    probe_total = doubled(part[None], core, lambda value: flip(value, 1))
     probe_next = probe - PROBE_RATE * probe_total
     return (object_next, probe_next)
 

time: 375 us -> 301 us (0.80)
  waiting for transfers between devices: 215 us -> 126 us
  blocking collectives: 27.5 us -> 53.6 us
  Pallas kernels: 55.7 us -> 37.1 us
  local copies, waits for them, and re-layouts: 16.1 us -> 22.6 us
  starting transfers between devices: 16.1 us -> 21.4 us
  other arithmetic: 30.2 us -> 25.3 us
    all_gather x1, waiting for transfers between devices: 93.2 us -> 0.25 us  [shards(): object_next = lax.all_gather(updated, 'pat', axis=1, tiled=True)]
    ppermute x0 -> x6, waiting for transfers between devices: none -> 52.1 us  [pat_flip(): lax.ppermute(value, 'pat', [(k, k ^ bit) for k in range(classes)])]
    psum x1 -> x0, waiting for transfers between devices: 43.8 us -> none  [shards(): quarter = lax.psum(quarter, 'pat')]
    all_to_all x0 -> x1, blocking collectives: none -> 26.9 us  [shards(): lax.all_to_all(grad_1, 'pat', split_axis=0, concat_axis=0, tiled=True)]
    all_to_all x1 -> x0, waiting for transfers between devices: 24.6 us -> none  [shards(): lax.all_to_all(grad_1, 'pat', split_axis=0, concat_axis=0, tiled=True)]
    ppermute x9 -> x12, waiting for transfers between devices: 53.2 us -> 73.5 us  [flip(): return lax.ppermute(value, 'obj', [(k, k ^ bit) for k in range(owners)])]
    ppermute x0 -> x6, starting transfers between devices: none -> 11.7 us  [pat_flip(): lax.ppermute(value, 'pat', [(k, k ^ bit) for k in range(classes)])]
    pallas_call x4 -> x5, Pallas kernels: 38.6 us -> 27.9 us  [the longest x2 19.7 us: wave(): pl.pallas_call(functools.partial(wave_kernel, which), in_specs=[smem, sme...]
  transfers between devices with their start and end apart: 14 -> 20, of which waited for: 8 -> 14; matrix products, arithmetic and copies ran while one was open for 9% -> 7% of each run, Pallas kernels for 10% -> 10%
where the time goes in v2:
time: 301 us; the launch traced here: 300 us
  waiting for transfers between devices  126 us (42%)
  blocking collectives  53.6 us (18%)
  Pallas kernels  37.1 us (12%)
  other arithmetic  25.3 us (8%)
  local copies, waits for them, and re-layouts  22.6 us (8%)
  starting transfers between devices  21.4 us (7%)
  between operations  14.5 us (5%)
    ppermute x12, waiting for transfers between devices, flip(): return lax.ppermute(value, 'obj', [(k, k ^ bit) for k in range(owners)])  73.5 us
    ppermute x6, waiting for transfers between devices, pat_flip(): lax.ppermute(value, 'pat', [(k, k ^ bit) for k in range(classes)])  52.1 us
    all_to_all x1, blocking collectives, shards(): lax.all_to_all(grad_1, 'pat', split_axis=0, concat_axis=0, tiled=True)  26.9 us
    unnamed x55, local copies, waits for them, and re-layouts  21.4 us
    all_gather x1, blocking collectives, shards(): pos_pat = lax.all_gather(own_pos, 'pat', axis=0, tiled=True)  20.8 us
    pallas_call x2, Pallas kernels, wave(): pl.pallas_call(functools.partial(wave_kernel, which), in_specs=[smem, sme...  19.7 us
    ppermute x6, starting transfers between devices, pat_flip(): lax.ppermute(value, 'pat', [(k, k ^ bit) for k in range(classes)])  11.7 us
    pallas_call x3, Pallas kernels, cut(): pl.pallas_call(functools.partial(cut_kernel, flip, first), grid_spec=pltp...  8.2 us
  transfers between devices with their start and end apart: 20, of which 14 were waited for; matrix products, arithmetic and copies ran while one was open for 7% of the time, Pallas kernels for 10%

profile of v2, /device:TPU:0, one launch (start us, length us, event | category | flops | bytes accessed | tf_op | source)
XLA Modules:
  0.0 300.5 jit_solution(1777156254524572895)
XLA Ops:
  7.9 6.0 %all-gather.1 = s32[4,2,4]{2,1,0:T(2,128)S(1)} all-gather(s32[1,2,4]{2,1,0:T(2,128)S(1)} %add_bitcast_fusion), channel_id=1, replica_groups=mesh['pat'=8,'obj'=4] {'obj'}, dimensions={0}, use_global_device_ids=true | all-gather | bytes 160 | tf_op jit(solution)/shard_map/all_gather | solution.py:424
  14.0 2.8 copy-done
  19.0 3.6 %shard_map.68 = bf16[2,2,512,512]{3,2,1,0:T(8,128)(2,1)S(1)} custom-call(s32[8,4]{1,0:T(8,128)S(1)} %bitcast.29, s32[2]{0:T(128)S(1)} %pad_add_fusion.me, bf16[2,512,3072]{2,1,0:T(8,128)(2,1)S(1)} %copy-done, bf16[2,512,3072]{2,1,0:T(8,128)(2,1)S(1)} %copy-done, bf16[2,512,3072]{2,1,0:T(8,128)(2,1)S(1)} %copy-done, bf16[2,512,3072]{2,1,0:T(8,128)(2,1)S(1)} %copy-done, ...), custom_call_target="tpu_custom_call" | custom-call | flops 1310720 | bytes 4600000 | tf_op jit(solution)/shard_map/pallas_call | solution.py:105
  29.7 4.0 %multiply_convert_fusion.1.refs_0_ = bf16[512,512]{1,0:T(8,128)(2,1)S(1)} fusion(), kind=kLoop, calls=%fused_computation.18 | loop fusion | flops 4194304 | bytes 524288 | tf_op jit(solution)/shard_map/convert_element_type | solution.py:30
  33.6 20.8 %all-gather = s32[8,2,4]{2,1,0:T(2,128)S(1)} all-gather(s32[1,2,4]{2,1,0:T(2,128)S(1)} %add_bitcast_fusion), channel_id=1, replica_groups=mesh['pat'=8,'obj'=4] {'pat'}, dimensions={0}, use_global_device_ids=true | all-gather | bytes 288 | tf_op jit(solution)/shard_map/all_gather | solution.py:425
  54.4 4.0 %multiply_convert_fusion.refs_1_ = bf16[512,512]{1,0:T(8,128)(2,1)S(1)} fusion(), kind=kLoop, calls=%fused_computation.17 | loop fusion | flops 4456448 | bytes 524288 | tf_op jit(solution)/shard_map/convert_element_type | solution.py:31
  58.4 4.0 %fusion.13.refs_2_ = bf16[512,512]{1,0:T(8,128)(2,1)S(1)} fusion(), kind=kLoop, calls=%fused_computation.28 | loop fusion | flops 5242880 | bytes 524288 | tf_op jit(solution)/shard_map/neg | solution.py:32
  62.5 9.6 %shard_map.73 = (bf16[8,2,64,512]{3,2,1,0:T(8,128)(2,1)S(1)}, f32[2,512,512]{2,1,0:T(8,128)S(1)}) custom-call(s32[8,4]{1,0:T(8,128)S(1)} %bitcast.32, s32[2]{0:T(128)S(1)} %pad_add_fusion.me, s32[16,4]{1,0:T(8,128)S(1)} %bitcast.35, bf16[2,512,3072]{2,1,0:T(8,128)(2,1)S(1)} %bitcast.27, bf16[2,2,512,512]{3,2,1,0:T(8,128)(2,1)S(1)} %collective-permute-done.sibling, ...), custom_call_target="tpu_custom_call" | custom-call | flops 4294967296 | bytes 14000000 | tf_op jit(solution)/shard_map/pallas_call | solution.py:321
  74.5 3.6 %all-to-all-start = ((bf16[8,2,64,512]{3,2,1,0:T(8,128)(2,1)}), bf16[8,2,64,512]{3,2,1,0:T(8,128)(2,1)S(1)}, u32[]{:S(2)}, u32[]{:S(2)}) async-start(bf16[8,2,64,512]{3,2,1,0:T(8,128)(2,1)} %copy-done.19), calls=%async_computation | async-start | bytes 2097152 | tf_op jit(solution)/shard_map/all_to_all | solution.py:436
  78.3 2.8 copy-done.1
  81.1 3.4 %shard_map.70 = bf16[2,512,512]{2,1,0:T(8,128)(2,1)S(1)} custom-call(s32[8,4]{1,0:T(8,128)S(1)} %bitcast.33, s32[2]{0:T(128)S(1)} %pad_add_fusion.me, bf16[2,512,3072]{2,1,0:T(8,128)(2,1)S(1)} %copy-done.1, bf16[2,512,3072]{2,1,0:T(8,128)(2,1)S(1)} %copy-done.1, bf16[2,512,3072]{2,1,0:T(8,128)(2,1)S(1)} %copy-done.1, bf16[2,512,3072]{2,1,0:T(8,128)(2,1)S(1)} %copy-done.1, ...), custom_call_target="tpu_custom_call" | custom-call | flops 655360 | bytes 3300000 | tf_op jit(solution)/shard_map/pallas_call | solution.py:146
  85.1 21.3 %collective-permute-done.2.across = bf16[2,512,512]{2,1,0:T(8,128)(2,1)S(1)} collective-permute-done((bf16[2,512,512]{2,1,0:T(8,128)(2,1)S(1)}, bf16[2,512,512]{2,1,0:T(8,128)(2,1)S(1)}, u32[]{:S(2)}, u32[]{:S(2)}) %collective-permute-start.2) | collective-permute-done | bytes 1048608 | tf_op jit(solution)/shard_map/ppermute | solution.py:421
  106.5 2.8 copy-done.2
  109.2 10.1 %shard_map.74 = (bf16[8,2,64,512]{3,2,1,0:T(8,128)(2,1)S(1)}, f32[512,512]{1,0:T(8,128)S(1)}, f32[512,512]{1,0:T(8,128)S(1)}) custom-call(s32[8,4]{1,0:T(8,128)S(1)} %bitcast.34, s32[2]{0:T(128)S(1)} %pad_add_fusion.me, s32[16,4]{1,0:T(8,128)S(1)} %bitcast.36, bf16[2,512,3072]{2,1,0:T(8,128)(2,1)S(1)} %copy-done.2, bf16[2,2,512,512]{3,2,1,0:T(8,128)(2,1)S(1)} %copy-done.6, ...), custom_call_target="tpu_custom_call" | custom-call | flops 4294967296 | bytes 14000000 | tf_op jit(solution)/shard_map/pallas_call | solution.py:321
  122.3 26.9 %all_to_all.10.second = bf16[8,2,64,512]{3,2,1,0:T(8,128)(2,1)S(1)} all-to-all(bf16[8,2,64,512]{3,2,1,0:T(8,128)(2,1)} %copy-done.20), channel_id=1, replica_groups=mesh['pat'=8,'obj'=4] {'pat'}, dimensions={0} | all-to-all | bytes 2097152 | tf_op jit(solution)/shard_map/all_to_all | solution.py:441
  149.2 4.0 %shard_map.75 = (f32[2,2,64,3072]{3,2,1,0:T(8,128)S(1)}, bf16[2,2,64,3072]{3,2,1,0:T(8,128)(2,1)S(1)}) custom-call(s32[16,4]{1,0:T(8,128)S(1)} %bitcast.37, s32[2]{0:T(128)S(1)} %pad_add_fusion.me, bf16[8,2,64,512]{3,2,1,0:T(8,128)(2,1)S(1)} %all-to-all-done.first, bf16[8,2,64,512]{3,2,1,0:T(8,128)(2,1)S(1)} %all_to_all.10.second), custom_call_target="tpu_custom_call" | custom-call | flops 4194304 | bytes 6815744 | tf_op jit(solution)/shard_map/pallas_call | solution.py:394
  154.8 2.9 collective-permute-done.6
  158.8 19.9 %collective-permute-done.7 = bf16[2,64,3072]{2,1,0:T(8,128)(2,1)} collective-permute-done((bf16[2,64,3072]{2,1,0:T(8,128)(2,1)}, bf16[2,64,3072]{2,1,0:T(8,128)(2,1)}, u32[]{:S(2)}, u32[]{:S(2)}) %collective-permute-start.7) | collective-permute-done | bytes 786464 | tf_op jit(solution)/shard_map/ppermute | solution.py:421
  178.6 3.4 %fusion.6 = bf16[2,64,3072]{2,1,0:T(8,128)(2,1)} fusion(bf16[2,64,3072]{2,1,0:T(8,128)(2,1)} %collective-permute-done.7, bf16[2,64,3072]{2,1,0:T(8,128)(2,1)} %collective-permute-done.5, f32[2,2,64,3072]{3,2,1,0:T(8,128)} %copy-done.4, bf16[2,512,3072]{2,1,0:T(8,128)(2,1)} %band.3, s32[]{:T(128)S(6)} %select_n.138), kind=kLoop, calls=%fused_computation.9 | loop fusion | flops 3145728 | bytes 4718596 | tf_op jit(solution)/shard_map/convert_element_type | solution.py:451
  182.2 3.0 collective-permute-done.8
  188.0 13.7 %collective-permute-done.9 = f32[256,512]{1,0:T(8,128)S(1)} collective-permute-done((f32[256,512]{1,0:T(8,128)S(1)}, f32[256,512]{1,0:T(8,128)S(1)}, u32[]{:S(2)}, u32[]{:S(2)}) %collective-permute-start.9) | collective-permute-done | bytes 524320 | tf_op jit(solution)/shard_map/ppermute | solution.py:421
  204.3 6.2 %collective-permute-done.10 = f32[128,512]{1,0:T(8,128)S(1)} collective-permute-done((f32[128,512]{1,0:T(8,128)S(1)}, f32[128,512]{1,0:T(8,128)S(1)}, u32[]{:S(2)}, u32[]{:S(2)}) %collective-permute-start.10) | collective-permute-done | bytes 262176 | tf_op jit(solution)/shard_map/ppermute | solution.py:468
  211.7 8.0 %collective-permute-done.11 = f32[64,512]{1,0:T(8,128)S(1)} collective-permute-done((f32[64,512]{1,0:T(8,128)S(1)}, f32[64,512]{1,0:T(8,128)S(1)}, u32[]{:S(2)}, u32[]{:S(2)}) %collective-permute-start.11) | collective-permute-done | bytes 131104 | tf_op jit(solution)/shard_map/ppermute | solution.py:468
  220.2 5.2 %collective-permute-done.12 = f32[32,512]{1,0:T(8,128)S(1)} collective-permute-done((f32[32,512]{1,0:T(8,128)S(1)}, f32[32,512]{1,0:T(8,128)S(1)}, u32[]{:S(2)}, u32[]{:S(2)}) %collective-permute-start.12) | collective-permute-done | bytes 65568 | tf_op jit(solution)/shard_map/ppermute | solution.py:468
  225.6 8.7 %collective-permute-done.13 = f32[32,512]{1,0:T(8,128)S(1)} collective-permute-done((f32[32,512]{1,0:T(8,128)S(1)}, f32[32,512]{1,0:T(8,128)S(1)}, u32[]{:S(2)}, u32[]{:S(2)}) %collective-permute-start.13) | collective-permute-done | bytes 65568 | tf_op jit(solution)/shard_map/ppermute | solution.py:468
  234.3 13.4 %collective-permute-done.14 = f32[64,512]{1,0:T(8,128)S(1)} collective-permute-done((f32[64,512]{1,0:T(8,128)S(1)}, f32[64,512]{1,0:T(8,128)S(1)}, u32[]{:S(2)}, u32[]{:S(2)}) %collective-permute-start.14) | collective-permute-done | bytes 131104 | tf_op jit(solution)/shard_map/ppermute | solution.py:468
  247.7 8.3 %collective-permute-start.15 = (f32[128,512]{1,0:T(8,128)S(1)}, f32[128,512]{1,0:T(8,128)S(1)}, u32[]{:S(2)}, u32[]{:S(2)}) collective-permute-start(f32[128,512]{1,0:T(8,128)S(1)} %maximum_select_fusion.3), channel_id=1, source_target_pairs={{0,4},{4,0},{8,12},{12,8},{16,20},{20,16},{24,28},{28,24},{1,5},{5... | collective-permute-start | bytes 786440 | tf_op jit(solution)/shard_map/ppermute | solution.py:468
  256.0 10.8 %collective-permute-done.15 = f32[128,512]{1,0:T(8,128)S(1)} collective-permute-done((f32[128,512]{1,0:T(8,128)S(1)}, f32[128,512]{1,0:T(8,128)S(1)}, u32[]{:S(2)}, u32[]{:S(2)}) %collective-permute-start.15) | collective-permute-done | bytes 262176 | tf_op jit(solution)/shard_map/ppermute | solution.py:468
  268.4 10.1 %collective-permute-done.16 = f32[256,512]{1,0:T(8,128)S(1)} collective-permute-done((f32[256,512]{1,0:T(8,128)S(1)}, f32[256,512]{1,0:T(8,128)S(1)}, u32[]{:S(2)}, u32[]{:S(2)}) %collective-permute-start.16) | collective-permute-done | bytes 524320 | tf_op jit(solution)/shard_map/ppermute | solution.py:421
  281.2 2.8 collective-permute-done.17
  283.9 3.5 %fusion.1 = f32[2,512,512]{2,1,0:T(8,128)} fusion(f32[2,512,512]{2,1,0:T(8,128)S(1)} %copy-done.3, f32[1,512,512]{2,1,0:T(8,128)} %collective-permute-done.17, f32[1,512,512]{2,1,0:T(8,128)S(1)} %maximum_select_fusion.1, pred[]{:T(512)S(6)} %eq.25), kind=kLoop, calls=%fused_computation.2 | loop fusion | flops 2621440 | bytes 6291457 | tf_op jit(solution)/shard_map/sub | solution.py:478
  287.7 5.9 %copy.8 = bf16[2,512,3072]{2,1,0:T(8,128)(2,1)} copy(bf16[2,512,3072]{2,1,0:T(8,128)(2,1)} %all-gather.4.cloned.1.call-done) | data formatting | bytes 12582912
  (98 shorter events, 31.0 us)
Async XLA Ops:
  18.6 4.3 %collective-permute-start.3 = (bf16[1,2,512,512]{3,2,1,0:T(8,128)(2,1)S(1)}, bf16[1,2,512,512]{3,2,1,0:T(8,128)(2,1)S(1)}, u32[]{:S(2)}, u32[]{:S(2)}) collective-permute-start(bf16[1,2,512,512]{3,2,1,0:T(8,128)(2,1)S(1)} %shard_map.71), channel_id=1, source_target_pairs={{0,1},{1,0},{2,3},{3,2},{4,5},{5,4},{6,7},{7,6},{8,9},{9,8},{10,11... | collective-permute-start | bytes 3145736 | tf_op jit(solution)/shard_map/ppermute | solution.py:421
  22.6 39.8 %collective-permute-start = (bf16[2,2,512,512]{3,2,1,0:T(8,128)(2,1)S(1)}, bf16[2,2,512,512]{3,2,1,0:T(8,128)(2,1)S(1)}, u32[]{:S(2)}, u32[]{:S(2)}) collective-permute-start(bf16[2,2,512,512]{3,2,1,0:T(8,128)(2,1)S(1)} %shard_map.68), channel_id=1, source_target_pairs={{0,1},{1,0},{2,3},{3,2},{4,5},{5,4},{6,7},{7,6},{8,9},{9,8},{10,11... | collective-permute-start | bytes 6291464 | tf_op jit(solution)/shard_map/ppermute | solution.py:421
  22.9 39.6 %slice-start = ((s8[6291456]{0:T(1024)(128)(4,1)}), s8[4194304]{0:T(1024)(128)(4,1)S(1)}, s32[]{:S(2)}) async-start(s8[6291456]{0:T(1024)(128)(4,1)} %bitcast.26), calls=%async_computation.3 | async-start | bytes 8388608
  24.7 37.8 %slice-start.1 = ((s8[6291456]{0:T(1024)(128)(4,1)}), s8[2097152]{0:T(1024)(128)(4,1)S(1)}, s32[]{:S(2)}) async-start(s8[6291456]{0:T(1024)(128)(4,1)} %bitcast.26), calls=%async_computation.4 | async-start | bytes 4194304
  24.7 37.8 %copy-start.3 = (f32[2,512,512]{2,1,0:T(8,128)S(1)}, f32[2,512,512]{2,1,0:T(8,128)}, u32[]{:S(2)}) copy-start(f32[2,512,512]{2,1,0:T(8,128)} %probe.3) | copy-start | bytes 6291460
  24.7 37.8 %copy-start.15 = (bf16[2,512,512]{2,1,0:T(8,128)(2,1)S(1)}, bf16[2,512,512]{2,1,0:T(8,128)(2,1)}, u32[]{:S(2)}) copy-start(bf16[2,512,512]{2,1,0:T(8,128)(2,1)} %amplitudes.3) | copy-start | bytes 3145732
  24.8 37.7 %collective-permute-start.4 = (bf16[2,512,512]{2,1,0:T(8,128)(2,1)S(1)}, bf16[2,512,512]{2,1,0:T(8,128)(2,1)S(1)}, u32[]{:S(2)}, u32[]{:S(2)}) collective-permute-start(bf16[2,512,512]{2,1,0:T(8,128)(2,1)S(1)} %shard_map.72), channel_id=1, source_target_pairs={{0,2},{1,3},{2,0},{3,1},{4,6},{5,7},{6,4},{7,5},{8,10},{9,11},{10,... | collective-permute-start | bytes 3145736 | tf_op jit(solution)/shard_map/ppermute | solution.py:421
  29.6 48.7 %collective-permute-start.1 = (bf16[1,2,512,512]{3,2,1,0:T(8,128)(2,1)}, bf16[1,2,512,512]{3,2,1,0:T(8,128)(2,1)}, u32[]{:S(2)}, u32[]{:S(2)}) collective-permute-start(bf16[1,2,512,512]{3,2,1,0:T(8,128)(2,1)} %shard_map.69), channel_id=1, source_target_pairs={{0,1},{1,0},{2,3},{3,2},{4,5},{5,4},{6,7},{7,6},{8,9},{9,8},{10,11... | collective-permute-start | bytes 3145736 | tf_op jit(solution)/shard_map/ppermute | solution.py:421
  33.6 38.5 %copy-start.9 = (bf16[512,512]{1,0:T(8,128)(2,1)}, bf16[512,512]{1,0:T(8,128)(2,1)S(1)}, u32[]{:S(2)}) copy-start(bf16[512,512]{1,0:T(8,128)(2,1)S(1)} %multiply_convert_fusion.1.refs_0_) | copy-start | bytes 1572868
  74.5 47.8 %all-to-all-start = ((bf16[8,2,64,512]{3,2,1,0:T(8,128)(2,1)}), bf16[8,2,64,512]{3,2,1,0:T(8,128)(2,1)S(1)}, u32[]{:S(2)}, u32[]{:S(2)}) async-start(bf16[8,2,64,512]{3,2,1,0:T(8,128)(2,1)} %copy-done.19), calls=%async_computation | async-start | bytes 2097152 | tf_op jit(solution)/shard_map/all_to_all | solution.py:436
  78.1 209.6 %all-gather.4.cloned.1.call-start = ((), (), s32[]{:S(2)}) async-start(), calls=%async_computation.2 | async-start | bytes 7077888 | tf_op jit(solution)/shard_map/all_gather | solution.py:452
  81.1 25.3 %copy-start.6 = (bf16[2,2,512,512]{3,2,1,0:T(8,128)(2,1)S(1)}, bf16[2,2,512,512]{3,2,1,0:T(8,128)(2,1)}, u32[]{:S(2)}) copy-start(bf16[2,2,512,512]{3,2,1,0:T(8,128)(2,1)} %copy-done.5) | copy-start | bytes 6291460
  81.1 25.3 %copy-start.8 = (f32[2,512,512]{2,1,0:T(8,128)S(1)}, f32[2,512,512]{2,1,0:T(8,128)}, u32[]{:S(2)}) copy-start(f32[2,512,512]{2,1,0:T(8,128)} %copy-done.7) | copy-start | bytes 6291460
  81.1 25.3 %copy-start.10 = (bf16[512,512]{1,0:T(8,128)(2,1)S(1)}, bf16[512,512]{1,0:T(8,128)(2,1)}, u32[]{:S(2)}) copy-start(bf16[512,512]{1,0:T(8,128)(2,1)} %copy-done.9) | copy-start | bytes 1572868
  81.1 25.3 %copy-start.12 = (bf16[512,512]{1,0:T(8,128)(2,1)S(1)}, bf16[512,512]{1,0:T(8,128)(2,1)}, u32[]{:S(2)}) copy-start(bf16[512,512]{1,0:T(8,128)(2,1)} %copy-done.11) | copy-start | bytes 1572868
  81.1 25.3 %copy-start.14 = (bf16[512,512]{1,0:T(8,128)(2,1)S(1)}, bf16[512,512]{1,0:T(8,128)(2,1)}, u32[]{:S(2)}) copy-start(bf16[512,512]{1,0:T(8,128)(2,1)} %copy-done.13) | copy-start | bytes 1572868
  81.1 25.3 %copy-start.16 = (bf16[2,512,512]{2,1,0:T(8,128)(2,1)S(1)}, bf16[2,512,512]{2,1,0:T(8,128)(2,1)}, u32[]{:S(2)}) copy-start(bf16[2,512,512]{2,1,0:T(8,128)(2,1)} %amplitudes.3) | copy-start | bytes 3145732
  84.6 21.8 %collective-permute-start.2 = (bf16[2,512,512]{2,1,0:T(8,128)(2,1)S(1)}, bf16[2,512,512]{2,1,0:T(8,128)(2,1)S(1)}, u32[]{:S(2)}, u32[]{:S(2)}) collective-permute-start(bf16[2,512,512]{2,1,0:T(8,128)(2,1)S(1)} %shard_map.70), channel_id=1, source_target_pairs={{0,2},{1,3},{2,0},{3,1},{4,6},{5,7},{6,4},{7,5},{8,10},{9,11},{10,... | collective-permute-start | bytes 3145736 | tf_op jit(solution)/shard_map/ppermute | solution.py:421
  154.3 3.4 %collective-permute-start.6 = (bf16[2,64,3072]{2,1,0:T(8,128)(2,1)S(1)}, bf16[2,64,3072]{2,1,0:T(8,128)(2,1)S(1)}, u32[]{:S(2)}, u32[]{:S(2)}) collective-permute-start(bf16[2,64,3072]{2,1,0:T(8,128)(2,1)S(1)} %get-tuple-element.21), channel_id=1, source_target_pairs={{0,1},{1,0},{2,3},{3,2},{4,5},{5,4},{6,7},{7,6},{8,9},{9,8},{10,11... | collective-permute-start | bytes 2359304 | tf_op jit(solution)/shard_map/ppermute | solution.py:421
  154.3 4.5 %collective-permute-start.5 = (bf16[2,64,3072]{2,1,0:T(8,128)(2,1)}, bf16[2,64,3072]{2,1,0:T(8,128)(2,1)}, u32[]{:S(2)}, u32[]{:S(2)}) collective-permute-start(bf16[2,64,3072]{2,1,0:T(8,128)(2,1)} %get-tuple-element.20), channel_id=1, source_target_pairs={{0,1},{1,0},{2,3},{3,2},{4,5},{5,4},{6,7},{7,6},{8,9},{9,8},{10,11... | collective-permute-start | bytes 2359304 | tf_op jit(solution)/shard_map/ppermute | solution.py:421
  158.7 19.9 %collective-permute-start.7 = (bf16[2,64,3072]{2,1,0:T(8,128)(2,1)}, bf16[2,64,3072]{2,1,0:T(8,128)(2,1)}, u32[]{:S(2)}, u32[]{:S(2)}) collective-permute-start(bf16[2,64,3072]{2,1,0:T(8,128)(2,1)} %fusion.2), channel_id=1, source_target_pairs={{0,2},{1,3},{2,0},{3,1},{4,6},{5,7},{6,4},{7,5},{8,10},{9,11},{10,... | collective-permute-start | bytes 2359304 | tf_op jit(solution)/shard_map/ppermute | solution.py:421
  158.8 26.4 %copy-start.18 = (f32[512,512]{1,0:T(8,128)S(1)}, f32[512,512]{1,0:T(8,128)}, u32[]{:S(2)}) copy-start(f32[512,512]{1,0:T(8,128)} %copy-done.17) | copy-start | bytes 3145732
  182.1 3.1 %collective-permute-start.8 = (f32[512,512]{1,0:T(8,128)}, f32[512,512]{1,0:T(8,128)}, u32[]{:S(2)}, u32[]{:S(2)}) collective-permute-start(f32[512,512]{1,0:T(8,128)} %copy-done.21), channel_id=1, source_target_pairs={{0,1},{1,0},{2,3},{3,2},{4,5},{5,4},{6,7},{7,6},{8,9},{9,8},{10,11... | collective-permute-start | bytes 3145736 | tf_op jit(solution)/shard_map/ppermute | solution.py:421
  187.6 14.0 %collective-permute-start.9 = (f32[256,512]{1,0:T(8,128)S(1)}, f32[256,512]{1,0:T(8,128)S(1)}, u32[]{:S(2)}, u32[]{:S(2)}) collective-permute-start(f32[256,512]{1,0:T(8,128)S(1)} %constant_dynamic-slice_fusion.3), channel_id=1, source_target_pairs={{0,2},{1,3},{2,0},{3,1},{4,6},{5,7},{6,4},{7,5},{8,10},{9,11},{10,... | collective-permute-start | bytes 1572872 | tf_op jit(solution)/shard_map/ppermute | solution.py:421
  202.8 7.7 %collective-permute-start.10 = (f32[128,512]{1,0:T(8,128)S(1)}, f32[128,512]{1,0:T(8,128)S(1)}, u32[]{:S(2)}, u32[]{:S(2)}) collective-permute-start(f32[128,512]{1,0:T(8,128)S(1)} %constant_dynamic-slice_fusion.2), channel_id=1, source_target_pairs={{0,4},{4,0},{8,12},{12,8},{16,20},{20,16},{24,28},{28,24},{1,5},{5... | collective-permute-start | bytes 786440 | tf_op jit(solution)/shard_map/ppermute | solution.py:468
  210.6 9.1 %collective-permute-start.11 = (f32[64,512]{1,0:T(8,128)S(1)}, f32[64,512]{1,0:T(8,128)S(1)}, u32[]{:S(2)}, u32[]{:S(2)}) collective-permute-start(f32[64,512]{1,0:T(8,128)S(1)} %constant_dynamic-slice_fusion.1), channel_id=1, source_target_pairs={{0,8},{4,12},{8,0},{12,4},{16,24},{20,28},{24,16},{28,20},{1,9},{5... | collective-permute-start | bytes 393224 | tf_op jit(solution)/shard_map/ppermute | solution.py:468
  219.7 5.7 %collective-permute-start.12 = (f32[32,512]{1,0:T(8,128)S(1)}, f32[32,512]{1,0:T(8,128)S(1)}, u32[]{:S(2)}, u32[]{:S(2)}) collective-permute-start(f32[32,512]{1,0:T(8,128)S(1)} %constant_dynamic-slice_fusion), channel_id=1, source_target_pairs={{0,16},{4,20},{8,24},{12,28},{16,0},{20,4},{24,8},{28,12},{1,17},{... | collective-permute-start | bytes 196616 | tf_op jit(solution)/shard_map/ppermute | solution.py:468
  225.4 8.8 %collective-permute-start.13 = (f32[32,512]{1,0:T(8,128)S(1)}, f32[32,512]{1,0:T(8,128)S(1)}, u32[]{:S(2)}, u32[]{:S(2)}) collective-permute-start(f32[32,512]{1,0:T(8,128)S(1)} %dynamic-slice_add_fusion.3), channel_id=1, source_target_pairs={{0,16},{4,20},{8,24},{12,28},{16,0},{20,4},{24,8},{28,12},{1,17},{... | collective-permute-start | bytes 196616 | tf_op jit(solution)/shard_map/ppermute | solution.py:468
  234.2 13.5 %collective-permute-start.14 = (f32[64,512]{1,0:T(8,128)S(1)}, f32[64,512]{1,0:T(8,128)S(1)}, u32[]{:S(2)}, u32[]{:S(2)}) collective-permute-start(f32[64,512]{1,0:T(8,128)S(1)} %maximum_select_fusion.4), channel_id=1, source_target_pairs={{0,8},{4,12},{8,0},{12,4},{16,24},{20,28},{24,16},{28,20},{1,9},{5... | collective-permute-start | bytes 393224 | tf_op jit(solution)/shard_map/ppermute | solution.py:468
  247.7 19.0 %collective-permute-start.15 = (f32[128,512]{1,0:T(8,128)S(1)}, f32[128,512]{1,0:T(8,128)S(1)}, u32[]{:S(2)}, u32[]{:S(2)}) collective-permute-start(f32[128,512]{1,0:T(8,128)S(1)} %maximum_select_fusion.3), channel_id=1, source_target_pairs={{0,4},{4,0},{8,12},{12,8},{16,20},{20,16},{24,28},{28,24},{1,5},{5... | collective-permute-start | bytes 786440 | tf_op jit(solution)/shard_map/ppermute | solution.py:468
  266.8 11.6 %collective-permute-start.16 = (f32[256,512]{1,0:T(8,128)S(1)}, f32[256,512]{1,0:T(8,128)S(1)}, u32[]{:S(2)}, u32[]{:S(2)}) collective-permute-start(f32[256,512]{1,0:T(8,128)S(1)} %maximum_select_fusion.2), channel_id=1, source_target_pairs={{0,2},{1,3},{2,0},{3,1},{4,6},{5,7},{6,4},{7,5},{8,10},{9,11},{10,... | collective-permute-start | bytes 1572872 | tf_op jit(solution)/shard_map/ppermute | solution.py:421
  281.1 2.9 collective-permute-start.17
  (15 other events, 65.8 us)
Sparse Core Ops, SparseCore 0:
  182.2 105.4 all-gather.3

commit v3 on v2

--- a/solution.py
+++ b/solution.py
@@ -16,13 +16,14 @@
 OBJECT_RATE = 0.1
 PROBE_RATE = 0.05
 MAGNITUDE_FLOOR = 0.5
+ALL_VMEM = 56 * 1024 * 1024
 CUT_VMEM = 14 * 1024 * 1024
 WAVE_VMEM = 32 * 1024 * 1024
 SUM_VMEM = 24 * 1024 * 1024
 
 
-def dft_tables(length):
-    counter = jnp.arange(length, dtype=jnp.int32)
+def dft_tables(counter):
+    length = counter.shape[0]
     phase_angle = (counter[:, None] * counter[None, :] % length).astype(jnp.float32) * (
         2.0 * math.pi / length
     )
@@ -95,7 +96,7 @@
     lax.fori_loop(0, PATCH // CHUNK, body, 0)
 
 
-def cut(band, pos, me, flip, first, count):
+def cut(band, pos, me, flip, first, count, vmem):
     def block(k):
         def index(i, pos, me):
             return (0, 0, first_col(pos, 2 * lax.bitwise_xor(me[0], flip) + first + i) // LANES + k)
@@ -111,7 +112,7 @@
             out_specs=pl.BlockSpec((1, 2, PATCH, PATCH), lambda i, pos, me: (i, 0, 0, 0)),
         ),
         out_shape=jax.ShapeDtypeStruct((count, 2, PATCH, PATCH), jnp.bfloat16),
-        compiler_params=pltpu.CompilerParams(vmem_limit_bytes=CUT_VMEM),
+        compiler_params=pltpu.CompilerParams(vmem_limit_bytes=vmem),
         cost_estimate=pl.CostEstimate(
             flops=count * 2 * PATCH * WIDE, bytes_accessed=count * 2300000, transcendentals=0
         ),
@@ -160,7 +161,7 @@
     )(pos, me, *([band] * (WIDE // LANES)), sibling)
 
 
-def wave_kernel(which, pos, me, spare, band, sibling, across, probe, amplitudes, *refs):
+def wave_kernel(which, pos, me, band, sibling, across, probe, amplitudes, *refs):
     tables, refs = refs[:3], refs[3:]
     last = which == 1
     if last:
@@ -270,7 +271,7 @@
             term_real = term_real + term_v[0, rows, :]
             term_imag = term_imag + term_v[1, rows, :]
             keep_term[rows, :] = jnp.where(core == 0, term_real, term_imag)
-            give_term[rows, :] = jnp.where(core == 0, term_imag, term_real)
+            give_term[rows, :] = jnp.where(core == 0, term_imag, term_real).astype(jnp.bfloat16)
         else:
             term_out[0, rows, :] = term_real
             term_out[1, rows, :] = term_imag
@@ -306,21 +307,21 @@
     lax.fori_loop(0, classes, spread, 0)
 
 
-def wave(which, classes, pos, me, spare, band, sibling, across, probe, amplitudes, tables, term):
+def wave(which, classes, pos, me, band, sibling, across, probe, amplitudes, tables, term):
     operands = [band, sibling, across, probe, amplitudes, *tables]
     smem = pl.BlockSpec(memory_space=pltpu.SMEM)
     hbm = pl.BlockSpec(memory_space=pl.ANY)
     vmem = pl.BlockSpec(memory_space=pltpu.VMEM)
     planes = (2, PATCH, PATCH)
-    plane = jax.ShapeDtypeStruct((PATCH, PATCH), jnp.float32)
+    plane = (PATCH, PATCH)
     if term is None:
         terms = [jax.ShapeDtypeStruct(planes, jnp.float32)]
     else:
         operands.append(term)
-        terms = [plane, plane]
+        terms = [jax.ShapeDtypeStruct(plane, t) for t in (jnp.float32, jnp.bfloat16)]
     return pl.pallas_call(
         functools.partial(wave_kernel, which),
-        in_specs=[smem, smem, smem] + [hbm] * len(operands),
+        in_specs=[smem, smem] + [hbm] * len(operands),
         out_specs=[vmem] * (1 + len(terms)),
         out_shape=[
             jax.ShapeDtypeStruct((classes, 2, PATCH // classes, PATCH), jnp.bfloat16),
@@ -343,9 +344,9 @@
         ],
         compiler_params=pltpu.CompilerParams(vmem_limit_bytes=WAVE_VMEM),
         cost_estimate=pl.CostEstimate(
-            flops=32 * PATCH**3, bytes_accessed=14000000, transcendentals=PATCH * PATCH
-        ),
-    )(pos, me, spare, *operands)
+            flops=PATCH**2, bytes_accessed=PATCH**2, transcendentals=0
+        ),
+    )(pos, me, *operands)
 
 
 def sum_kernel(pos, me, first, second, own, away, canvas):
@@ -420,22 +421,36 @@
     def flip(value, bit):
         return lax.ppermute(value, "obj", [(k, k ^ bit) for k in range(owners)])
 
+    def pat_flip(bit):
+        return lambda value: lax.ppermute(value, "pat", [(k, k ^ bit) for k in range(classes)])
+
+    def halved(part, bit, other):
+        rows = part.shape[0] // 2
+        give = lax.dynamic_slice_in_dim(part, (1 - bit) * rows, rows, 0).astype(jnp.bfloat16)
+        return lax.dynamic_slice_in_dim(part, bit * rows, rows, 0) + other(give).astype(jnp.float32)
+
+    def doubled(part, bit, other):
+        got = other(part)
+        return jnp.where(bit == 0, jnp.concatenate([part, got]), jnp.concatenate([got, part]))
+
+    bits = [1 << k for k in range(classes.bit_length() - 1)]
     own_pos = jnp.concatenate([pos_tile, pos_offset], 1)
     pos = lax.all_gather(own_pos, "obj", axis=0, tiled=True)
-    pos_pat = lax.all_gather(own_pos, "pat", axis=0, tiled=True)
-
-    relay = [flip(cut(object_image, pos, me, 3, k, 1), 1) for k in range(2)]
-    across = [flip(cut_and_merge(object_image, relay[k], pos, me, k), 2) for k in range(2)]
-    sibling = flip(cut(object_image, pos, me, 1, 0, 2), 1)
-
-    tables = dft_tables(PATCH)
-    operands = (probe, amplitudes, tables)
-    grad_0, term = wave(
-        0, classes, pos, me, pos_pat, object_image, sibling, across[0], *operands, None
-    )
+
+    relay = [flip(cut(object_image, pos, me, 3, k, 1, ALL_VMEM), 1) for k in range(2)]
+    merged = [cut_and_merge(object_image, relay[k], pos, me, k) for k in range(2)]
+    counter = jnp.arange(PATCH, dtype=jnp.int32)
+    merged[1], counter, pos_pat = lax.optimization_barrier((merged[1], counter, own_pos))
+    across = [flip(m, 2) for m in merged]
+    sibling = flip(cut(object_image, pos, me, 1, 0, 2, CUT_VMEM), 1)
+    for bit in bits:
+        pos_pat = doubled(pos_pat, my_class // bit % 2, pat_flip(bit))
+
+    operands = (probe, amplitudes, dft_tables(counter))
+    grad_0, term = wave(0, classes, pos, me, object_image, sibling, across[0], *operands, None)
     part_0 = lax.all_to_all(grad_0, "pat", split_axis=0, concat_axis=0, tiled=True)
     grad_1, keep_term, give_term = wave(
-        1, classes, pos, me, pos_pat, object_image, sibling, across[1], *operands, term
+        1, classes, pos, me, object_image, sibling, across[1], *operands, term
     )
     grad_1, part_0 = lax.optimization_barrier((grad_1, part_0))
     part_1 = lax.all_to_all(grad_1, "pat", split_axis=0, concat_axis=0, tiled=True)
@@ -453,28 +468,15 @@
 
     core = my_owner % 2
     line = my_owner // 2
-    part = keep_term + flip(give_term, 1)
-
-    def halved(part, bit, other):
-        rows = part.shape[0] // 2
-        give = lax.dynamic_slice_in_dim(part, (1 - bit) * rows, rows, 0)
-        return lax.dynamic_slice_in_dim(part, bit * rows, rows, 0) + other(give)
-
-    def doubled(part, bit, other):
-        got = other(part)
-        return jnp.where(bit == 0, jnp.concatenate([part, got]), jnp.concatenate([got, part]))
-
-    def pat_flip(bit):
-        return lambda value: lax.ppermute(value, "pat", [(k, k ^ bit) for k in range(classes)])
-
+    part = keep_term + flip(give_term, 1).astype(jnp.float32)
     part = halved(part, line, lambda value: flip(value, 2))
-    bits = [1 << k for k in range(classes.bit_length() - 1)]
     for bit in bits:
         part = halved(part, my_class // bit % 2, pat_flip(bit))
+    part = part.astype(jnp.bfloat16)
     for bit in reversed(bits):
         part = doubled(part, my_class // bit % 2, pat_flip(bit))
     part = doubled(part, line, lambda value: flip(value, 2))
-    probe_total = doubled(part[None], core, lambda value: flip(value, 1))
+    probe_total = doubled(part[None], core, lambda value: flip(value, 1)).astype(jnp.float32)
     probe_next = probe - PROBE_RATE * probe_total
     return (object_next, probe_next)
 

time: 301 us -> 300 us (level)
  blocking collectives: 53.6 us -> 6.44 us
  waiting for transfers between devices: 126 us -> 163 us
  starting transfers between devices: 21.4 us -> 33.3 us
  other arithmetic: 25.3 us -> 18.6 us
  Pallas kernels: 37.1 us -> 41.4 us
    all_gather x1, waiting for transfers between devices: 0.25 us -> 35.2 us  [shards(): object_next = lax.all_gather(updated, 'pat', axis=1, tiled=True)]
    all_to_all x1 -> x0, blocking collectives: 26.9 us -> none  [shards(): lax.all_to_all(grad_1, 'pat', split_axis=0, concat_axis=0, tiled=True)]
    all_gather x1 -> x0, blocking collectives: 20.8 us -> none  [shards(): pos_pat = lax.all_gather(own_pos, 'pat', axis=0, tiled=True)]
    all_to_all x0 -> x1, starting transfers between devices: none -> 5.73 us  [shards(): lax.all_to_all(grad_1, 'pat', split_axis=0, concat_axis=0, tiled=True)]
    pallas_call x3, Pallas kernels: 8.2 us -> 13.4 us  [cut(): pl.pallas_call(functools.partial(cut_kernel, flip, first), grid_spec=pltp...]
    convert_element_type x1, other arithmetic: 3.96 us -> 0.01 us  [shards(): part = part.astype(jnp.bfloat16)]
    ppermute x12, starting transfers between devices: 5.93 us -> 9.6 us  [flip(): return lax.ppermute(value, 'obj', [(k, k ^ bit) for k in range(owners)])]
    ppermute x6 -> x9, waiting for transfers between devices: 52.1 us -> 54.5 us  [pat_flip(): lax.ppermute(value, 'pat', [(k, k ^ bit) for k in range(classes)])]
  transfers between devices with their start and end apart: 20 -> 24, of which waited for: 14 -> 18; matrix products, arithmetic and copies ran while one was open for 7% -> 5% of each run, Pallas kernels for 10% -> 8%
where the time goes in v3:
time: 300 us; the launch traced here: 299 us
  waiting for transfers between devices  163 us (54%)
  Pallas kernels  41.4 us (14%)
  starting transfers between devices  33.3 us (11%)
  local copies, waits for them, and re-layouts  22.4 us (7%)
  other arithmetic  18.6 us (6%)
  between operations  14.4 us (5%)
  blocking collectives  6.44 us (2%)
    ppermute x12, waiting for transfers between devices, flip(): return lax.ppermute(value, 'obj', [(k, k ^ bit) for k in range(owners)])  72.8 us
    ppermute x9, waiting for transfers between devices, pat_flip(): lax.ppermute(value, 'pat', [(k, k ^ bit) for k in range(classes)])  54.5 us
    all_gather x1, waiting for transfers between devices, shards(): object_next = lax.all_gather(updated, 'pat', axis=1, tiled=True)  35.2 us
    unnamed x49, local copies, waits for them, and re-layouts  21 us
    pallas_call x2, Pallas kernels, wave(): pl.pallas_call(functools.partial(wave_kernel, which), in_specs=[smem, sme...  19.8 us
    pallas_call x3, Pallas kernels, cut(): pl.pallas_call(functools.partial(cut_kernel, flip, first), grid_spec=pltp...  13.4 us
    ppermute x9, starting transfers between devices, pat_flip(): lax.ppermute(value, 'pat', [(k, k ^ bit) for k in range(classes)])  11.8 us
    ppermute x12, starting transfers between devices, flip(): return lax.ppermute(value, 'obj', [(k, k ^ bit) for k in range(owners)])  9.6 us
  transfers between devices with their start and end apart: 24, of which 18 were waited for; matrix products, arithmetic and copies ran while one was open for 5% of the time, Pallas kernels for 8%

profile of v3, /device:TPU:0, one launch (start us, length us, event | category | flops | bytes accessed | tf_op | source)
XLA Modules:
  0.0 299.1 jit_solution(16126003995884345539)
XLA Ops:
  8.8 6.4 %all-gather = s32[4,2,4]{2,1,0:T(2,128)} all-gather(s32[1,2,4]{2,1,0:T(2,128)S(1)} %bitcast.33), channel_id=1, replica_groups=mesh['pat'=8,'obj'=4] {'obj'}, dimensions={0}, use_global_device_ids=true | all-gather | bytes 160 | tf_op jit(solution)/shard_map/all_gather | solution.py:438
  15.9 4.4 %shard_map.71 = bf16[1,2,512,512]{3,2,1,0:T(8,128)(2,1)} custom-call(s32[8,4]{1,0:T(8,128)} %bitcast.24, s32[2]{0:T(128)} %pad_add_fusion.3.me, bf16[2,512,3072]{2,1,0:T(8,128)(2,1)} %band.3, bf16[2,512,3072]{2,1,0:T(8,128)(2,1)} %band.3, bf16[2,512,3072]{2,1,0:T(8,128)(2,1)} %band.3, bf16[2,512,3072]{2,1,0:T(8,128)(2,1)} %band.3, bf16[2,512,3072]{2,1,0:T(8,128)(2,1)} %band.3), custom_call_target="tpu_custom_call" | custom-call | flops 655360 | bytes 2300000 | tf_op jit(solution)/shard_map/pallas_call | solution.py:106
  20.6 4.6 %shard_map.70 = bf16[2,2,512,512]{3,2,1,0:T(8,128)(2,1)} custom-call(s32[8,4]{1,0:T(8,128)S(1)} %bitcast.26, s32[2]{0:T(128)S(1)} %copy-done.19, bf16[2,512,3072]{2,1,0:T(8,128)(2,1)S(1)} %copy-done, bf16[2,512,3072]{2,1,0:T(8,128)(2,1)S(1)} %copy-done, bf16[2,512,3072]{2,1,0:T(8,128)(2,1)S(1)} %copy-done, bf16[2,512,3072]{2,1,0:T(8,128)(2,1)S(1)} %copy-done, ...), custom_call_target="tpu_custom_call" | custom-call | flops 1310720 | bytes 4600000 | tf_op jit(solution)/shard_map/pallas_call | solution.py:106
  25.4 4.5 %shard_map.68 = bf16[1,2,512,512]{3,2,1,0:T(8,128)(2,1)} custom-call(s32[8,4]{1,0:T(8,128)} %bitcast.25, s32[2]{0:T(128)} %pad_add_fusion.3.me, bf16[2,512,3072]{2,1,0:T(8,128)(2,1)} %band.3, bf16[2,512,3072]{2,1,0:T(8,128)(2,1)} %band.3, bf16[2,512,3072]{2,1,0:T(8,128)(2,1)} %band.3, bf16[2,512,3072]{2,1,0:T(8,128)(2,1)} %band.3, bf16[2,512,3072]{2,1,0:T(8,128)(2,1)} %band.3), custom_call_target="tpu_custom_call" | custom-call | flops 655360 | bytes 2300000 | tf_op jit(solution)/shard_map/pallas_call | solution.py:106
  35.9 4.3 %fusion.8.refs_2_ = bf16[512,512]{1,0:T(8,128)(2,1)S(1)} fusion(s32[512]{0:T(512)S(1)} %iota.3), kind=kLoop, calls=%fused_computation.28 | loop fusion | flops 5242880 | bytes 526336 | tf_op jit(solution)/shard_map/neg | solution.py:33
  40.2 4.6 %multiply_convert_fusion = (bf16[512,512]{1,0:T(8,128)(2,1)S(1)}, bf16[512,512]{1,0:T(8,128)(2,1)S(1)}) fusion(s32[512]{0:T(512)S(1)} %iota.3), kind=kLoop, calls=%fused_computation.18 | loop fusion | flops 4980736 | bytes 1050624 | tf_op jit(solution)/shard_map/convert_element_type | solution.py:32
  44.9 12.7 %collective-permute-done.7.across = bf16[2,512,512]{2,1,0:T(8,128)(2,1)S(1)} collective-permute-done((bf16[2,512,512]{2,1,0:T(8,128)(2,1)S(1)}, bf16[2,512,512]{2,1,0:T(8,128)(2,1)S(1)}, u32[]{:S(2)}, u32[]{:S(2)}) %collective-permute-start.7) | collective-permute-done | bytes 1048608 | tf_op jit(solution)/shard_map/ppermute | solution.py:422
  57.6 9.7 %shard_map.73 = (bf16[8,2,64,512]{3,2,1,0:T(8,128)(2,1)S(1)}, f32[2,512,512]{2,1,0:T(8,128)S(1)}) custom-call(s32[8,4]{1,0:T(8,128)S(1)} %bitcast.29, s32[2]{0:T(128)S(1)} %copy-done.20, bf16[2,512,3072]{2,1,0:T(8,128)(2,1)S(1)} %copy-done.1, bf16[2,2,512,512]{3,2,1,0:T(8,128)(2,1)} %collective-permute-done.4.sibling, ...), custom_call_target="tpu_custom_call" | custom-call | flops 262144 | bytes 262144 | tf_op jit(solution)/shard_map/pallas_call | solution.py:322
  70.5 6.2 %all-to-all-start = ((bf16[8,2,64,512]{3,2,1,0:T(8,128)(2,1)}), bf16[8,2,64,512]{3,2,1,0:T(8,128)(2,1)}, u32[]{:S(2)}, u32[]{:S(2)}) async-start(bf16[8,2,64,512]{3,2,1,0:T(8,128)(2,1)} %copy-done.16), calls=%async_computation | async-start | bytes 2097152 | tf_op jit(solution)/shard_map/all_to_all | solution.py:451
  78.1 22.8 %collective-permute-done.5.across = bf16[2,512,512]{2,1,0:T(8,128)(2,1)S(1)} collective-permute-done((bf16[2,512,512]{2,1,0:T(8,128)(2,1)}, bf16[2,512,512]{2,1,0:T(8,128)(2,1)S(1)}, u32[]{:S(2)}, u32[]{:S(2)}) %collective-permute-start.5) | collective-permute-done | bytes 1048608 | tf_op jit(solution)/shard_map/ppermute | solution.py:422
  101.0 2.8 copy-done.2
  107.6 10.1 %shard_map.74 = (bf16[8,2,64,512]{3,2,1,0:T(8,128)(2,1)S(1)}, f32[512,512]{1,0:T(8,128)S(1)}, bf16[512,512]{1,0:T(8,128)(2,1)S(1)}) custom-call(s32[8,4]{1,0:T(8,128)S(1)} %bitcast.30, s32[2]{0:T(128)S(1)} %copy-done.20, bf16[2,512,3072]{2,1,0:T(8,128)(2,1)S(1)} %copy-done.2, bf16[2,2,512,512]{3,2,1,0:T(8,128)(2,1)} %collective-permute-done.4.sibling, ...), custom_call_target="tpu_custom_call" | custom-call | flops 262144 | bytes 262144 | tf_op jit(solution)/shard_map/pallas_call | solution.py:322
  120.5 5.7 %all-to-all-start.1 = ((bf16[8,2,64,512]{3,2,1,0:T(8,128)(2,1)}), bf16[8,2,64,512]{3,2,1,0:T(8,128)(2,1)S(1)}, u32[]{:S(2)}, u32[]{:S(2)}) async-start(bf16[8,2,64,512]{3,2,1,0:T(8,128)(2,1)} %copy-done.15), calls=%async_computation.1 | async-start | bytes 2097152 | tf_op jit(solution)/shard_map/all_to_all | solution.py:456
  128.2 5.2 %collective-permute-done.1 = s32[2,4]{0,1:T(4,128)S(1)} collective-permute-done((s32[2,4]{0,1:T(4,128)S(1)}, s32[2,4]{0,1:T(4,128)S(1)}, u32[]{:S(2)}, u32[]{:S(2)}) %collective-permute-start.1) | collective-permute-done | bytes 64 | tf_op jit(solution)/shard_map/ppermute | solution.py:425
  134.6 7.4 %collective-permute-done.2 = s32[4,4]{0,1:T(4,128)S(1)} collective-permute-done((s32[4,4]{0,1:T(4,128)S(1)}, s32[4,4]{0,1:T(4,128)S(1)}, u32[]{:S(2)}, u32[]{:S(2)}) %collective-permute-start.2) | collective-permute-done | bytes 96 | tf_op jit(solution)/shard_map/ppermute | solution.py:425
  142.1 4.3 %collective-permute-start.3 = (s32[8,4]{0,1:T(4,128)S(1)}, s32[8,4]{0,1:T(4,128)S(1)}, u32[]{:S(2)}, u32[]{:S(2)}) collective-permute-start(s32[8,4]{0,1:T(4,128)S(1)} %add_select_fusion.2), channel_id=1, source_target_pairs={{0,16},{4,20},{8,24},{12,28},{16,0},{20,4},{24,8},{28,12},{1,17},{... | collective-permute-start | bytes 392 | tf_op jit(solution)/shard_map/ppermute | solution.py:425
  146.4 4.1 %collective-permute-done.3 = s32[8,4]{0,1:T(4,128)S(1)} collective-permute-done((s32[8,4]{0,1:T(4,128)S(1)}, s32[8,4]{0,1:T(4,128)S(1)}, u32[]{:S(2)}, u32[]{:S(2)}) %collective-permute-start.3) | collective-permute-done | bytes 160 | tf_op jit(solution)/shard_map/ppermute | solution.py:425
  150.7 4.5 %shard_map.75 = (f32[2,2,64,3072]{3,2,1,0:T(8,128)S(1)}, bf16[2,2,64,3072]{3,2,1,0:T(8,128)(2,1)S(1)}) custom-call(s32[16,4]{1,0:T(8,128)S(1)} %broadcast_select_fusion.pos, s32[2]{0:T(128)S(1)} %copy-done.20, bf16[8,2,64,512]{3,2,1,0:T(8,128)(2,1)} %all-to-all-done.first, bf16[8,2,64,512]{3,2,1,0:T(8,128)(2,1)S(1)} %all-to-all-done.1.second), custom_call_target="tpu_custom_call" | custom-call | flops 4194304 | bytes 6815744 | tf_op jit(solution)/shard_map/pallas_call | solution.py:395
  156.8 2.9 collective-permute-done.9
  162.2 18.4 %collective-permute-done.10 = bf16[2,64,3072]{2,1,0:T(8,128)(2,1)} collective-permute-done((bf16[2,64,3072]{2,1,0:T(8,128)(2,1)}, bf16[2,64,3072]{2,1,0:T(8,128)(2,1)}, u32[]{:S(2)}, u32[]{:S(2)}) %collective-permute-start.10) | collective-permute-done | bytes 786464 | tf_op jit(solution)/shard_map/ppermute | solution.py:422
  180.6 3.5 %fusion.4 = bf16[2,64,3072]{2,1,0:T(8,128)(2,1)} fusion(bf16[2,64,3072]{2,1,0:T(8,128)(2,1)} %collective-permute-done.10, bf16[2,64,3072]{2,1,0:T(8,128)(2,1)} %collective-permute-done.8, f32[2,2,64,3072]{3,2,1,0:T(8,128)} %copy-done.9, bf16[2,512,3072]{2,1,0:T(8,128)(2,1)} %band.3, s32[]{:T(128)S(6)} %select_n.161), kind=kLoop, calls=%fused_computation.10 | loop fusion | flops 3145728 | bytes 4718596 | tf_op jit(solution)/shard_map/convert_element_type | solution.py:466
  184.2 2.2 collective-permute-done.11
  190.2 6.9 %collective-permute-done.12 = bf16[256,512]{1,0:T(8,128)(2,1)S(1)} collective-permute-done((bf16[256,512]{1,0:T(8,128)(2,1)S(1)}, bf16[256,512]{1,0:T(8,128)(2,1)S(1)}, u32[]{:S(2)}, u32[]{:S(2)}) %collective-permute-start.12) | collective-permute-done | bytes 262176 | tf_op jit(solution)/shard_map/ppermute | solution.py:422
  199.5 5.9 %collective-permute-done.13 = bf16[128,512]{1,0:T(8,128)(2,1)S(1)} collective-permute-done((bf16[128,512]{1,0:T(8,128)(2,1)S(1)}, bf16[128,512]{1,0:T(8,128)(2,1)S(1)}, u32[]{:S(2)}, u32[]{:S(2)}) %collective-permute-start.13) | collective-permute-done | bytes 131104 | tf_op jit(solution)/shard_map/ppermute | solution.py:425
  206.6 8.6 %collective-permute-done.14 = bf16[64,512]{1,0:T(8,128)(2,1)S(1)} collective-permute-done((bf16[64,512]{1,0:T(8,128)(2,1)S(1)}, bf16[64,512]{1,0:T(8,128)(2,1)S(1)}, u32[]{:S(2)}, u32[]{:S(2)}) %collective-permute-start.14) | collective-permute-done | bytes 65568 | tf_op jit(solution)/shard_map/ppermute | solution.py:425
  215.7 5.8 %collective-permute-done.15 = bf16[32,512]{1,0:T(8,128)(2,1)S(1)} collective-permute-done((bf16[32,512]{1,0:T(8,128)(2,1)S(1)}, bf16[32,512]{1,0:T(8,128)(2,1)S(1)}, u32[]{:S(2)}, u32[]{:S(2)}) %collective-permute-start.15) | collective-permute-done | bytes 32800 | tf_op jit(solution)/shard_map/ppermute | solution.py:425
  221.5 4.8 %collective-permute-done.16 = bf16[32,512]{1,0:T(8,128)(2,1)S(1)} collective-permute-done((bf16[32,512]{1,0:T(8,128)(2,1)S(1)}, bf16[32,512]{1,0:T(8,128)(2,1)S(1)}, u32[]{:S(2)}, u32[]{:S(2)}) %collective-permute-start.16) | collective-permute-done | bytes 32800 | tf_op jit(solution)/shard_map/ppermute | solution.py:425
  226.4 6.4 %collective-permute-done.17 = bf16[64,512]{1,0:T(8,128)(2,1)S(1)} collective-permute-done((bf16[64,512]{1,0:T(8,128)(2,1)S(1)}, bf16[64,512]{1,0:T(8,128)(2,1)S(1)}, u32[]{:S(2)}, u32[]{:S(2)}) %collective-permute-start.17) | collective-permute-done | bytes 65568 | tf_op jit(solution)/shard_map/ppermute | solution.py:425
  234.4 6.3 %collective-permute-done.18 = bf16[128,512]{1,0:T(8,128)(2,1)S(1)} collective-permute-done((bf16[128,512]{1,0:T(8,128)(2,1)S(1)}, bf16[128,512]{1,0:T(8,128)(2,1)S(1)}, u32[]{:S(2)}, u32[]{:S(2)}) %collective-permute-start.18) | collective-permute-done | bytes 131104 | tf_op jit(solution)/shard_map/ppermute | solution.py:425
  242.3 4.9 %collective-permute-done.19 = bf16[256,512]{1,0:T(8,128)(2,1)S(1)} collective-permute-done((bf16[256,512]{1,0:T(8,128)(2,1)S(1)}, bf16[256,512]{1,0:T(8,128)(2,1)S(1)}, u32[]{:S(2)}, u32[]{:S(2)}) %collective-permute-start.19) | collective-permute-done | bytes 262176 | tf_op jit(solution)/shard_map/ppermute | solution.py:422
  251.1 35.2 %all-gather.3.cloned.1.call-done = bf16[2,512,3072]{2,1,0:T(8,128)(2,1)} async-done(((bf16[2,64,3072]{2,1,0:T(8,128)(2,1)}), bf16[2,512,3072]{2,1,0:T(8,128)(2,1)}) %all-gather.3.cloned.1.call-update) | async-done | bytes 6291472 | tf_op jit(solution)/shard_map/all_gather | solution.py:467
  286.3 5.9 %copy.13 = bf16[2,512,3072]{2,1,0:T(8,128)(2,1)} copy(bf16[2,512,3072]{2,1,0:T(8,128)(2,1)} %all-gather.3.cloned.1.call-done) | data formatting | bytes 12582912
  (104 shorter events, 42.6 us)
Async XLA Ops:
  20.3 9.9 %collective-permute-start.6 = (bf16[1,2,512,512]{3,2,1,0:T(8,128)(2,1)}, bf16[1,2,512,512]{3,2,1,0:T(8,128)(2,1)S(1)}, u32[]{:S(2)}, u32[]{:S(2)}) collective-permute-start(bf16[1,2,512,512]{3,2,1,0:T(8,128)(2,1)} %shard_map.71), channel_id=1, source_target_pairs={{0,1},{1,0},{2,3},{3,2},{4,5},{5,4},{6,7},{7,6},{8,9},{9,8},{10,11... | collective-permute-start | bytes 3145736 | tf_op jit(solution)/shard_map/ppermute | solution.py:422
  25.2 5.0 %copy-start.18 = (s32[4,2,4]{2,1,0:T(2,128)S(1)}, s32[4,2,4]{2,1,0:T(2,128)}, u32[]{:S(2)}) copy-start(s32[4,2,4]{2,1,0:T(2,128)} %all-gather) | copy-start | bytes 388
  25.2 5.0 %copy-start.20 = (s32[2]{0:T(128)S(1)}, s32[2]{0:T(128)}, u32[]{:S(2)}) copy-start(s32[2]{0:T(128)} %pad_add_fusion.3.me) | copy-start | bytes 28
  25.2 19.7 %collective-permute-start.4 = (bf16[2,2,512,512]{3,2,1,0:T(8,128)(2,1)}, bf16[2,2,512,512]{3,2,1,0:T(8,128)(2,1)}, u32[]{:S(2)}, u32[]{:S(2)}) collective-permute-start(bf16[2,2,512,512]{3,2,1,0:T(8,128)(2,1)} %shard_map.70), channel_id=1, source_target_pairs={{0,1},{1,0},{2,3},{3,2},{4,5},{5,4},{6,7},{7,6},{8,9},{9,8},{10,11... | collective-permute-start | bytes 6291464 | tf_op jit(solution)/shard_map/ppermute | solution.py:422
  25.4 4.8 %copy-start.1 = (bf16[2,512,3072]{2,1,0:T(8,128)(2,1)S(1)}, bf16[2,512,3072]{2,1,0:T(8,128)(2,1)}, u32[]{:S(2)}) copy-start(bf16[2,512,3072]{2,1,0:T(8,128)(2,1)} %band.3) | copy-start | bytes 18874372
  29.8 4.3 %collective-permute-start = (bf16[1,2,512,512]{3,2,1,0:T(8,128)(2,1)}, bf16[1,2,512,512]{3,2,1,0:T(8,128)(2,1)S(1)}, u32[]{:S(2)}, u32[]{:S(2)}) collective-permute-start(bf16[1,2,512,512]{3,2,1,0:T(8,128)(2,1)} %shard_map.68), channel_id=1, source_target_pairs={{0,1},{1,0},{2,3},{3,2},{4,5},{5,4},{6,7},{7,6},{8,9},{9,8},{10,11... | collective-permute-start | bytes 3145736 | tf_op jit(solution)/shard_map/ppermute | solution.py:422
  32.0 25.6 %collective-permute-start.7 = (bf16[2,512,512]{2,1,0:T(8,128)(2,1)S(1)}, bf16[2,512,512]{2,1,0:T(8,128)(2,1)S(1)}, u32[]{:S(2)}, u32[]{:S(2)}) collective-permute-start(bf16[2,512,512]{2,1,0:T(8,128)(2,1)S(1)} %shard_map.72), channel_id=1, source_target_pairs={{0,2},{1,3},{2,0},{3,1},{4,6},{5,7},{6,4},{7,5},{8,10},{9,11},{10,... | collective-permute-start | bytes 3145736 | tf_op jit(solution)/shard_map/ppermute | solution.py:422
  34.1 23.5 %copy-start.3 = (f32[2,512,512]{2,1,0:T(8,128)S(1)}, f32[2,512,512]{2,1,0:T(8,128)}, u32[]{:S(2)}) copy-start(f32[2,512,512]{2,1,0:T(8,128)} %probe.3) | copy-start | bytes 6291460
  35.9 21.7 %copy-start.12 = (bf16[2,512,512]{2,1,0:T(8,128)(2,1)}, bf16[2,512,512]{2,1,0:T(8,128)(2,1)S(1)}, u32[]{:S(2)}) copy-start(bf16[2,512,512]{2,1,0:T(8,128)(2,1)S(1)} %shard_map.69) | copy-start | bytes 3145732
  35.9 21.7 %copy-start.7 = (bf16[2,512,512]{2,1,0:T(8,128)(2,1)S(1)}, bf16[2,512,512]{2,1,0:T(8,128)(2,1)}, u32[]{:S(2)}) copy-start(bf16[2,512,512]{2,1,0:T(8,128)(2,1)} %amplitudes.3) | copy-start | bytes 3145732
  70.5 30.5 %copy-start.4 = (f32[2,512,512]{2,1,0:T(8,128)S(1)}, f32[2,512,512]{2,1,0:T(8,128)}, u32[]{:S(2)}) copy-start(f32[2,512,512]{2,1,0:T(8,128)} %probe.3) | copy-start | bytes 6291460
  70.5 50.0 %all-to-all-start = ((bf16[8,2,64,512]{3,2,1,0:T(8,128)(2,1)}), bf16[8,2,64,512]{3,2,1,0:T(8,128)(2,1)}, u32[]{:S(2)}, u32[]{:S(2)}) async-start(bf16[8,2,64,512]{3,2,1,0:T(8,128)(2,1)} %copy-done.16), calls=%async_computation | async-start | bytes 2097152 | tf_op jit(solution)/shard_map/all_to_all | solution.py:451
  76.6 24.4 %collective-permute-start.5 = (bf16[2,512,512]{2,1,0:T(8,128)(2,1)}, bf16[2,512,512]{2,1,0:T(8,128)(2,1)S(1)}, u32[]{:S(2)}, u32[]{:S(2)}) collective-permute-start(bf16[2,512,512]{2,1,0:T(8,128)(2,1)} %copy-done.12), channel_id=1, source_target_pairs={{0,2},{1,3},{2,0},{3,1},{4,6},{5,7},{6,4},{7,5},{8,10},{9,11},{10,... | collective-permute-start | bytes 3145736 | tf_op jit(solution)/shard_map/ppermute | solution.py:422
  120.5 30.2 %all-to-all-start.1 = ((bf16[8,2,64,512]{3,2,1,0:T(8,128)(2,1)}), bf16[8,2,64,512]{3,2,1,0:T(8,128)(2,1)S(1)}, u32[]{:S(2)}, u32[]{:S(2)}) async-start(bf16[8,2,64,512]{3,2,1,0:T(8,128)(2,1)} %copy-done.15), calls=%async_computation.1 | async-start | bytes 2097152 | tf_op jit(solution)/shard_map/all_to_all | solution.py:456
  126.2 160.1 %all-gather.3.cloned.1.call-start = ((), (), s32[]{:S(2)}) async-start(), calls=%async_computation.2 | async-start | bytes 7077888 | tf_op jit(solution)/shard_map/all_gather | solution.py:467
  126.3 7.2 %collective-permute-start.1 = (s32[2,4]{0,1:T(4,128)S(1)}, s32[2,4]{0,1:T(4,128)S(1)}, u32[]{:S(2)}, u32[]{:S(2)}) collective-permute-start(s32[2,4]{0,1:T(4,128)S(1)} %pad_add_fusion), channel_id=1, source_target_pairs={{0,4},{4,0},{8,12},{12,8},{16,20},{20,16},{24,28},{28,24},{1,5},{5... | collective-permute-start | bytes 104 | tf_op jit(solution)/shard_map/ppermute | solution.py:425
  133.6 8.4 %collective-permute-start.2 = (s32[4,4]{0,1:T(4,128)S(1)}, s32[4,4]{0,1:T(4,128)S(1)}, u32[]{:S(2)}, u32[]{:S(2)}) collective-permute-start(s32[4,4]{0,1:T(4,128)S(1)} %add_select_fusion.1), channel_id=1, source_target_pairs={{0,8},{4,12},{8,0},{12,4},{16,24},{20,28},{24,16},{28,20},{1,9},{5... | collective-permute-start | bytes 200 | tf_op jit(solution)/shard_map/ppermute | solution.py:425
  142.1 8.4 %collective-permute-start.3 = (s32[8,4]{0,1:T(4,128)S(1)}, s32[8,4]{0,1:T(4,128)S(1)}, u32[]{:S(2)}, u32[]{:S(2)}) collective-permute-start(s32[8,4]{0,1:T(4,128)S(1)} %add_select_fusion.2), channel_id=1, source_target_pairs={{0,16},{4,20},{8,24},{12,28},{16,0},{20,4},{24,8},{28,12},{1,17},{... | collective-permute-start | bytes 392 | tf_op jit(solution)/shard_map/ppermute | solution.py:425
  156.3 3.4 %collective-permute-start.9 = (bf16[2,64,3072]{2,1,0:T(8,128)(2,1)S(1)}, bf16[2,64,3072]{2,1,0:T(8,128)(2,1)S(1)}, u32[]{:S(2)}, u32[]{:S(2)}) collective-permute-start(bf16[2,64,3072]{2,1,0:T(8,128)(2,1)S(1)} %get-tuple-element.27), channel_id=1, source_target_pairs={{0,1},{1,0},{2,3},{3,2},{4,5},{5,4},{6,7},{7,6},{8,9},{9,8},{10,11... | collective-permute-start | bytes 2359304 | tf_op jit(solution)/shard_map/ppermute | solution.py:422
  156.3 5.9 %collective-permute-start.8 = (bf16[2,64,3072]{2,1,0:T(8,128)(2,1)}, bf16[2,64,3072]{2,1,0:T(8,128)(2,1)}, u32[]{:S(2)}, u32[]{:S(2)}) collective-permute-start(bf16[2,64,3072]{2,1,0:T(8,128)(2,1)} %get-tuple-element.26), channel_id=1, source_target_pairs={{0,1},{1,0},{2,3},{3,2},{4,5},{5,4},{6,7},{7,6},{8,9},{9,8},{10,11... | collective-permute-start | bytes 2359304 | tf_op jit(solution)/shard_map/ppermute | solution.py:422
  160.7 19.9 %collective-permute-start.10 = (bf16[2,64,3072]{2,1,0:T(8,128)(2,1)}, bf16[2,64,3072]{2,1,0:T(8,128)(2,1)}, u32[]{:S(2)}, u32[]{:S(2)}) collective-permute-start(bf16[2,64,3072]{2,1,0:T(8,128)(2,1)} %fusion), channel_id=1, source_target_pairs={{0,2},{1,3},{2,0},{3,1},{4,6},{5,7},{6,4},{7,5},{8,10},{9,11},{10,... | collective-permute-start | bytes 2359304 | tf_op jit(solution)/shard_map/ppermute | solution.py:422
  162.2 24.3 %copy-start.14 = (f32[512,512]{1,0:T(8,128)S(1)}, f32[512,512]{1,0:T(8,128)}, u32[]{:S(2)}) copy-start(f32[512,512]{1,0:T(8,128)} %copy-done.13) | copy-start | bytes 3145732
  184.1 2.3 collective-permute-start.11
  188.7 8.4 %collective-permute-start.12 = (bf16[256,512]{1,0:T(8,128)(2,1)S(1)}, bf16[256,512]{1,0:T(8,128)(2,1)S(1)}, u32[]{:S(2)}, u32[]{:S(2)}) collective-permute-start(bf16[256,512]{1,0:T(8,128)(2,1)S(1)} %dynamic-slice_convert_fusion), channel_id=1, source_target_pairs={{0,2},{1,3},{2,0},{3,1},{4,6},{5,7},{6,4},{7,5},{8,10},{9,11},{10,... | collective-permute-start | bytes 786440 | tf_op jit(solution)/shard_map/ppermute | solution.py:422
  198.2 7.1 %collective-permute-start.13 = (bf16[128,512]{1,0:T(8,128)(2,1)S(1)}, bf16[128,512]{1,0:T(8,128)(2,1)S(1)}, u32[]{:S(2)}, u32[]{:S(2)}) collective-permute-start(bf16[128,512]{1,0:T(8,128)(2,1)S(1)} %dynamic-slice_convert_fusion.1), channel_id=1, source_target_pairs={{0,4},{4,0},{8,12},{12,8},{16,20},{20,16},{24,28},{28,24},{1,5},{5... | collective-permute-start | bytes 393224 | tf_op jit(solution)/shard_map/ppermute | solution.py:425
  205.4 9.8 %collective-permute-start.14 = (bf16[64,512]{1,0:T(8,128)(2,1)S(1)}, bf16[64,512]{1,0:T(8,128)(2,1)S(1)}, u32[]{:S(2)}, u32[]{:S(2)}) collective-permute-start(bf16[64,512]{1,0:T(8,128)(2,1)S(1)} %dynamic-slice_convert_fusion.2), channel_id=1, source_target_pairs={{0,8},{4,12},{8,0},{12,4},{16,24},{20,28},{24,16},{28,20},{1,9},{5... | collective-permute-start | bytes 196616 | tf_op jit(solution)/shard_map/ppermute | solution.py:425
  215.2 6.2 %collective-permute-start.15 = (bf16[32,512]{1,0:T(8,128)(2,1)S(1)}, bf16[32,512]{1,0:T(8,128)(2,1)S(1)}, u32[]{:S(2)}, u32[]{:S(2)}) collective-permute-start(bf16[32,512]{1,0:T(8,128)(2,1)S(1)} %dynamic-slice_convert_fusion.3), channel_id=1, source_target_pairs={{0,16},{4,20},{8,24},{12,28},{16,0},{20,4},{24,8},{28,12},{1,17},{... | collective-permute-start | bytes 98312 | tf_op jit(solution)/shard_map/ppermute | solution.py:425
  221.5 4.9 %collective-permute-start.16 = (bf16[32,512]{1,0:T(8,128)(2,1)S(1)}, bf16[32,512]{1,0:T(8,128)(2,1)S(1)}, u32[]{:S(2)}, u32[]{:S(2)}) collective-permute-start(bf16[32,512]{1,0:T(8,128)(2,1)S(1)} %add_convert_fusion), channel_id=1, source_target_pairs={{0,16},{4,20},{8,24},{12,28},{16,0},{20,4},{24,8},{28,12},{1,17},{... | collective-permute-start | bytes 98312 | tf_op jit(solution)/shard_map/ppermute | solution.py:425
  226.4 6.5 %collective-permute-start.17 = (bf16[64,512]{1,0:T(8,128)(2,1)S(1)}, bf16[64,512]{1,0:T(8,128)(2,1)S(1)}, u32[]{:S(2)}, u32[]{:S(2)}) collective-permute-start(bf16[64,512]{1,0:T(8,128)(2,1)S(1)} %maximum_select_fusion.4), channel_id=1, source_target_pairs={{0,8},{4,12},{8,0},{12,4},{16,24},{20,28},{24,16},{28,20},{1,9},{5... | collective-permute-start | bytes 196616 | tf_op jit(solution)/shard_map/ppermute | solution.py:425
  232.9 7.8 %collective-permute-start.18 = (bf16[128,512]{1,0:T(8,128)(2,1)S(1)}, bf16[128,512]{1,0:T(8,128)(2,1)S(1)}, u32[]{:S(2)}, u32[]{:S(2)}) collective-permute-start(bf16[128,512]{1,0:T(8,128)(2,1)S(1)} %maximum_select_fusion.3), channel_id=1, source_target_pairs={{0,4},{4,0},{8,12},{12,8},{16,20},{20,16},{24,28},{28,24},{1,5},{5... | collective-permute-start | bytes 393224 | tf_op jit(solution)/shard_map/ppermute | solution.py:425
  240.8 6.4 %collective-permute-start.19 = (bf16[256,512]{1,0:T(8,128)(2,1)S(1)}, bf16[256,512]{1,0:T(8,128)(2,1)S(1)}, u32[]{:S(2)}, u32[]{:S(2)}) collective-permute-start(bf16[256,512]{1,0:T(8,128)(2,1)S(1)} %maximum_select_fusion.2), channel_id=1, source_target_pairs={{0,2},{1,3},{2,0},{3,1},{4,6},{5,7},{6,4},{7,5},{8,10},{9,11},{10,... | collective-permute-start | bytes 786440 | tf_op jit(solution)/shard_map/ppermute | solution.py:422
  247.4 2.0 collective-permute-start.20
  (15 other events, 32.3 us)
Sparse Core Ops, SparseCore 0:
  184.3 102.0 all-gather.2

commit v4 on v3

--- a/solution.py
+++ b/solution.py
@@ -3,6 +3,7 @@
 
 import jax
 import jax.numpy as jnp
+import numpy as np
 from jax import lax
 from jax.experimental import pallas as pl
 from jax.experimental.pallas import tpu as pltpu
@@ -16,21 +17,21 @@
 OBJECT_RATE = 0.1
 PROBE_RATE = 0.05
 MAGNITUDE_FLOOR = 0.5
-ALL_VMEM = 56 * 1024 * 1024
 CUT_VMEM = 14 * 1024 * 1024
 WAVE_VMEM = 32 * 1024 * 1024
 SUM_VMEM = 24 * 1024 * 1024
-
-
-def dft_tables(counter):
-    length = counter.shape[0]
-    phase_angle = (counter[:, None] * counter[None, :] % length).astype(jnp.float32) * (
+BY_PERMUTE = (4, 8)
+
+
+def dft_tables(length):
+    counter = np.arange(length, dtype=np.int32)
+    phase_angle = (counter[:, None] * counter[None, :] % length).astype(np.float32) * np.float32(
         2.0 * math.pi / length
     )
-    factor = 1.0 / math.sqrt(length)
-    cosine = (jnp.cos(phase_angle) * factor).astype(jnp.bfloat16)
-    sine_part = (-jnp.sin(phase_angle) * factor).astype(jnp.bfloat16)
-    return cosine, sine_part, -sine_part
+    factor = np.float32(1.0 / math.sqrt(length))
+    cosine = (np.cos(phase_angle) * factor).astype(jnp.bfloat16)
+    sine_part = (-np.sin(phase_angle) * factor).astype(jnp.bfloat16)
+    return jnp.asarray(cosine), jnp.asarray(sine_part), jnp.asarray(-sine_part)
 
 
 def first_row(pos, index):
@@ -96,7 +97,7 @@
     lax.fori_loop(0, PATCH // CHUNK, body, 0)
 
 
-def cut(band, pos, me, flip, first, count, vmem):
+def cut(band, pos, me, flip, first, count):
     def block(k):
         def index(i, pos, me):
             return (0, 0, first_col(pos, 2 * lax.bitwise_xor(me[0], flip) + first + i) // LANES + k)
@@ -112,7 +113,7 @@
             out_specs=pl.BlockSpec((1, 2, PATCH, PATCH), lambda i, pos, me: (i, 0, 0, 0)),
         ),
         out_shape=jax.ShapeDtypeStruct((count, 2, PATCH, PATCH), jnp.bfloat16),
-        compiler_params=pltpu.CompilerParams(vmem_limit_bytes=vmem),
+        compiler_params=pltpu.CompilerParams(vmem_limit_bytes=CUT_VMEM),
         cost_estimate=pl.CostEstimate(
             flops=count * 2 * PATCH * WIDE, bytes_accessed=count * 2300000, transcendentals=0
         ),
@@ -161,7 +162,59 @@
     )(pos, me, *([band] * (WIDE // LANES)), sibling)
 
 
-def wave_kernel(which, pos, me, band, sibling, across, probe, amplitudes, *refs):
+def rest_index(step, pos, me):
+    return jnp.where(step == 0, 2 * lax.bitwise_xor(me[0], 3) + 1, 2 * lax.bitwise_xor(me[0], 1) + step - 1)
+
+
+def rest_kernel(pos, me, *refs):
+    blocks, second, pieces = refs[:-2], refs[-2], refs[-1]
+    step = pl.program_id(0)
+    amount = lax.rem(first_col(pos, rest_index(step, pos, me)), LANES)
+
+    def take(out):
+        def body(i, carry):
+            rows = pl.ds(pl.multiple_of(i * CHUNK, CHUNK), CHUNK)
+            for plane in range(2):
+                out[0, plane, rows, :] = cut_rows(blocks, plane, rows, amount).astype(jnp.bfloat16)
+            return carry
+
+        lax.fori_loop(0, PATCH // CHUNK, body, 0)
+
+    pl.when(step == 0)(lambda: take(second))
+    pl.when(step > 0)(lambda: take(pieces))
+
+
+def cut_rest(band, pos, me):
+    def block(k):
+        def index(i, pos, me):
+            return (0, 0, first_col(pos, rest_index(i, pos, me)) // LANES + k)
+
+        return pl.BlockSpec((2, PATCH, LANES), index)
+
+    shape = (2, PATCH, PATCH)
+    return pl.pallas_call(
+        rest_kernel,
+        grid_spec=pltpu.PrefetchScalarGridSpec(
+            num_scalar_prefetch=2,
+            grid=(3,),
+            in_specs=[block(k) for k in range(WIDE // LANES)],
+            out_specs=[
+                pl.BlockSpec((1, *shape), lambda i, pos, me: (0, 0, 0, 0)),
+                pl.BlockSpec((1, *shape), lambda i, pos, me: (jnp.maximum(i - 1, 0), 0, 0, 0)),
+            ],
+        ),
+        out_shape=[
+            jax.ShapeDtypeStruct((1, *shape), jnp.bfloat16),
+            jax.ShapeDtypeStruct((2, *shape), jnp.bfloat16),
+        ],
+        compiler_params=pltpu.CompilerParams(vmem_limit_bytes=CUT_VMEM),
+        cost_estimate=pl.CostEstimate(
+            flops=6 * PATCH * WIDE, bytes_accessed=7000000, transcendentals=0
+        ),
+    )(pos, me, *([band] * (WIDE // LANES)))
+
+
+def wave_kernel(which, pos, me, spare, band, sibling, across, probe, amplitudes, *refs):
     tables, refs = refs[:3], refs[3:]
     last = which == 1
     if last:
@@ -307,7 +360,7 @@
     lax.fori_loop(0, classes, spread, 0)
 
 
-def wave(which, classes, pos, me, band, sibling, across, probe, amplitudes, tables, term):
+def wave(which, classes, pos, me, spare, band, sibling, across, probe, amplitudes, tables, term):
     operands = [band, sibling, across, probe, amplitudes, *tables]
     smem = pl.BlockSpec(memory_space=pltpu.SMEM)
     hbm = pl.BlockSpec(memory_space=pl.ANY)
@@ -321,7 +374,7 @@
         terms = [jax.ShapeDtypeStruct(plane, t) for t in (jnp.float32, jnp.bfloat16)]
     return pl.pallas_call(
         functools.partial(wave_kernel, which),
-        in_specs=[smem, smem] + [hbm] * len(operands),
+        in_specs=[smem, smem, smem] + [hbm] * len(operands),
         out_specs=[vmem] * (1 + len(terms)),
         out_shape=[
             jax.ShapeDtypeStruct((classes, 2, PATCH // classes, PATCH), jnp.bfloat16),
@@ -344,9 +397,9 @@
         ],
         compiler_params=pltpu.CompilerParams(vmem_limit_bytes=WAVE_VMEM),
         cost_estimate=pl.CostEstimate(
-            flops=PATCH**2, bytes_accessed=PATCH**2, transcendentals=0
-        ),
-    )(pos, me, *operands)
+            flops=32 * PATCH**3, bytes_accessed=100_000_000, transcendentals=0
+        ),
+    )(pos, me, spare, *operands)
 
 
 def sum_kernel(pos, me, first, second, own, away, canvas):
@@ -408,6 +461,89 @@
     )(pos, me, first, second)
 
 
+def assemble_kernel(length, me, *refs):
+    steps = length - 1
+    own, refs = refs[0], refs[1:]
+    ups, downs, overs = refs[:steps], refs[steps : 2 * steps], refs[2 * steps : 3 * steps + 1]
+    out, sems = refs[3 * steps + 1 :]
+    height = own.shape[1]
+    place = me[1] // 2
+    side = lax.rem(me[1], 2)
+
+    def copy(source, at, column, k):
+        rows = pl.ds(pl.multiple_of((2 * at + column) * height, height), height)
+        return pltpu.make_async_copy(source, out.at[:, rows, :], sems.at[k])
+
+    always = [copy(own, place, side, 0)]
+    for k in range(length):
+        always.append(copy(overs[k], sent_over(place, k, length), 1 - side, k + 1))
+    some = []
+    for k in range(1, length):
+        below, above = place - k, place + k
+        held = length + 2 * k - 1
+        some.append((below >= 0, copy(ups[k - 1], below, side, held)))
+        some.append((above < length, copy(downs[k - 1], above, side, held + 1)))
+    for part in always:
+        part.start()
+    for has, part in some:
+        pl.when(has)(part.start)
+    for part in always:
+        part.wait()
+    for has, part in some:
+        pl.when(has)(part.wait)
+
+
+def sent_over(place, k, length):
+    low = jnp.where(place >= k, place - k, place + k)
+    if k == length - 1:
+        high = jnp.where(place == 0, length - 1, jnp.where(place == length - 1, 0, place + 1))
+        return high
+    return low
+
+
+def gather_classes(own, me, classes, term, term_steps):
+    length = classes // 2
+    place = me[1] // 2
+
+    def along(value, held, step):
+        pairs = [(2 * z + x, 2 * (z + step) + x) for z in held if 0 <= z + step < length for x in range(2)]
+        return lax.ppermute(value, "pat", pairs)
+
+    def over(value):
+        return lax.ppermute(value, "pat", [(k, k ^ 1) for k in range(classes)])
+
+    ups, downs, overs = [own], [own], []
+    for k in range(length - 1):
+        overs.append(over(jnp.where(place >= k, ups[k], downs[k]) if k else own))
+        ups.append(along(ups[k], range(k, length), 1))
+        downs.append(along(downs[k], range(length - k), -1))
+        for step in term_steps[k : k + 1] if k < length - 2 else term_steps[k:-1]:
+            term = step(term)
+        overs[k], ups[k + 1], downs[k + 1], term = lax.optimization_barrier(
+            (overs[k], ups[k + 1], downs[k + 1], term)
+        )
+    end = jnp.where(place == 0, downs[-1], ups[-1])
+    if length > 2:
+        middle = (place > 0) & (place < length - 1)
+        end = jnp.where(middle, downs[1], end)
+    last, term = lax.optimization_barrier((over(end), term_steps[-1](term)))
+    overs.append(last)
+    operands = [own, *ups[1:], *downs[1:], *overs]
+    hbm = pl.BlockSpec(memory_space=pl.ANY)
+    object_next = pl.pallas_call(
+        functools.partial(assemble_kernel, length),
+        in_specs=[pl.BlockSpec(memory_space=pltpu.SMEM)] + [hbm] * len(operands),
+        out_specs=hbm,
+        out_shape=jax.ShapeDtypeStruct((2, classes * own.shape[1], own.shape[2]), own.dtype),
+        scratch_shapes=[pltpu.SemaphoreType.DMA((3 * length - 1,))],
+        compiler_params=pltpu.CompilerParams(vmem_limit_bytes=CUT_VMEM),
+        cost_estimate=pl.CostEstimate(
+            flops=0, bytes_accessed=4 * own.size * classes, transcendentals=0
+        ),
+    )(me, *operands)
+    return object_next, term
+
+
 def shards(object_image, probe, amplitudes, pos_tile, pos_offset):
     owners = lax.axis_size("obj")
     classes = lax.axis_size("pat")
@@ -437,46 +573,55 @@
     own_pos = jnp.concatenate([pos_tile, pos_offset], 1)
     pos = lax.all_gather(own_pos, "obj", axis=0, tiled=True)
 
-    relay = [flip(cut(object_image, pos, me, 3, k, 1, ALL_VMEM), 1) for k in range(2)]
-    merged = [cut_and_merge(object_image, relay[k], pos, me, k) for k in range(2)]
-    counter = jnp.arange(PATCH, dtype=jnp.int32)
-    merged[1], counter, pos_pat = lax.optimization_barrier((merged[1], counter, own_pos))
+    first = cut(object_image, pos, me, 3, 0, 1)
+    second, pieces = cut_rest(object_image, pos, me)
+    second, pieces, then = lax.optimization_barrier((second, pieces, me))
+    relay = [flip(first, 1), flip(second, 1)]
+    sibling = flip(pieces, 1)
+    merged = [cut_and_merge(object_image, relay[k], pos, then, k) for k in range(2)]
+    merged[1], pos_pat = lax.optimization_barrier((merged[1], own_pos))
     across = [flip(m, 2) for m in merged]
-    sibling = flip(cut(object_image, pos, me, 1, 0, 2, CUT_VMEM), 1)
     for bit in bits:
         pos_pat = doubled(pos_pat, my_class // bit % 2, pat_flip(bit))
 
-    operands = (probe, amplitudes, dft_tables(counter))
-    grad_0, term = wave(0, classes, pos, me, object_image, sibling, across[0], *operands, None)
+    operands = (probe, amplitudes, dft_tables(PATCH))
+    grad_0, term = wave(0, classes, pos, me, me, object_image, sibling, across[0], *operands, None)
     part_0 = lax.all_to_all(grad_0, "pat", split_axis=0, concat_axis=0, tiled=True)
     grad_1, keep_term, give_term = wave(
-        1, classes, pos, me, object_image, sibling, across[1], *operands, term
+        1, classes, pos, me, pos_pat, object_image, sibling, across[1], *operands, term
     )
     grad_1, part_0 = lax.optimization_barrier((grad_1, part_0))
     part_1 = lax.all_to_all(grad_1, "pat", split_axis=0, concat_axis=0, tiled=True)
 
-    own, away = sum_pieces(pos_pat, me, part_0, part_1, owners, width)
+    core = my_owner % 2
+    line = my_owner // 2
+    term = keep_term + flip(give_term, 1).astype(jnp.float32)
+    term = halved(term, line, lambda value: flip(value, 2))
+    term, then = lax.optimization_barrier((term, me))
+    own, away = sum_pieces(pos_pat, then, part_0, part_1, owners, width)
     from_sibling_far = flip(away[0], 1)
     from_sibling = flip(away[1], 1)
     from_across = flip(
         (own[0] + from_sibling_far.astype(jnp.float32)).astype(jnp.bfloat16), 2
     )
+    for bit in bits:
+        term = halved(term, my_class // bit % 2, pat_flip(bit))
     total = own[1] + from_sibling.astype(jnp.float32) + from_across.astype(jnp.float32)
     mine = lax.dynamic_slice_in_dim(object_image, my_class * height, height, 1)
     updated = (mine.astype(jnp.float32) - OBJECT_RATE * total).astype(jnp.bfloat16)
-    object_next = lax.all_gather(updated, "pat", axis=1, tiled=True)
-
-    core = my_owner % 2
-    line = my_owner // 2
-    part = keep_term + flip(give_term, 1).astype(jnp.float32)
-    part = halved(part, line, lambda value: flip(value, 2))
-    for bit in bits:
-        part = halved(part, my_class // bit % 2, pat_flip(bit))
-    part = part.astype(jnp.bfloat16)
-    for bit in reversed(bits):
-        part = doubled(part, my_class // bit % 2, pat_flip(bit))
-    part = doubled(part, line, lambda value: flip(value, 2))
-    probe_total = doubled(part[None], core, lambda value: flip(value, 1)).astype(jnp.float32)
+    updated, term = lax.optimization_barrier((updated, term.astype(jnp.bfloat16)))
+    steps = [
+        functools.partial(doubled, bit=my_class // bit % 2, other=pat_flip(bit)) for bit in reversed(bits)
+    ]
+    steps.append(functools.partial(doubled, bit=line, other=lambda value: flip(value, 2)))
+    steps.append(lambda part: doubled(part[None], core, lambda value: flip(value, 1)))
+    if classes in BY_PERMUTE:
+        object_next, term = gather_classes(updated, me, classes, term, steps)
+    else:
+        object_next = lax.all_gather(updated, "pat", axis=1, tiled=True)
+        for step in steps:
+            term = step(term)
+    probe_total = term.astype(jnp.float32)
     probe_next = probe - PROBE_RATE * probe_total
     return (object_next, probe_next)
 

time: 300 us -> 471 us (1.57)
  the two profiles are of different devices: /device:TPU:0 before, /device:TPU:24 now
where the time goes in v4:
time: 471 us
  Pallas kernels  230 us (49%)
  waiting for transfers between devices  135 us (29%)
  starting transfers between devices  51.1 us (11%)
  local copies, waits for them, and re-layouts  27.4 us (6%)
  other arithmetic  20.9 us (4%)
  blocking collectives  5.06 us (1%)
    pallas_call x1, Pallas kernels, gather_classes(): pl.pallas_call(functools.partial(assemble_kernel, length), in_specs=[pl.B...  192 us
    ppermute x9, waiting for transfers between devices, pat_flip(): lax.ppermute(value, 'pat', [(k, k ^ bit) for k in range(classes)])  62.1 us
    ppermute x12, waiting for transfers between devices, flip(): return lax.ppermute(value, 'obj', [(k, k ^ bit) for k in range(owners)])  57.8 us
    unnamed x52, local copies, waits for them, and re-layouts  25.1 us
    pallas_call x2, Pallas kernels, wave(): pl.pallas_call(functools.partial(wave_kernel, which), in_specs=[smem, sme...  19.8 us
    ppermute x9, starting transfers between devices, pat_flip(): lax.ppermute(value, 'pat', [(k, k ^ bit) for k in range(classes)])  17.1 us
    ppermute x4, waiting for transfers between devices, over(): return lax.ppermute(value, 'pat', [(k, k ^ 1) for k in range(classes)])  9.64 us
  transfers between devices with their start and end apart: 33, of which 18 were waited for; matrix products, arithmetic and copies ran while one was open for 2% of the time, Pallas kernels for 7%

profile of v4, /device:TPU:24, one launch (start us, length us, event | category | flops | bytes accessed | tf_op | source)
XLA Modules:
  0.0 471.1 jit_solution(9138687909020105371)
XLA Ops:
  2.3 5.1 %all-gather = s32[4,2,4]{2,1,0:T(2,128)S(1)} all-gather(s32[1,2,4]{2,1,0:T(2,128)S(1)} %bitcast.31), channel_id=1, replica_groups=mesh['pat'=8,'obj'=4] {'obj'}, dimensions={0}, use_global_device_ids=true | all-gather | bytes 160 | tf_op jit(solution)/shard_map/all_gather | solution.py:574
  7.4 2.8 copy-done
  12.4 6.0 %shard_map.95 = (bf16[1,2,512,512]{3,2,1,0:T(8,128)(2,1)}, bf16[2,2,512,512]{3,2,1,0:T(8,128)(2,1)S(1)}) custom-call(s32[8,4]{1,0:T(8,128)S(1)} %bitcast.26, s32[2]{0:T(128)S(1)} %pad_add_fusion.3.me.spare, bf16[2,512,3072]{2,1,0:T(8,128)(2,1)S(1)} %copy-done, bf16[2,512,3072]{2,1,0:T(8,128)(2,1)S(1)} %copy-done, bf16[2,512,3072]{2,1,0:T(8,128)(2,1)S(1)} %copy-done, ...), custom_call_target="tpu_custom_call" | custom-call | flops 1966080 | bytes 7000000 | tf_op jit(solution)/shard_map/pallas_call | solution.py:195
  22.2 23.8 %collective-permute-done.7.across = bf16[2,512,512]{2,1,0:T(8,128)(2,1)S(1)} collective-permute-done((bf16[2,512,512]{2,1,0:T(8,128)(2,1)S(1)}, bf16[2,512,512]{2,1,0:T(8,128)(2,1)S(1)}, u32[]{:S(2)}, u32[]{:S(2)}) %collective-permute-start.7) | collective-permute-done | bytes 1048608 | tf_op jit(solution)/shard_map/ppermute | solution.py:558
  46.1 9.5 %shard_map.99 = (bf16[8,2,64,512]{3,2,1,0:T(8,128)(2,1)S(1)}, f32[2,512,512]{2,1,0:T(8,128)S(1)}) custom-call(s32[8,4]{1,0:T(8,128)S(1)} %bitcast.28, s32[2]{0:T(128)S(1)} %pad_add_fusion.3.me.spare, s32[2]{0:T(128)S(1)} %pad_add_fusion.3.me.spare, bf16[2,512,3072]{2,1,0:T(8,128)(2,1)S(1)} %bitcast.24, ...), custom_call_target="tpu_custom_call" | custom-call | flops 4294967296 | bytes 100000000 | tf_op jit(solution)/shard_map/pallas_call | solution.py:375
  57.9 6.0 %all-to-all-start = ((bf16[8,2,64,512]{3,2,1,0:T(8,128)(2,1)}), bf16[8,2,64,512]{3,2,1,0:T(8,128)(2,1)S(1)}, u32[]{:S(2)}, u32[]{:S(2)}) async-start(bf16[8,2,64,512]{3,2,1,0:T(8,128)(2,1)} %copy-done.11), calls=%async_computation | async-start | bytes 2097152 | tf_op jit(solution)/shard_map/all_to_all | solution.py:589
  63.9 2.8 copy-done.1
  66.7 4.0 shard_map.96
  76.5 4.1 collective-permute-done.2
  81.8 5.0 %collective-permute-done.3 = s32[8,4]{0,1:T(4,128)S(1)} collective-permute-done((s32[8,4]{0,1:T(4,128)S(1)}, s32[8,4]{0,1:T(4,128)S(1)}, u32[]{:S(2)}, u32[]{:S(2)}) %collective-permute-start.3) | collective-permute-done | bytes 160 | tf_op jit(solution)/shard_map/ppermute | solution.py:561
  87.0 8.0 %collective-permute-done.5.across = bf16[2,512,512]{2,1,0:T(8,128)(2,1)} collective-permute-done((bf16[2,512,512]{2,1,0:T(8,128)(2,1)}, bf16[2,512,512]{2,1,0:T(8,128)(2,1)}, u32[]{:S(2)}, u32[]{:S(2)}) %collective-permute-start.5) | collective-permute-done | bytes 1048608 | tf_op jit(solution)/shard_map/ppermute | solution.py:558
  95.0 2.8 copy-done.2
  105.3 10.3 %shard_map.100 = (bf16[8,2,64,512]{3,2,1,0:T(8,128)(2,1)S(1)}, f32[512,512]{1,0:T(8,128)S(1)}, bf16[512,512]{1,0:T(8,128)(2,1)S(1)}) custom-call(s32[8,4]{1,0:T(8,128)S(1)} %bitcast.30, s32[2]{0:T(128)S(1)} %pad_add_fusion.3.me.spare, s32[16,4]{1,0:T(8,128)S(1)} %broadcast_select_fusion.2.spare.pos, bf16[2,512,3072]{2,1,0:T(8,128)(2,1)S(1)} %copy-done.2, ...), custom_call_target="tpu_custom_call" | custom-call | flops 4294967296 | bytes 100000000 | tf_op jit(solution)/shard_map/pallas_call | solution.py:375
  118.4 6.0 %all-to-all-start.1 = ((bf16[8,2,64,512]{3,2,1,0:T(8,128)(2,1)}), bf16[8,2,64,512]{3,2,1,0:T(8,128)(2,1)}, u32[]{:S(2)}, u32[]{:S(2)}) async-start(bf16[8,2,64,512]{3,2,1,0:T(8,128)(2,1)} %copy-done.12), calls=%async_computation.1 | async-start | bytes 2097152 | tf_op jit(solution)/shard_map/all_to_all | solution.py:594
  124.4 2.2 collective-permute-done.8
  131.6 6.8 %collective-permute-done.9 = bf16[256,512]{1,0:T(8,128)(2,1)S(1)} collective-permute-done((bf16[256,512]{1,0:T(8,128)(2,1)}, bf16[256,512]{1,0:T(8,128)(2,1)S(1)}, u32[]{:S(2)}, u32[]{:S(2)}) %collective-permute-start.9) | collective-permute-done | bytes 262176 | tf_op jit(solution)/shard_map/ppermute | solution.py:558
  140.3 5.7 %all-to-all-done.1.second = bf16[8,2,64,512]{3,2,1,0:T(8,128)(2,1)} async-done(((bf16[8,2,64,512]{3,2,1,0:T(8,128)(2,1)}), bf16[8,2,64,512]{3,2,1,0:T(8,128)(2,1)}, u32[]{:S(2)}, u32[]{:S(2)}) %all-to-all-start.1) | async-done | bytes 1048608 | tf_op jit(solution)/shard_map/all_to_all | solution.py:594
  146.1 4.4 shard_map.101
  156.1 2.7 fusion
  160.9 4.2 collective-permute-done.14
  166.4 3.7 collective-permute-done.15
  170.1 8.8 %collective-permute-done.12 = bf16[2,64,3072]{2,1,0:T(8,128)(2,1)} collective-permute-done((bf16[2,64,3072]{2,1,0:T(8,128)(2,1)}, bf16[2,64,3072]{2,1,0:T(8,128)(2,1)}, u32[]{:S(2)}, u32[]{:S(2)}) %collective-permute-start.12) | collective-permute-done | bytes 786464 | tf_op jit(solution)/shard_map/ppermute | solution.py:558
  178.9 3.4 fusion.4.refs_0_
  186.7 3.8 collective-permute-start.19
  190.5 16.9 %collective-permute-done.19 = bf16[32,512]{1,0:T(8,128)(2,1)S(1)} collective-permute-done((bf16[32,512]{1,0:T(8,128)(2,1)S(1)}, bf16[32,512]{1,0:T(8,128)(2,1)S(1)}, u32[]{:S(2)}, u32[]{:S(2)}) %collective-permute-start.19) | collective-permute-done | bytes 32800 | tf_op jit(solution)/shard_map/ppermute | solution.py:561
  213.5 6.1 %collective-permute-start.23 = (bf16[64,512]{1,0:T(8,128)(2,1)S(1)}, bf16[64,512]{1,0:T(8,128)(2,1)S(1)}, u32[]{:S(2)}, u32[]{:S(2)}) collective-permute-start(bf16[64,512]{1,0:T(8,128)(2,1)S(1)} %maximum_select_fusion.4), channel_id=1, source_target_pairs={{0,8},{4,12},{8,0},{12,4},{16,24},{20,28},{24,16},{28,20},{1,9},{5... | collective-permute-start | bytes 196616 | tf_op jit(solution)/shard_map/ppermute | solution.py:561
  219.7 11.6 %collective-permute-done.23 = bf16[64,512]{1,0:T(8,128)(2,1)S(1)} collective-permute-done((bf16[64,512]{1,0:T(8,128)(2,1)S(1)}, bf16[64,512]{1,0:T(8,128)(2,1)S(1)}, u32[]{:S(2)}, u32[]{:S(2)}) %collective-permute-start.23) | collective-permute-done | bytes 65568 | tf_op jit(solution)/shard_map/ppermute | solution.py:561
  238.3 14.4 %collective-permute-done.27 = bf16[128,512]{1,0:T(8,128)(2,1)S(1)} collective-permute-done((bf16[128,512]{1,0:T(8,128)(2,1)S(1)}, bf16[128,512]{1,0:T(8,128)(2,1)S(1)}, u32[]{:S(2)}, u32[]{:S(2)}) %collective-permute-start.27) | collective-permute-done | bytes 131104 | tf_op jit(solution)/shard_map/ppermute | solution.py:561
  254.1 5.1 %collective-permute-done.28 = bf16[256,512]{1,0:T(8,128)(2,1)S(1)} collective-permute-done((bf16[256,512]{1,0:T(8,128)(2,1)S(1)}, bf16[256,512]{1,0:T(8,128)(2,1)S(1)}, u32[]{:S(2)}, u32[]{:S(2)}) %collective-permute-start.28) | collective-permute-done | bytes 262176 | tf_op jit(solution)/shard_map/ppermute | solution.py:558
  263.2 2.2 collective-permute-done.30
  267.3 9.6 %collective-permute-done.29.refs_10_ = bf16[2,64,3072]{2,1,0:T(8,128)(2,1)} collective-permute-done((bf16[2,64,3072]{2,1,0:T(8,128)(2,1)}, bf16[2,64,3072]{2,1,0:T(8,128)(2,1)}, u32[]{:S(2)}, u32[]{:S(2)}) %collective-permute-start.29) | collective-permute-done | bytes 786464 | tf_op jit(solution)/shard_map/ppermute | solution.py:513
  278.6 192.3 %shard_map.102 = bf16[2,512,3072]{2,1,0:T(8,128)(2,1)} custom-call(s32[2]{0:T(128)S(1)} %pad_add_fusion.3.me.spare, bf16[2,64,3072]{2,1,0:T(8,128)(2,1)} %fusion.4.refs_0_, bf16[2,64,3072]{2,1,0:T(8,128)(2,1)} %collective-permute-done.17.refs_1_, bf16[2,64,3072]{2,1,0:T(8,128)(2,1)} %collective-permute-done.21.refs_2_, ...), custom_call_target="tpu_custom_call" | custom-call | bytes 12582912 | tf_op jit(solution)/shard_map/pallas_call | solution.py:533
  (126 shorter events, 69.5 us)
Async XLA Ops:
  12.0 6.7 %collective-permute-start.6 = (bf16[1,2,512,512]{3,2,1,0:T(8,128)(2,1)S(1)}, bf16[1,2,512,512]{3,2,1,0:T(8,128)(2,1)S(1)}, u32[]{:S(2)}, u32[]{:S(2)}) collective-permute-start(bf16[1,2,512,512]{3,2,1,0:T(8,128)(2,1)S(1)} %shard_map.97), channel_id=1, source_target_pairs={{0,1},{1,0},{2,3},{3,2},{4,5},{5,4},{6,7},{7,6},{8,9},{9,8},{10,11... | collective-permute-start | bytes 3145736 | tf_op jit(solution)/shard_map/ppermute | solution.py:558
  18.5 27.5 %collective-permute-start.4 = (bf16[2,2,512,512]{3,2,1,0:T(8,128)(2,1)S(1)}, bf16[2,2,512,512]{3,2,1,0:T(8,128)(2,1)S(1)}, u32[]{:S(2)}, u32[]{:S(2)}) collective-permute-start(bf16[2,2,512,512]{3,2,1,0:T(8,128)(2,1)S(1)} %get-tuple-element.41), channel_id=1, source_target_pairs={{0,1},{1,0},{2,3},{3,2},{4,5},{5,4},{6,7},{7,6},{8,9},{9,8},{10,11... | collective-permute-start | bytes 6291464 | tf_op jit(solution)/shard_map/ppermute | solution.py:558
  20.5 25.5 %collective-permute-start.7 = (bf16[2,512,512]{2,1,0:T(8,128)(2,1)S(1)}, bf16[2,512,512]{2,1,0:T(8,128)(2,1)S(1)}, u32[]{:S(2)}, u32[]{:S(2)}) collective-permute-start(bf16[2,512,512]{2,1,0:T(8,128)(2,1)S(1)} %shard_map.98), channel_id=1, source_target_pairs={{0,2},{1,3},{2,0},{3,1},{4,6},{5,7},{6,4},{7,5},{8,10},{9,11},{10,... | collective-permute-start | bytes 3145736 | tf_op jit(solution)/shard_map/ppermute | solution.py:558
  22.1 41.8 %collective-permute-start = (bf16[1,2,512,512]{3,2,1,0:T(8,128)(2,1)}, bf16[1,2,512,512]{3,2,1,0:T(8,128)(2,1)}, u32[]{:S(2)}, u32[]{:S(2)}) collective-permute-start(bf16[1,2,512,512]{3,2,1,0:T(8,128)(2,1)} %get-tuple-element.39), channel_id=1, source_target_pairs={{0,1},{1,0},{2,3},{3,2},{4,5},{5,4},{6,7},{7,6},{8,9},{9,8},{10,11... | collective-permute-start | bytes 3145736 | tf_op jit(solution)/shard_map/ppermute | solution.py:558
  57.9 60.5 %all-to-all-start = ((bf16[8,2,64,512]{3,2,1,0:T(8,128)(2,1)}), bf16[8,2,64,512]{3,2,1,0:T(8,128)(2,1)S(1)}, u32[]{:S(2)}, u32[]{:S(2)}) async-start(bf16[8,2,64,512]{3,2,1,0:T(8,128)(2,1)} %copy-done.11), calls=%async_computation | async-start | bytes 2097152 | tf_op jit(solution)/shard_map/all_to_all | solution.py:589
  70.7 24.3 %collective-permute-start.5 = (bf16[2,512,512]{2,1,0:T(8,128)(2,1)}, bf16[2,512,512]{2,1,0:T(8,128)(2,1)}, u32[]{:S(2)}, u32[]{:S(2)}) collective-permute-start(bf16[2,512,512]{2,1,0:T(8,128)(2,1)} %shard_map.96), channel_id=1, source_target_pairs={{0,2},{1,3},{2,0},{3,1},{4,6},{5,7},{6,4},{7,5},{8,10},{9,11},{10,... | collective-permute-start | bytes 3145736 | tf_op jit(solution)/shard_map/ppermute | solution.py:558
  72.2 3.6 collective-permute-start.1
  75.9 4.7 collective-permute-start.2
  80.7 6.1 %collective-permute-start.3 = (s32[8,4]{0,1:T(4,128)S(1)}, s32[8,4]{0,1:T(4,128)S(1)}, u32[]{:S(2)}, u32[]{:S(2)}) collective-permute-start(s32[8,4]{0,1:T(4,128)S(1)} %add_select_fusion.1), channel_id=1, source_target_pairs={{0,16},{4,20},{8,24},{12,28},{16,0},{20,4},{24,8},{28,12},{1,17},{... | collective-permute-start | bytes 392 | tf_op jit(solution)/shard_map/ppermute | solution.py:561
  118.4 27.7 %all-to-all-start.1 = ((bf16[8,2,64,512]{3,2,1,0:T(8,128)(2,1)}), bf16[8,2,64,512]{3,2,1,0:T(8,128)(2,1)}, u32[]{:S(2)}, u32[]{:S(2)}) async-start(bf16[8,2,64,512]{3,2,1,0:T(8,128)(2,1)} %copy-done.12), calls=%async_computation.1 | async-start | bytes 2097152 | tf_op jit(solution)/shard_map/all_to_all | solution.py:594
  124.4 2.3 collective-permute-start.8
  129.9 8.6 %collective-permute-start.9 = (bf16[256,512]{1,0:T(8,128)(2,1)}, bf16[256,512]{1,0:T(8,128)(2,1)S(1)}, u32[]{:S(2)}, u32[]{:S(2)}) collective-permute-start(bf16[256,512]{1,0:T(8,128)(2,1)} %dynamic-slice_convert_fusion), channel_id=1, source_target_pairs={{0,2},{1,3},{2,0},{3,1},{4,6},{5,7},{6,4},{7,5},{8,10},{9,11},{10,... | collective-permute-start | bytes 786440 | tf_op jit(solution)/shard_map/ppermute | solution.py:558
  153.4 2.6 collective-permute-start.11
  153.5 7.3 %collective-permute-start.13 = (bf16[128,512]{1,0:T(8,128)(2,1)S(1)}, bf16[128,512]{1,0:T(8,128)(2,1)S(1)}, u32[]{:S(2)}, u32[]{:S(2)}) collective-permute-start(bf16[128,512]{1,0:T(8,128)(2,1)S(1)} %dynamic-slice_convert_fusion.1), channel_id=1, source_target_pairs={{0,4},{4,0},{8,12},{12,8},{16,20},{20,16},{24,28},{28,24},{1,5},{5... | collective-permute-start | bytes 393224 | tf_op jit(solution)/shard_map/ppermute | solution.py:561
  155.1 15.0 %collective-permute-start.10 = (bf16[2,64,3072]{2,1,0:T(8,128)(2,1)}, bf16[2,64,3072]{2,1,0:T(8,128)(2,1)}, u32[]{:S(2)}, u32[]{:S(2)}) collective-permute-start(bf16[2,64,3072]{2,1,0:T(8,128)(2,1)} %get-tuple-element.70), channel_id=1, source_target_pairs={{0,1},{1,0},{2,3},{3,2},{4,5},{5,4},{6,7},{7,6},{8,9},{9,8},{10,11... | collective-permute-start | bytes 2359304 | tf_op jit(solution)/shard_map/ppermute | solution.py:558
  158.8 20.1 %collective-permute-start.12 = (bf16[2,64,3072]{2,1,0:T(8,128)(2,1)}, bf16[2,64,3072]{2,1,0:T(8,128)(2,1)}, u32[]{:S(2)}, u32[]{:S(2)}) collective-permute-start(bf16[2,64,3072]{2,1,0:T(8,128)(2,1)} %fusion), channel_id=1, source_target_pairs={{0,2},{1,3},{2,0},{3,1},{4,6},{5,7},{6,4},{7,5},{8,10},{9,11},{10,... | collective-permute-start | bytes 2359304 | tf_op jit(solution)/shard_map/ppermute | solution.py:558
  160.8 4.3 collective-permute-start.14
  165.2 4.9 %collective-permute-start.15 = (bf16[32,512]{1,0:T(8,128)(2,1)S(1)}, bf16[32,512]{1,0:T(8,128)(2,1)S(1)}, u32[]{:S(2)}, u32[]{:S(2)}) collective-permute-start(bf16[32,512]{1,0:T(8,128)(2,1)S(1)} %dynamic-slice_convert_fusion.3), channel_id=1, source_target_pairs={{0,16},{4,20},{8,24},{12,28},{16,0},{20,4},{24,8},{28,12},{1,17},{... | collective-permute-start | bytes 98312 | tf_op jit(solution)/shard_map/ppermute | solution.py:561
  182.3 25.1 %collective-permute-start.18 = (bf16[2,64,3072]{2,1,0:T(8,128)(2,1)}, bf16[2,64,3072]{2,1,0:T(8,128)(2,1)S(1)}, u32[]{:S(2)}, u32[]{:S(2)}) collective-permute-start(bf16[2,64,3072]{2,1,0:T(8,128)(2,1)} %fusion.4.refs_0_), channel_id=1, source_target_pairs={{8,0},{12,4},{16,8},{20,12},{24,16},{28,20},{9,1},{13,5},{17,9},{2... | collective-permute-start | bytes 2359304 | tf_op jit(solution)/shard_map/ppermute | solution.py:510
  184.0 23.4 %collective-permute-start.17 = (bf16[2,64,3072]{2,1,0:T(8,128)(2,1)}, bf16[2,64,3072]{2,1,0:T(8,128)(2,1)}, u32[]{:S(2)}, u32[]{:S(2)}) collective-permute-start(bf16[2,64,3072]{2,1,0:T(8,128)(2,1)} %fusion.4.refs_0_), channel_id=1, source_target_pairs={{0,8},{4,12},{8,16},{12,20},{16,24},{20,28},{1,9},{5,13},{9,17},{1... | collective-permute-start | bytes 2359304 | tf_op jit(solution)/shard_map/ppermute | solution.py:510
  185.3 22.1 %collective-permute-start.16 = (bf16[2,64,3072]{2,1,0:T(8,128)(2,1)}, bf16[2,64,3072]{2,1,0:T(8,128)(2,1)}, u32[]{:S(2)}, u32[]{:S(2)}) collective-permute-start(bf16[2,64,3072]{2,1,0:T(8,128)(2,1)} %fusion.4.refs_0_), channel_id=1, source_target_pairs={{0,4},{4,0},{8,12},{12,8},{16,20},{20,16},{24,28},{28,24},{1,5},{5... | collective-permute-start | bytes 2359304 | tf_op jit(solution)/shard_map/ppermute | solution.py:513
  186.7 20.7 %collective-permute-start.19 = (bf16[32,512]{1,0:T(8,128)(2,1)S(1)}, bf16[32,512]{1,0:T(8,128)(2,1)S(1)}, u32[]{:S(2)}, u32[]{:S(2)}) collective-permute-start(bf16[32,512]{1,0:T(8,128)(2,1)S(1)} %add_convert_fusion), channel_id=1, source_target_pairs={{0,16},{4,20},{8,24},{12,28},{16,0},{20,4},{24,8},{28,12},{1,17},{... | collective-permute-start | bytes 98312 | tf_op jit(solution)/shard_map/ppermute | solution.py:561
  209.5 21.7 %collective-permute-start.20 = (bf16[2,64,3072]{2,1,0:T(8,128)(2,1)}, bf16[2,64,3072]{2,1,0:T(8,128)(2,1)}, u32[]{:S(2)}, u32[]{:S(2)}) collective-permute-start(bf16[2,64,3072]{2,1,0:T(8,128)(2,1)} %broadcast_select_fusion.1), channel_id=1, source_target_pairs={{0,4},{4,0},{8,12},{12,8},{16,20},{20,16},{24,28},{28,24},{1,5},{5... | collective-permute-start | bytes 2359304 | tf_op jit(solution)/shard_map/ppermute | solution.py:513
  210.7 20.6 %collective-permute-start.21 = (bf16[2,64,3072]{2,1,0:T(8,128)(2,1)}, bf16[2,64,3072]{2,1,0:T(8,128)(2,1)}, u32[]{:S(2)}, u32[]{:S(2)}) collective-permute-start(bf16[2,64,3072]{2,1,0:T(8,128)(2,1)} %collective-permute-done.17.refs_1_), channel_id=1, source_target_pairs={{8,16},{12,20},{16,24},{20,28},{9,17},{13,21},{17,25},{21,29},{10,... | collective-permute-start | bytes 2359304 | tf_op jit(solution)/shard_map/ppermute | solution.py:510
  212.0 19.3 %collective-permute-start.22 = (bf16[2,64,3072]{2,1,0:T(8,128)(2,1)S(1)}, bf16[2,64,3072]{2,1,0:T(8,128)(2,1)}, u32[]{:S(2)}, u32[]{:S(2)}) collective-permute-start(bf16[2,64,3072]{2,1,0:T(8,128)(2,1)S(1)} %collective-permute-done.18.refs_4_), channel_id=1, source_target_pairs={{8,0},{12,4},{16,8},{20,12},{9,1},{13,5},{17,9},{21,13},{10,2},{14... | collective-permute-start | bytes 2359304 | tf_op jit(solution)/shard_map/ppermute | solution.py:510
  213.5 17.7 %collective-permute-start.23 = (bf16[64,512]{1,0:T(8,128)(2,1)S(1)}, bf16[64,512]{1,0:T(8,128)(2,1)S(1)}, u32[]{:S(2)}, u32[]{:S(2)}) collective-permute-start(bf16[64,512]{1,0:T(8,128)(2,1)S(1)} %maximum_select_fusion.4), channel_id=1, source_target_pairs={{0,8},{4,12},{8,0},{12,4},{16,24},{20,28},{24,16},{28,20},{1,9},{5... | collective-permute-start | bytes 196616 | tf_op jit(solution)/shard_map/ppermute | solution.py:561
  233.4 26.8 %collective-permute-start.24 = (bf16[2,64,3072]{2,1,0:T(8,128)(2,1)}, bf16[2,64,3072]{2,1,0:T(8,128)(2,1)}, u32[]{:S(2)}, u32[]{:S(2)}) collective-permute-start(bf16[2,64,3072]{2,1,0:T(8,128)(2,1)} %broadcast_select_fusion), channel_id=1, source_target_pairs={{0,4},{4,0},{8,12},{12,8},{16,20},{20,16},{24,28},{28,24},{1,5},{5... | collective-permute-start | bytes 2359304 | tf_op jit(solution)/shard_map/ppermute | solution.py:513
  234.3 25.9 %collective-permute-start.25 = (bf16[2,64,3072]{2,1,0:T(8,128)(2,1)}, bf16[2,64,3072]{2,1,0:T(8,128)(2,1)}, u32[]{:S(2)}, u32[]{:S(2)}) collective-permute-start(bf16[2,64,3072]{2,1,0:T(8,128)(2,1)} %collective-permute-done.21.refs_2_), channel_id=1, source_target_pairs={{16,24},{20,28},{17,25},{21,29},{18,26},{22,30},{19,27},{23,31}} | collective-permute-start | bytes 2359304 | tf_op jit(solution)/shard_map/ppermute | solution.py:510
  235.6 24.6 %collective-permute-start.26 = (bf16[2,64,3072]{2,1,0:T(8,128)(2,1)}, bf16[2,64,3072]{2,1,0:T(8,128)(2,1)}, u32[]{:S(2)}, u32[]{:S(2)}) collective-permute-start(bf16[2,64,3072]{2,1,0:T(8,128)(2,1)} %collective-permute-done.22.refs_5_), channel_id=1, source_target_pairs={{8,0},{12,4},{9,1},{13,5},{10,2},{14,6},{11,3},{15,7}} | collective-permute-start | bytes 2359304 | tf_op jit(solution)/shard_map/ppermute | solution.py:510
  237.2 15.5 %collective-permute-start.27 = (bf16[128,512]{1,0:T(8,128)(2,1)S(1)}, bf16[128,512]{1,0:T(8,128)(2,1)S(1)}, u32[]{:S(2)}, u32[]{:S(2)}) collective-permute-start(bf16[128,512]{1,0:T(8,128)(2,1)S(1)} %maximum_select_fusion.3), channel_id=1, source_target_pairs={{0,4},{4,0},{8,12},{12,8},{16,20},{20,16},{24,28},{28,24},{1,5},{5... | collective-permute-start | bytes 393224 | tf_op jit(solution)/shard_map/ppermute | solution.py:561
  252.7 6.4 %collective-permute-start.28 = (bf16[256,512]{1,0:T(8,128)(2,1)S(1)}, bf16[256,512]{1,0:T(8,128)(2,1)S(1)}, u32[]{:S(2)}, u32[]{:S(2)}) collective-permute-start(bf16[256,512]{1,0:T(8,128)(2,1)S(1)} %maximum_select_fusion.2), channel_id=1, source_target_pairs={{0,2},{1,3},{2,0},{3,1},{4,6},{5,7},{6,4},{7,5},{8,10},{9,11},{10,... | collective-permute-start | bytes 786440 | tf_op jit(solution)/shard_map/ppermute | solution.py:558
  262.3 14.6 %collective-permute-start.29 = (bf16[2,64,3072]{2,1,0:T(8,128)(2,1)}, bf16[2,64,3072]{2,1,0:T(8,128)(2,1)}, u32[]{:S(2)}, u32[]{:S(2)}) collective-permute-start(bf16[2,64,3072]{2,1,0:T(8,128)(2,1)} %select_select_fusion), channel_id=1, source_target_pairs={{0,4},{4,0},{8,12},{12,8},{16,20},{20,16},{24,28},{28,24},{1,5},{5... | collective-permute-start | bytes 2359304 | tf_op jit(solution)/shard_map/ppermute | solution.py:513
  (26 other events, 229.8 us)

commit v5 on v4

--- a/solution.py
+++ b/solution.py
@@ -18,9 +18,8 @@
 PROBE_RATE = 0.05
 MAGNITUDE_FLOOR = 0.5
 CUT_VMEM = 14 * 1024 * 1024
-WAVE_VMEM = 32 * 1024 * 1024
+WAVE_VMEM = 56 * 1024 * 1024
 SUM_VMEM = 24 * 1024 * 1024
-BY_PERMUTE = (4, 8)
 
 
 def dft_tables(length):
@@ -461,89 +460,6 @@
     )(pos, me, first, second)
 
 
-def assemble_kernel(length, me, *refs):
-    steps = length - 1
-    own, refs = refs[0], refs[1:]
-    ups, downs, overs = refs[:steps], refs[steps : 2 * steps], refs[2 * steps : 3 * steps + 1]
-    out, sems = refs[3 * steps + 1 :]
-    height = own.shape[1]
-    place = me[1] // 2
-    side = lax.rem(me[1], 2)
-
-    def copy(source, at, column, k):
-        rows = pl.ds(pl.multiple_of((2 * at + column) * height, height), height)
-        return pltpu.make_async_copy(source, out.at[:, rows, :], sems.at[k])
-
-    always = [copy(own, place, side, 0)]
-    for k in range(length):
-        always.append(copy(overs[k], sent_over(place, k, length), 1 - side, k + 1))
-    some = []
-    for k in range(1, length):
-        below, above = place - k, place + k
-        held = length + 2 * k - 1
-        some.append((below >= 0, copy(ups[k - 1], below, side, held)))
-        some.append((above < length, copy(downs[k - 1], above, side, held + 1)))
-    for part in always:
-        part.start()
-    for has, part in some:
-        pl.when(has)(part.start)
-    for part in always:
-        part.wait()
-    for has, part in some:
-        pl.when(has)(part.wait)
-
-
-def sent_over(place, k, length):
-    low = jnp.where(place >= k, place - k, place + k)
-    if k == length - 1:
-        high = jnp.where(place == 0, length - 1, jnp.where(place == length - 1, 0, place + 1))
-        return high
-    return low
-
-
-def gather_classes(own, me, classes, term, term_steps):
-    length = classes // 2
-    place = me[1] // 2
-
-    def along(value, held, step):
-        pairs = [(2 * z + x, 2 * (z + step) + x) for z in held if 0 <= z + step < length for x in range(2)]
-        return lax.ppermute(value, "pat", pairs)
-
-    def over(value):
-        return lax.ppermute(value, "pat", [(k, k ^ 1) for k in range(classes)])
-
-    ups, downs, overs = [own], [own], []
-    for k in range(length - 1):
-        overs.append(over(jnp.where(place >= k, ups[k], downs[k]) if k else own))
-        ups.append(along(ups[k], range(k, length), 1))
-        downs.append(along(downs[k], range(length - k), -1))
-        for step in term_steps[k : k + 1] if k < length - 2 else term_steps[k:-1]:
-            term = step(term)
-        overs[k], ups[k + 1], downs[k + 1], term = lax.optimization_barrier(
-            (overs[k], ups[k + 1], downs[k + 1], term)
-        )
-    end = jnp.where(place == 0, downs[-1], ups[-1])
-    if length > 2:
-        middle = (place > 0) & (place < length - 1)
-        end = jnp.where(middle, downs[1], end)
-    last, term = lax.optimization_barrier((over(end), term_steps[-1](term)))
-    overs.append(last)
-    operands = [own, *ups[1:], *downs[1:], *overs]
-    hbm = pl.BlockSpec(memory_space=pl.ANY)
-    object_next = pl.pallas_call(
-        functools.partial(assemble_kernel, length),
-        in_specs=[pl.BlockSpec(memory_space=pltpu.SMEM)] + [hbm] * len(operands),
-        out_specs=hbm,
-        out_shape=jax.ShapeDtypeStruct((2, classes * own.shape[1], own.shape[2]), own.dtype),
-        scratch_shapes=[pltpu.SemaphoreType.DMA((3 * length - 1,))],
-        compiler_params=pltpu.CompilerParams(vmem_limit_bytes=CUT_VMEM),
-        cost_estimate=pl.CostEstimate(
-            flops=0, bytes_accessed=4 * own.size * classes, transcendentals=0
-        ),
-    )(me, *operands)
-    return object_next, term
-
-
 def shards(object_image, probe, amplitudes, pos_tile, pos_offset):
     owners = lax.axis_size("obj")
     classes = lax.axis_size("pat")
@@ -586,6 +502,7 @@
 
     operands = (probe, amplitudes, dft_tables(PATCH))
     grad_0, term = wave(0, classes, pos, me, me, object_image, sibling, across[0], *operands, None)
+    grad_0, across[1] = lax.optimization_barrier((grad_0, across[1]))
     part_0 = lax.all_to_all(grad_0, "pat", split_axis=0, concat_axis=0, tiled=True)
     grad_1, keep_term, give_term = wave(
         1, classes, pos, me, pos_pat, object_image, sibling, across[1], *operands, term
@@ -615,12 +532,9 @@
     ]
     steps.append(functools.partial(doubled, bit=line, other=lambda value: flip(value, 2)))
     steps.append(lambda part: doubled(part[None], core, lambda value: flip(value, 1)))
-    if classes in BY_PERMUTE:
-        object_next, term = gather_classes(updated, me, classes, term, steps)
-    else:
-        object_next = lax.all_gather(updated, "pat", axis=1, tiled=True)
-        for step in steps:
-            term = step(term)
+    object_next = lax.all_gather(updated, "pat", axis=1, tiled=True)
+    for step in steps:
+        term = step(term)
     probe_total = term.astype(jnp.float32)
     probe_next = probe - PROBE_RATE * probe_total
     return (object_next, probe_next)

time: 471 us -> 296 us (0.63)
  the two profiles are of different devices: /device:TPU:24 before, /device:TPU:0 now
where the time goes in v5:
time: 296 us
  waiting for transfers between devices  175 us (59%)
  Pallas kernels  39.6 us (13%)
  starting transfers between devices  30.7 us (10%)
  local copies, waits for them, and re-layouts  18.6 us (6%)
  between operations  14.3 us (5%)
  other arithmetic  11.3 us (4%)
  blocking collectives  5.99 us (2%)
    all_gather x1, waiting for transfers between devices, shards(): object_next = lax.all_gather(updated, 'pat', axis=1, tiled=True)  69.8 us
    ppermute x12, waiting for transfers between devices, flip(): return lax.ppermute(value, 'obj', [(k, k ^ bit) for k in range(owners)])  51.6 us
    ppermute x9, waiting for transfers between devices, pat_flip(): lax.ppermute(value, 'pat', [(k, k ^ bit) for k in range(classes)])  42.6 us
    pallas_call x2, Pallas kernels, wave(): pl.pallas_call(functools.partial(wave_kernel, which), in_specs=[smem, sme...  25.1 us
    unnamed x31, local copies, waits for them, and re-layouts  15 us
    ppermute x9, starting transfers between devices, pat_flip(): lax.ppermute(value, 'pat', [(k, k ^ bit) for k in range(classes)])  11.8 us
    all_to_all x1, waiting for transfers between devices, shards(): lax.all_to_all(grad_1, 'pat', split_axis=0, concat_axis=0, tiled=True)  11.3 us
    ppermute x12, starting transfers between devices, flip(): return lax.ppermute(value, 'obj', [(k, k ^ bit) for k in range(owners)])  9.13 us
  transfers between devices with their start and end apart: 24, of which 19 were waited for; matrix products, arithmetic and copies ran while one was open for 4% of the time, Pallas kernels for 11%

profile of v5, /device:TPU:0, one launch (start us, length us, event | category | flops | bytes accessed | tf_op | source)
XLA Modules:
  0.0 295.7 jit_solution(11255863642704041562)
XLA Ops:
  8.8 6.0 %all-gather = s32[4,2,4]{2,1,0:T(2,128)S(1)} all-gather(s32[1,2,4]{2,1,0:T(2,128)S(1)} %bitcast.32), channel_id=1, replica_groups=mesh['pat'=8,'obj'=4] {'obj'}, dimensions={0}, use_global_device_ids=true | all-gather | bytes 160 | tf_op jit(solution)/shard_map/all_gather | solution.py:490
  14.9 2.8 copy-done
  19.9 5.1 %shard_map.95 = (bf16[1,2,512,512]{3,2,1,0:T(8,128)(2,1)S(1)}, bf16[2,2,512,512]{3,2,1,0:T(8,128)(2,1)S(1)}) custom-call(s32[8,4]{1,0:T(8,128)S(1)} %bitcast.25, s32[2]{0:T(128)S(1)} %pad_add_fusion.3.me.spare, bf16[2,512,3072]{2,1,0:T(8,128)(2,1)S(1)} %copy-done, bf16[2,512,3072]{2,1,0:T(8,128)(2,1)S(1)} %copy-done, bf16[2,512,3072]{2,1,0:T(8,128)(2,1)S(1)} %copy-done, ...), custom_call_target="tpu_custom_call" | custom-call | flops 1966080 | bytes 7000000 | tf_op jit(solution)/shard_map/pallas_call | solution.py:194
  27.4 2.1 collective-permute-start.6
  32.5 2.1 collective-permute-start.7
  34.6 18.8 %collective-permute-done.6.across = bf16[2,512,512]{2,1,0:T(8,128)(2,1)S(1)} collective-permute-done((bf16[2,512,512]{2,1,0:T(8,128)(2,1)S(1)}, bf16[2,512,512]{2,1,0:T(8,128)(2,1)S(1)}, u32[]{:S(2)}, u32[]{:S(2)}) %collective-permute-start.6) | collective-permute-done | bytes 1048608 | tf_op jit(solution)/shard_map/ppermute | solution.py:474
  55.7 12.1 %shard_map.99 = (bf16[8,2,64,512]{3,2,1,0:T(8,128)(2,1)}, f32[2,512,512]{2,1,0:T(8,128)}) custom-call(s32[8,4]{1,0:T(8,128)} %bitcast.28, s32[2]{0:T(128)} %copy-done.5, s32[2]{0:T(128)} %copy-done.5, bf16[2,512,3072]{2,1,0:T(8,128)(2,1)} %band.3, bf16[2,2,512,512]{3,2,1,0:T(8,128)(2,1)} %copy-done.8, bf16[2,512,512]{2,1,0:T(8,128)(2,1)} %copy-done.12, ...), custom_call_target="tpu_custom_call" | custom-call | flops 4294967296 | bytes 100000000 | tf_op jit(solution)/shard_map/pallas_call | solution.py:374
  67.8 7.6 %collective-permute-done.7.across = bf16[2,512,512]{2,1,0:T(8,128)(2,1)S(1)} collective-permute-done((bf16[2,512,512]{2,1,0:T(8,128)(2,1)S(1)}, bf16[2,512,512]{2,1,0:T(8,128)(2,1)S(1)}, u32[]{:S(2)}, u32[]{:S(2)}) %collective-permute-start.7) | collective-permute-done | bytes 1048608 | tf_op jit(solution)/shard_map/ppermute | solution.py:474
  75.5 6.0 %all-to-all-start = ((bf16[8,2,64,512]{3,2,1,0:T(8,128)(2,1)}), bf16[8,2,64,512]{3,2,1,0:T(8,128)(2,1)S(1)}, u32[]{:S(2)}, u32[]{:S(2)}) async-start(bf16[8,2,64,512]{3,2,1,0:T(8,128)(2,1)} %get-tuple-element.38), calls=%async_computation | async-start | bytes 2097152 | tf_op jit(solution)/shard_map/all_to_all | solution.py:506
  81.5 2.0 collective-permute-start.1
  83.5 5.7 %collective-permute-done.1 = s32[2,4]{0,1:T(4,128)S(1)} collective-permute-done((s32[2,4]{0,1:T(4,128)S(1)}, s32[2,4]{0,1:T(4,128)S(1)}, u32[]{:S(2)}, u32[]{:S(2)}) %collective-permute-start.1) | collective-permute-done | bytes 64 | tf_op jit(solution)/shard_map/ppermute | solution.py:477
  89.3 2.3 collective-permute-start.2
  91.6 6.6 %collective-permute-done.2 = s32[4,4]{0,1:T(4,128)S(1)} collective-permute-done((s32[4,4]{0,1:T(4,128)S(1)}, s32[4,4]{0,1:T(4,128)S(1)}, u32[]{:S(2)}, u32[]{:S(2)}) %collective-permute-start.2) | collective-permute-done | bytes 96 | tf_op jit(solution)/shard_map/ppermute | solution.py:477
  98.2 4.7 %collective-permute-start.3 = (s32[8,4]{0,1:T(4,128)S(1)}, s32[8,4]{0,1:T(4,128)S(1)}, u32[]{:S(2)}, u32[]{:S(2)}) collective-permute-start(s32[8,4]{0,1:T(4,128)S(1)} %add_select_fusion.1), channel_id=1, source_target_pairs={{0,16},{4,20},{8,24},{12,28},{16,0},{20,4},{24,8},{28,12},{1,17},{... | collective-permute-start | bytes 392 | tf_op jit(solution)/shard_map/ppermute | solution.py:477
  102.9 4.2 %collective-permute-done.3 = s32[8,4]{0,1:T(4,128)S(1)} collective-permute-done((s32[8,4]{0,1:T(4,128)S(1)}, s32[8,4]{0,1:T(4,128)S(1)}, u32[]{:S(2)}, u32[]{:S(2)}) %collective-permute-start.3) | collective-permute-done | bytes 160 | tf_op jit(solution)/shard_map/ppermute | solution.py:477
  108.0 12.9 %shard_map.100 = (bf16[8,2,64,512]{3,2,1,0:T(8,128)(2,1)}, f32[512,512]{1,0:T(8,128)}, bf16[512,512]{1,0:T(8,128)(2,1)}) custom-call(s32[8,4]{1,0:T(8,128)} %bitcast.29, s32[2]{0:T(128)} %copy-done.5, s32[16,4]{1,0:T(8,128)} %broadcast_select_fusion.spare.pos, bf16[2,512,3072]{2,1,0:T(8,128)(2,1)} %band.3, bf16[2,2,512,512]{3,2,1,0:T(8,128)(2,1)} %copy-done.8, ...), custom_call_target="tpu_custom_call" | custom-call | flops 4294967296 | bytes 100000000 | tf_op jit(solution)/shard_map/pallas_call | solution.py:374
  120.9 3.7 %all-to-all-start.1 = ((bf16[8,2,64,512]{3,2,1,0:T(8,128)(2,1)}), bf16[8,2,64,512]{3,2,1,0:T(8,128)(2,1)S(1)}, u32[]{:S(2)}, u32[]{:S(2)}) async-start(bf16[8,2,64,512]{3,2,1,0:T(8,128)(2,1)} %get-tuple-element.40), calls=%async_computation.1 | async-start | bytes 2097152 | tf_op jit(solution)/shard_map/all_to_all | solution.py:511
  131.2 7.1 %collective-permute-done.9 = bf16[256,512]{1,0:T(8,128)(2,1)S(1)} collective-permute-done((bf16[256,512]{1,0:T(8,128)(2,1)}, bf16[256,512]{1,0:T(8,128)(2,1)S(1)}, u32[]{:S(2)}, u32[]{:S(2)}) %collective-permute-start.9) | collective-permute-done | bytes 262176 | tf_op jit(solution)/shard_map/ppermute | solution.py:474
  139.2 11.3 %all-to-all-done.1.second = bf16[8,2,64,512]{3,2,1,0:T(8,128)(2,1)S(1)} async-done(((bf16[8,2,64,512]{3,2,1,0:T(8,128)(2,1)}), bf16[8,2,64,512]{3,2,1,0:T(8,128)(2,1)S(1)}, u32[]{:S(2)}, u32[]{:S(2)}) %all-to-all-start.1) | async-done | bytes 1048608 | tf_op jit(solution)/shard_map/all_to_all | solution.py:511
  150.5 4.0 %shard_map.101 = (f32[2,2,64,3072]{3,2,1,0:T(8,128)S(1)}, bf16[2,2,64,3072]{3,2,1,0:T(8,128)(2,1)S(1)}) custom-call(s32[16,4]{1,0:T(8,128)S(1)} %copy-done.4, s32[2]{0:T(128)S(1)} %copy-done.6, bf16[8,2,64,512]{3,2,1,0:T(8,128)(2,1)S(1)} %all-to-all-done.first, bf16[8,2,64,512]{3,2,1,0:T(8,128)(2,1)S(1)} %all-to-all-done.1.second), custom_call_target="tpu_custom_call" | custom-call | flops 4194304 | bytes 6815744 | tf_op jit(solution)/shard_map/pallas_call | solution.py:447
  160.2 2.2 fusion
  164.6 4.3 %collective-permute-done.14 = bf16[64,512]{1,0:T(8,128)(2,1)} collective-permute-done((bf16[64,512]{1,0:T(8,128)(2,1)S(1)}, bf16[64,512]{1,0:T(8,128)(2,1)}, u32[]{:S(2)}, u32[]{:S(2)}) %collective-permute-start.14) | collective-permute-done | bytes 65568 | tf_op jit(solution)/shard_map/ppermute | solution.py:477
  169.9 4.8 %collective-permute-done.15 = bf16[32,512]{1,0:T(8,128)(2,1)S(1)} collective-permute-done((bf16[32,512]{1,0:T(8,128)(2,1)S(1)}, bf16[32,512]{1,0:T(8,128)(2,1)S(1)}, u32[]{:S(2)}, u32[]{:S(2)}) %collective-permute-start.15) | collective-permute-done | bytes 32800 | tf_op jit(solution)/shard_map/ppermute | solution.py:477
  174.7 7.9 %collective-permute-done.12 = bf16[2,64,3072]{2,1,0:T(8,128)(2,1)} collective-permute-done((bf16[2,64,3072]{2,1,0:T(8,128)(2,1)}, bf16[2,64,3072]{2,1,0:T(8,128)(2,1)}, u32[]{:S(2)}, u32[]{:S(2)}) %collective-permute-start.12) | collective-permute-done | bytes 786464 | tf_op jit(solution)/shard_map/ppermute | solution.py:474
  182.6 2.9 fusion.4
  185.6 4.8 %collective-permute-done.16 = bf16[32,512]{1,0:T(8,128)(2,1)S(1)} collective-permute-done((bf16[32,512]{1,0:T(8,128)(2,1)S(1)}, bf16[32,512]{1,0:T(8,128)(2,1)S(1)}, u32[]{:S(2)}, u32[]{:S(2)}) %collective-permute-start.16) | collective-permute-done | bytes 32800 | tf_op jit(solution)/shard_map/ppermute | solution.py:477
  190.5 4.3 %collective-permute-done.17 = bf16[64,512]{1,0:T(8,128)(2,1)S(1)} collective-permute-done((bf16[64,512]{1,0:T(8,128)(2,1)S(1)}, bf16[64,512]{1,0:T(8,128)(2,1)S(1)}, u32[]{:S(2)}, u32[]{:S(2)}) %collective-permute-start.17) | collective-permute-done | bytes 65568 | tf_op jit(solution)/shard_map/ppermute | solution.py:477
  195.8 7.0 %collective-permute-done.18 = bf16[128,512]{1,0:T(8,128)(2,1)S(1)} collective-permute-done((bf16[128,512]{1,0:T(8,128)(2,1)S(1)}, bf16[128,512]{1,0:T(8,128)(2,1)S(1)}, u32[]{:S(2)}, u32[]{:S(2)}) %collective-permute-start.18) | collective-permute-done | bytes 131104 | tf_op jit(solution)/shard_map/ppermute | solution.py:477
  204.1 5.2 %collective-permute-done.19 = bf16[256,512]{1,0:T(8,128)(2,1)S(1)} collective-permute-done((bf16[256,512]{1,0:T(8,128)(2,1)S(1)}, bf16[256,512]{1,0:T(8,128)(2,1)S(1)}, u32[]{:S(2)}, u32[]{:S(2)}) %collective-permute-start.19) | collective-permute-done | bytes 262176 | tf_op jit(solution)/shard_map/ppermute | solution.py:474
  209.6 1.9 collective-permute-done.20
  213.2 69.8 %all-gather.3.cloned.1.call-done = bf16[2,512,3072]{2,1,0:T(8,128)(2,1)} async-done(((bf16[2,64,3072]{2,1,0:T(8,128)(2,1)}), bf16[2,512,3072]{2,1,0:T(8,128)(2,1)}) %all-gather.3.cloned.1.call-update) | async-done | bytes 6291472 | tf_op jit(solution)/shard_map/all_gather | solution.py:535
  282.9 5.9 %copy.16 = bf16[2,512,3072]{2,1,0:T(8,128)(2,1)} copy(bf16[2,512,3072]{2,1,0:T(8,128)(2,1)} %all-gather.3.cloned.1.call-done) | data formatting | bytes 12582912
  (82 shorter events, 33.3 us)
Async XLA Ops:
  14.8 15.9 %copy-start.3 = (s32[4,2,4]{2,1,0:T(2,128)}, s32[4,2,4]{2,1,0:T(2,128)S(1)}, u32[]{:S(2)}) copy-start(s32[4,2,4]{2,1,0:T(2,128)S(1)} %all-gather) | copy-start | bytes 388
  14.9 15.8 %copy-start.5 = (s32[2]{0:T(128)}, s32[2]{0:T(128)S(1)}, u32[]{:S(2)}) copy-start(s32[2]{0:T(128)S(1)} %pad_add_fusion.3.me.spare) | copy-start | bytes 28
  19.5 6.1 %collective-permute-start.5 = (bf16[1,2,512,512]{3,2,1,0:T(8,128)(2,1)S(1)}, bf16[1,2,512,512]{3,2,1,0:T(8,128)(2,1)S(1)}, u32[]{:S(2)}, u32[]{:S(2)}) collective-permute-start(bf16[1,2,512,512]{3,2,1,0:T(8,128)(2,1)S(1)} %shard_map.97), channel_id=1, source_target_pairs={{0,1},{1,0},{2,3},{3,2},{4,5},{5,4},{6,7},{7,6},{8,9},{9,8},{10,11... | collective-permute-start | bytes 3145736 | tf_op jit(solution)/shard_map/ppermute | solution.py:474
  25.0 28.4 %collective-permute-start.4 = (bf16[2,2,512,512]{3,2,1,0:T(8,128)(2,1)S(1)}, bf16[2,2,512,512]{3,2,1,0:T(8,128)(2,1)S(1)}, u32[]{:S(2)}, u32[]{:S(2)}) collective-permute-start(bf16[2,2,512,512]{3,2,1,0:T(8,128)(2,1)S(1)} %get-tuple-element.29), channel_id=1, source_target_pairs={{0,1},{1,0},{2,3},{3,2},{4,5},{5,4},{6,7},{7,6},{8,9},{9,8},{10,11... | collective-permute-start | bytes 6291464 | tf_op jit(solution)/shard_map/ppermute | solution.py:474
  25.2 5.5 %collective-permute-start = (bf16[1,2,512,512]{3,2,1,0:T(8,128)(2,1)S(1)}, bf16[1,2,512,512]{3,2,1,0:T(8,128)(2,1)S(1)}, u32[]{:S(2)}, u32[]{:S(2)}) collective-permute-start(bf16[1,2,512,512]{3,2,1,0:T(8,128)(2,1)S(1)} %get-tuple-element.27), channel_id=1, source_target_pairs={{0,1},{1,0},{2,3},{3,2},{4,5},{5,4},{6,7},{7,6},{8,9},{9,8},{10,11... | collective-permute-start | bytes 3145736 | tf_op jit(solution)/shard_map/ppermute | solution.py:474
  27.4 26.0 %collective-permute-start.6 = (bf16[2,512,512]{2,1,0:T(8,128)(2,1)S(1)}, bf16[2,512,512]{2,1,0:T(8,128)(2,1)S(1)}, u32[]{:S(2)}, u32[]{:S(2)}) collective-permute-start(bf16[2,512,512]{2,1,0:T(8,128)(2,1)S(1)} %shard_map.98), channel_id=1, source_target_pairs={{0,2},{1,3},{2,0},{3,1},{4,6},{5,7},{6,4},{7,5},{8,10},{9,11},{10,... | collective-permute-start | bytes 3145736 | tf_op jit(solution)/shard_map/ppermute | solution.py:474
  32.5 42.9 %collective-permute-start.7 = (bf16[2,512,512]{2,1,0:T(8,128)(2,1)S(1)}, bf16[2,512,512]{2,1,0:T(8,128)(2,1)S(1)}, u32[]{:S(2)}, u32[]{:S(2)}) collective-permute-start(bf16[2,512,512]{2,1,0:T(8,128)(2,1)S(1)} %shard_map.96), channel_id=1, source_target_pairs={{0,2},{1,3},{2,0},{3,1},{4,6},{5,7},{6,4},{7,5},{8,10},{9,11},{10,... | collective-permute-start | bytes 3145736 | tf_op jit(solution)/shard_map/ppermute | solution.py:474
  75.5 32.5 %copy-start.10 = (bf16[2,512,512]{2,1,0:T(8,128)(2,1)}, bf16[2,512,512]{2,1,0:T(8,128)(2,1)S(1)}, u32[]{:S(2)}) copy-start(bf16[2,512,512]{2,1,0:T(8,128)(2,1)S(1)} %collective-permute-done.7.across) | copy-start | bytes 3145732
  75.5 45.5 %all-to-all-start = ((bf16[8,2,64,512]{3,2,1,0:T(8,128)(2,1)}), bf16[8,2,64,512]{3,2,1,0:T(8,128)(2,1)S(1)}, u32[]{:S(2)}, u32[]{:S(2)}) async-start(bf16[8,2,64,512]{3,2,1,0:T(8,128)(2,1)} %get-tuple-element.38), calls=%async_computation | async-start | bytes 2097152 | tf_op jit(solution)/shard_map/all_to_all | solution.py:506
  81.5 7.7 %collective-permute-start.1 = (s32[2,4]{0,1:T(4,128)S(1)}, s32[2,4]{0,1:T(4,128)S(1)}, u32[]{:S(2)}, u32[]{:S(2)}) collective-permute-start(s32[2,4]{0,1:T(4,128)S(1)} %pad_add_fusion), channel_id=1, source_target_pairs={{0,4},{4,0},{8,12},{12,8},{16,20},{20,16},{24,28},{28,24},{1,5},{5... | collective-permute-start | bytes 104 | tf_op jit(solution)/shard_map/ppermute | solution.py:477
  89.3 8.9 %collective-permute-start.2 = (s32[4,4]{0,1:T(4,128)S(1)}, s32[4,4]{0,1:T(4,128)S(1)}, u32[]{:S(2)}, u32[]{:S(2)}) collective-permute-start(s32[4,4]{0,1:T(4,128)S(1)} %add_select_fusion), channel_id=1, source_target_pairs={{0,8},{4,12},{8,0},{12,4},{16,24},{20,28},{24,16},{28,20},{1,9},{5... | collective-permute-start | bytes 200 | tf_op jit(solution)/shard_map/ppermute | solution.py:477
  98.2 8.9 %collective-permute-start.3 = (s32[8,4]{0,1:T(4,128)S(1)}, s32[8,4]{0,1:T(4,128)S(1)}, u32[]{:S(2)}, u32[]{:S(2)}) collective-permute-start(s32[8,4]{0,1:T(4,128)S(1)} %add_select_fusion.1), channel_id=1, source_target_pairs={{0,16},{4,20},{8,24},{12,28},{16,0},{20,4},{24,8},{28,12},{1,17},{... | collective-permute-start | bytes 392 | tf_op jit(solution)/shard_map/ppermute | solution.py:477
  120.9 29.6 %all-to-all-start.1 = ((bf16[8,2,64,512]{3,2,1,0:T(8,128)(2,1)}), bf16[8,2,64,512]{3,2,1,0:T(8,128)(2,1)S(1)}, u32[]{:S(2)}, u32[]{:S(2)}) async-start(bf16[8,2,64,512]{3,2,1,0:T(8,128)(2,1)} %get-tuple-element.40), calls=%async_computation.1 | async-start | bytes 2097152 | tf_op jit(solution)/shard_map/all_to_all | solution.py:511
  124.6 158.3 %all-gather.3.cloned.1.call-start = ((), (), s32[]{:S(2)}) async-start(), calls=%async_computation.2 | async-start | bytes 7077888 | tf_op jit(solution)/shard_map/all_gather | solution.py:535
  124.7 2.0 collective-permute-start.8
  127.5 23.0 %copy-start.4 = (s32[16,4]{1,0:T(8,128)S(1)}, s32[16,4]{1,0:T(8,128)}, u32[]{:S(2)}) copy-start(s32[16,4]{1,0:T(8,128)} %broadcast_select_fusion.spare.pos) | copy-start | bytes 772
  127.5 23.0 %copy-start.6 = (s32[2]{0:T(128)S(1)}, s32[2]{0:T(128)}, u32[]{:S(2)}) copy-start(s32[2]{0:T(128)} %copy-done.5) | copy-start | bytes 28
  129.8 8.6 %collective-permute-start.9 = (bf16[256,512]{1,0:T(8,128)(2,1)}, bf16[256,512]{1,0:T(8,128)(2,1)S(1)}, u32[]{:S(2)}, u32[]{:S(2)}) collective-permute-start(bf16[256,512]{1,0:T(8,128)(2,1)} %dynamic-slice_convert_fusion), channel_id=1, source_target_pairs={{0,2},{1,3},{2,0},{3,1},{4,6},{5,7},{6,4},{7,5},{8,10},{9,11},{10,... | collective-permute-start | bytes 786440 | tf_op jit(solution)/shard_map/ppermute | solution.py:474
  156.2 4.0 %copy-start.2 = (f32[2,2,64,3072]{3,2,1,0:T(8,128)S(1)}, f32[2,2,64,3072]{3,2,1,0:T(8,128)}, u32[]{:S(2)}) copy-start(f32[2,2,64,3072]{3,2,1,0:T(8,128)} %copy-done.1) | copy-start | bytes 9437188
  157.4 2.8 collective-permute-start.11
  157.4 7.0 %copy-start.9 = (f32[256,512]{1,0:T(8,128)S(1)}, f32[256,512]{1,0:T(8,128)}, u32[]{:S(2)}) copy-start(f32[256,512]{1,0:T(8,128)} %convert_add_fusion.1) | copy-start | bytes 1572868
  158.7 5.8 %collective-permute-start.13 = (bf16[128,512]{1,0:T(8,128)(2,1)S(1)}, bf16[128,512]{1,0:T(8,128)(2,1)S(1)}, u32[]{:S(2)}, u32[]{:S(2)}) collective-permute-start(bf16[128,512]{1,0:T(8,128)(2,1)S(1)} %dynamic-slice_convert_fusion.1), channel_id=1, source_target_pairs={{0,4},{4,0},{8,12},{12,8},{16,20},{20,16},{24,28},{28,24},{1,5},{5... | collective-permute-start | bytes 393224 | tf_op jit(solution)/shard_map/ppermute | solution.py:477
  160.1 14.6 %collective-permute-start.10 = (bf16[2,64,3072]{2,1,0:T(8,128)(2,1)}, bf16[2,64,3072]{2,1,0:T(8,128)(2,1)}, u32[]{:S(2)}, u32[]{:S(2)}) collective-permute-start(bf16[2,64,3072]{2,1,0:T(8,128)(2,1)} %get-tuple-element.46), channel_id=1, source_target_pairs={{0,1},{1,0},{2,3},{3,2},{4,5},{5,4},{6,7},{7,6},{8,9},{9,8},{10,11... | collective-permute-start | bytes 2359304 | tf_op jit(solution)/shard_map/ppermute | solution.py:474
  162.4 20.2 %collective-permute-start.12 = (bf16[2,64,3072]{2,1,0:T(8,128)(2,1)}, bf16[2,64,3072]{2,1,0:T(8,128)(2,1)}, u32[]{:S(2)}, u32[]{:S(2)}) collective-permute-start(bf16[2,64,3072]{2,1,0:T(8,128)(2,1)} %fusion), channel_id=1, source_target_pairs={{0,2},{1,3},{2,0},{3,1},{4,6},{5,7},{6,4},{7,5},{8,10},{9,11},{10,... | collective-permute-start | bytes 2359304 | tf_op jit(solution)/shard_map/ppermute | solution.py:474
  164.5 4.4 %collective-permute-start.14 = (bf16[64,512]{1,0:T(8,128)(2,1)S(1)}, bf16[64,512]{1,0:T(8,128)(2,1)}, u32[]{:S(2)}, u32[]{:S(2)}) collective-permute-start(bf16[64,512]{1,0:T(8,128)(2,1)S(1)} %dynamic-slice_convert_fusion.2), channel_id=1, source_target_pairs={{0,8},{4,12},{8,0},{12,4},{16,24},{20,28},{24,16},{28,20},{1,9},{5... | collective-permute-start | bytes 196616 | tf_op jit(solution)/shard_map/ppermute | solution.py:477
  169.8 4.9 %collective-permute-start.15 = (bf16[32,512]{1,0:T(8,128)(2,1)S(1)}, bf16[32,512]{1,0:T(8,128)(2,1)S(1)}, u32[]{:S(2)}, u32[]{:S(2)}) collective-permute-start(bf16[32,512]{1,0:T(8,128)(2,1)S(1)} %dynamic-slice_convert_fusion.3), channel_id=1, source_target_pairs={{0,16},{4,20},{8,24},{12,28},{16,0},{20,4},{24,8},{28,12},{1,17},{... | collective-permute-start | bytes 98312 | tf_op jit(solution)/shard_map/ppermute | solution.py:477
  185.5 26.0 %copy-start.7 = (f32[2,512,512]{2,1,0:T(8,128)S(1)}, f32[2,512,512]{2,1,0:T(8,128)}, u32[]{:S(2)}) copy-start(f32[2,512,512]{2,1,0:T(8,128)} %probe.3) | copy-start | bytes 6291460
  185.5 4.9 %collective-permute-start.16 = (bf16[32,512]{1,0:T(8,128)(2,1)S(1)}, bf16[32,512]{1,0:T(8,128)(2,1)S(1)}, u32[]{:S(2)}, u32[]{:S(2)}) collective-permute-start(bf16[32,512]{1,0:T(8,128)(2,1)S(1)} %add_convert_fusion), channel_id=1, source_target_pairs={{0,16},{4,20},{8,24},{12,28},{16,0},{20,4},{24,8},{28,12},{1,17},{... | collective-permute-start | bytes 98312 | tf_op jit(solution)/shard_map/ppermute | solution.py:477
  190.4 4.3 %collective-permute-start.17 = (bf16[64,512]{1,0:T(8,128)(2,1)S(1)}, bf16[64,512]{1,0:T(8,128)(2,1)S(1)}, u32[]{:S(2)}, u32[]{:S(2)}) collective-permute-start(bf16[64,512]{1,0:T(8,128)(2,1)S(1)} %maximum_select_fusion.4), channel_id=1, source_target_pairs={{0,8},{4,12},{8,0},{12,4},{16,24},{20,28},{24,16},{28,20},{1,9},{5... | collective-permute-start | bytes 196616 | tf_op jit(solution)/shard_map/ppermute | solution.py:477
  194.8 8.0 %collective-permute-start.18 = (bf16[128,512]{1,0:T(8,128)(2,1)S(1)}, bf16[128,512]{1,0:T(8,128)(2,1)S(1)}, u32[]{:S(2)}, u32[]{:S(2)}) collective-permute-start(bf16[128,512]{1,0:T(8,128)(2,1)S(1)} %maximum_select_fusion.3), channel_id=1, source_target_pairs={{0,4},{4,0},{8,12},{12,8},{16,20},{20,16},{24,28},{28,24},{1,5},{5... | collective-permute-start | bytes 393224 | tf_op jit(solution)/shard_map/ppermute | solution.py:477
  202.9 6.4 %collective-permute-start.19 = (bf16[256,512]{1,0:T(8,128)(2,1)S(1)}, bf16[256,512]{1,0:T(8,128)(2,1)S(1)}, u32[]{:S(2)}, u32[]{:S(2)}) collective-permute-start(bf16[256,512]{1,0:T(8,128)(2,1)S(1)} %maximum_select_fusion.2), channel_id=1, source_target_pairs={{0,2},{1,3},{2,0},{3,1},{4,6},{5,7},{6,4},{7,5},{8,10},{9,11},{10,... | collective-permute-start | bytes 786440 | tf_op jit(solution)/shard_map/ppermute | solution.py:474
  209.5 2.0 collective-permute-start.20
  (6 other events, 11.3 us)
Sparse Core Ops, SparseCore 0:
  185.7 97.2 all-gather.2

commit v6 on v5

--- a/solution.py
+++ b/solution.py
@@ -220,7 +220,7 @@
         term_in, grad, keep_term, give_term, *scratch = refs
     else:
         grad, term_out, *scratch = refs
-    window, sib_v, far_v, probe_v, amp_v, left_v, right_v, term_v, patch_v, twice, field, half, sems = scratch
+    window, sib_v, far_v, probe_v, amp_v, matrix, term_v, patch_v, twice, field, half, sems = scratch
     index = 2 * me[0] + which
     col_at = first_col(pos, index)
     row_at = first_row(pos, index)
@@ -234,9 +234,8 @@
     cosine, sine, minus = tables
     quarters = [(slice(0, PATCH), slice(0, PATCH)), (slice(0, PATCH), slice(PATCH, 2 * PATCH))]
     quarters += [(slice(PATCH, 2 * PATCH), slice(0, PATCH)), (slice(PATCH, 2 * PATCH), slice(PATCH, 2 * PATCH))]
-    pairs += [(t, left_v.at[q]) for t, q in zip((cosine, minus, sine, cosine), quarters)]
+    pairs += [(t, matrix.at[q]) for t, q in zip((cosine, minus, sine, cosine), quarters)]
     pairs.append((amplitudes.at[which], amp_v))
-    pairs += [(t, right_v.at[q]) for t, q in zip((cosine, sine, minus, cosine), quarters)]
     if last:
         pairs.append((term_in, term_v))
     copies = [pltpu.make_async_copy(a, b, sems.at[k]) for k, (a, b) in enumerate(pairs)]
@@ -285,34 +284,34 @@
     for copy in copies[4:8]:
         copy.wait()
 
-    def over_rows(table):
+    def over_rows():
         for k in range(4):
             part = jnp.dot(
-                table[256 * k : 256 * (k + 1), :], field[...], preferred_element_type=jnp.float32
+                matrix[256 * k : 256 * (k + 1), :], field[...], preferred_element_type=jnp.float32
             ).astype(jnp.bfloat16)
-            half[256 * (k % 2) : 256 * (k % 2 + 1), PATCH * (k // 2) : PATCH * (k // 2 + 1)] = part
-
-    over_rows(left_v)
-    for copy in copies[8:13]:
-        copy.wait()
+            at = PATCH * (1 - k // 2)
+            half[256 * (k % 2) : 256 * (k % 2 + 1), at : at + PATCH] = part
+
+    over_rows()
+    copies[8].wait()
     for k in range(2):
         rows = slice(256 * k, 256 * (k + 1))
-        far = jnp.dot(half[rows, :], right_v[...], preferred_element_type=jnp.float32)
-        far_real = far[:, :PATCH]
-        far_imag = far[:, PATCH:]
+        far = jnp.dot(half[rows, :], matrix[...], preferred_element_type=jnp.float32)
+        far_imag = far[:, :PATCH]
+        far_real = far[:, PATCH:]
         power = far_real * far_real + far_imag * far_imag
         keep = 1.0 - amp_v[rows, :].astype(jnp.float32) * lax.rsqrt(
             jnp.maximum(power, MAGNITUDE_FLOOR * MAGNITUDE_FLOOR)
         )
-        field[rows, :] = (far_real * keep).astype(jnp.bfloat16)
-        field[PATCH + 256 * k : PATCH + 256 * (k + 1), :] = (far_imag * keep).astype(jnp.bfloat16)
-    over_rows(right_v)
+        field[rows, :] = (far_imag * keep).astype(jnp.bfloat16)
+        field[PATCH + 256 * k : PATCH + 256 * (k + 1), :] = (far_real * keep).astype(jnp.bfloat16)
+    over_rows()
     if last:
-        copies[13].wait()
+        copies[9].wait()
         core = lax.rem(me[0], 2)
     for k in range(2):
         rows = slice(256 * k, 256 * (k + 1))
-        back = jnp.dot(half[rows, :], left_v[...], preferred_element_type=jnp.float32)
+        back = jnp.dot(half[rows, :], matrix[...], preferred_element_type=jnp.float32)
         back_real = back[:, :PATCH]
         back_imag = back[:, PATCH:]
         patch_real = patch_v[0, rows, :].astype(jnp.float32)
@@ -386,13 +385,12 @@
             pltpu.VMEM(planes, jnp.float32),
             pltpu.VMEM((PATCH, PATCH), jnp.bfloat16),
             pltpu.VMEM((2 * PATCH, 2 * PATCH), jnp.bfloat16),
-            pltpu.VMEM((2 * PATCH, 2 * PATCH), jnp.bfloat16),
             pltpu.VMEM(planes, jnp.float32),
             pltpu.VMEM(planes, jnp.bfloat16),
             pltpu.VMEM((2, 2 * PATCH + SUBLANES, PATCH), jnp.float32),
             pltpu.VMEM((2 * PATCH, PATCH), jnp.bfloat16),
             pltpu.VMEM((PATCH, 2 * PATCH), jnp.bfloat16),
-            pltpu.SemaphoreType.DMA((14,)),
+            pltpu.SemaphoreType.DMA((10,)),
         ],
         compiler_params=pltpu.CompilerParams(vmem_limit_bytes=WAVE_VMEM),
         cost_estimate=pl.CostEstimate(
@@ -401,7 +399,7 @@
     )(pos, me, spare, *operands)
 
 
-def sum_kernel(pos, me, first, second, own, away, canvas):
+def sum_kernel(pos, me, first, second, own_far, own_near, away_far, away_near, canvas):
     classes, height = first.shape[0], first.shape[2]
     start = me[1] * height
     canvas[...] = jnp.zeros_like(canvas)
@@ -431,31 +429,31 @@
         return carry
 
     lax.fori_loop(0, classes, body, 0)
-    shape = own.shape[1:]
-    for k in range(2):
+    shape = own_far.shape
+    for k, (own, away) in enumerate([(own_far, away_far), (own_near, away_near)]):
         keep = lax.bitwise_xor(me[0], 2 - 2 * k)
         give = lax.bitwise_xor(me[0], 3 - 2 * k)
-        own[k] = canvas[keep].reshape(shape)
-        away[k] = canvas[give].reshape(shape).astype(jnp.bfloat16)
+        own[...] = canvas[keep].reshape(shape)
+        away[...] = canvas[give].reshape(shape).astype(jnp.bfloat16)
 
 
 def sum_pieces(pos, me, first, second, bands, width):
     height = first.shape[2]
     smem = pl.BlockSpec(memory_space=pltpu.SMEM)
     vmem = pl.BlockSpec(memory_space=pltpu.VMEM)
-    shape = (2, 2, height, width)
+    shape = (2, height, width)
     return pl.pallas_call(
         sum_kernel,
         in_specs=[smem, smem, vmem, vmem],
-        out_specs=[vmem, vmem],
+        out_specs=[vmem] * 4,
         out_shape=[
-            jax.ShapeDtypeStruct(shape, jnp.float32),
-            jax.ShapeDtypeStruct(shape, jnp.bfloat16),
+            jax.ShapeDtypeStruct(shape, kind)
+            for kind in (jnp.float32, jnp.float32, jnp.bfloat16, jnp.bfloat16)
         ],
         scratch_shapes=[pltpu.VMEM((bands, 2 * height, width), jnp.float32)],
         compiler_params=pltpu.CompilerParams(vmem_limit_bytes=SUM_VMEM),
         cost_estimate=pl.CostEstimate(
-            flops=8 * first.size, bytes_accessed=4 * first.size + 6 * math.prod(shape), transcendentals=0
+            flops=8 * first.size, bytes_accessed=4 * first.size + 12 * math.prod(shape), transcendentals=0
         ),
     )(pos, me, first, second)
 
@@ -501,11 +499,11 @@
         pos_pat = doubled(pos_pat, my_class // bit % 2, pat_flip(bit))
 
     operands = (probe, amplitudes, dft_tables(PATCH))
-    grad_0, term = wave(0, classes, pos, me, me, object_image, sibling, across[0], *operands, None)
+    grad_0, term = wave(0, classes, pos, me, pos_pat, object_image, sibling, across[0], *operands, None)
     grad_0, across[1] = lax.optimization_barrier((grad_0, across[1]))
     part_0 = lax.all_to_all(grad_0, "pat", split_axis=0, concat_axis=0, tiled=True)
     grad_1, keep_term, give_term = wave(
-        1, classes, pos, me, pos_pat, object_image, sibling, across[1], *operands, term
+        1, classes, pos, me, me, object_image, sibling, across[1], *operands, term
     )
     grad_1, part_0 = lax.optimization_barrier((grad_1, part_0))
     part_1 = lax.all_to_all(grad_1, "pat", split_axis=0, concat_axis=0, tiled=True)
@@ -515,15 +513,17 @@
     term = keep_term + flip(give_term, 1).astype(jnp.float32)
     term = halved(term, line, lambda value: flip(value, 2))
     term, then = lax.optimization_barrier((term, me))
-    own, away = sum_pieces(pos_pat, then, part_0, part_1, owners, width)
-    from_sibling_far = flip(away[0], 1)
-    from_sibling = flip(away[1], 1)
+    own_far, own_near, away_far, away_near = sum_pieces(
+        pos_pat, then, part_0, part_1, owners, width
+    )
+    from_sibling_far = flip(away_far, 1)
+    from_sibling = flip(away_near, 1)
     from_across = flip(
-        (own[0] + from_sibling_far.astype(jnp.float32)).astype(jnp.bfloat16), 2
+        (own_far + from_sibling_far.astype(jnp.float32)).astype(jnp.bfloat16), 2
     )
     for bit in bits:
         term = halved(term, my_class // bit % 2, pat_flip(bit))
-    total = own[1] + from_sibling.astype(jnp.float32) + from_across.astype(jnp.float32)
+    total = own_near + from_sibling.astype(jnp.float32) + from_across.astype(jnp.float32)
     mine = lax.dynamic_slice_in_dim(object_image, my_class * height, height, 1)
     updated = (mine.astype(jnp.float32) - OBJECT_RATE * total).astype(jnp.bfloat16)
     updated, term = lax.optimization_barrier((updated, term.astype(jnp.bfloat16)))

time: 296 us -> 284 us (0.959)
  waiting for transfers between devices: 175 us -> 169 us
  local copies, waits for them, and re-layouts: 18.6 us -> 14.8 us
  starting transfers between devices: 30.7 us -> 27.4 us
    all_to_all x1, waiting for transfers between devices: 0.01 us -> 13 us  [shards(): lax.all_to_all(grad_0, 'pat', split_axis=0, concat_axis=0, tiled=True)]
    ppermute x9, waiting for transfers between devices: 42.6 us -> 30.7 us  [pat_flip(): lax.ppermute(value, 'pat', [(k, k ^ bit) for k in range(classes)])]
    ppermute x12, waiting for transfers between devices: 51.6 us -> 43.5 us  [flip(): return lax.ppermute(value, 'obj', [(k, k ^ bit) for k in range(owners)])]
    ppermute x9, starting transfers between devices: 11.8 us -> 8.6 us  [pat_flip(): lax.ppermute(value, 'pat', [(k, k ^ bit) for k in range(classes)])]
    unnamed x31 -> x29, local copies, waits for them, and re-layouts: 15 us -> 14.4 us
  transfers between devices with their start and end apart: 24 -> 24, of which waited for: 19 -> 20; matrix products, arithmetic and copies ran while one was open for 4% -> 3% of each run, Pallas kernels for 11% -> 12%
where the time goes in v6:
time: 284 us
  waiting for transfers between devices  169 us (60%)
  Pallas kernels  41 us (14%)
  starting transfers between devices  27.4 us (10%)
  local copies, waits for them, and re-layouts  14.8 us (5%)
  between operations  14.3 us (5%)
  other arithmetic  11.1 us (4%)
  blocking collectives  5.99 us (2%)
    all_gather x1, waiting for transfers between devices, shards(): object_next = lax.all_gather(updated, 'pat', axis=1, tiled=True)  70.4 us
    ppermute x12, waiting for transfers between devices, flip(): return lax.ppermute(value, 'obj', [(k, k ^ bit) for k in range(owners)])  43.5 us
    ppermute x9, waiting for transfers between devices, pat_flip(): lax.ppermute(value, 'pat', [(k, k ^ bit) for k in range(classes)])  30.7 us
    pallas_call x2, Pallas kernels, wave(): pl.pallas_call(functools.partial(wave_kernel, which), in_specs=[smem, sme...  24.7 us
    unnamed x29, local copies, waits for them, and re-layouts  14.4 us
    all_to_all x1, waiting for transfers between devices, shards(): lax.all_to_all(grad_0, 'pat', split_axis=0, concat_axis=0, tiled=True)  13 us
    all_to_all x1, waiting for transfers between devices, shards(): lax.all_to_all(grad_1, 'pat', split_axis=0, concat_axis=0, tiled=True)  11.8 us
    ppermute x12, starting transfers between devices, flip(): return lax.ppermute(value, 'obj', [(k, k ^ bit) for k in range(owners)])  9.15 us
  transfers between devices with their start and end apart: 24, of which 20 were waited for; matrix products, arithmetic and copies ran while one was open for 3% of the time, Pallas kernels for 12%

profile of v6, /device:TPU:0, one launch (start us, length us, event | category | flops | bytes accessed | tf_op | source)
XLA Modules:
  0.0 284.0 jit_solution(17894034091445061004)
XLA Ops:
  8.8 6.0 %all-gather = s32[4,2,4]{2,1,0:T(2,128)S(1)} all-gather(s32[1,2,4]{2,1,0:T(2,128)S(1)} %bitcast.14), channel_id=1, replica_groups=mesh['pat'=8,'obj'=4] {'obj'}, dimensions={0}, use_global_device_ids=true | all-gather | bytes 160 | tf_op jit(solution)/shard_map/all_gather | solution.py:488
  14.9 2.8 copy-done
  19.9 6.0 %shard_map.95 = (bf16[1,2,512,512]{3,2,1,0:T(8,128)(2,1)S(1)}, bf16[2,2,512,512]{3,2,1,0:T(8,128)(2,1)}) custom-call(s32[8,4]{1,0:T(8,128)S(1)} %bitcast.7, s32[2]{0:T(128)S(1)} %pad_add_fusion.3.me.spare, bf16[2,512,3072]{2,1,0:T(8,128)(2,1)S(1)} %copy-done, bf16[2,512,3072]{2,1,0:T(8,128)(2,1)S(1)} %copy-done, bf16[2,512,3072]{2,1,0:T(8,128)(2,1)S(1)} %copy-done, ...), custom_call_target="tpu_custom_call" | custom-call | flops 1966080 | bytes 7000000 | tf_op jit(solution)/shard_map/pallas_call | solution.py:194
  28.2 2.1 collective-permute-start.6
  33.0 2.5 collective-permute-start.7
  37.0 2.1 collective-permute-done.1
  40.7 2.0 collective-permute-done.2
  42.8 2.3 collective-permute-start.3
  45.1 2.2 collective-permute-done.3
  48.1 6.2 %collective-permute-done.6.across = bf16[2,512,512]{2,1,0:T(8,128)(2,1)} collective-permute-done((bf16[2,512,512]{2,1,0:T(8,128)(2,1)S(1)}, bf16[2,512,512]{2,1,0:T(8,128)(2,1)}, u32[]{:S(2)}, u32[]{:S(2)}) %collective-permute-start.6) | collective-permute-done | bytes 1048608 | tf_op jit(solution)/shard_map/ppermute | solution.py:472
  54.4 12.2 %shard_map.99 = (bf16[8,2,64,512]{3,2,1,0:T(8,128)(2,1)}, f32[2,512,512]{2,1,0:T(8,128)}) custom-call(s32[8,4]{1,0:T(8,128)} %bitcast.10, s32[2]{0:T(128)} %copy-done.6, s32[16,4]{1,0:T(8,128)} %broadcast_select_fusion.spare.pos, bf16[2,512,3072]{2,1,0:T(8,128)(2,1)} %band.3, bf16[2,2,512,512]{3,2,1,0:T(8,128)(2,1)} %collective-permute-done.4.sibling, ...), custom_call_target="tpu_custom_call" | custom-call | flops 4294967296 | bytes 100000000 | tf_op jit(solution)/shard_map/pallas_call | solution.py:373
  66.6 9.8 %collective-permute-done.7.across = bf16[2,512,512]{2,1,0:T(8,128)(2,1)S(1)} collective-permute-done((bf16[2,512,512]{2,1,0:T(8,128)(2,1)S(1)}, bf16[2,512,512]{2,1,0:T(8,128)(2,1)S(1)}, u32[]{:S(2)}, u32[]{:S(2)}) %collective-permute-start.7) | collective-permute-done | bytes 1048608 | tf_op jit(solution)/shard_map/ppermute | solution.py:472
  76.3 6.0 %all-to-all-start = ((bf16[8,2,64,512]{3,2,1,0:T(8,128)(2,1)}), bf16[8,2,64,512]{3,2,1,0:T(8,128)(2,1)S(1)}, u32[]{:S(2)}, u32[]{:S(2)}) async-start(bf16[8,2,64,512]{3,2,1,0:T(8,128)(2,1)} %get-tuple-element.40), calls=%async_computation | async-start | bytes 2097152 | tf_op jit(solution)/shard_map/all_to_all | solution.py:504
  82.3 12.5 %shard_map.100 = (bf16[8,2,64,512]{3,2,1,0:T(8,128)(2,1)}, f32[512,512]{1,0:T(8,128)}, bf16[512,512]{1,0:T(8,128)(2,1)}) custom-call(s32[8,4]{1,0:T(8,128)} %bitcast.11, s32[2]{0:T(128)} %copy-done.6, s32[2]{0:T(128)} %copy-done.6, bf16[2,512,3072]{2,1,0:T(8,128)(2,1)} %band.3, bf16[2,2,512,512]{3,2,1,0:T(8,128)(2,1)} %collective-permute-done.4.sibling, ...), custom_call_target="tpu_custom_call" | custom-call | flops 4294967296 | bytes 100000000 | tf_op jit(solution)/shard_map/pallas_call | solution.py:373
  94.9 13.0 %all-to-all-done.first = bf16[8,2,64,512]{3,2,1,0:T(8,128)(2,1)S(1)} async-done(((bf16[8,2,64,512]{3,2,1,0:T(8,128)(2,1)}), bf16[8,2,64,512]{3,2,1,0:T(8,128)(2,1)S(1)}, u32[]{:S(2)}, u32[]{:S(2)}) %all-to-all-start) | async-done | bytes 1048608 | tf_op jit(solution)/shard_map/all_to_all | solution.py:504
  107.9 3.6 %all-to-all-start.1 = ((bf16[8,2,64,512]{3,2,1,0:T(8,128)(2,1)}), bf16[8,2,64,512]{3,2,1,0:T(8,128)(2,1)S(1)}, u32[]{:S(2)}, u32[]{:S(2)}) async-start(bf16[8,2,64,512]{3,2,1,0:T(8,128)(2,1)} %get-tuple-element.42), calls=%async_computation.1 | async-start | bytes 2097152 | tf_op jit(solution)/shard_map/all_to_all | solution.py:509
  111.6 1.9 collective-permute-done.8
  117.1 7.2 %collective-permute-done.9 = bf16[256,512]{1,0:T(8,128)(2,1)S(1)} collective-permute-done((bf16[256,512]{1,0:T(8,128)(2,1)S(1)}, bf16[256,512]{1,0:T(8,128)(2,1)S(1)}, u32[]{:S(2)}, u32[]{:S(2)}) %collective-permute-start.9) | collective-permute-done | bytes 262176 | tf_op jit(solution)/shard_map/ppermute | solution.py:472
  125.4 11.8 %all-to-all-done.1.second = bf16[8,2,64,512]{3,2,1,0:T(8,128)(2,1)S(1)} async-done(((bf16[8,2,64,512]{3,2,1,0:T(8,128)(2,1)}), bf16[8,2,64,512]{3,2,1,0:T(8,128)(2,1)S(1)}, u32[]{:S(2)}, u32[]{:S(2)}) %all-to-all-start.1) | async-done | bytes 1048608 | tf_op jit(solution)/shard_map/all_to_all | solution.py:509
  137.2 4.9 %shard_map.101 = (f32[2,64,3072]{2,1,0:T(8,128)S(1)}, f32[2,64,3072]{2,1,0:T(8,128)S(1)}, bf16[2,64,3072]{2,1,0:T(8,128)(2,1)}, bf16[2,64,3072]{2,1,0:T(8,128)(2,1)S(1)}) custom-call(s32[16,4]{1,0:T(8,128)S(1)} %copy-done.5, s32[2]{0:T(128)S(1)} %copy-done.7, bf16[8,2,64,512]{3,2,1,0:T(8,128)(2,1)S(1)} %all-to-all-done.first, ...), custom_call_target="tpu_custom_call" | custom-call | flops 4194304 | bytes 6815744 | tf_op jit(solution)/shard_map/pallas_call | solution.py:445
  147.7 2.8 add_convert_fusion
  151.7 4.2 %collective-permute-done.14 = bf16[64,512]{1,0:T(8,128)(2,1)S(1)} collective-permute-done((bf16[64,512]{1,0:T(8,128)(2,1)S(1)}, bf16[64,512]{1,0:T(8,128)(2,1)S(1)}, u32[]{:S(2)}, u32[]{:S(2)}) %collective-permute-start.14) | collective-permute-done | bytes 65568 | tf_op jit(solution)/shard_map/ppermute | solution.py:475
  156.0 4.8 %collective-permute-done.15 = bf16[32,512]{1,0:T(8,128)(2,1)S(1)} collective-permute-done((bf16[32,512]{1,0:T(8,128)(2,1)S(1)}, bf16[32,512]{1,0:T(8,128)(2,1)S(1)}, u32[]{:S(2)}, u32[]{:S(2)}) %collective-permute-start.15) | collective-permute-done | bytes 32800 | tf_op jit(solution)/shard_map/ppermute | solution.py:475
  160.9 9.5 %collective-permute-done.12 = bf16[2,64,3072]{2,1,0:T(8,128)(2,1)} collective-permute-done((bf16[2,64,3072]{2,1,0:T(8,128)(2,1)}, bf16[2,64,3072]{2,1,0:T(8,128)(2,1)}, u32[]{:S(2)}, u32[]{:S(2)}) %collective-permute-start.12) | collective-permute-done | bytes 786464 | tf_op jit(solution)/shard_map/ppermute | solution.py:472
  170.4 2.9 %subtract_convert_fusion = bf16[2,64,3072]{2,1,0:T(8,128)(2,1)} fusion(bf16[2,64,3072]{2,1,0:T(8,128)(2,1)} %collective-permute-done.12, f32[2,64,3072]{2,1,0:T(8,128)S(1)} %copy-done.2, bf16[2,64,3072]{2,1,0:T(8,128)(2,1)} %collective-permute-done.10, bf16[2,512,3072]{2,1,0:T(8,128)(2,1)} %band.3, s32[]{:T(128)S(6)} %select_n.155), kind=kLoop, calls=%fused_computation.1 | loop fusion | flops 3145728 | bytes 4718596 | tf_op jit(solution)/shard_map/convert_element_type | solution.py:528
  173.4 4.8 %collective-permute-done.16 = bf16[32,512]{1,0:T(8,128)(2,1)S(1)} collective-permute-done((bf16[32,512]{1,0:T(8,128)(2,1)S(1)}, bf16[32,512]{1,0:T(8,128)(2,1)S(1)}, u32[]{:S(2)}, u32[]{:S(2)}) %collective-permute-start.16) | collective-permute-done | bytes 32800 | tf_op jit(solution)/shard_map/ppermute | solution.py:475
  178.3 4.3 %collective-permute-done.17 = bf16[64,512]{1,0:T(8,128)(2,1)S(1)} collective-permute-done((bf16[64,512]{1,0:T(8,128)(2,1)S(1)}, bf16[64,512]{1,0:T(8,128)(2,1)S(1)}, u32[]{:S(2)}, u32[]{:S(2)}) %collective-permute-start.17) | collective-permute-done | bytes 65568 | tf_op jit(solution)/shard_map/ppermute | solution.py:475
  184.1 6.3 %collective-permute-done.18 = bf16[128,512]{1,0:T(8,128)(2,1)S(1)} collective-permute-done((bf16[128,512]{1,0:T(8,128)(2,1)S(1)}, bf16[128,512]{1,0:T(8,128)(2,1)S(1)}, u32[]{:S(2)}, u32[]{:S(2)}) %collective-permute-start.18) | collective-permute-done | bytes 131104 | tf_op jit(solution)/shard_map/ppermute | solution.py:475
  191.6 5.3 %collective-permute-done.19 = bf16[256,512]{1,0:T(8,128)(2,1)S(1)} collective-permute-done((bf16[256,512]{1,0:T(8,128)(2,1)S(1)}, bf16[256,512]{1,0:T(8,128)(2,1)S(1)}, u32[]{:S(2)}, u32[]{:S(2)}) %collective-permute-start.19) | collective-permute-done | bytes 262176 | tf_op jit(solution)/shard_map/ppermute | solution.py:472
  197.2 1.9 collective-permute-done.20
  200.8 70.4 %all-gather.3.cloned.1.call-done = bf16[2,512,3072]{2,1,0:T(8,128)(2,1)} async-done(((bf16[2,64,3072]{2,1,0:T(8,128)(2,1)}), bf16[2,512,3072]{2,1,0:T(8,128)(2,1)}) %all-gather.3.cloned.1.call-update) | async-done | bytes 6291472 | tf_op jit(solution)/shard_map/all_gather | solution.py:535
  271.2 5.9 %copy.16 = bf16[2,512,3072]{2,1,0:T(8,128)(2,1)} copy(bf16[2,512,3072]{2,1,0:T(8,128)(2,1)} %all-gather.3.cloned.1.call-done) | data formatting | bytes 12582912
  (79 shorter events, 29.5 us)
Async XLA Ops:
  14.8 16.4 %copy-start.4 = (s32[4,2,4]{2,1,0:T(2,128)}, s32[4,2,4]{2,1,0:T(2,128)S(1)}, u32[]{:S(2)}) copy-start(s32[4,2,4]{2,1,0:T(2,128)S(1)} %all-gather) | copy-start | bytes 388
  14.9 16.3 %copy-start.6 = (s32[2]{0:T(128)}, s32[2]{0:T(128)S(1)}, u32[]{:S(2)}) copy-start(s32[2]{0:T(128)S(1)} %pad_add_fusion.3.me.spare) | copy-start | bytes 28
  19.5 7.0 %collective-permute-start.5 = (bf16[1,2,512,512]{3,2,1,0:T(8,128)(2,1)S(1)}, bf16[1,2,512,512]{3,2,1,0:T(8,128)(2,1)S(1)}, u32[]{:S(2)}, u32[]{:S(2)}) collective-permute-start(bf16[1,2,512,512]{3,2,1,0:T(8,128)(2,1)S(1)} %shard_map.97), channel_id=1, source_target_pairs={{0,1},{1,0},{2,3},{3,2},{4,5},{5,4},{6,7},{7,6},{8,9},{9,8},{10,11... | collective-permute-start | bytes 3145736 | tf_op jit(solution)/shard_map/ppermute | solution.py:472
  25.9 28.5 %collective-permute-start.4 = (bf16[2,2,512,512]{3,2,1,0:T(8,128)(2,1)}, bf16[2,2,512,512]{3,2,1,0:T(8,128)(2,1)}, u32[]{:S(2)}, u32[]{:S(2)}) collective-permute-start(bf16[2,2,512,512]{3,2,1,0:T(8,128)(2,1)} %get-tuple-element.31), channel_id=1, source_target_pairs={{0,1},{1,0},{2,3},{3,2},{4,5},{5,4},{6,7},{7,6},{8,9},{9,8},{10,11... | collective-permute-start | bytes 6291464 | tf_op jit(solution)/shard_map/ppermute | solution.py:472
  25.9 5.3 %collective-permute-start = (bf16[1,2,512,512]{3,2,1,0:T(8,128)(2,1)S(1)}, bf16[1,2,512,512]{3,2,1,0:T(8,128)(2,1)S(1)}, u32[]{:S(2)}, u32[]{:S(2)}) collective-permute-start(bf16[1,2,512,512]{3,2,1,0:T(8,128)(2,1)S(1)} %get-tuple-element.29), channel_id=1, source_target_pairs={{0,1},{1,0},{2,3},{3,2},{4,5},{5,4},{6,7},{7,6},{8,9},{9,8},{10,11... | collective-permute-start | bytes 3145736 | tf_op jit(solution)/shard_map/ppermute | solution.py:472
  28.2 26.1 %collective-permute-start.6 = (bf16[2,512,512]{2,1,0:T(8,128)(2,1)S(1)}, bf16[2,512,512]{2,1,0:T(8,128)(2,1)}, u32[]{:S(2)}, u32[]{:S(2)}) collective-permute-start(bf16[2,512,512]{2,1,0:T(8,128)(2,1)S(1)} %shard_map.98), channel_id=1, source_target_pairs={{0,2},{1,3},{2,0},{3,1},{4,6},{5,7},{6,4},{7,5},{8,10},{9,11},{10,... | collective-permute-start | bytes 3145736 | tf_op jit(solution)/shard_map/ppermute | solution.py:472
  33.0 43.3 %collective-permute-start.7 = (bf16[2,512,512]{2,1,0:T(8,128)(2,1)S(1)}, bf16[2,512,512]{2,1,0:T(8,128)(2,1)S(1)}, u32[]{:S(2)}, u32[]{:S(2)}) collective-permute-start(bf16[2,512,512]{2,1,0:T(8,128)(2,1)S(1)} %shard_map.96), channel_id=1, source_target_pairs={{0,2},{1,3},{2,0},{3,1},{4,6},{5,7},{6,4},{7,5},{8,10},{9,11},{10,... | collective-permute-start | bytes 3145736 | tf_op jit(solution)/shard_map/ppermute | solution.py:472
  35.5 3.6 %collective-permute-start.1 = (s32[2,4]{0,1:T(4,128)S(1)}, s32[2,4]{0,1:T(4,128)S(1)}, u32[]{:S(2)}, u32[]{:S(2)}) collective-permute-start(s32[2,4]{0,1:T(4,128)S(1)} %pad_add_fusion), channel_id=1, source_target_pairs={{0,4},{4,0},{8,12},{12,8},{16,20},{20,16},{24,28},{28,24},{1,5},{5... | collective-permute-start | bytes 104 | tf_op jit(solution)/shard_map/ppermute | solution.py:475
  39.1 3.6 %collective-permute-start.2 = (s32[4,4]{0,1:T(4,128)S(1)}, s32[4,4]{0,1:T(4,128)S(1)}, u32[]{:S(2)}, u32[]{:S(2)}) collective-permute-start(s32[4,4]{0,1:T(4,128)S(1)} %add_select_fusion), channel_id=1, source_target_pairs={{0,8},{4,12},{8,0},{12,4},{16,24},{20,28},{24,16},{28,20},{1,9},{5... | collective-permute-start | bytes 200 | tf_op jit(solution)/shard_map/ppermute | solution.py:475
  42.8 4.5 %collective-permute-start.3 = (s32[8,4]{0,1:T(4,128)S(1)}, s32[8,4]{0,1:T(4,128)S(1)}, u32[]{:S(2)}, u32[]{:S(2)}) collective-permute-start(s32[8,4]{0,1:T(4,128)S(1)} %add_select_fusion.1), channel_id=1, source_target_pairs={{0,16},{4,20},{8,24},{12,28},{16,0},{20,4},{24,8},{28,12},{1,17},{... | collective-permute-start | bytes 392 | tf_op jit(solution)/shard_map/ppermute | solution.py:475
  76.3 6.0 %copy-start.10 = (bf16[2,512,512]{2,1,0:T(8,128)(2,1)}, bf16[2,512,512]{2,1,0:T(8,128)(2,1)S(1)}, u32[]{:S(2)}) copy-start(bf16[2,512,512]{2,1,0:T(8,128)(2,1)S(1)} %collective-permute-done.7.across) | copy-start | bytes 3145732
  76.3 31.5 %all-to-all-start = ((bf16[8,2,64,512]{3,2,1,0:T(8,128)(2,1)}), bf16[8,2,64,512]{3,2,1,0:T(8,128)(2,1)S(1)}, u32[]{:S(2)}, u32[]{:S(2)}) async-start(bf16[8,2,64,512]{3,2,1,0:T(8,128)(2,1)} %get-tuple-element.40), calls=%async_computation | async-start | bytes 2097152 | tf_op jit(solution)/shard_map/all_to_all | solution.py:504
  94.9 16.6 %copy-start.12 = (bf16[512,512]{1,0:T(8,128)(2,1)S(1)}, bf16[512,512]{1,0:T(8,128)(2,1)}, u32[]{:S(2)}) copy-start(bf16[512,512]{1,0:T(8,128)(2,1)} %get-tuple-element.37) | copy-start | bytes 1572868
  107.9 29.3 %all-to-all-start.1 = ((bf16[8,2,64,512]{3,2,1,0:T(8,128)(2,1)}), bf16[8,2,64,512]{3,2,1,0:T(8,128)(2,1)S(1)}, u32[]{:S(2)}, u32[]{:S(2)}) async-start(bf16[8,2,64,512]{3,2,1,0:T(8,128)(2,1)} %get-tuple-element.42), calls=%async_computation.1 | async-start | bytes 2097152 | tf_op jit(solution)/shard_map/all_to_all | solution.py:509
  111.4 159.8 %all-gather.3.cloned.1.call-start = ((), (), s32[]{:S(2)}) async-start(), calls=%async_computation.2 | async-start | bytes 7077888 | tf_op jit(solution)/shard_map/all_gather | solution.py:535
  111.5 2.0 collective-permute-start.8
  113.5 23.7 %copy-start.5 = (s32[16,4]{1,0:T(8,128)S(1)}, s32[16,4]{1,0:T(8,128)}, u32[]{:S(2)}) copy-start(s32[16,4]{1,0:T(8,128)} %broadcast_select_fusion.spare.pos) | copy-start | bytes 772
  113.5 23.7 %copy-start.7 = (s32[2]{0:T(128)S(1)}, s32[2]{0:T(128)}, u32[]{:S(2)}) copy-start(s32[2]{0:T(128)} %copy-done.6) | copy-start | bytes 28
  115.9 8.4 %collective-permute-start.9 = (bf16[256,512]{1,0:T(8,128)(2,1)S(1)}, bf16[256,512]{1,0:T(8,128)(2,1)S(1)}, u32[]{:S(2)}, u32[]{:S(2)}) collective-permute-start(bf16[256,512]{1,0:T(8,128)(2,1)S(1)} %dynamic-slice_convert_fusion), channel_id=1, source_target_pairs={{0,2},{1,3},{2,0},{3,1},{4,6},{5,7},{6,4},{7,5},{8,10},{9,11},{10,... | collective-permute-start | bytes 786440 | tf_op jit(solution)/shard_map/ppermute | solution.py:472
  144.3 2.5 collective-permute-start.11
  144.4 7.2 %collective-permute-start.13 = (bf16[128,512]{1,0:T(8,128)(2,1)S(1)}, bf16[128,512]{1,0:T(8,128)(2,1)S(1)}, u32[]{:S(2)}, u32[]{:S(2)}) collective-permute-start(bf16[128,512]{1,0:T(8,128)(2,1)S(1)} %dynamic-slice_convert_fusion.1), channel_id=1, source_target_pairs={{0,4},{4,0},{8,12},{12,8},{16,20},{20,16},{24,28},{28,24},{1,5},{5... | collective-permute-start | bytes 393224 | tf_op jit(solution)/shard_map/ppermute | solution.py:475
  145.8 15.0 %collective-permute-start.10 = (bf16[2,64,3072]{2,1,0:T(8,128)(2,1)S(1)}, bf16[2,64,3072]{2,1,0:T(8,128)(2,1)}, u32[]{:S(2)}, u32[]{:S(2)}) collective-permute-start(bf16[2,64,3072]{2,1,0:T(8,128)(2,1)S(1)} %get-tuple-element.44), channel_id=1, source_target_pairs={{0,1},{1,0},{2,3},{3,2},{4,5},{5,4},{6,7},{7,6},{8,9},{9,8},{10,11... | collective-permute-start | bytes 2359304 | tf_op jit(solution)/shard_map/ppermute | solution.py:472
  147.7 22.7 %copy-start.2 = (f32[2,64,3072]{2,1,0:T(8,128)S(1)}, f32[2,64,3072]{2,1,0:T(8,128)}, u32[]{:S(2)}) copy-start(f32[2,64,3072]{2,1,0:T(8,128)} %copy-done.1) | copy-start | bytes 4718596
  150.5 19.9 %collective-permute-start.12 = (bf16[2,64,3072]{2,1,0:T(8,128)(2,1)}, bf16[2,64,3072]{2,1,0:T(8,128)(2,1)}, u32[]{:S(2)}, u32[]{:S(2)}) collective-permute-start(bf16[2,64,3072]{2,1,0:T(8,128)(2,1)} %add_convert_fusion), channel_id=1, source_target_pairs={{0,2},{1,3},{2,0},{3,1},{4,6},{5,7},{6,4},{7,5},{8,10},{9,11},{10,... | collective-permute-start | bytes 2359304 | tf_op jit(solution)/shard_map/ppermute | solution.py:472
  151.6 4.3 %collective-permute-start.14 = (bf16[64,512]{1,0:T(8,128)(2,1)S(1)}, bf16[64,512]{1,0:T(8,128)(2,1)S(1)}, u32[]{:S(2)}, u32[]{:S(2)}) collective-permute-start(bf16[64,512]{1,0:T(8,128)(2,1)S(1)} %dynamic-slice_convert_fusion.2), channel_id=1, source_target_pairs={{0,8},{4,12},{8,0},{12,4},{16,24},{20,28},{24,16},{28,20},{1,9},{5... | collective-permute-start | bytes 196616 | tf_op jit(solution)/shard_map/ppermute | solution.py:475
  156.0 4.9 %collective-permute-start.15 = (bf16[32,512]{1,0:T(8,128)(2,1)S(1)}, bf16[32,512]{1,0:T(8,128)(2,1)S(1)}, u32[]{:S(2)}, u32[]{:S(2)}) collective-permute-start(bf16[32,512]{1,0:T(8,128)(2,1)S(1)} %dynamic-slice_convert_fusion.3), channel_id=1, source_target_pairs={{0,16},{4,20},{8,24},{12,28},{16,0},{20,4},{24,8},{28,12},{1,17},{... | collective-permute-start | bytes 98312 | tf_op jit(solution)/shard_map/ppermute | solution.py:475
  173.3 25.8 %copy-start.8 = (f32[2,512,512]{2,1,0:T(8,128)S(1)}, f32[2,512,512]{2,1,0:T(8,128)}, u32[]{:S(2)}) copy-start(f32[2,512,512]{2,1,0:T(8,128)} %probe.3) | copy-start | bytes 6291460
  173.3 4.9 %collective-permute-start.16 = (bf16[32,512]{1,0:T(8,128)(2,1)S(1)}, bf16[32,512]{1,0:T(8,128)(2,1)S(1)}, u32[]{:S(2)}, u32[]{:S(2)}) collective-permute-start(bf16[32,512]{1,0:T(8,128)(2,1)S(1)} %add_convert_fusion.1), channel_id=1, source_target_pairs={{0,16},{4,20},{8,24},{12,28},{16,0},{20,4},{24,8},{28,12},{1,17},{... | collective-permute-start | bytes 98312 | tf_op jit(solution)/shard_map/ppermute | solution.py:475
  178.2 4.3 %collective-permute-start.17 = (bf16[64,512]{1,0:T(8,128)(2,1)S(1)}, bf16[64,512]{1,0:T(8,128)(2,1)S(1)}, u32[]{:S(2)}, u32[]{:S(2)}) collective-permute-start(bf16[64,512]{1,0:T(8,128)(2,1)S(1)} %maximum_select_fusion.4), channel_id=1, source_target_pairs={{0,8},{4,12},{8,0},{12,4},{16,24},{20,28},{24,16},{28,20},{1,9},{5... | collective-permute-start | bytes 196616 | tf_op jit(solution)/shard_map/ppermute | solution.py:475
  182.6 7.8 %collective-permute-start.18 = (bf16[128,512]{1,0:T(8,128)(2,1)S(1)}, bf16[128,512]{1,0:T(8,128)(2,1)S(1)}, u32[]{:S(2)}, u32[]{:S(2)}) collective-permute-start(bf16[128,512]{1,0:T(8,128)(2,1)S(1)} %maximum_select_fusion.3), channel_id=1, source_target_pairs={{0,4},{4,0},{8,12},{12,8},{16,20},{20,16},{24,28},{28,24},{1,5},{5... | collective-permute-start | bytes 393224 | tf_op jit(solution)/shard_map/ppermute | solution.py:475
  190.5 6.4 %collective-permute-start.19 = (bf16[256,512]{1,0:T(8,128)(2,1)S(1)}, bf16[256,512]{1,0:T(8,128)(2,1)S(1)}, u32[]{:S(2)}, u32[]{:S(2)}) collective-permute-start(bf16[256,512]{1,0:T(8,128)(2,1)S(1)} %maximum_select_fusion.2), channel_id=1, source_target_pairs={{0,2},{1,3},{2,0},{3,1},{4,6},{5,7},{6,4},{7,5},{8,10},{9,11},{10,... | collective-permute-start | bytes 786440 | tf_op jit(solution)/shard_map/ppermute | solution.py:472
  197.1 2.0 collective-permute-start.20
  (5 other events, 6.9 us)
Sparse Core Ops, SparseCore 0:
  173.5 97.6 all-gather.2

commit v7 on v6

--- a/solution.py
+++ b/solution.py
@@ -217,9 +217,11 @@
     tables, refs = refs[:3], refs[3:]
     last = which == 1
     if last:
-        term_in, grad, keep_term, give_term, *scratch = refs
+        term_in, real_grad, imag_grad, keep_term, give_term, *scratch = refs
+        grads = [real_grad, imag_grad]
     else:
-        grad, term_out, *scratch = refs
+        both, term_out, *scratch = refs
+        grads = [both.at[:, plane] for plane in range(2)]
     window, sib_v, far_v, probe_v, amp_v, matrix, term_v, patch_v, twice, field, half, sems = scratch
     index = 2 * me[0] + which
     col_at = first_col(pos, index)
@@ -346,11 +348,11 @@
         return carry
 
     lax.fori_loop(0, PATCH // CHUNK, weigh, 0)
-    classes, height = grad.shape[0], grad.shape[2]
+    classes, height = grads[0].shape[0], grads[0].shape[1]
 
     def spread(k, carry):
         for plane in range(2):
-            grad[k, plane] = rows_from(twice, plane, PATCH - down + k * height, height).astype(
+            grads[plane][k] = rows_from(twice, plane, PATCH - down + k * height, height).astype(
                 jnp.bfloat16
             )
         return carry
@@ -365,19 +367,19 @@
     vmem = pl.BlockSpec(memory_space=pltpu.VMEM)
     planes = (2, PATCH, PATCH)
     plane = (PATCH, PATCH)
+    height = PATCH // classes
     if term is None:
+        grads = [jax.ShapeDtypeStruct((classes, 2, height, PATCH), jnp.bfloat16)]
         terms = [jax.ShapeDtypeStruct(planes, jnp.float32)]
     else:
         operands.append(term)
+        grads = [jax.ShapeDtypeStruct((classes, height, PATCH), jnp.bfloat16)] * 2
         terms = [jax.ShapeDtypeStruct(plane, t) for t in (jnp.float32, jnp.bfloat16)]
     return pl.pallas_call(
         functools.partial(wave_kernel, which),
         in_specs=[smem, smem, smem] + [hbm] * len(operands),
-        out_specs=[vmem] * (1 + len(terms)),
-        out_shape=[
-            jax.ShapeDtypeStruct((classes, 2, PATCH // classes, PATCH), jnp.bfloat16),
-            *terms,
-        ],
+        out_specs=[vmem] * len(grads + terms),
+        out_shape=grads + terms,
         scratch_shapes=[
             pltpu.VMEM((2, PATCH, WIDE), jnp.bfloat16),
             pltpu.VMEM(planes, jnp.bfloat16),
@@ -394,26 +396,23 @@
         ],
         compiler_params=pltpu.CompilerParams(vmem_limit_bytes=WAVE_VMEM),
         cost_estimate=pl.CostEstimate(
-            flops=32 * PATCH**3, bytes_accessed=100_000_000, transcendentals=0
+            flops=32 * PATCH**3, bytes_accessed=300_000_000, transcendentals=0
         ),
     )(pos, me, spare, *operands)
 
 
 def sum_kernel(pos, me, first, second, own_far, own_near, away_far, away_near, canvas):
-    classes, height = first.shape[0], first.shape[2]
+    classes, height = second.shape[0], second.shape[1]
     start = me[1] * height
     canvas[...] = jnp.zeros_like(canvas)
-    rows = lax.broadcasted_iota(jnp.int32, (2 * height, WIDE), 0)
-    rows = start + jnp.where(rows >= height, rows - height, rows)
-
-    def piece(k, source, which):
-        index = 2 * k + which
+    rows = start + lax.broadcasted_iota(jnp.int32, (height, WIDE), 0)
+
+    def piece(data, index):
         row_at = first_row(pos, index)
         col_at = first_col(pos, index)
         down = lax.rem(row_at, PATCH)
         at = pl.ds(pl.multiple_of(col_at // LANES * LANES, LANES), WIDE)
-        data = source[k].astype(jnp.float32).reshape(2 * height, PATCH)
-        data = shifted_right(data, lax.rem(col_at, LANES))
+        data = shifted_right(data.astype(jnp.float32), lax.rem(col_at, LANES))
 
         @pl.when(down < start + height)
         def _():
@@ -424,38 +423,61 @@
             canvas[row_at // PATCH + 1, :, at] += jnp.where(rows < down, data, 0.0)
 
     def body(k, carry):
-        piece(k, first, 0)
-        piece(k, second, 1)
+        piece(first[k, 0], 2 * k)
+        piece(second[k], 2 * k + 1)
         return carry
 
     lax.fori_loop(0, classes, body, 0)
-    shape = own_far.shape
     for k, (own, away) in enumerate([(own_far, away_far), (own_near, away_near)]):
-        keep = lax.bitwise_xor(me[0], 2 - 2 * k)
-        give = lax.bitwise_xor(me[0], 3 - 2 * k)
-        own[...] = canvas[keep].reshape(shape)
-        away[...] = canvas[give].reshape(shape).astype(jnp.bfloat16)
-
-
-def sum_pieces(pos, me, first, second, bands, width):
-    height = first.shape[2]
+        own[...] = canvas[lax.bitwise_xor(me[0], 2 - 2 * k)]
+        away[...] = canvas[lax.bitwise_xor(me[0], 3 - 2 * k)].astype(jnp.bfloat16)
+
+
+def sum_pieces(plane, pos, me, first, second, bands, width):
+    classes, height = second.shape[0], second.shape[1]
     smem = pl.BlockSpec(memory_space=pltpu.SMEM)
-    vmem = pl.BlockSpec(memory_space=pltpu.VMEM)
-    shape = (2, height, width)
+    shape = (height, width)
     return pl.pallas_call(
         sum_kernel,
-        in_specs=[smem, smem, vmem, vmem],
-        out_specs=[vmem] * 4,
+        grid=(1,),
+        in_specs=[
+            smem,
+            smem,
+            pl.BlockSpec((classes, 1, height, PATCH), lambda i: (0, plane, 0, 0)),
+            pl.BlockSpec((classes, height, PATCH), lambda i: (0, 0, 0)),
+        ],
+        out_specs=[pl.BlockSpec(shape, lambda i: (0, 0))] * 4,
         out_shape=[
             jax.ShapeDtypeStruct(shape, kind)
             for kind in (jnp.float32, jnp.float32, jnp.bfloat16, jnp.bfloat16)
         ],
-        scratch_shapes=[pltpu.VMEM((bands, 2 * height, width), jnp.float32)],
+        scratch_shapes=[pltpu.VMEM((bands, height, width), jnp.float32)],
         compiler_params=pltpu.CompilerParams(vmem_limit_bytes=SUM_VMEM),
         cost_estimate=pl.CostEstimate(
-            flops=8 * first.size, bytes_accessed=4 * first.size + 12 * math.prod(shape), transcendentals=0
+            flops=8 * second.size, bytes_accessed=4 * second.size + 12 * math.prod(shape), transcendentals=0
         ),
     )(pos, me, first, second)
+
+
+def put_kernel(source, *refs):
+    refs[-1][0] = source[...]
+
+
+def put_plane(plane, source, buffer):
+    parts = 4
+    height, width = source.shape
+    operands = [source] if buffer is None else [source, buffer]
+    return pl.pallas_call(
+        put_kernel,
+        grid=(parts,),
+        in_specs=[pl.BlockSpec((height // parts, width), lambda i: (i, 0))]
+        + [pl.BlockSpec(memory_space=pl.ANY)] * (len(operands) - 1),
+        out_specs=pl.BlockSpec((1, height // parts, width), lambda i: (plane, i, 0)),
+        out_shape=jax.ShapeDtypeStruct((2, height, width), source.dtype),
+        input_output_aliases={} if buffer is None else {1: 0},
+        compiler_params=pltpu.CompilerParams(vmem_limit_bytes=SUM_VMEM),
+        cost_estimate=pl.CostEstimate(flops=0, bytes_accessed=4 * source.size, transcendentals=0),
+    )(*operands)
 
 
 def shards(object_image, probe, amplitudes, pos_tile, pos_offset):
@@ -500,39 +522,47 @@
 
     operands = (probe, amplitudes, dft_tables(PATCH))
     grad_0, term = wave(0, classes, pos, me, pos_pat, object_image, sibling, across[0], *operands, None)
-    grad_0, across[1] = lax.optimization_barrier((grad_0, across[1]))
     part_0 = lax.all_to_all(grad_0, "pat", split_axis=0, concat_axis=0, tiled=True)
-    grad_1, keep_term, give_term = wave(
+    real_grad, imag_grad, keep_term, give_term = wave(
         1, classes, pos, me, me, object_image, sibling, across[1], *operands, term
     )
-    grad_1, part_0 = lax.optimization_barrier((grad_1, part_0))
-    part_1 = lax.all_to_all(grad_1, "pat", split_axis=0, concat_axis=0, tiled=True)
+    real_grad, part_0 = lax.optimization_barrier((real_grad, part_0))
+    real_part = lax.all_to_all(real_grad, "pat", split_axis=0, concat_axis=0, tiled=True)
+    imag_grad, real_part = lax.optimization_barrier((imag_grad, real_part))
+    imag_part = lax.all_to_all(imag_grad, "pat", split_axis=0, concat_axis=0, tiled=True)
 
     core = my_owner % 2
     line = my_owner // 2
     term = keep_term + flip(give_term, 1).astype(jnp.float32)
     term = halved(term, line, lambda value: flip(value, 2))
-    term, then = lax.optimization_barrier((term, me))
-    own_far, own_near, away_far, away_near = sum_pieces(
-        pos_pat, then, part_0, part_1, owners, width
-    )
-    from_sibling_far = flip(away_far, 1)
-    from_sibling = flip(away_near, 1)
-    from_across = flip(
-        (own_far + from_sibling_far.astype(jnp.float32)).astype(jnp.bfloat16), 2
-    )
+
+    def return_plane(plane, part, then, wait):
+        own_far, own_near, away_far, away_near = sum_pieces(
+            plane, pos_pat, then, part_0, part, owners, width
+        )
+        from_sibling_far = flip(away_far, 1)
+        from_sibling = flip(away_near, 1)
+        send = (own_far + from_sibling_far.astype(jnp.float32)).astype(jnp.bfloat16)
+        send, wait = lax.optimization_barrier((send, wait))
+        from_across = flip(send, 2)
+        total = own_near + from_sibling.astype(jnp.float32) + from_across.astype(jnp.float32)
+        mine = lax.dynamic_slice_in_dim(object_image[plane], my_class * height, height, 0)
+        return (mine.astype(jnp.float32) - OBJECT_RATE * total).astype(jnp.bfloat16), wait
+
+    real_rows, then = return_plane(0, real_part, me, me)
+    term, then = lax.optimization_barrier((term, then))
+    imag_rows, then = return_plane(1, imag_part, then, then)
+    real_rows, term = lax.optimization_barrier((real_rows, term))
     for bit in bits:
         term = halved(term, my_class // bit % 2, pat_flip(bit))
-    total = own_near + from_sibling.astype(jnp.float32) + from_across.astype(jnp.float32)
-    mine = lax.dynamic_slice_in_dim(object_image, my_class * height, height, 1)
-    updated = (mine.astype(jnp.float32) - OBJECT_RATE * total).astype(jnp.bfloat16)
-    updated, term = lax.optimization_barrier((updated, term.astype(jnp.bfloat16)))
+    term = term.astype(jnp.bfloat16)
     steps = [
         functools.partial(doubled, bit=my_class // bit % 2, other=pat_flip(bit)) for bit in reversed(bits)
     ]
     steps.append(functools.partial(doubled, bit=line, other=lambda value: flip(value, 2)))
     steps.append(lambda part: doubled(part[None], core, lambda value: flip(value, 1)))
-    object_next = lax.all_gather(updated, "pat", axis=1, tiled=True)
+    object_next = put_plane(0, lax.all_gather(real_rows, "pat", axis=0, tiled=True), None)
+    object_next = put_plane(1, lax.all_gather(imag_rows, "pat", axis=0, tiled=True), object_next)
     for step in steps:
         term = step(term)
     probe_total = term.astype(jnp.float32)

time: 284 us -> 296 us (1.042)
  waiting for transfers between devices: 169 us -> 136 us
  blocking collectives: 5.99 us -> 33.9 us
  starting transfers between devices: 27.4 us -> 36.2 us
  Pallas kernels: 41 us -> 46.4 us
  local copies, waits for them, and re-layouts: 14.8 us -> 18.2 us
    all_gather x1 -> x2, waiting for transfers between devices: 70.4 us -> 33.2 us  [the longest x1 33.2 us: shards(): lax.all_gather(imag_rows, 'pat', axis=0, tiled=True)]
    all_to_all x0 -> x1, blocking collectives: none -> 28 us  [shards(): lax.all_to_all(imag_grad, 'pat', split_axis=0, concat_axis=0, tiled=True)]
    all_to_all x1, waiting for transfers between devices: 13 us -> 0.01 us  [shards(): lax.all_to_all(grad_0, 'pat', split_axis=0, concat_axis=0, tiled=True)]
    ppermute x12 -> x15, waiting for transfers between devices: 43.5 us -> 53.2 us  [flip(): return lax.ppermute(value, 'obj', [(k, k ^ bit) for k in range(owners)])]
    ppermute x9, waiting for transfers between devices: 30.7 us -> 37 us  [pat_flip(): lax.ppermute(value, 'pat', [(k, k ^ bit) for k in range(classes)])]
    slice x0 -> x1, local copies, waits for them, and re-layouts: none -> 5.94 us  [return_plane(): object_image[plane]]
    pallas_call x1 -> x4, Pallas kernels: 4.86 us -> 10.1 us  [the longest x2 5.85 us: sum_pieces(): pl.pallas_call(sum_kernel, grid=(1,), in_specs=[smem, smem, pl.BlockSpec(...]
    ppermute x9, starting transfers between devices: 8.6 us -> 13.4 us  [pat_flip(): lax.ppermute(value, 'pat', [(k, k ^ bit) for k in range(classes)])]
  transfers between devices with their start and end apart: 24 -> 28, of which waited for: 20 -> 20; matrix products, arithmetic and copies ran while one was open for 3% -> 5% of each run, Pallas kernels for 12% -> 10%
where the time goes in v7:
time: 296 us
  waiting for transfers between devices  136 us (46%)
  Pallas kernels  46.4 us (16%)
  starting transfers between devices  36.2 us (12%)
  blocking collectives  33.9 us (11%)
  local copies, waits for them, and re-layouts  18.2 us (6%)
  between operations  14.4 us (5%)
  other arithmetic  10.8 us (4%)
    ppermute x15, waiting for transfers between devices, flip(): return lax.ppermute(value, 'obj', [(k, k ^ bit) for k in range(owners)])  53.2 us
    ppermute x9, waiting for transfers between devices, pat_flip(): lax.ppermute(value, 'pat', [(k, k ^ bit) for k in range(classes)])  37 us
    all_gather x1, waiting for transfers between devices, shards(): lax.all_gather(imag_rows, 'pat', axis=0, tiled=True)  33.2 us
    all_to_all x1, blocking collectives, shards(): lax.all_to_all(imag_grad, 'pat', split_axis=0, concat_axis=0, tiled=True)  28 us
    pallas_call x2, Pallas kernels, wave(): pl.pallas_call(functools.partial(wave_kernel, which), in_specs=[smem, sme...  24.8 us
    ppermute x9, starting transfers between devices, pat_flip(): lax.ppermute(value, 'pat', [(k, k ^ bit) for k in range(classes)])  13.4 us
    all_to_all x1, waiting for transfers between devices, shards(): lax.all_to_all(real_grad, 'pat', split_axis=0, concat_axis=0, tiled=True)  12.4 us
    unnamed x26, local copies, waits for them, and re-layouts  11.9 us
  transfers between devices with their start and end apart: 28, of which 20 were waited for; matrix products, arithmetic and copies ran while one was open for 5% of the time, Pallas kernels for 10%

profile of v7, /device:TPU:0, one launch (start us, length us, event | category | flops | bytes accessed | tf_op | source)
XLA Modules:
  0.0 295.6 jit_solution(17925186847054425347)
XLA Ops:
  8.8 6.0 %all-gather = s32[4,2,4]{2,1,0:T(2,128)S(1)} all-gather(s32[1,2,4]{2,1,0:T(2,128)S(1)} %bitcast.20), channel_id=1, replica_groups=mesh['pat'=8,'obj'=4] {'obj'}, dimensions={0}, use_global_device_ids=true | all-gather | bytes 160 | tf_op jit(solution)/shard_map/all_gather | solution.py:510
  14.9 2.8 copy-done
  19.9 6.0 %shard_map.95 = (bf16[1,2,512,512]{3,2,1,0:T(8,128)(2,1)S(1)}, bf16[2,2,512,512]{3,2,1,0:T(8,128)(2,1)}) custom-call(s32[8,4]{1,0:T(8,128)S(1)} %bitcast.13, s32[2]{0:T(128)S(1)} %pad_add_fusion.3.me.spare, bf16[2,512,3072]{2,1,0:T(8,128)(2,1)S(1)} %copy-done, bf16[2,512,3072]{2,1,0:T(8,128)(2,1)S(1)} %copy-done, bf16[2,512,3072]{2,1,0:T(8,128)(2,1)S(1)} %copy-done, ...), custom_call_target="tpu_custom_call" | custom-call | flops 1966080 | bytes 7000000 | tf_op jit(solution)/shard_map/pallas_call | solution.py:194
  28.2 2.1 collective-permute-start.7
  31.6 2.8 copy-done.1
  43.6 2.5 collective-permute-start.3
  49.0 4.8 %collective-permute-done.7.across = bf16[2,512,512]{2,1,0:T(8,128)(2,1)} collective-permute-done((bf16[2,512,512]{2,1,0:T(8,128)(2,1)S(1)}, bf16[2,512,512]{2,1,0:T(8,128)(2,1)}, u32[]{:S(2)}, u32[]{:S(2)}) %collective-permute-start.7) | collective-permute-done | bytes 1048608 | tf_op jit(solution)/shard_map/ppermute | solution.py:494
  53.8 12.2 %shard_map.99 = (bf16[8,2,64,512]{3,2,1,0:T(8,128)(2,1)}, f32[2,512,512]{2,1,0:T(8,128)}) custom-call(s32[8,4]{1,0:T(8,128)} %bitcast.16, s32[2]{0:T(128)} %copy-done.6, s32[16,4]{1,0:T(8,128)} %broadcast_select_fusion.spare.pos, bf16[2,512,3072]{2,1,0:T(8,128)(2,1)} %band.3, bf16[2,2,512,512]{3,2,1,0:T(8,128)(2,1)} %collective-permute-done.4.sibling, ...), custom_call_target="tpu_custom_call" | custom-call | flops 4294967296 | bytes 300000000 | tf_op jit(solution)/shard_map/pallas_call | solution.py:378
  65.9 6.2 %all-to-all-start = ((bf16[8,2,64,512]{3,2,1,0:T(8,128)(2,1)}), bf16[8,2,64,512]{3,2,1,0:T(8,128)(2,1)S(1)}, u32[]{:S(2)}, u32[]{:S(2)}) async-start(bf16[8,2,64,512]{3,2,1,0:T(8,128)(2,1)} %get-tuple-element.45), calls=%async_computation | async-start | bytes 2097152 | tf_op jit(solution)/shard_map/all_to_all | solution.py:525
  73.7 22.6 %collective-permute-done.5.across = bf16[2,512,512]{2,1,0:T(8,128)(2,1)S(1)} collective-permute-done((bf16[2,512,512]{2,1,0:T(8,128)(2,1)S(1)}, bf16[2,512,512]{2,1,0:T(8,128)(2,1)S(1)}, u32[]{:S(2)}, u32[]{:S(2)}) %collective-permute-start.5) | collective-permute-done | bytes 1048608 | tf_op jit(solution)/shard_map/ppermute | solution.py:494
  97.3 12.7 %shard_map.100 = (bf16[8,64,512]{2,1,0:T(8,128)(2,1)}, bf16[8,64,512]{2,1,0:T(8,128)(2,1)}, f32[512,512]{1,0:T(8,128)}, bf16[512,512]{1,0:T(8,128)(2,1)}) custom-call(s32[8,4]{1,0:T(8,128)} %bitcast.17, s32[2]{0:T(128)} %copy-done.6, s32[2]{0:T(128)} %copy-done.6, bf16[2,512,3072]{2,1,0:T(8,128)(2,1)} %band.3, ...), custom_call_target="tpu_custom_call" | custom-call | flops 4294967296 | bytes 300000000 | tf_op jit(solution)/shard_map/pallas_call | solution.py:378
  110.0 5.7 %all-to-all-start.1 = ((bf16[8,64,512]{2,1,0:T(8,128)(2,1)}), bf16[8,64,512]{2,1,0:T(8,128)(2,1)S(1)}, u32[]{:S(2)}, u32[]{:S(2)}) async-start(bf16[8,64,512]{2,1,0:T(8,128)(2,1)} %get-tuple-element.48), calls=%async_computation.1 | async-start | bytes 1048576 | tf_op jit(solution)/shard_map/all_to_all | solution.py:530
  115.9 12.4 %all-to-all-done.1.second = bf16[8,64,512]{2,1,0:T(8,128)(2,1)S(1)} async-done(((bf16[8,64,512]{2,1,0:T(8,128)(2,1)}), bf16[8,64,512]{2,1,0:T(8,128)(2,1)S(1)}, u32[]{:S(2)}, u32[]{:S(2)}) %all-to-all-start.1) | async-done | bytes 524320 | tf_op jit(solution)/shard_map/all_to_all | solution.py:530
  128.3 2.9 shard_map.101
  135.9 5.9 %fusion.2 = (bf16[1,512,3072]{2,1,0:T(8,128)(2,1)}, bf16[1,512,3072]{2,1,0:T(8,128)(2,1)}) fusion(bf16[2,512,3072]{2,1,0:T(8,128)(2,1)} %band.3), kind=kLoop, calls=%fused_computation.28 | loop fusion | bytes 12582912 | tf_op jit(solution)/shard_map/slice | solution.py:549
  143.3 6.8 %collective-permute-done.15 = bf16[64,3072]{1,0:T(8,128)(2,1)} collective-permute-done((bf16[64,3072]{1,0:T(8,128)(2,1)}, bf16[64,3072]{1,0:T(8,128)(2,1)}, u32[]{:S(2)}, u32[]{:S(2)}) %collective-permute-start.15) | collective-permute-done | bytes 393248 | tf_op jit(solution)/shard_map/ppermute | solution.py:494
  150.0 2.2 fusion
  152.3 28.0 %all_to_all.15.second = bf16[8,64,512]{2,1,0:T(8,128)(2,1)S(1)} all-to-all(bf16[8,64,512]{2,1,0:T(8,128)(2,1)S(1)} %copy-done.11), channel_id=1, replica_groups=mesh['pat'=8,'obj'=4] {'pat'}, dimensions={0} | all-to-all | bytes 1048576 | tf_op jit(solution)/shard_map/all_to_all | solution.py:532
  180.3 2.9 shard_map.102
  186.6 9.7 %collective-permute-done.13 = bf16[64,3072]{1,0:T(8,128)(2,1)S(1)} collective-permute-done((bf16[64,3072]{1,0:T(8,128)(2,1)S(1)}, bf16[64,3072]{1,0:T(8,128)(2,1)S(1)}, u32[]{:S(2)}, u32[]{:S(2)}) %collective-permute-start.13) | collective-permute-done | bytes 393248 | tf_op jit(solution)/shard_map/ppermute | solution.py:494
  196.3 2.1 fusion.1
  200.3 6.9 %collective-permute-done.16 = bf16[128,512]{1,0:T(8,128)(2,1)S(1)} collective-permute-done((bf16[128,512]{1,0:T(8,128)(2,1)S(1)}, bf16[128,512]{1,0:T(8,128)(2,1)S(1)}, u32[]{:S(2)}, u32[]{:S(2)}) %collective-permute-start.16) | collective-permute-done | bytes 131104 | tf_op jit(solution)/shard_map/ppermute | solution.py:497
  207.5 4.2 %collective-permute-done.17 = bf16[64,512]{1,0:T(8,128)(2,1)S(1)} collective-permute-done((bf16[64,512]{1,0:T(8,128)(2,1)S(1)}, bf16[64,512]{1,0:T(8,128)(2,1)S(1)}, u32[]{:S(2)}, u32[]{:S(2)}) %collective-permute-start.17) | collective-permute-done | bytes 65568 | tf_op jit(solution)/shard_map/ppermute | solution.py:497
  211.9 6.7 %collective-permute-done.18 = bf16[32,512]{1,0:T(8,128)(2,1)S(1)} collective-permute-done((bf16[32,512]{1,0:T(8,128)(2,1)S(1)}, bf16[32,512]{1,0:T(8,128)(2,1)S(1)}, u32[]{:S(2)}, u32[]{:S(2)}) %collective-permute-start.18) | collective-permute-done | bytes 32800 | tf_op jit(solution)/shard_map/ppermute | solution.py:497
  218.6 5.0 %collective-permute-done.19 = bf16[32,512]{1,0:T(8,128)(2,1)S(1)} collective-permute-done((bf16[32,512]{1,0:T(8,128)(2,1)S(1)}, bf16[32,512]{1,0:T(8,128)(2,1)S(1)}, u32[]{:S(2)}, u32[]{:S(2)}) %collective-permute-start.19) | collective-permute-done | bytes 32800 | tf_op jit(solution)/shard_map/ppermute | solution.py:497
  223.7 4.3 %collective-permute-done.20 = bf16[64,512]{1,0:T(8,128)(2,1)S(1)} collective-permute-done((bf16[64,512]{1,0:T(8,128)(2,1)S(1)}, bf16[64,512]{1,0:T(8,128)(2,1)S(1)}, u32[]{:S(2)}, u32[]{:S(2)}) %collective-permute-start.20) | collective-permute-done | bytes 65568 | tf_op jit(solution)/shard_map/ppermute | solution.py:497
  228.0 4.3 %collective-permute-start.21 = (bf16[128,512]{1,0:T(8,128)(2,1)S(1)}, bf16[128,512]{1,0:T(8,128)(2,1)S(1)}, u32[]{:S(2)}, u32[]{:S(2)}) collective-permute-start(bf16[128,512]{1,0:T(8,128)(2,1)S(1)} %maximum_select_fusion.3), channel_id=1, source_target_pairs={{0,4},{4,0},{8,12},{12,8},{16,20},{20,16},{24,28},{28,24},{1,5},{5... | collective-permute-start | bytes 393224 | tf_op jit(solution)/shard_map/ppermute | solution.py:497
  232.3 4.9 %collective-permute-done.21 = bf16[128,512]{1,0:T(8,128)(2,1)S(1)} collective-permute-done((bf16[128,512]{1,0:T(8,128)(2,1)S(1)}, bf16[128,512]{1,0:T(8,128)(2,1)S(1)}, u32[]{:S(2)}, u32[]{:S(2)}) %collective-permute-start.21) | collective-permute-done | bytes 131104 | tf_op jit(solution)/shard_map/ppermute | solution.py:497
  239.0 4.7 %collective-permute-done.22 = bf16[256,512]{1,0:T(8,128)(2,1)S(1)} collective-permute-done((bf16[256,512]{1,0:T(8,128)(2,1)S(1)}, bf16[256,512]{1,0:T(8,128)(2,1)S(1)}, u32[]{:S(2)}, u32[]{:S(2)}) %collective-permute-start.22) | collective-permute-done | bytes 262176 | tf_op jit(solution)/shard_map/ppermute | solution.py:494
  249.4 2.1 shard_map.103.refs_0_
  251.6 33.2 %all-gather.4.cloned.1.call-done.source = bf16[512,3072]{1,0:T(8,128)(2,1)} async-done(((bf16[64,3072]{1,0:T(8,128)(2,1)}), bf16[512,3072]{1,0:T(8,128)(2,1)}) %all-gather.4.cloned.1.call-update) | async-done | bytes 3145744 | tf_op jit(solution)/shard_map/all_gather | solution.py:565
  286.6 2.1 shard_map.104
  (92 shorter events, 43.5 us)
Async XLA Ops:
  14.8 16.8 %copy-start.4 = (s32[4,2,4]{2,1,0:T(2,128)}, s32[4,2,4]{2,1,0:T(2,128)S(1)}, u32[]{:S(2)}) copy-start(s32[4,2,4]{2,1,0:T(2,128)S(1)} %all-gather) | copy-start | bytes 388
  19.5 7.0 %collective-permute-start.6 = (bf16[1,2,512,512]{3,2,1,0:T(8,128)(2,1)S(1)}, bf16[1,2,512,512]{3,2,1,0:T(8,128)(2,1)S(1)}, u32[]{:S(2)}, u32[]{:S(2)}) collective-permute-start(bf16[1,2,512,512]{3,2,1,0:T(8,128)(2,1)S(1)} %shard_map.97), channel_id=1, source_target_pairs={{0,1},{1,0},{2,3},{3,2},{4,5},{5,4},{6,7},{7,6},{8,9},{9,8},{10,11... | collective-permute-start | bytes 3145736 | tf_op jit(solution)/shard_map/ppermute | solution.py:494
  25.9 23.1 %collective-permute-start.4 = (bf16[2,2,512,512]{3,2,1,0:T(8,128)(2,1)}, bf16[2,2,512,512]{3,2,1,0:T(8,128)(2,1)}, u32[]{:S(2)}, u32[]{:S(2)}) collective-permute-start(bf16[2,2,512,512]{3,2,1,0:T(8,128)(2,1)} %get-tuple-element.39), channel_id=1, source_target_pairs={{0,1},{1,0},{2,3},{3,2},{4,5},{5,4},{6,7},{7,6},{8,9},{9,8},{10,11... | collective-permute-start | bytes 6291464 | tf_op jit(solution)/shard_map/ppermute | solution.py:494
  26.1 5.5 %collective-permute-start = (bf16[1,2,512,512]{3,2,1,0:T(8,128)(2,1)S(1)}, bf16[1,2,512,512]{3,2,1,0:T(8,128)(2,1)S(1)}, u32[]{:S(2)}, u32[]{:S(2)}) collective-permute-start(bf16[1,2,512,512]{3,2,1,0:T(8,128)(2,1)S(1)} %get-tuple-element.37), channel_id=1, source_target_pairs={{0,1},{1,0},{2,3},{3,2},{4,5},{5,4},{6,7},{7,6},{8,9},{9,8},{10,11... | collective-permute-start | bytes 3145736 | tf_op jit(solution)/shard_map/ppermute | solution.py:494
  28.2 25.5 %collective-permute-start.7 = (bf16[2,512,512]{2,1,0:T(8,128)(2,1)S(1)}, bf16[2,512,512]{2,1,0:T(8,128)(2,1)}, u32[]{:S(2)}, u32[]{:S(2)}) collective-permute-start(bf16[2,512,512]{2,1,0:T(8,128)(2,1)S(1)} %shard_map.98), channel_id=1, source_target_pairs={{0,2},{1,3},{2,0},{3,1},{4,6},{5,7},{6,4},{7,5},{8,10},{9,11},{10,... | collective-permute-start | bytes 3145736 | tf_op jit(solution)/shard_map/ppermute | solution.py:494
  36.2 3.7 %collective-permute-start.1 = (s32[2,4]{0,1:T(4,128)S(1)}, s32[2,4]{0,1:T(4,128)S(1)}, u32[]{:S(2)}, u32[]{:S(2)}) collective-permute-start(s32[2,4]{0,1:T(4,128)S(1)} %pad_add_fusion), channel_id=1, source_target_pairs={{0,4},{4,0},{8,12},{12,8},{16,20},{20,16},{24,28},{28,24},{1,5},{5... | collective-permute-start | bytes 104 | tf_op jit(solution)/shard_map/ppermute | solution.py:497
  39.9 3.7 %collective-permute-start.2 = (s32[4,4]{0,1:T(4,128)S(1)}, s32[4,4]{0,1:T(4,128)S(1)}, u32[]{:S(2)}, u32[]{:S(2)}) collective-permute-start(s32[4,4]{0,1:T(4,128)S(1)} %add_select_fusion), channel_id=1, source_target_pairs={{0,8},{4,12},{8,0},{12,4},{16,24},{20,28},{24,16},{28,20},{1,9},{5... | collective-permute-start | bytes 200 | tf_op jit(solution)/shard_map/ppermute | solution.py:497
  43.6 4.5 %collective-permute-start.3 = (s32[8,4]{0,1:T(4,128)S(1)}, s32[8,4]{0,1:T(4,128)S(1)}, u32[]{:S(2)}, u32[]{:S(2)}) collective-permute-start(s32[8,4]{0,1:T(4,128)S(1)} %add_select_fusion.1), channel_id=1, source_target_pairs={{0,16},{4,20},{8,24},{12,28},{16,0},{20,4},{24,8},{28,12},{1,17},{... | collective-permute-start | bytes 392 | tf_op jit(solution)/shard_map/ppermute | solution.py:497
  65.9 44.0 %all-to-all-start = ((bf16[8,2,64,512]{3,2,1,0:T(8,128)(2,1)}), bf16[8,2,64,512]{3,2,1,0:T(8,128)(2,1)S(1)}, u32[]{:S(2)}, u32[]{:S(2)}) async-start(bf16[8,2,64,512]{3,2,1,0:T(8,128)(2,1)} %get-tuple-element.45), calls=%async_computation | async-start | bytes 2097152 | tf_op jit(solution)/shard_map/all_to_all | solution.py:525
  72.2 24.1 %collective-permute-start.5 = (bf16[2,512,512]{2,1,0:T(8,128)(2,1)S(1)}, bf16[2,512,512]{2,1,0:T(8,128)(2,1)S(1)}, u32[]{:S(2)}, u32[]{:S(2)}) collective-permute-start(bf16[2,512,512]{2,1,0:T(8,128)(2,1)S(1)} %shard_map.96), channel_id=1, source_target_pairs={{0,2},{1,3},{2,0},{3,1},{4,6},{5,7},{6,4},{7,5},{8,10},{9,11},{10,... | collective-permute-start | bytes 3145736 | tf_op jit(solution)/shard_map/ppermute | solution.py:494
  97.3 31.0 %copy-start.5 = (s32[16,4]{1,0:T(8,128)S(1)}, s32[16,4]{1,0:T(8,128)}, u32[]{:S(2)}) copy-start(s32[16,4]{1,0:T(8,128)} %broadcast_select_fusion.spare.pos) | copy-start | bytes 772
  97.3 31.0 %copy-start.7 = (s32[2]{0:T(128)S(1)}, s32[2]{0:T(128)}, u32[]{:S(2)}) copy-start(s32[2]{0:T(128)} %copy-done.6) | copy-start | bytes 28
  110.0 18.3 %all-to-all-start.1 = ((bf16[8,64,512]{2,1,0:T(8,128)(2,1)}), bf16[8,64,512]{2,1,0:T(8,128)(2,1)S(1)}, u32[]{:S(2)}, u32[]{:S(2)}) async-start(bf16[8,64,512]{2,1,0:T(8,128)(2,1)} %get-tuple-element.48), calls=%async_computation.1 | async-start | bytes 1048576 | tf_op jit(solution)/shard_map/all_to_all | solution.py:530
  115.7 131.8 %all-gather.6.cloned.1.call-start = ((), (), s32[]{:S(2)}) async-start(), calls=%async_computation.4 | async-start | bytes 3538944 | tf_op jit(solution)/shard_map/all_gather | solution.py:564
  115.8 15.5 %collective-permute-start.8 = (bf16[512,512]{1,0:T(8,128)(2,1)}, bf16[512,512]{1,0:T(8,128)(2,1)S(1)}, u32[]{:S(2)}, u32[]{:S(2)}) collective-permute-start(bf16[512,512]{1,0:T(8,128)(2,1)} %get-tuple-element.43), channel_id=1, source_target_pairs={{0,1},{1,0},{2,3},{3,2},{4,5},{5,4},{6,7},{7,6},{8,9},{9,8},{10,11... | collective-permute-start | bytes 1572872 | tf_op jit(solution)/shard_map/ppermute | solution.py:494
  131.2 3.3 %collective-permute-start.10 = (bf16[64,3072]{1,0:T(8,128)(2,1)S(1)}, bf16[64,3072]{1,0:T(8,128)(2,1)S(1)}, u32[]{:S(2)}, u32[]{:S(2)}) collective-permute-start(bf16[64,3072]{1,0:T(8,128)(2,1)S(1)} %get-tuple-element.51), channel_id=1, source_target_pairs={{0,1},{1,0},{2,3},{3,2},{4,5},{5,4},{6,7},{7,6},{8,9},{9,8},{10,11... | collective-permute-start | bytes 1179656 | tf_op jit(solution)/shard_map/ppermute | solution.py:494
  132.7 9.3 %collective-permute-start.9 = (bf16[256,512]{1,0:T(8,128)(2,1)S(1)}, bf16[256,512]{1,0:T(8,128)(2,1)}, u32[]{:S(2)}, u32[]{:S(2)}) collective-permute-start(bf16[256,512]{1,0:T(8,128)(2,1)S(1)} %dynamic-slice_convert_fusion), channel_id=1, source_target_pairs={{0,2},{1,3},{2,0},{3,1},{4,6},{5,7},{6,4},{7,5},{8,10},{9,11},{10,... | collective-permute-start | bytes 786440 | tf_op jit(solution)/shard_map/ppermute | solution.py:494
  134.3 8.9 %collective-permute-start.14 = (bf16[64,3072]{1,0:T(8,128)(2,1)S(1)}, bf16[64,3072]{1,0:T(8,128)(2,1)}, u32[]{:S(2)}, u32[]{:S(2)}) collective-permute-start(bf16[64,3072]{1,0:T(8,128)(2,1)S(1)} %get-tuple-element.61), channel_id=1, source_target_pairs={{0,1},{1,0},{2,3},{3,2},{4,5},{5,4},{6,7},{7,6},{8,9},{9,8},{10,11... | collective-permute-start | bytes 1179656 | tf_op jit(solution)/shard_map/ppermute | solution.py:494
  135.4 14.6 %collective-permute-start.15 = (bf16[64,3072]{1,0:T(8,128)(2,1)}, bf16[64,3072]{1,0:T(8,128)(2,1)}, u32[]{:S(2)}, u32[]{:S(2)}) collective-permute-start(bf16[64,3072]{1,0:T(8,128)(2,1)} %add_convert_fusion.1), channel_id=1, source_target_pairs={{0,2},{1,3},{2,0},{3,1},{4,6},{5,7},{6,4},{7,5},{8,10},{9,11},{10,... | collective-permute-start | bytes 1179656 | tf_op jit(solution)/shard_map/ppermute | solution.py:494
  152.3 132.5 %all-gather.4.cloned.1.call-start = ((), (), s32[]{:S(2)}) async-start(), calls=%async_computation.3 | async-start | bytes 3538944 | tf_op jit(solution)/shard_map/all_gather | solution.py:565
  183.2 1.8 collective-permute-start.12
  183.3 3.3 %collective-permute-start.11 = (bf16[64,3072]{1,0:T(8,128)(2,1)S(1)}, bf16[64,3072]{1,0:T(8,128)(2,1)S(1)}, u32[]{:S(2)}, u32[]{:S(2)}) collective-permute-start(bf16[64,3072]{1,0:T(8,128)(2,1)S(1)} %get-tuple-element.56), channel_id=1, source_target_pairs={{0,1},{1,0},{2,3},{3,2},{4,5},{5,4},{6,7},{7,6},{8,9},{9,8},{10,11... | collective-permute-start | bytes 1179656 | tf_op jit(solution)/shard_map/ppermute | solution.py:494
  185.1 11.2 %collective-permute-start.13 = (bf16[64,3072]{1,0:T(8,128)(2,1)S(1)}, bf16[64,3072]{1,0:T(8,128)(2,1)S(1)}, u32[]{:S(2)}, u32[]{:S(2)}) collective-permute-start(bf16[64,3072]{1,0:T(8,128)(2,1)S(1)} %add_convert_fusion), channel_id=1, source_target_pairs={{0,2},{1,3},{2,0},{3,1},{4,6},{5,7},{6,4},{7,5},{8,10},{9,11},{10,... | collective-permute-start | bytes 1179656 | tf_op jit(solution)/shard_map/ppermute | solution.py:494
  196.3 49.6 %copy-start.8 = (f32[2,512,512]{2,1,0:T(8,128)S(1)}, f32[2,512,512]{2,1,0:T(8,128)}, u32[]{:S(2)}) copy-start(f32[2,512,512]{2,1,0:T(8,128)} %probe.3) | copy-start | bytes 6291460
  198.5 8.7 %collective-permute-start.16 = (bf16[128,512]{1,0:T(8,128)(2,1)S(1)}, bf16[128,512]{1,0:T(8,128)(2,1)S(1)}, u32[]{:S(2)}, u32[]{:S(2)}) collective-permute-start(bf16[128,512]{1,0:T(8,128)(2,1)S(1)} %dynamic-slice_convert_fusion.1), channel_id=1, source_target_pairs={{0,4},{4,0},{8,12},{12,8},{16,20},{20,16},{24,28},{28,24},{1,5},{5... | collective-permute-start | bytes 393224 | tf_op jit(solution)/shard_map/ppermute | solution.py:497
  207.2 4.5 %collective-permute-start.17 = (bf16[64,512]{1,0:T(8,128)(2,1)S(1)}, bf16[64,512]{1,0:T(8,128)(2,1)S(1)}, u32[]{:S(2)}, u32[]{:S(2)}) collective-permute-start(bf16[64,512]{1,0:T(8,128)(2,1)S(1)} %dynamic-slice_convert_fusion.2), channel_id=1, source_target_pairs={{0,8},{4,12},{8,0},{12,4},{16,24},{20,28},{24,16},{28,20},{1,9},{5... | collective-permute-start | bytes 196616 | tf_op jit(solution)/shard_map/ppermute | solution.py:497
  211.8 6.8 %collective-permute-start.18 = (bf16[32,512]{1,0:T(8,128)(2,1)S(1)}, bf16[32,512]{1,0:T(8,128)(2,1)S(1)}, u32[]{:S(2)}, u32[]{:S(2)}) collective-permute-start(bf16[32,512]{1,0:T(8,128)(2,1)S(1)} %dynamic-slice_convert_fusion.3), channel_id=1, source_target_pairs={{0,16},{4,20},{8,24},{12,28},{16,0},{20,4},{24,8},{28,12},{1,17},{... | collective-permute-start | bytes 98312 | tf_op jit(solution)/shard_map/ppermute | solution.py:497
  218.6 5.1 %collective-permute-start.19 = (bf16[32,512]{1,0:T(8,128)(2,1)S(1)}, bf16[32,512]{1,0:T(8,128)(2,1)S(1)}, u32[]{:S(2)}, u32[]{:S(2)}) collective-permute-start(bf16[32,512]{1,0:T(8,128)(2,1)S(1)} %add_convert_fusion.2), channel_id=1, source_target_pairs={{0,16},{4,20},{8,24},{12,28},{16,0},{20,4},{24,8},{28,12},{1,17},{... | collective-permute-start | bytes 98312 | tf_op jit(solution)/shard_map/ppermute | solution.py:497
  223.6 4.3 %collective-permute-start.20 = (bf16[64,512]{1,0:T(8,128)(2,1)S(1)}, bf16[64,512]{1,0:T(8,128)(2,1)S(1)}, u32[]{:S(2)}, u32[]{:S(2)}) collective-permute-start(bf16[64,512]{1,0:T(8,128)(2,1)S(1)} %maximum_select_fusion.4), channel_id=1, source_target_pairs={{0,8},{4,12},{8,0},{12,4},{16,24},{20,28},{24,16},{28,20},{1,9},{5... | collective-permute-start | bytes 196616 | tf_op jit(solution)/shard_map/ppermute | solution.py:497
  228.0 9.2 %collective-permute-start.21 = (bf16[128,512]{1,0:T(8,128)(2,1)S(1)}, bf16[128,512]{1,0:T(8,128)(2,1)S(1)}, u32[]{:S(2)}, u32[]{:S(2)}) collective-permute-start(bf16[128,512]{1,0:T(8,128)(2,1)S(1)} %maximum_select_fusion.3), channel_id=1, source_target_pairs={{0,4},{4,0},{8,12},{12,8},{16,20},{20,16},{24,28},{28,24},{1,5},{5... | collective-permute-start | bytes 393224 | tf_op jit(solution)/shard_map/ppermute | solution.py:497
  237.3 6.4 %collective-permute-start.22 = (bf16[256,512]{1,0:T(8,128)(2,1)S(1)}, bf16[256,512]{1,0:T(8,128)(2,1)S(1)}, u32[]{:S(2)}, u32[]{:S(2)}) collective-permute-start(bf16[256,512]{1,0:T(8,128)(2,1)S(1)} %maximum_select_fusion.2), channel_id=1, source_target_pairs={{0,2},{1,3},{2,0},{3,1},{4,6},{5,7},{6,4},{7,5},{8,10},{9,11},{10,... | collective-permute-start | bytes 786440 | tf_op jit(solution)/shard_map/ppermute | solution.py:494
  243.9 2.0 collective-permute-start.23
  (8 other events, 40.2 us)
Sparse Core Ops, SparseCore 0:
  152.4 71.5 all-gather.5
  226.1 58.5 all-gather.3

commit v8 on v7

--- a/solution.py
+++ b/solution.py
@@ -120,7 +120,7 @@
 
 
 def merge_kernel(which, pos, me, *refs):
-    blocks, sibling, out = refs[:-2], refs[-2], refs[-1]
+    blocks, sibling, outs = refs[:-3], refs[-3], refs[-2:]
     index = 2 * lax.bitwise_xor(me[0], 2) + which
     amount = lax.rem(first_col(pos, index), LANES)
     row_at = first_row(pos, index)
@@ -131,7 +131,7 @@
         for plane in range(2):
             own = cut_rows(blocks, plane, rows, amount)
             other = sibling[0, plane, rows, :].astype(jnp.float32)
-            out[plane, rows, :] = jnp.where(mine, own, other).astype(jnp.bfloat16)
+            outs[plane][rows, :] = jnp.where(mine, own, other).astype(jnp.bfloat16)
         return carry
 
     lax.fori_loop(0, PATCH // CHUNK, body, 0)
@@ -151,9 +151,9 @@
             grid=(1,),
             in_specs=[block(k) for k in range(WIDE // LANES)]
             + [pl.BlockSpec((1, 2, PATCH, PATCH), lambda i, pos, me: (0, 0, 0, 0))],
-            out_specs=pl.BlockSpec((2, PATCH, PATCH), lambda i, pos, me: (0, 0, 0)),
-        ),
-        out_shape=jax.ShapeDtypeStruct((2, PATCH, PATCH), jnp.bfloat16),
+            out_specs=[pl.BlockSpec((PATCH, PATCH), lambda i, pos, me: (0, 0))] * 2,
+        ),
+        out_shape=[jax.ShapeDtypeStruct((PATCH, PATCH), jnp.bfloat16)] * 2,
         compiler_params=pltpu.CompilerParams(vmem_limit_bytes=CUT_VMEM),
         cost_estimate=pl.CostEstimate(
             flops=2 * PATCH * WIDE, bytes_accessed=3300000, transcendentals=0
@@ -213,15 +213,13 @@
     )(pos, me, *([band] * (WIDE // LANES)))
 
 
-def wave_kernel(which, pos, me, spare, band, sibling, across, probe, amplitudes, *refs):
+def wave_kernel(which, pos, me, spare, band, sibling, across_real, across_imag, probe, amplitudes, *refs):
     tables, refs = refs[:3], refs[3:]
     last = which == 1
     if last:
-        term_in, real_grad, imag_grad, keep_term, give_term, *scratch = refs
-        grads = [real_grad, imag_grad]
+        term_in, both, keep_term, give_term, *scratch = refs
     else:
         both, term_out, *scratch = refs
-        grads = [both.at[:, plane] for plane in range(2)]
     window, sib_v, far_v, probe_v, amp_v, matrix, term_v, patch_v, twice, field, half, sems = scratch
     index = 2 * me[0] + which
     col_at = first_col(pos, index)
@@ -230,7 +228,8 @@
     pairs = [
         (band.at[:, :, pl.ds(start, WIDE)], window),
         (sibling.at[which], sib_v),
-        (across, far_v),
+        (across_real, far_v.at[0]),
+        (across_imag, far_v.at[1]),
         (probe, probe_v),
     ]
     cosine, sine, minus = tables
@@ -243,7 +242,7 @@
     copies = [pltpu.make_async_copy(a, b, sems.at[k]) for k, (a, b) in enumerate(pairs)]
     for copy in copies:
         copy.start()
-    for copy in copies[:3]:
+    for copy in copies[:4]:
         copy.wait()
     amount = lax.rem(col_at, LANES)
     down = lax.rem(row_at, PATCH)
@@ -265,7 +264,7 @@
         return carry
 
     lax.fori_loop(0, PATCH // CHUNK, assemble, 0)
-    copies[3].wait()
+    copies[4].wait()
 
     def illuminate(i, carry):
         at = pl.multiple_of(i * CHUNK, CHUNK)
@@ -283,7 +282,7 @@
         return carry
 
     lax.fori_loop(0, PATCH // CHUNK, illuminate, 0)
-    for copy in copies[4:8]:
+    for copy in copies[5:9]:
         copy.wait()
 
     def over_rows():
@@ -295,7 +294,7 @@
             half[256 * (k % 2) : 256 * (k % 2 + 1), at : at + PATCH] = part
 
     over_rows()
-    copies[8].wait()
+    copies[9].wait()
     for k in range(2):
         rows = slice(256 * k, 256 * (k + 1))
         far = jnp.dot(half[rows, :], matrix[...], preferred_element_type=jnp.float32)
@@ -309,7 +308,7 @@
         field[PATCH + 256 * k : PATCH + 256 * (k + 1), :] = (far_real * keep).astype(jnp.bfloat16)
     over_rows()
     if last:
-        copies[9].wait()
+        copies[10].wait()
         core = lax.rem(me[0], 2)
     for k in range(2):
         rows = slice(256 * k, 256 * (k + 1))
@@ -348,11 +347,11 @@
         return carry
 
     lax.fori_loop(0, PATCH // CHUNK, weigh, 0)
-    classes, height = grads[0].shape[0], grads[0].shape[1]
+    classes, height = both.shape[0], both.shape[2]
 
     def spread(k, carry):
         for plane in range(2):
-            grads[plane][k] = rows_from(twice, plane, PATCH - down + k * height, height).astype(
+            both[k, plane] = rows_from(twice, plane, PATCH - down + k * height, height).astype(
                 jnp.bfloat16
             )
         return carry
@@ -361,19 +360,18 @@
 
 
 def wave(which, classes, pos, me, spare, band, sibling, across, probe, amplitudes, tables, term):
-    operands = [band, sibling, across, probe, amplitudes, *tables]
+    operands = [band, sibling, *across, probe, amplitudes, *tables]
     smem = pl.BlockSpec(memory_space=pltpu.SMEM)
     hbm = pl.BlockSpec(memory_space=pl.ANY)
     vmem = pl.BlockSpec(memory_space=pltpu.VMEM)
     planes = (2, PATCH, PATCH)
     plane = (PATCH, PATCH)
     height = PATCH // classes
+    grads = [jax.ShapeDtypeStruct((classes, 2, height, PATCH), jnp.bfloat16)]
     if term is None:
-        grads = [jax.ShapeDtypeStruct((classes, 2, height, PATCH), jnp.bfloat16)]
         terms = [jax.ShapeDtypeStruct(planes, jnp.float32)]
     else:
         operands.append(term)
-        grads = [jax.ShapeDtypeStruct((classes, height, PATCH), jnp.bfloat16)] * 2
         terms = [jax.ShapeDtypeStruct(plane, t) for t in (jnp.float32, jnp.bfloat16)]
     return pl.pallas_call(
         functools.partial(wave_kernel, which),
@@ -392,7 +390,7 @@
             pltpu.VMEM((2, 2 * PATCH + SUBLANES, PATCH), jnp.float32),
             pltpu.VMEM((2 * PATCH, PATCH), jnp.bfloat16),
             pltpu.VMEM((PATCH, 2 * PATCH), jnp.bfloat16),
-            pltpu.SemaphoreType.DMA((10,)),
+            pltpu.SemaphoreType.DMA((11,)),
         ],
         compiler_params=pltpu.CompilerParams(vmem_limit_bytes=WAVE_VMEM),
         cost_estimate=pl.CostEstimate(
@@ -402,7 +400,7 @@
 
 
 def sum_kernel(pos, me, first, second, own_far, own_near, away_far, away_near, canvas):
-    classes, height = second.shape[0], second.shape[1]
+    classes, height = second.shape[0], second.shape[2]
     start = me[1] * height
     canvas[...] = jnp.zeros_like(canvas)
     rows = start + lax.broadcasted_iota(jnp.int32, (height, WIDE), 0)
@@ -424,7 +422,7 @@
 
     def body(k, carry):
         piece(first[k, 0], 2 * k)
-        piece(second[k], 2 * k + 1)
+        piece(second[k, 0], 2 * k + 1)
         return carry
 
     lax.fori_loop(0, classes, body, 0)
@@ -434,7 +432,7 @@
 
 
 def sum_pieces(plane, pos, me, first, second, bands, width):
-    classes, height = second.shape[0], second.shape[1]
+    classes, height = second.shape[0], second.shape[2]
     smem = pl.BlockSpec(memory_space=pltpu.SMEM)
     shape = (height, width)
     return pl.pallas_call(
@@ -444,7 +442,7 @@
             smem,
             smem,
             pl.BlockSpec((classes, 1, height, PATCH), lambda i: (0, plane, 0, 0)),
-            pl.BlockSpec((classes, height, PATCH), lambda i: (0, 0, 0)),
+            pl.BlockSpec((classes, 1, height, PATCH), lambda i: (0, plane, 0, 0)),
         ],
         out_specs=[pl.BlockSpec(shape, lambda i: (0, 0))] * 4,
         out_shape=[
@@ -516,29 +514,28 @@
     sibling = flip(pieces, 1)
     merged = [cut_and_merge(object_image, relay[k], pos, then, k) for k in range(2)]
     merged[1], pos_pat = lax.optimization_barrier((merged[1], own_pos))
-    across = [flip(m, 2) for m in merged]
+    across = [[flip(plane, 2) for plane in planes] for planes in merged]
     for bit in bits:
         pos_pat = doubled(pos_pat, my_class // bit % 2, pat_flip(bit))
 
     operands = (probe, amplitudes, dft_tables(PATCH))
     grad_0, term = wave(0, classes, pos, me, pos_pat, object_image, sibling, across[0], *operands, None)
+    grad_0, across[1][0] = lax.optimization_barrier((grad_0, across[1][0]))
     part_0 = lax.all_to_all(grad_0, "pat", split_axis=0, concat_axis=0, tiled=True)
-    real_grad, imag_grad, keep_term, give_term = wave(
+    grad_1, keep_term, give_term = wave(
         1, classes, pos, me, me, object_image, sibling, across[1], *operands, term
     )
-    real_grad, part_0 = lax.optimization_barrier((real_grad, part_0))
-    real_part = lax.all_to_all(real_grad, "pat", split_axis=0, concat_axis=0, tiled=True)
-    imag_grad, real_part = lax.optimization_barrier((imag_grad, real_part))
-    imag_part = lax.all_to_all(imag_grad, "pat", split_axis=0, concat_axis=0, tiled=True)
+    grad_1, part_0 = lax.optimization_barrier((grad_1, part_0))
+    part_1 = lax.all_to_all(grad_1, "pat", split_axis=0, concat_axis=0, tiled=True)
 
     core = my_owner % 2
     line = my_owner // 2
     term = keep_term + flip(give_term, 1).astype(jnp.float32)
     term = halved(term, line, lambda value: flip(value, 2))
 
-    def return_plane(plane, part, then, wait):
+    def return_plane(plane, then, wait):
         own_far, own_near, away_far, away_near = sum_pieces(
-            plane, pos_pat, then, part_0, part, owners, width
+            plane, pos_pat, then, part_0, part_1, owners, width
         )
         from_sibling_far = flip(away_far, 1)
         from_sibling = flip(away_near, 1)
@@ -546,12 +543,14 @@
         send, wait = lax.optimization_barrier((send, wait))
         from_across = flip(send, 2)
         total = own_near + from_sibling.astype(jnp.float32) + from_across.astype(jnp.float32)
-        mine = lax.dynamic_slice_in_dim(object_image[plane], my_class * height, height, 0)
+        mine = lax.dynamic_slice(
+            object_image, (plane, my_class * height, 0), (1, height, width)
+        ).reshape(height, width)
         return (mine.astype(jnp.float32) - OBJECT_RATE * total).astype(jnp.bfloat16), wait
 
-    real_rows, then = return_plane(0, real_part, me, me)
-    term, then = lax.optimization_barrier((term, then))
-    imag_rows, then = return_plane(1, imag_part, then, then)
+    term, then = lax.optimization_barrier((term, me))
+    real_rows, then = return_plane(0, then, me)
+    imag_rows, then = return_plane(1, then, then)
     real_rows, term = lax.optimization_barrier((real_rows, term))
     for bit in bits:
         term = halved(term, my_class // bit % 2, pat_flip(bit))

time: 296 us -> 305 us (1.030)
  waiting for transfers between devices: 136 us -> 180 us
  blocking collectives: 33.9 us -> 5.99 us
  starting transfers between devices: 36.2 us -> 31.3 us
    all_to_all x1 -> x0, blocking collectives: 28 us -> none  [shards(): lax.all_to_all(imag_grad, 'pat', split_axis=0, concat_axis=0, tiled=True)]
    all_gather x1, waiting for transfers between devices: 33.2 us -> 57.3 us  [shards(): lax.all_gather(imag_rows, 'pat', axis=0, tiled=True)]
    all_gather x1, waiting for transfers between devices: 0.01 us -> 14.2 us  [shards(): lax.all_gather(real_rows, 'pat', axis=0, tiled=True)]
    ppermute x15 -> x17, waiting for transfers between devices: 53.2 us -> 63.4 us  [flip(): return lax.ppermute(value, 'obj', [(k, k ^ bit) for k in range(owners)])]
    slice x1 -> x0, local copies, waits for them, and re-layouts: 5.94 us -> none  [return_plane(): object_image[plane]]
    ppermute x9, starting transfers between devices: 13.4 us -> 8.09 us  [pat_flip(): lax.ppermute(value, 'pat', [(k, k ^ bit) for k in range(classes)])]
    all_to_all x1, waiting for transfers between devices: 12.4 us -> 8.15 us  [shards(): lax.all_to_all(grad_1, 'pat', split_axis=0, concat_axis=0, tiled=True)]
    unnamed x26 -> x44, local copies, waits for them, and re-layouts: 11.9 us -> 14.2 us
  transfers between devices with their start and end apart: 28 -> 30, of which waited for: 20 -> 22; matrix products, arithmetic and copies ran while one was open for 5% -> 2% of each run, Pallas kernels for 10% -> 11%
where the time goes in v8:
time: 305 us; the launch traced here: 304 us
  waiting for transfers between devices  180 us (59%)
  Pallas kernels  47.3 us (16%)
  starting transfers between devices  31.3 us (10%)
  local copies, waits for them, and re-layouts  15.3 us (5%)
  between operations  14.4 us (5%)
  other arithmetic  9.56 us (3%)
  blocking collectives  5.99 us (2%)
    ppermute x17, waiting for transfers between devices, flip(): return lax.ppermute(value, 'obj', [(k, k ^ bit) for k in range(owners)])  63.4 us
    all_gather x1, waiting for transfers between devices, shards(): lax.all_gather(imag_rows, 'pat', axis=0, tiled=True)  57.3 us
    ppermute x9, waiting for transfers between devices, pat_flip(): lax.ppermute(value, 'pat', [(k, k ^ bit) for k in range(classes)])  36.6 us
    pallas_call x2, Pallas kernels, wave(): pl.pallas_call(functools.partial(wave_kernel, which), in_specs=[smem, sme...  24.7 us
    unnamed x44, local copies, waits for them, and re-layouts  14.2 us
    all_gather x1, waiting for transfers between devices, shards(): lax.all_gather(real_rows, 'pat', axis=0, tiled=True)  14.2 us
    ppermute x17, starting transfers between devices, flip(): return lax.ppermute(value, 'obj', [(k, k ^ bit) for k in range(owners)])  12.3 us
    all_to_all x1, waiting for transfers between devices, shards(): lax.all_to_all(grad_1, 'pat', split_axis=0, concat_axis=0, tiled=True)  8.15 us
  transfers between devices with their start and end apart: 30, of which 22 were waited for; matrix products, arithmetic and copies ran while one was open for 2% of the time, Pallas kernels for 11%

profile of v8, /device:TPU:0, one launch (start us, length us, event | category | flops | bytes accessed | tf_op | source)
XLA Modules:
  0.0 304.2 jit_solution(13109736892015629005)
XLA Ops:
  8.8 6.0 %all-gather = s32[4,2,4]{2,1,0:T(2,128)S(1)} all-gather(s32[1,2,4]{2,1,0:T(2,128)S(1)} %bitcast.20), channel_id=1, replica_groups=mesh['pat'=8,'obj'=4] {'obj'}, dimensions={0}, use_global_device_ids=true | all-gather | bytes 160 | tf_op jit(solution)/shard_map/all_gather | solution.py:508
  14.9 2.8 copy-done
  17.7 6.4 %shard_map.95 = (bf16[1,2,512,512]{3,2,1,0:T(8,128)(2,1)}, bf16[2,2,512,512]{3,2,1,0:T(8,128)(2,1)}) custom-call(s32[8,4]{1,0:T(8,128)S(1)} %bitcast.12, s32[2]{0:T(128)S(1)} %pad_add_fusion.3.me.spare, bf16[2,512,3072]{2,1,0:T(8,128)(2,1)S(1)} %copy-done, bf16[2,512,3072]{2,1,0:T(8,128)(2,1)S(1)} %copy-done, bf16[2,512,3072]{2,1,0:T(8,128)(2,1)S(1)} %copy-done, ...), custom_call_target="tpu_custom_call" | custom-call | flops 1966080 | bytes 7000000 | tf_op jit(solution)/shard_map/pallas_call | solution.py:194
  26.8 4.7 %collective-permute-done.refs_5_ = bf16[1,2,512,512]{3,2,1,0:T(8,128)(2,1)S(1)} collective-permute-done((bf16[1,2,512,512]{3,2,1,0:T(8,128)(2,1)}, bf16[1,2,512,512]{3,2,1,0:T(8,128)(2,1)S(1)}, u32[]{:S(2)}, u32[]{:S(2)}) %collective-permute-start) | collective-permute-done | bytes 1048608 | tf_op jit(solution)/shard_map/ppermute | solution.py:492
  31.4 2.8 copy-done.1
  36.1 2.1 collective-permute-start.1
  45.8 2.4 collective-permute-start.3
  51.1 3.7 %collective-permute-done.6.across_real = bf16[512,512]{1,0:T(8,128)(2,1)S(1)} collective-permute-done((bf16[512,512]{1,0:T(8,128)(2,1)S(1)}, bf16[512,512]{1,0:T(8,128)(2,1)S(1)}, u32[]{:S(2)}, u32[]{:S(2)}) %collective-permute-start.6) | collective-permute-done | bytes 524320 | tf_op jit(solution)/shard_map/ppermute | solution.py:492
  54.9 11.2 %collective-permute-done.7.across_imag = bf16[512,512]{1,0:T(8,128)(2,1)S(1)} collective-permute-done((bf16[512,512]{1,0:T(8,128)(2,1)S(1)}, bf16[512,512]{1,0:T(8,128)(2,1)S(1)}, u32[]{:S(2)}, u32[]{:S(2)}) %collective-permute-start.7) | collective-permute-done | bytes 524320 | tf_op jit(solution)/shard_map/ppermute | solution.py:492
  66.9 12.1 %shard_map.99 = (bf16[8,2,64,512]{3,2,1,0:T(8,128)(2,1)}, f32[2,512,512]{2,1,0:T(8,128)}) custom-call(s32[8,4]{1,0:T(8,128)} %bitcast.16, s32[2]{0:T(128)} %copy-done.8, s32[16,4]{1,0:T(8,128)} %broadcast_select_fusion.spare.pos, bf16[2,512,3072]{2,1,0:T(8,128)(2,1)} %band.3, bf16[2,2,512,512]{3,2,1,0:T(8,128)(2,1)} %collective-permute-done.4.sibling, ...), custom_call_target="tpu_custom_call" | custom-call | flops 4294967296 | bytes 300000000 | tf_op jit(solution)/shard_map/pallas_call | solution.py:376
  79.1 5.0 %all-to-all-start = ((bf16[8,2,64,512]{3,2,1,0:T(8,128)(2,1)}), bf16[8,2,64,512]{3,2,1,0:T(8,128)(2,1)S(1)}, u32[]{:S(2)}, u32[]{:S(2)}) async-start(bf16[8,2,64,512]{3,2,1,0:T(8,128)(2,1)} %get-tuple-element.57), calls=%async_computation | async-start | bytes 2097152 | tf_op jit(solution)/shard_map/all_to_all | solution.py:524
  85.7 9.9 %collective-permute-done.9.across_imag = bf16[512,512]{1,0:T(8,128)(2,1)S(1)} collective-permute-done((bf16[512,512]{1,0:T(8,128)(2,1)S(1)}, bf16[512,512]{1,0:T(8,128)(2,1)S(1)}, u32[]{:S(2)}, u32[]{:S(2)}) %collective-permute-start.9) | collective-permute-done | bytes 524320 | tf_op jit(solution)/shard_map/ppermute | solution.py:492
  96.4 12.6 %shard_map.100 = (bf16[8,2,64,512]{3,2,1,0:T(8,128)(2,1)}, f32[512,512]{1,0:T(8,128)}, bf16[512,512]{1,0:T(8,128)(2,1)}) custom-call(s32[8,4]{1,0:T(8,128)} %bitcast.17, s32[2]{0:T(128)} %copy-done.8, s32[2]{0:T(128)} %copy-done.8, bf16[2,512,3072]{2,1,0:T(8,128)(2,1)} %band.3, bf16[2,2,512,512]{3,2,1,0:T(8,128)(2,1)} %collective-permute-done.4.sibling, ...), custom_call_target="tpu_custom_call" | custom-call | flops 4294967296 | bytes 300000000 | tf_op jit(solution)/shard_map/pallas_call | solution.py:376
  109.0 5.8 %all-to-all-start.1 = ((bf16[8,2,64,512]{3,2,1,0:T(8,128)(2,1)}), bf16[8,2,64,512]{3,2,1,0:T(8,128)(2,1)S(1)}, u32[]{:S(2)}, u32[]{:S(2)}) async-start(bf16[8,2,64,512]{3,2,1,0:T(8,128)(2,1)} %get-tuple-element.59), calls=%async_computation.1 | async-start | bytes 2097152 | tf_op jit(solution)/shard_map/all_to_all | solution.py:529
  121.4 7.0 %collective-permute-done.11 = bf16[256,512]{1,0:T(8,128)(2,1)S(1)} collective-permute-done((bf16[256,512]{1,0:T(8,128)(2,1)}, bf16[256,512]{1,0:T(8,128)(2,1)S(1)}, u32[]{:S(2)}, u32[]{:S(2)}) %collective-permute-start.11) | collective-permute-done | bytes 262176 | tf_op jit(solution)/shard_map/ppermute | solution.py:492
  129.3 8.2 %all-to-all-done.1.second = bf16[8,2,64,512]{3,2,1,0:T(8,128)(2,1)S(1)} async-done(((bf16[8,2,64,512]{3,2,1,0:T(8,128)(2,1)}), bf16[8,2,64,512]{3,2,1,0:T(8,128)(2,1)S(1)}, u32[]{:S(2)}, u32[]{:S(2)}) %all-to-all-start.1) | async-done | bytes 1048608 | tf_op jit(solution)/shard_map/all_to_all | solution.py:529
  137.5 2.9 shard_map.101
  143.0 3.6 %shard_map.102 = (f32[64,3072]{1,0:T(8,128)S(1)}, f32[64,3072]{1,0:T(8,128)S(1)}, bf16[64,3072]{1,0:T(8,128)(2,1)S(1)}, bf16[64,3072]{1,0:T(8,128)(2,1)}) custom-call(s32[16,4]{1,0:T(8,128)S(1)} %copy-done.7, s32[2]{0:T(128)S(1)} %copy-done.9, bf16[8,2,64,512]{3,2,1,0:T(8,128)(2,1)S(1)} %all-to-all-done.first, bf16[8,2,64,512]{3,2,1,0:T(8,128)(2,1)S(1)} %all-to-all-done.1.second), custom_call_target="tpu_custom_call" | custom-call | flops 4194304 | bytes 4456448 | tf_op jit(solution)/shard_map/pallas_call | solution.py:438
  151.5 8.7 %collective-permute-done.17 = bf16[64,3072]{1,0:T(8,128)(2,1)S(1)} collective-permute-done((bf16[64,3072]{1,0:T(8,128)(2,1)}, bf16[64,3072]{1,0:T(8,128)(2,1)S(1)}, u32[]{:S(2)}, u32[]{:S(2)}) %collective-permute-start.17) | collective-permute-done | bytes 393248 | tf_op jit(solution)/shard_map/ppermute | solution.py:492
  160.2 7.8 %collective-permute-done.15 = bf16[64,3072]{1,0:T(8,128)(2,1)} collective-permute-done((bf16[64,3072]{1,0:T(8,128)(2,1)}, bf16[64,3072]{1,0:T(8,128)(2,1)}, u32[]{:S(2)}, u32[]{:S(2)}) %collective-permute-start.15) | collective-permute-done | bytes 393248 | tf_op jit(solution)/shard_map/ppermute | solution.py:492
  168.0 2.6 fusion
  172.6 3.8 %collective-permute-done.18 = bf16[128,512]{1,0:T(8,128)(2,1)S(1)} collective-permute-done((bf16[128,512]{1,0:T(8,128)(2,1)S(1)}, bf16[128,512]{1,0:T(8,128)(2,1)S(1)}, u32[]{:S(2)}, u32[]{:S(2)}) %collective-permute-start.18) | collective-permute-done | bytes 131104 | tf_op jit(solution)/shard_map/ppermute | solution.py:495
  176.6 5.1 %collective-permute-done.19 = bf16[64,512]{1,0:T(8,128)(2,1)S(1)} collective-permute-done((bf16[64,512]{1,0:T(8,128)(2,1)S(1)}, bf16[64,512]{1,0:T(8,128)(2,1)S(1)}, u32[]{:S(2)}, u32[]{:S(2)}) %collective-permute-start.19) | collective-permute-done | bytes 65568 | tf_op jit(solution)/shard_map/ppermute | solution.py:495
  181.8 7.3 %collective-permute-done.20 = bf16[32,512]{1,0:T(8,128)(2,1)S(1)} collective-permute-done((bf16[32,512]{1,0:T(8,128)(2,1)S(1)}, bf16[32,512]{1,0:T(8,128)(2,1)S(1)}, u32[]{:S(2)}, u32[]{:S(2)}) %collective-permute-start.20) | collective-permute-done | bytes 32800 | tf_op jit(solution)/shard_map/ppermute | solution.py:495
  189.2 6.3 %collective-permute-done.21 = bf16[32,512]{1,0:T(8,128)(2,1)S(1)} collective-permute-done((bf16[32,512]{1,0:T(8,128)(2,1)S(1)}, bf16[32,512]{1,0:T(8,128)(2,1)S(1)}, u32[]{:S(2)}, u32[]{:S(2)}) %collective-permute-start.21) | collective-permute-done | bytes 32800 | tf_op jit(solution)/shard_map/ppermute | solution.py:495
  195.5 4.3 %collective-permute-done.22 = bf16[64,512]{1,0:T(8,128)(2,1)S(1)} collective-permute-done((bf16[64,512]{1,0:T(8,128)(2,1)S(1)}, bf16[64,512]{1,0:T(8,128)(2,1)S(1)}, u32[]{:S(2)}, u32[]{:S(2)}) %collective-permute-start.22) | collective-permute-done | bytes 65568 | tf_op jit(solution)/shard_map/ppermute | solution.py:495
  200.3 7.1 %collective-permute-done.23 = bf16[128,512]{1,0:T(8,128)(2,1)S(1)} collective-permute-done((bf16[128,512]{1,0:T(8,128)(2,1)S(1)}, bf16[128,512]{1,0:T(8,128)(2,1)S(1)}, u32[]{:S(2)}, u32[]{:S(2)}) %collective-permute-start.23) | collective-permute-done | bytes 131104 | tf_op jit(solution)/shard_map/ppermute | solution.py:495
  209.0 5.0 %collective-permute-done.24 = bf16[256,512]{1,0:T(8,128)(2,1)S(1)} collective-permute-done((bf16[256,512]{1,0:T(8,128)(2,1)S(1)}, bf16[256,512]{1,0:T(8,128)(2,1)S(1)}, u32[]{:S(2)}, u32[]{:S(2)}) %collective-permute-start.24) | collective-permute-done | bytes 262176 | tf_op jit(solution)/shard_map/ppermute | solution.py:492
  217.8 14.2 %all-gather.6.cloned.1.call-done.source = bf16[512,3072]{1,0:T(8,128)(2,1)} async-done(((bf16[64,3072]{1,0:T(8,128)(2,1)}), bf16[512,3072]{1,0:T(8,128)(2,1)}) %all-gather.6.cloned.1.call-update) | async-done | bytes 3145744 | tf_op jit(solution)/shard_map/all_gather | solution.py:563
  233.9 2.1 shard_map.103.refs_0_
  236.0 57.3 %all-gather.4.cloned.1.call-done.source = bf16[512,3072]{1,0:T(8,128)(2,1)} async-done(((bf16[64,3072]{1,0:T(8,128)(2,1)}), bf16[512,3072]{1,0:T(8,128)(2,1)}) %all-gather.4.cloned.1.call-update) | async-done | bytes 3145744 | tf_op jit(solution)/shard_map/all_gather | solution.py:564
  295.2 2.1 shard_map.104
  (111 shorter events, 47.1 us)
Async XLA Ops:
  14.8 23.3 %copy-start.6 = (s32[4,2,4]{2,1,0:T(2,128)}, s32[4,2,4]{2,1,0:T(2,128)S(1)}, u32[]{:S(2)}) copy-start(s32[4,2,4]{2,1,0:T(2,128)S(1)} %all-gather) | copy-start | bytes 388
  24.1 42.0 %collective-permute-start.4 = (bf16[2,2,512,512]{3,2,1,0:T(8,128)(2,1)}, bf16[2,2,512,512]{3,2,1,0:T(8,128)(2,1)}, u32[]{:S(2)}, u32[]{:S(2)}) collective-permute-start(bf16[2,2,512,512]{3,2,1,0:T(8,128)(2,1)} %get-tuple-element.45), channel_id=1, source_target_pairs={{0,1},{1,0},{2,3},{3,2},{4,5},{5,4},{6,7},{7,6},{8,9},{9,8},{10,11... | collective-permute-start | bytes 6291464 | tf_op jit(solution)/shard_map/ppermute | solution.py:492
  24.4 7.0 %collective-permute-start = (bf16[1,2,512,512]{3,2,1,0:T(8,128)(2,1)}, bf16[1,2,512,512]{3,2,1,0:T(8,128)(2,1)S(1)}, u32[]{:S(2)}, u32[]{:S(2)}) collective-permute-start(bf16[1,2,512,512]{3,2,1,0:T(8,128)(2,1)} %get-tuple-element.41), channel_id=1, source_target_pairs={{0,1},{1,0},{2,3},{3,2},{4,5},{5,4},{6,7},{7,6},{8,9},{9,8},{10,11... | collective-permute-start | bytes 3145736 | tf_op jit(solution)/shard_map/ppermute | solution.py:492
  26.4 11.8 %collective-permute-start.5 = (bf16[1,2,512,512]{3,2,1,0:T(8,128)(2,1)S(1)}, bf16[1,2,512,512]{3,2,1,0:T(8,128)(2,1)S(1)}, u32[]{:S(2)}, u32[]{:S(2)}) collective-permute-start(bf16[1,2,512,512]{3,2,1,0:T(8,128)(2,1)S(1)} %shard_map.97), channel_id=1, source_target_pairs={{0,1},{1,0},{2,3},{3,2},{4,5},{5,4},{6,7},{7,6},{8,9},{9,8},{10,11... | collective-permute-start | bytes 3145736 | tf_op jit(solution)/shard_map/ppermute | solution.py:492
  36.1 6.0 %collective-permute-start.1 = (s32[2,4]{0,1:T(4,128)S(1)}, s32[2,4]{0,1:T(4,128)S(1)}, u32[]{:S(2)}, u32[]{:S(2)}) collective-permute-start(s32[2,4]{0,1:T(4,128)S(1)} %pad_add_fusion), channel_id=1, source_target_pairs={{0,4},{4,0},{8,12},{12,8},{16,20},{20,16},{24,28},{28,24},{1,5},{5... | collective-permute-start | bytes 104 | tf_op jit(solution)/shard_map/ppermute | solution.py:495
  40.0 14.9 %collective-permute-start.6 = (bf16[512,512]{1,0:T(8,128)(2,1)S(1)}, bf16[512,512]{1,0:T(8,128)(2,1)S(1)}, u32[]{:S(2)}, u32[]{:S(2)}) collective-permute-start(bf16[512,512]{1,0:T(8,128)(2,1)S(1)} %get-tuple-element.46), channel_id=1, source_target_pairs={{0,2},{1,3},{2,0},{3,1},{4,6},{5,7},{6,4},{7,5},{8,10},{9,11},{10,... | collective-permute-start | bytes 1572872 | tf_op jit(solution)/shard_map/ppermute | solution.py:492
  41.6 24.5 %collective-permute-start.7 = (bf16[512,512]{1,0:T(8,128)(2,1)S(1)}, bf16[512,512]{1,0:T(8,128)(2,1)S(1)}, u32[]{:S(2)}, u32[]{:S(2)}) collective-permute-start(bf16[512,512]{1,0:T(8,128)(2,1)S(1)} %get-tuple-element.47), channel_id=1, source_target_pairs={{0,2},{1,3},{2,0},{3,1},{4,6},{5,7},{6,4},{7,5},{8,10},{9,11},{10,... | collective-permute-start | bytes 1572872 | tf_op jit(solution)/shard_map/ppermute | solution.py:492
  42.1 3.6 %collective-permute-start.2 = (s32[4,4]{0,1:T(4,128)S(1)}, s32[4,4]{0,1:T(4,128)S(1)}, u32[]{:S(2)}, u32[]{:S(2)}) collective-permute-start(s32[4,4]{0,1:T(4,128)S(1)} %add_select_fusion), channel_id=1, source_target_pairs={{0,8},{4,12},{8,0},{12,4},{16,24},{20,28},{24,16},{28,20},{1,9},{5... | collective-permute-start | bytes 200 | tf_op jit(solution)/shard_map/ppermute | solution.py:495
  45.8 4.5 %collective-permute-start.3 = (s32[8,4]{0,1:T(4,128)S(1)}, s32[8,4]{0,1:T(4,128)S(1)}, u32[]{:S(2)}, u32[]{:S(2)}) collective-permute-start(s32[8,4]{0,1:T(4,128)S(1)} %add_select_fusion.1), channel_id=1, source_target_pairs={{0,16},{4,20},{8,24},{12,28},{16,0},{20,4},{24,8},{28,12},{1,17},{... | collective-permute-start | bytes 392 | tf_op jit(solution)/shard_map/ppermute | solution.py:495
  48.2 30.8 %collective-permute-start.8 = (bf16[512,512]{1,0:T(8,128)(2,1)}, bf16[512,512]{1,0:T(8,128)(2,1)S(1)}, u32[]{:S(2)}, u32[]{:S(2)}) collective-permute-start(bf16[512,512]{1,0:T(8,128)(2,1)} %copy-done.12), channel_id=1, source_target_pairs={{0,2},{1,3},{2,0},{3,1},{4,6},{5,7},{6,4},{7,5},{8,10},{9,11},{10,... | collective-permute-start | bytes 1572872 | tf_op jit(solution)/shard_map/ppermute | solution.py:492
  79.1 29.9 %all-to-all-start = ((bf16[8,2,64,512]{3,2,1,0:T(8,128)(2,1)}), bf16[8,2,64,512]{3,2,1,0:T(8,128)(2,1)S(1)}, u32[]{:S(2)}, u32[]{:S(2)}) async-start(bf16[8,2,64,512]{3,2,1,0:T(8,128)(2,1)} %get-tuple-element.57), calls=%async_computation | async-start | bytes 2097152 | tf_op jit(solution)/shard_map/all_to_all | solution.py:524
  84.1 11.5 %collective-permute-start.9 = (bf16[512,512]{1,0:T(8,128)(2,1)S(1)}, bf16[512,512]{1,0:T(8,128)(2,1)S(1)}, u32[]{:S(2)}, u32[]{:S(2)}) collective-permute-start(bf16[512,512]{1,0:T(8,128)(2,1)S(1)} %copy-done.11), channel_id=1, source_target_pairs={{0,2},{1,3},{2,0},{3,1},{4,6},{5,7},{6,4},{7,5},{8,10},{9,11},{10,... | collective-permute-start | bytes 1572872 | tf_op jit(solution)/shard_map/ppermute | solution.py:492
  109.0 28.5 %all-to-all-start.1 = ((bf16[8,2,64,512]{3,2,1,0:T(8,128)(2,1)}), bf16[8,2,64,512]{3,2,1,0:T(8,128)(2,1)S(1)}, u32[]{:S(2)}, u32[]{:S(2)}) async-start(bf16[8,2,64,512]{3,2,1,0:T(8,128)(2,1)} %get-tuple-element.59), calls=%async_computation.1 | async-start | bytes 2097152 | tf_op jit(solution)/shard_map/all_to_all | solution.py:529
  114.8 117.2 %all-gather.6.cloned.1.call-start = ((), (), s32[]{:S(2)}) async-start(), calls=%async_computation.3 | async-start | bytes 3538944 | tf_op jit(solution)/shard_map/all_gather | solution.py:563
  114.8 2.0 collective-permute-start.10
  119.9 8.6 %collective-permute-start.11 = (bf16[256,512]{1,0:T(8,128)(2,1)}, bf16[256,512]{1,0:T(8,128)(2,1)S(1)}, u32[]{:S(2)}, u32[]{:S(2)}) collective-permute-start(bf16[256,512]{1,0:T(8,128)(2,1)} %dynamic-slice_convert_fusion), channel_id=1, source_target_pairs={{0,2},{1,3},{2,0},{3,1},{4,6},{5,7},{6,4},{7,5},{8,10},{9,11},{10,... | collective-permute-start | bytes 786440 | tf_op jit(solution)/shard_map/ppermute | solution.py:492
  140.4 1.8 collective-permute-start.12
  147.5 2.0 collective-permute-start.14
  147.7 3.8 %collective-permute-start.16 = (bf16[64,3072]{1,0:T(8,128)(2,1)S(1)}, bf16[64,3072]{1,0:T(8,128)(2,1)S(1)}, u32[]{:S(2)}, u32[]{:S(2)}) collective-permute-start(bf16[64,3072]{1,0:T(8,128)(2,1)S(1)} %get-tuple-element.69), channel_id=1, source_target_pairs={{0,1},{1,0},{2,3},{3,2},{4,5},{5,4},{6,7},{7,6},{8,9},{9,8},{10,11... | collective-permute-start | bytes 1179656 | tf_op jit(solution)/shard_map/ppermute | solution.py:492
  148.0 12.2 %collective-permute-start.17 = (bf16[64,3072]{1,0:T(8,128)(2,1)}, bf16[64,3072]{1,0:T(8,128)(2,1)S(1)}, u32[]{:S(2)}, u32[]{:S(2)}) collective-permute-start(bf16[64,3072]{1,0:T(8,128)(2,1)} %add_convert_fusion.1), channel_id=1, source_target_pairs={{0,2},{1,3},{2,0},{3,1},{4,6},{5,7},{6,4},{7,5},{8,10},{9,11},{10,... | collective-permute-start | bytes 1179656 | tf_op jit(solution)/shard_map/ppermute | solution.py:492
  149.5 10.7 %collective-permute-start.13 = (bf16[64,3072]{1,0:T(8,128)(2,1)}, bf16[64,3072]{1,0:T(8,128)(2,1)S(1)}, u32[]{:S(2)}, u32[]{:S(2)}) collective-permute-start(bf16[64,3072]{1,0:T(8,128)(2,1)} %get-tuple-element.64), channel_id=1, source_target_pairs={{0,1},{1,0},{2,3},{3,2},{4,5},{5,4},{6,7},{7,6},{8,9},{9,8},{10,11... | collective-permute-start | bytes 1179656 | tf_op jit(solution)/shard_map/ppermute | solution.py:492
  150.3 17.6 %collective-permute-start.15 = (bf16[64,3072]{1,0:T(8,128)(2,1)}, bf16[64,3072]{1,0:T(8,128)(2,1)}, u32[]{:S(2)}, u32[]{:S(2)}) collective-permute-start(bf16[64,3072]{1,0:T(8,128)(2,1)} %add_convert_fusion), channel_id=1, source_target_pairs={{0,2},{1,3},{2,0},{3,1},{4,6},{5,7},{6,4},{7,5},{8,10},{9,11},{10,... | collective-permute-start | bytes 1179656 | tf_op jit(solution)/shard_map/ppermute | solution.py:492
  170.6 45.6 %copy-start.13 = (f32[2,512,512]{2,1,0:T(8,128)S(1)}, f32[2,512,512]{2,1,0:T(8,128)}, u32[]{:S(2)}) copy-start(f32[2,512,512]{2,1,0:T(8,128)} %probe.3) | copy-start | bytes 6291460
  170.6 122.7 %all-gather.4.cloned.1.call-start = ((), (), s32[]{:S(2)}) async-start(), calls=%async_computation.2 | async-start | bytes 3538944 | tf_op jit(solution)/shard_map/all_gather | solution.py:564
  171.4 5.0 %collective-permute-start.18 = (bf16[128,512]{1,0:T(8,128)(2,1)S(1)}, bf16[128,512]{1,0:T(8,128)(2,1)S(1)}, u32[]{:S(2)}, u32[]{:S(2)}) collective-permute-start(bf16[128,512]{1,0:T(8,128)(2,1)S(1)} %dynamic-slice_convert_fusion.1), channel_id=1, source_target_pairs={{0,4},{4,0},{8,12},{12,8},{16,20},{20,16},{24,28},{28,24},{1,5},{5... | collective-permute-start | bytes 393224 | tf_op jit(solution)/shard_map/ppermute | solution.py:495
  176.5 5.2 %collective-permute-start.19 = (bf16[64,512]{1,0:T(8,128)(2,1)S(1)}, bf16[64,512]{1,0:T(8,128)(2,1)S(1)}, u32[]{:S(2)}, u32[]{:S(2)}) collective-permute-start(bf16[64,512]{1,0:T(8,128)(2,1)S(1)} %dynamic-slice_convert_fusion.2), channel_id=1, source_target_pairs={{0,8},{4,12},{8,0},{12,4},{16,24},{20,28},{24,16},{28,20},{1,9},{5... | collective-permute-start | bytes 196616 | tf_op jit(solution)/shard_map/ppermute | solution.py:495
  181.7 7.4 %collective-permute-start.20 = (bf16[32,512]{1,0:T(8,128)(2,1)S(1)}, bf16[32,512]{1,0:T(8,128)(2,1)S(1)}, u32[]{:S(2)}, u32[]{:S(2)}) collective-permute-start(bf16[32,512]{1,0:T(8,128)(2,1)S(1)} %dynamic-slice_convert_fusion.3), channel_id=1, source_target_pairs={{0,16},{4,20},{8,24},{12,28},{16,0},{20,4},{24,8},{28,12},{1,17},{... | collective-permute-start | bytes 98312 | tf_op jit(solution)/shard_map/ppermute | solution.py:495
  189.1 6.3 %collective-permute-start.21 = (bf16[32,512]{1,0:T(8,128)(2,1)S(1)}, bf16[32,512]{1,0:T(8,128)(2,1)S(1)}, u32[]{:S(2)}, u32[]{:S(2)}) collective-permute-start(bf16[32,512]{1,0:T(8,128)(2,1)S(1)} %add_convert_fusion.2), channel_id=1, source_target_pairs={{0,16},{4,20},{8,24},{12,28},{16,0},{20,4},{24,8},{28,12},{1,17},{... | collective-permute-start | bytes 98312 | tf_op jit(solution)/shard_map/ppermute | solution.py:495
  195.5 4.3 %collective-permute-start.22 = (bf16[64,512]{1,0:T(8,128)(2,1)S(1)}, bf16[64,512]{1,0:T(8,128)(2,1)S(1)}, u32[]{:S(2)}, u32[]{:S(2)}) collective-permute-start(bf16[64,512]{1,0:T(8,128)(2,1)S(1)} %maximum_select_fusion.4), channel_id=1, source_target_pairs={{0,8},{4,12},{8,0},{12,4},{16,24},{20,28},{24,16},{28,20},{1,9},{5... | collective-permute-start | bytes 196616 | tf_op jit(solution)/shard_map/ppermute | solution.py:495
  199.8 7.7 %collective-permute-start.23 = (bf16[128,512]{1,0:T(8,128)(2,1)S(1)}, bf16[128,512]{1,0:T(8,128)(2,1)S(1)}, u32[]{:S(2)}, u32[]{:S(2)}) collective-permute-start(bf16[128,512]{1,0:T(8,128)(2,1)S(1)} %maximum_select_fusion.3), channel_id=1, source_target_pairs={{0,4},{4,0},{8,12},{12,8},{16,20},{20,16},{24,28},{28,24},{1,5},{5... | collective-permute-start | bytes 393224 | tf_op jit(solution)/shard_map/ppermute | solution.py:495
  207.5 6.4 %collective-permute-start.24 = (bf16[256,512]{1,0:T(8,128)(2,1)S(1)}, bf16[256,512]{1,0:T(8,128)(2,1)S(1)}, u32[]{:S(2)}, u32[]{:S(2)}) collective-permute-start(bf16[256,512]{1,0:T(8,128)(2,1)S(1)} %maximum_select_fusion.2), channel_id=1, source_target_pairs={{0,2},{1,3},{2,0},{3,1},{4,6},{5,7},{6,4},{7,5},{8,10},{9,11},{10,... | collective-permute-start | bytes 786440 | tf_op jit(solution)/shard_map/ppermute | solution.py:492
  214.2 2.0 collective-permute-start.25
  (19 other events, 146.0 us)
Sparse Core Ops, SparseCore 0:
  170.7 61.2 all-gather.5
  234.2 59.0 all-gather.3

commit v9 on v6

--- a/solution.py
+++ b/solution.py
@@ -20,6 +20,7 @@
 CUT_VMEM = 14 * 1024 * 1024
 WAVE_VMEM = 56 * 1024 * 1024
 SUM_VMEM = 24 * 1024 * 1024
+BY_PERMUTE = (4, 8)
 
 
 def dft_tables(length):
@@ -458,6 +459,90 @@
     )(pos, me, first, second)
 
 
+def assemble_kernel(length, me, *refs):
+    steps = length - 1
+    own, refs = refs[0], refs[1:]
+    ups, downs, overs = refs[:steps], refs[steps : 2 * steps], refs[2 * steps : 3 * steps + 1]
+    out, sems = refs[3 * steps + 1 :]
+    height = own.shape[1]
+    place = me[1] // 2
+    side = lax.rem(me[1], 2)
+
+    def copy(source, at, column, k):
+        rows = pl.ds(pl.multiple_of((2 * at + column) * height, height), height)
+        return pltpu.make_async_copy(source, out.at[:, rows, :], sems.at[k])
+
+    always = [copy(own, place, side, 0)]
+    for k in range(length):
+        always.append(copy(overs[k], sent_over(place, k, length), 1 - side, k + 1))
+    some = []
+    for k in range(1, length):
+        below, above = place - k, place + k
+        held = length + 2 * k - 1
+        some.append((below >= 0, copy(ups[k - 1], below, side, held)))
+        some.append((above < length, copy(downs[k - 1], above, side, held + 1)))
+    for part in always:
+        part.start()
+    for has, part in some:
+        pl.when(has)(part.start)
+    for part in always:
+        part.wait()
+    for has, part in some:
+        pl.when(has)(part.wait)
+
+
+def sent_over(place, k, length):
+    low = jnp.where(place >= k, place - k, place + k)
+    if k == length - 1:
+        high = jnp.where(place == 0, length - 1, jnp.where(place == length - 1, 0, place + 1))
+        return high
+    return low
+
+
+def gather_classes(own, me, classes, term, term_steps):
+    length = classes // 2
+    place = me[1] // 2
+
+    def along(value, held, step):
+        pairs = [(2 * z + x, 2 * (z + step) + x) for z in held if 0 <= z + step < length for x in range(2)]
+        return lax.ppermute(value, "pat", pairs)
+
+    def over(value):
+        return lax.ppermute(value, "pat", [(k, k ^ 1) for k in range(classes)])
+
+    ups, downs, overs = [own], [own], []
+    for k in range(length - 1):
+        overs.append(over(jnp.where(place >= k, ups[k], downs[k]) if k else own))
+        ups.append(along(ups[k], range(k, length), 1))
+        downs.append(along(downs[k], range(length - k), -1))
+        if k == length - 2:
+            for step in term_steps[:-1]:
+                term = step(term)
+        overs[k], ups[k + 1], downs[k + 1], term = lax.optimization_barrier(
+            (overs[k], ups[k + 1], downs[k + 1], term)
+        )
+    end = jnp.where(place == 0, downs[-1], ups[-1])
+    if length > 2:
+        middle = (place > 0) & (place < length - 1)
+        end = jnp.where(middle, downs[1], end)
+    last, term = lax.optimization_barrier((over(end), term_steps[-1](term)))
+    overs.append(last)
+    operands = [own, *ups[1:], *downs[1:], *overs]
+    object_next = pl.pallas_call(
+        functools.partial(assemble_kernel, length),
+        in_specs=[pl.BlockSpec(memory_space=pltpu.SMEM)]
+        + [pl.BlockSpec(memory_space=pltpu.VMEM)] * len(operands),
+        out_specs=pl.BlockSpec(memory_space=pl.ANY),
+        out_shape=jax.ShapeDtypeStruct((2, classes * own.shape[1], own.shape[2]), own.dtype),
+        scratch_shapes=[pltpu.SemaphoreType.DMA((3 * length - 1,))],
+        compiler_params=pltpu.CompilerParams(vmem_limit_bytes=CUT_VMEM),
+        cost_estimate=pl.CostEstimate(
+            flops=0, bytes_accessed=4 * own.size * classes, transcendentals=0
+        ),
+    )(me, *operands)
+    return object_next, term
+
+
 def shards(object_image, probe, amplitudes, pos_tile, pos_offset):
     owners = lax.axis_size("obj")
     classes = lax.axis_size("pat")
@@ -484,6 +569,7 @@
         return jnp.where(bit == 0, jnp.concatenate([part, got]), jnp.concatenate([got, part]))
 
     bits = [1 << k for k in range(classes.bit_length() - 1)]
+    halving = bits[1:] + bits[:1]
     own_pos = jnp.concatenate([pos_tile, pos_offset], 1)
     pos = lax.all_gather(own_pos, "obj", axis=0, tiled=True)
 
@@ -521,20 +607,24 @@
     from_across = flip(
         (own_far + from_sibling_far.astype(jnp.float32)).astype(jnp.bfloat16), 2
     )
-    for bit in bits:
+    for bit in halving:
         term = halved(term, my_class // bit % 2, pat_flip(bit))
+    term = doubled(term.astype(jnp.bfloat16), my_class % 2, pat_flip(1))
     total = own_near + from_sibling.astype(jnp.float32) + from_across.astype(jnp.float32)
     mine = lax.dynamic_slice_in_dim(object_image, my_class * height, height, 1)
     updated = (mine.astype(jnp.float32) - OBJECT_RATE * total).astype(jnp.bfloat16)
-    updated, term = lax.optimization_barrier((updated, term.astype(jnp.bfloat16)))
+    updated, term = lax.optimization_barrier((updated, term))
     steps = [
-        functools.partial(doubled, bit=my_class // bit % 2, other=pat_flip(bit)) for bit in reversed(bits)
+        functools.partial(doubled, bit=my_class // bit % 2, other=pat_flip(bit)) for bit in reversed(bits[1:])
     ]
     steps.append(functools.partial(doubled, bit=line, other=lambda value: flip(value, 2)))
     steps.append(lambda part: doubled(part[None], core, lambda value: flip(value, 1)))
-    object_next = lax.all_gather(updated, "pat", axis=1, tiled=True)
-    for step in steps:
-        term = step(term)
+    if classes in BY_PERMUTE:
+        object_next, term = gather_classes(updated, me, classes, term, steps)
+    else:
+        object_next = lax.all_gather(updated, "pat", axis=1, tiled=True)
+        for step in steps:
+            term = step(term)
     probe_total = term.astype(jnp.float32)
     probe_next = probe - PROBE_RATE * probe_total
     return (object_next, probe_next)

time: 284 us -> 277 us (0.975)
  waiting for transfers between devices: 169 us -> 147 us
  starting transfers between devices: 27.4 us -> 47.9 us
  between operations: 14.3 us -> 1.14 us
  other arithmetic: 11.1 us -> 18.7 us
  local copies, waits for them, and re-layouts: 14.8 us -> 8.93 us
  Pallas kernels: 41 us -> 46.1 us
    all_gather x1 -> x0, waiting for transfers between devices: 70.4 us -> none  [shards(): object_next = lax.all_gather(updated, 'pat', axis=1, tiled=True)]
    ppermute x0 -> x10, waiting for transfers between devices: none -> 45.6 us  [the longest x4 24.7 us: over(): return lax.ppermute(value, 'pat', [(k, k ^ 1) for k in range(classes)])]
    ppermute x0 -> x10, starting transfers between devices: none -> 16 us  [the longest x6 10.7 us: along(): return lax.ppermute(value, 'pat', pairs)]
    unnamed x29 -> x32, local copies, waits for them, and re-layouts: 14.4 us -> 8.58 us
    select_n x0 -> x3, other arithmetic: none -> 5.35 us  [the longest x2 3.12 us: gather_classes(): overs.append(over(jnp.where(place >= k, ups[k], downs[k]) if k else own))]
    pallas_call x0 -> x1, Pallas kernels: none -> 5.1 us  [gather_classes(): pl.pallas_call(functools.partial(assemble_kernel, length), in_specs=[pl.B...]
    ppermute x9, starting transfers between devices: 8.6 us -> 12.7 us  [pat_flip(): lax.ppermute(value, 'pat', [(k, k ^ bit) for k in range(classes)])]
    select_n x7 -> x8, other arithmetic: 1.05 us -> 4.58 us  [doubled(): jnp.where(bit == 0, jnp.concatenate([part, got]), jnp.concatenate([got, p...]
  transfers between devices with their start and end apart: 24 -> 33, of which waited for: 20 -> 24; matrix products, arithmetic and copies ran while one was open for 3% -> 4% of each run, Pallas kernels for 12% -> 12%
where the time goes in v9:
time: 277 us; the launch traced here: 276 us
  waiting for transfers between devices  147 us (53%)
  starting transfers between devices  47.9 us (17%)
  Pallas kernels  46.1 us (17%)
  other arithmetic  18.7 us (7%)
  local copies, waits for them, and re-layouts  8.93 us (3%)
  blocking collectives  5.99 us (2%)
    ppermute x12, waiting for transfers between devices, flip(): return lax.ppermute(value, 'obj', [(k, k ^ bit) for k in range(owners)])  43.6 us
    ppermute x9, waiting for transfers between devices, pat_flip(): lax.ppermute(value, 'pat', [(k, k ^ bit) for k in range(classes)])  33.6 us
    ppermute x4, waiting for transfers between devices, over(): return lax.ppermute(value, 'pat', [(k, k ^ 1) for k in range(classes)])  24.7 us
    pallas_call x2, Pallas kernels, wave(): pl.pallas_call(functools.partial(wave_kernel, which), in_specs=[smem, sme...  24.7 us
    ppermute x6, waiting for transfers between devices, along(): return lax.ppermute(value, 'pat', pairs)  20.8 us
    all_to_all x1, waiting for transfers between devices, shards(): lax.all_to_all(grad_0, 'pat', split_axis=0, concat_axis=0, tiled=True)  13 us
    ppermute x9, starting transfers between devices, pat_flip(): lax.ppermute(value, 'pat', [(k, k ^ bit) for k in range(classes)])  12.7 us
    all_to_all x1, waiting for transfers between devices, shards(): lax.all_to_all(grad_1, 'pat', split_axis=0, concat_axis=0, tiled=True)  11.7 us
  transfers between devices with their start and end apart: 33, of which 24 were waited for; matrix products, arithmetic and copies ran while one was open for 4% of the time, Pallas kernels for 12%

profile of v9, /device:TPU:0, one launch (start us, length us, event | category | flops | bytes accessed | tf_op | source)
XLA Modules:
  0.0 276.2 jit_solution(15389749595637465884)
XLA Ops:
  2.3 6.0 %all-gather = s32[4,2,4]{2,1,0:T(2,128)S(1)} all-gather(s32[1,2,4]{2,1,0:T(2,128)S(1)} %bitcast.11), channel_id=1, replica_groups=mesh['pat'=8,'obj'=4] {'obj'}, dimensions={0}, use_global_device_ids=true | all-gather | bytes 160 | tf_op jit(solution)/shard_map/all_gather | solution.py:574
  8.4 2.8 %copy-done = bf16[2,512,3072]{2,1,0:T(8,128)(2,1)S(1)} copy-done((bf16[2,512,3072]{2,1,0:T(8,128)(2,1)S(1)}, bf16[2,512,3072]{2,1,0:T(8,128)(2,1)}, u32[]{:S(2)}) %copy-start) | copy-done | bytes 6291480
  13.3 6.0 %shard_map.95 = (bf16[1,2,512,512]{3,2,1,0:T(8,128)(2,1)S(1)}, bf16[2,2,512,512]{3,2,1,0:T(8,128)(2,1)}) custom-call(s32[8,4]{1,0:T(8,128)S(1)} %bitcast.6, s32[2]{0:T(128)S(1)} %pad_add_fusion.3.me.spare, bf16[2,512,3072]{2,1,0:T(8,128)(2,1)S(1)} %copy-done, bf16[2,512,3072]{2,1,0:T(8,128)(2,1)S(1)} %copy-done, bf16[2,512,3072]{2,1,0:T(8,128)(2,1)S(1)} %copy-done, ...), custom_call_target="tpu_custom_call" | custom-call | flops 1966080 | bytes 7000000 | tf_op jit(solution)/shard_map/pallas_call | solution.py:195
  33.8 2.4 collective-permute-done.2
  36.3 2.2 collective-permute-start.3
  38.5 2.3 collective-permute-done.3
  41.6 6.2 %collective-permute-done.6.across = bf16[2,512,512]{2,1,0:T(8,128)(2,1)} collective-permute-done((bf16[2,512,512]{2,1,0:T(8,128)(2,1)S(1)}, bf16[2,512,512]{2,1,0:T(8,128)(2,1)}, u32[]{:S(2)}, u32[]{:S(2)}) %collective-permute-start.6) | collective-permute-done | bytes 1048608 | tf_op jit(solution)/shard_map/ppermute | solution.py:557
  47.8 12.2 %shard_map.99 = (bf16[8,2,64,512]{3,2,1,0:T(8,128)(2,1)}, f32[2,512,512]{2,1,0:T(8,128)}) custom-call(s32[8,4]{1,0:T(8,128)} %bitcast.9, s32[2]{0:T(128)} %copy-done.7, s32[16,4]{1,0:T(8,128)} %broadcast_select_fusion.2.spare.pos, bf16[2,512,3072]{2,1,0:T(8,128)(2,1)} %band.3, bf16[2,2,512,512]{3,2,1,0:T(8,128)(2,1)} %collective-permute-done.4.sibling, ...), custom_call_target="tpu_custom_call" | custom-call | flops 4294967296 | bytes 100000000 | tf_op jit(solution)/shard_map/pallas_call | solution.py:374
  60.0 9.8 %collective-permute-done.7.across = bf16[2,512,512]{2,1,0:T(8,128)(2,1)S(1)} collective-permute-done((bf16[2,512,512]{2,1,0:T(8,128)(2,1)S(1)}, bf16[2,512,512]{2,1,0:T(8,128)(2,1)S(1)}, u32[]{:S(2)}, u32[]{:S(2)}) %collective-permute-start.7) | collective-permute-done | bytes 1048608 | tf_op jit(solution)/shard_map/ppermute | solution.py:557
  69.8 6.0 %all-to-all-start = ((bf16[8,2,64,512]{3,2,1,0:T(8,128)(2,1)}), bf16[8,2,64,512]{3,2,1,0:T(8,128)(2,1)S(1)}, u32[]{:S(2)}, u32[]{:S(2)}) async-start(bf16[8,2,64,512]{3,2,1,0:T(8,128)(2,1)} %get-tuple-element.54), calls=%async_computation | async-start | bytes 2097152 | tf_op jit(solution)/shard_map/all_to_all | solution.py:590
  75.8 12.5 %shard_map.100 = (bf16[8,2,64,512]{3,2,1,0:T(8,128)(2,1)}, f32[512,512]{1,0:T(8,128)}, bf16[512,512]{1,0:T(8,128)(2,1)}) custom-call(s32[8,4]{1,0:T(8,128)} %bitcast.10, s32[2]{0:T(128)} %copy-done.7, s32[2]{0:T(128)} %copy-done.7, bf16[2,512,3072]{2,1,0:T(8,128)(2,1)} %band.3, bf16[2,2,512,512]{3,2,1,0:T(8,128)(2,1)} %collective-permute-done.4.sibling, ...), custom_call_target="tpu_custom_call" | custom-call | flops 4294967296 | bytes 100000000 | tf_op jit(solution)/shard_map/pallas_call | solution.py:374
  88.3 13.0 %all-to-all-done.first = bf16[8,2,64,512]{3,2,1,0:T(8,128)(2,1)S(1)} async-done(((bf16[8,2,64,512]{3,2,1,0:T(8,128)(2,1)}), bf16[8,2,64,512]{3,2,1,0:T(8,128)(2,1)S(1)}, u32[]{:S(2)}, u32[]{:S(2)}) %all-to-all-start) | async-done | bytes 1048608 | tf_op jit(solution)/shard_map/all_to_all | solution.py:590
  101.3 3.6 %all-to-all-start.1 = ((bf16[8,2,64,512]{3,2,1,0:T(8,128)(2,1)}), bf16[8,2,64,512]{3,2,1,0:T(8,128)(2,1)S(1)}, u32[]{:S(2)}, u32[]{:S(2)}) async-start(bf16[8,2,64,512]{3,2,1,0:T(8,128)(2,1)} %get-tuple-element.56), calls=%async_computation.1 | async-start | bytes 2097152 | tf_op jit(solution)/shard_map/all_to_all | solution.py:595
  111.0 6.8 %collective-permute-done.9 = bf16[256,512]{1,0:T(8,128)(2,1)S(1)} collective-permute-done((bf16[256,512]{1,0:T(8,128)(2,1)S(1)}, bf16[256,512]{1,0:T(8,128)(2,1)S(1)}, u32[]{:S(2)}, u32[]{:S(2)}) %collective-permute-start.9) | collective-permute-done | bytes 262176 | tf_op jit(solution)/shard_map/ppermute | solution.py:557
  119.0 11.7 %all-to-all-done.1.second = bf16[8,2,64,512]{3,2,1,0:T(8,128)(2,1)S(1)} async-done(((bf16[8,2,64,512]{3,2,1,0:T(8,128)(2,1)}), bf16[8,2,64,512]{3,2,1,0:T(8,128)(2,1)S(1)}, u32[]{:S(2)}, u32[]{:S(2)}) %all-to-all-start.1) | async-done | bytes 1048608 | tf_op jit(solution)/shard_map/all_to_all | solution.py:595
  130.7 4.9 %shard_map.101 = (f32[2,64,3072]{2,1,0:T(8,128)S(1)}, f32[2,64,3072]{2,1,0:T(8,128)S(1)}, bf16[2,64,3072]{2,1,0:T(8,128)(2,1)S(1)}, bf16[2,64,3072]{2,1,0:T(8,128)(2,1)}) custom-call(s32[16,4]{1,0:T(8,128)S(1)} %copy-done.9, s32[2]{0:T(128)S(1)} %copy-done.8, bf16[8,2,64,512]{3,2,1,0:T(8,128)(2,1)S(1)} %all-to-all-done.first, ...), custom_call_target="tpu_custom_call" | custom-call | flops 4194304 | bytes 6815744 | tf_op jit(solution)/shard_map/pallas_call | solution.py:446
  138.0 5.9 %collective-permute-done.13 = bf16[128,512]{1,0:T(8,128)(2,1)S(1)} collective-permute-done((bf16[128,512]{1,0:T(8,128)(2,1)S(1)}, bf16[128,512]{1,0:T(8,128)(2,1)S(1)}, u32[]{:S(2)}, u32[]{:S(2)}) %collective-permute-start.13) | collective-permute-done | bytes 131104 | tf_op jit(solution)/shard_map/ppermute | solution.py:560
  145.0 2.8 %add_convert_fusion = bf16[2,64,3072]{2,1,0:T(8,128)(2,1)} fusion(f32[2,64,3072]{2,1,0:T(8,128)} %copy-done.3, bf16[2,64,3072]{2,1,0:T(8,128)(2,1)} %copy-done.14), kind=kLoop, calls=%fused_computation.2 | loop fusion | flops 1179648 | bytes 3145728 | tf_op jit(solution)/shard_map/convert_element_type | solution.py:608
  151.4 2.6 collective-permute-done.15
  155.4 2.6 collective-permute-done.16
  158.0 9.9 %collective-permute-done.12 = bf16[2,64,3072]{2,1,0:T(8,128)(2,1)S(1)} collective-permute-done((bf16[2,64,3072]{2,1,0:T(8,128)(2,1)}, bf16[2,64,3072]{2,1,0:T(8,128)(2,1)S(1)}, u32[]{:S(2)}, u32[]{:S(2)}) %collective-permute-start.12) | collective-permute-done | bytes 786464 | tf_op jit(solution)/shard_map/ppermute | solution.py:557
  171.0 4.6 %collective-permute-start.18 = (bf16[2,64,3072]{2,1,0:T(8,128)(2,1)S(1)}, bf16[2,64,3072]{2,1,0:T(8,128)(2,1)S(1)}, u32[]{:S(2)}, u32[]{:S(2)}) collective-permute-start(bf16[2,64,3072]{2,1,0:T(8,128)(2,1)S(1)} %subtract_convert_fusion.refs_0_), channel_id=1, source_target_pairs={{0,8},{4,12},{8,16},{12,20},{16,24},{20,28},{1,9},{5,13},{9,17},{1... | collective-permute-start | bytes 2359304 | tf_op jit(solution)/shard_map/ppermute | solution.py:508
  177.3 13.5 %collective-permute-done.19.refs_4_ = bf16[2,64,3072]{2,1,0:T(8,128)(2,1)S(1)} collective-permute-done((bf16[2,64,3072]{2,1,0:T(8,128)(2,1)S(1)}, bf16[2,64,3072]{2,1,0:T(8,128)(2,1)S(1)}, u32[]{:S(2)}, u32[]{:S(2)}) %collective-permute-start.19) | collective-permute-done | bytes 786464 | tf_op jit(solution)/shard_map/ppermute | solution.py:508
  191.9 2.3 collective-permute-done.17.refs_7_
  199.0 14.4 %collective-permute-done.20.refs_8_ = bf16[2,64,3072]{2,1,0:T(8,128)(2,1)} collective-permute-done((bf16[2,64,3072]{2,1,0:T(8,128)(2,1)}, bf16[2,64,3072]{2,1,0:T(8,128)(2,1)}, u32[]{:S(2)}, u32[]{:S(2)}) %collective-permute-start.20) | collective-permute-done | bytes 786464 | tf_op jit(solution)/shard_map/ppermute | solution.py:511
  213.4 6.1 %collective-permute-done.22.refs_5_ = bf16[2,64,3072]{2,1,0:T(8,128)(2,1)} collective-permute-done((bf16[2,64,3072]{2,1,0:T(8,128)(2,1)S(1)}, bf16[2,64,3072]{2,1,0:T(8,128)(2,1)}, u32[]{:S(2)}, u32[]{:S(2)}) %collective-permute-start.22) | collective-permute-done | bytes 786464 | tf_op jit(solution)/shard_map/ppermute | solution.py:508
  226.4 3.6 %collective-permute-start.27 = (bf16[128,512]{1,0:T(8,128)(2,1)S(1)}, bf16[128,512]{1,0:T(8,128)(2,1)S(1)}, u32[]{:S(2)}, u32[]{:S(2)}) collective-permute-start(bf16[128,512]{1,0:T(8,128)(2,1)S(1)} %maximum_select_fusion.3), channel_id=1, source_target_pairs={{0,8},{4,12},{8,0},{12,4},{16,24},{20,28},{24,16},{28,20},{1,9},{5... | collective-permute-start | bytes 393224 | tf_op jit(solution)/shard_map/ppermute | solution.py:560
  230.0 15.1 %collective-permute-done.27 = bf16[128,512]{1,0:T(8,128)(2,1)S(1)} collective-permute-done((bf16[128,512]{1,0:T(8,128)(2,1)S(1)}, bf16[128,512]{1,0:T(8,128)(2,1)S(1)}, u32[]{:S(2)}, u32[]{:S(2)}) %collective-permute-start.27) | collective-permute-done | bytes 131104 | tf_op jit(solution)/shard_map/ppermute | solution.py:560
  246.5 5.1 %collective-permute-done.28 = bf16[256,512]{1,0:T(8,128)(2,1)} collective-permute-done((bf16[256,512]{1,0:T(8,128)(2,1)S(1)}, bf16[256,512]{1,0:T(8,128)(2,1)}, u32[]{:S(2)}, u32[]{:S(2)}) %collective-permute-start.28) | collective-permute-done | bytes 262176 | tf_op jit(solution)/shard_map/ppermute | solution.py:557
  257.2 2.2 collective-permute-done.30
  261.2 8.0 %collective-permute-done.29.refs_10_ = bf16[2,64,3072]{2,1,0:T(8,128)(2,1)} collective-permute-done((bf16[2,64,3072]{2,1,0:T(8,128)(2,1)}, bf16[2,64,3072]{2,1,0:T(8,128)(2,1)}, u32[]{:S(2)}, u32[]{:S(2)}) %collective-permute-start.29) | collective-permute-done | bytes 786464 | tf_op jit(solution)/shard_map/ppermute | solution.py:511
  270.9 5.1 %shard_map.102 = bf16[2,512,3072]{2,1,0:T(8,128)(2,1)} custom-call(s32[2]{0:T(128)S(1)} %copy-done.8, bf16[2,64,3072]{2,1,0:T(8,128)(2,1)S(1)} %subtract_convert_fusion.refs_0_, bf16[2,64,3072]{2,1,0:T(8,128)(2,1)S(1)} %collective-permute-done.18.refs_1_, bf16[2,64,3072]{2,1,0:T(8,128)(2,1)S(1)} %collective-permute-done.21.refs_2_, ...), custom_call_target="tpu_custom_call" | custom-call | bytes 12582912 | tf_op jit(solution)/shard_map/pallas_call | solution.py:531
  (104 shorter events, 63.0 us)
Async XLA Ops:
  12.9 7.0 %collective-permute-start.5 = (bf16[1,2,512,512]{3,2,1,0:T(8,128)(2,1)S(1)}, bf16[1,2,512,512]{3,2,1,0:T(8,128)(2,1)S(1)}, u32[]{:S(2)}, u32[]{:S(2)}) collective-permute-start(bf16[1,2,512,512]{3,2,1,0:T(8,128)(2,1)S(1)} %shard_map.97), channel_id=1, source_target_pairs={{0,1},{1,0},{2,3},{3,2},{4,5},{5,4},{6,7},{7,6},{8,9},{9,8},{10,11... | collective-permute-start | bytes 3145736 | tf_op jit(solution)/shard_map/ppermute | solution.py:557
  19.4 28.5 %collective-permute-start.4 = (bf16[2,2,512,512]{3,2,1,0:T(8,128)(2,1)}, bf16[2,2,512,512]{3,2,1,0:T(8,128)(2,1)}, u32[]{:S(2)}, u32[]{:S(2)}) collective-permute-start(bf16[2,2,512,512]{3,2,1,0:T(8,128)(2,1)} %get-tuple-element.45), channel_id=1, source_target_pairs={{0,1},{1,0},{2,3},{3,2},{4,5},{5,4},{6,7},{7,6},{8,9},{9,8},{10,11... | collective-permute-start | bytes 6291464 | tf_op jit(solution)/shard_map/ppermute | solution.py:557
  19.6 5.5 %collective-permute-start = (bf16[1,2,512,512]{3,2,1,0:T(8,128)(2,1)S(1)}, bf16[1,2,512,512]{3,2,1,0:T(8,128)(2,1)S(1)}, u32[]{:S(2)}, u32[]{:S(2)}) collective-permute-start(bf16[1,2,512,512]{3,2,1,0:T(8,128)(2,1)S(1)} %get-tuple-element.43), channel_id=1, source_target_pairs={{0,1},{1,0},{2,3},{3,2},{4,5},{5,4},{6,7},{7,6},{8,9},{9,8},{10,11... | collective-permute-start | bytes 3145736 | tf_op jit(solution)/shard_map/ppermute | solution.py:557
  21.7 26.1 %collective-permute-start.6 = (bf16[2,512,512]{2,1,0:T(8,128)(2,1)S(1)}, bf16[2,512,512]{2,1,0:T(8,128)(2,1)}, u32[]{:S(2)}, u32[]{:S(2)}) collective-permute-start(bf16[2,512,512]{2,1,0:T(8,128)(2,1)S(1)} %shard_map.98), channel_id=1, source_target_pairs={{0,2},{1,3},{2,0},{3,1},{4,6},{5,7},{6,4},{7,5},{8,10},{9,11},{10,... | collective-permute-start | bytes 3145736 | tf_op jit(solution)/shard_map/ppermute | solution.py:557
  26.9 42.9 %collective-permute-start.7 = (bf16[2,512,512]{2,1,0:T(8,128)(2,1)S(1)}, bf16[2,512,512]{2,1,0:T(8,128)(2,1)S(1)}, u32[]{:S(2)}, u32[]{:S(2)}) collective-permute-start(bf16[2,512,512]{2,1,0:T(8,128)(2,1)S(1)} %shard_map.96), channel_id=1, source_target_pairs={{0,2},{1,3},{2,0},{3,1},{4,6},{5,7},{6,4},{7,5},{8,10},{9,11},{10,... | collective-permute-start | bytes 3145736 | tf_op jit(solution)/shard_map/ppermute | solution.py:557
  28.9 3.6 %collective-permute-start.1 = (s32[2,4]{0,1:T(4,128)S(1)}, s32[2,4]{0,1:T(4,128)S(1)}, u32[]{:S(2)}, u32[]{:S(2)}) collective-permute-start(s32[2,4]{0,1:T(4,128)S(1)} %pad_add_fusion), channel_id=1, source_target_pairs={{0,4},{4,0},{8,12},{12,8},{16,20},{20,16},{24,28},{28,24},{1,5},{5... | collective-permute-start | bytes 104 | tf_op jit(solution)/shard_map/ppermute | solution.py:560
  32.6 3.6 %collective-permute-start.2 = (s32[4,4]{0,1:T(4,128)S(1)}, s32[4,4]{0,1:T(4,128)S(1)}, u32[]{:S(2)}, u32[]{:S(2)}) collective-permute-start(s32[4,4]{0,1:T(4,128)S(1)} %add_select_fusion), channel_id=1, source_target_pairs={{0,8},{4,12},{8,0},{12,4},{16,24},{20,28},{24,16},{28,20},{1,9},{5... | collective-permute-start | bytes 200 | tf_op jit(solution)/shard_map/ppermute | solution.py:560
  36.3 4.5 %collective-permute-start.3 = (s32[8,4]{0,1:T(4,128)S(1)}, s32[8,4]{0,1:T(4,128)S(1)}, u32[]{:S(2)}, u32[]{:S(2)}) collective-permute-start(s32[8,4]{0,1:T(4,128)S(1)} %add_select_fusion.1), channel_id=1, source_target_pairs={{0,16},{4,20},{8,24},{12,28},{16,0},{20,4},{24,8},{28,12},{1,17},{... | collective-permute-start | bytes 392 | tf_op jit(solution)/shard_map/ppermute | solution.py:560
  69.8 31.5 %all-to-all-start = ((bf16[8,2,64,512]{3,2,1,0:T(8,128)(2,1)}), bf16[8,2,64,512]{3,2,1,0:T(8,128)(2,1)S(1)}, u32[]{:S(2)}, u32[]{:S(2)}) async-start(bf16[8,2,64,512]{3,2,1,0:T(8,128)(2,1)} %get-tuple-element.54), calls=%async_computation | async-start | bytes 2097152 | tf_op jit(solution)/shard_map/all_to_all | solution.py:590
  101.3 29.3 %all-to-all-start.1 = ((bf16[8,2,64,512]{3,2,1,0:T(8,128)(2,1)}), bf16[8,2,64,512]{3,2,1,0:T(8,128)(2,1)S(1)}, u32[]{:S(2)}, u32[]{:S(2)}) async-start(bf16[8,2,64,512]{3,2,1,0:T(8,128)(2,1)} %get-tuple-element.56), calls=%async_computation.1 | async-start | bytes 2097152 | tf_op jit(solution)/shard_map/all_to_all | solution.py:595
  104.9 2.3 collective-permute-start.8
  109.4 8.4 %collective-permute-start.9 = (bf16[256,512]{1,0:T(8,128)(2,1)S(1)}, bf16[256,512]{1,0:T(8,128)(2,1)S(1)}, u32[]{:S(2)}, u32[]{:S(2)}) collective-permute-start(bf16[256,512]{1,0:T(8,128)(2,1)S(1)} %dynamic-slice_convert_fusion), channel_id=1, source_target_pairs={{0,2},{1,3},{2,0},{3,1},{4,6},{5,7},{6,4},{7,5},{8,10},{9,11},{10,... | collective-permute-start | bytes 786440 | tf_op jit(solution)/shard_map/ppermute | solution.py:557
  137.8 6.2 %collective-permute-start.11 = (bf16[2,64,3072]{2,1,0:T(8,128)(2,1)S(1)}, bf16[2,64,3072]{2,1,0:T(8,128)(2,1)S(1)}, u32[]{:S(2)}, u32[]{:S(2)}) collective-permute-start(bf16[2,64,3072]{2,1,0:T(8,128)(2,1)S(1)} %get-tuple-element.60), channel_id=1, source_target_pairs={{0,1},{1,0},{2,3},{3,2},{4,5},{5,4},{6,7},{7,6},{8,9},{9,8},{10,11... | collective-permute-start | bytes 2359304 | tf_op jit(solution)/shard_map/ppermute | solution.py:557
  137.9 6.0 %collective-permute-start.13 = (bf16[128,512]{1,0:T(8,128)(2,1)S(1)}, bf16[128,512]{1,0:T(8,128)(2,1)S(1)}, u32[]{:S(2)}, u32[]{:S(2)}) collective-permute-start(bf16[128,512]{1,0:T(8,128)(2,1)S(1)} %dynamic-slice_convert_fusion.1), channel_id=1, source_target_pairs={{0,8},{4,12},{8,0},{12,4},{16,24},{20,28},{24,16},{28,20},{1,9},{5... | collective-permute-start | bytes 393224 | tf_op jit(solution)/shard_map/ppermute | solution.py:560
  143.9 6.0 %collective-permute-start.14 = (bf16[64,512]{1,0:T(8,128)(2,1)S(1)}, bf16[64,512]{1,0:T(8,128)(2,1)S(1)}, u32[]{:S(2)}, u32[]{:S(2)}) collective-permute-start(bf16[64,512]{1,0:T(8,128)(2,1)S(1)} %dynamic-slice_convert_fusion.2), channel_id=1, source_target_pairs={{0,16},{4,20},{8,24},{12,28},{16,0},{20,4},{24,8},{28,12},{1,17},{... | collective-permute-start | bytes 196616 | tf_op jit(solution)/shard_map/ppermute | solution.py:560
  144.0 14.0 %collective-permute-start.10 = (bf16[2,64,3072]{2,1,0:T(8,128)(2,1)}, bf16[2,64,3072]{2,1,0:T(8,128)(2,1)}, u32[]{:S(2)}, u32[]{:S(2)}) collective-permute-start(bf16[2,64,3072]{2,1,0:T(8,128)(2,1)} %get-tuple-element.58), channel_id=1, source_target_pairs={{0,1},{1,0},{2,3},{3,2},{4,5},{5,4},{6,7},{7,6},{8,9},{9,8},{10,11... | collective-permute-start | bytes 2359304 | tf_op jit(solution)/shard_map/ppermute | solution.py:557
  147.7 20.1 %collective-permute-start.12 = (bf16[2,64,3072]{2,1,0:T(8,128)(2,1)}, bf16[2,64,3072]{2,1,0:T(8,128)(2,1)S(1)}, u32[]{:S(2)}, u32[]{:S(2)}) collective-permute-start(bf16[2,64,3072]{2,1,0:T(8,128)(2,1)} %add_convert_fusion), channel_id=1, source_target_pairs={{0,2},{1,3},{2,0},{3,1},{4,6},{5,7},{6,4},{7,5},{8,10},{9,11},{10,... | collective-permute-start | bytes 2359304 | tf_op jit(solution)/shard_map/ppermute | solution.py:557
  150.0 4.0 %collective-permute-start.15 = (bf16[32,512]{1,0:T(8,128)(2,1)S(1)}, bf16[32,512]{1,0:T(8,128)(2,1)S(1)}, u32[]{:S(2)}, u32[]{:S(2)}) collective-permute-start(bf16[32,512]{1,0:T(8,128)(2,1)S(1)} %dynamic-slice_convert_fusion.3), channel_id=1, source_target_pairs={{0,4},{4,0},{8,12},{12,8},{16,20},{20,16},{24,28},{28,24},{1,5},{5... | collective-permute-start | bytes 98312 | tf_op jit(solution)/shard_map/ppermute | solution.py:560
  154.0 4.0 %collective-permute-start.16 = (bf16[32,512]{1,0:T(8,128)(2,1)S(1)}, bf16[32,512]{1,0:T(8,128)(2,1)S(1)}, u32[]{:S(2)}, u32[]{:S(2)}) collective-permute-start(bf16[32,512]{1,0:T(8,128)(2,1)S(1)} %add_convert_fusion.1), channel_id=1, source_target_pairs={{0,4},{4,0},{8,12},{12,8},{16,20},{20,16},{24,28},{28,24},{1,5},{5... | collective-permute-start | bytes 98312 | tf_op jit(solution)/shard_map/ppermute | solution.py:560
  169.7 21.0 %collective-permute-start.19 = (bf16[2,64,3072]{2,1,0:T(8,128)(2,1)S(1)}, bf16[2,64,3072]{2,1,0:T(8,128)(2,1)S(1)}, u32[]{:S(2)}, u32[]{:S(2)}) collective-permute-start(bf16[2,64,3072]{2,1,0:T(8,128)(2,1)S(1)} %subtract_convert_fusion.refs_0_), channel_id=1, source_target_pairs={{8,0},{12,4},{16,8},{20,12},{24,16},{28,20},{9,1},{13,5},{17,9},{2... | collective-permute-start | bytes 2359304 | tf_op jit(solution)/shard_map/ppermute | solution.py:508
  171.0 20.9 %collective-permute-start.18 = (bf16[2,64,3072]{2,1,0:T(8,128)(2,1)S(1)}, bf16[2,64,3072]{2,1,0:T(8,128)(2,1)S(1)}, u32[]{:S(2)}, u32[]{:S(2)}) collective-permute-start(bf16[2,64,3072]{2,1,0:T(8,128)(2,1)S(1)} %subtract_convert_fusion.refs_0_), channel_id=1, source_target_pairs={{0,8},{4,12},{8,16},{12,20},{16,24},{20,28},{1,9},{5,13},{9,17},{1... | collective-permute-start | bytes 2359304 | tf_op jit(solution)/shard_map/ppermute | solution.py:508
  175.6 18.7 %collective-permute-start.17 = (bf16[2,64,3072]{2,1,0:T(8,128)(2,1)S(1)}, bf16[2,64,3072]{2,1,0:T(8,128)(2,1)S(1)}, u32[]{:S(2)}, u32[]{:S(2)}) collective-permute-start(bf16[2,64,3072]{2,1,0:T(8,128)(2,1)S(1)} %subtract_convert_fusion.refs_0_), channel_id=1, source_target_pairs={{0,4},{4,0},{8,12},{12,8},{16,20},{20,16},{24,28},{28,24},{1,5},{5... | collective-permute-start | bytes 2359304 | tf_op jit(solution)/shard_map/ppermute | solution.py:511
  195.4 18.0 %collective-permute-start.20 = (bf16[2,64,3072]{2,1,0:T(8,128)(2,1)}, bf16[2,64,3072]{2,1,0:T(8,128)(2,1)}, u32[]{:S(2)}, u32[]{:S(2)}) collective-permute-start(bf16[2,64,3072]{2,1,0:T(8,128)(2,1)} %broadcast_select_fusion.1), channel_id=1, source_target_pairs={{0,4},{4,0},{8,12},{12,8},{16,20},{20,16},{24,28},{28,24},{1,5},{5... | collective-permute-start | bytes 2359304 | tf_op jit(solution)/shard_map/ppermute | solution.py:511
  197.0 16.4 %collective-permute-start.21 = (bf16[2,64,3072]{2,1,0:T(8,128)(2,1)S(1)}, bf16[2,64,3072]{2,1,0:T(8,128)(2,1)S(1)}, u32[]{:S(2)}, u32[]{:S(2)}) collective-permute-start(bf16[2,64,3072]{2,1,0:T(8,128)(2,1)S(1)} %collective-permute-done.18.refs_1_), channel_id=1, source_target_pairs={{8,16},{12,20},{16,24},{20,28},{9,17},{13,21},{17,25},{21,29},{10,... | collective-permute-start | bytes 2359304 | tf_op jit(solution)/shard_map/ppermute | solution.py:508
  197.7 21.8 %collective-permute-start.22 = (bf16[2,64,3072]{2,1,0:T(8,128)(2,1)S(1)}, bf16[2,64,3072]{2,1,0:T(8,128)(2,1)}, u32[]{:S(2)}, u32[]{:S(2)}) collective-permute-start(bf16[2,64,3072]{2,1,0:T(8,128)(2,1)S(1)} %collective-permute-done.19.refs_4_), channel_id=1, source_target_pairs={{8,0},{12,4},{16,8},{20,12},{9,1},{13,5},{17,9},{21,13},{10,2},{14... | collective-permute-start | bytes 2359304 | tf_op jit(solution)/shard_map/ppermute | solution.py:508
  219.6 6.8 %collective-permute-start.26 = (bf16[64,512]{1,0:T(8,128)(2,1)S(1)}, bf16[64,512]{1,0:T(8,128)(2,1)S(1)}, u32[]{:S(2)}, u32[]{:S(2)}) collective-permute-start(bf16[64,512]{1,0:T(8,128)(2,1)S(1)} %maximum_select_fusion.4), channel_id=1, source_target_pairs={{0,16},{4,20},{8,24},{12,28},{16,0},{20,4},{24,8},{28,12},{1,17},{... | collective-permute-start | bytes 196616 | tf_op jit(solution)/shard_map/ppermute | solution.py:560
  222.8 30.8 %collective-permute-start.23 = (bf16[2,64,3072]{2,1,0:T(8,128)(2,1)}, bf16[2,64,3072]{2,1,0:T(8,128)(2,1)}, u32[]{:S(2)}, u32[]{:S(2)}) collective-permute-start(bf16[2,64,3072]{2,1,0:T(8,128)(2,1)} %broadcast_select_fusion), channel_id=1, source_target_pairs={{0,4},{4,0},{8,12},{12,8},{16,20},{20,16},{24,28},{28,24},{1,5},{5... | collective-permute-start | bytes 2359304 | tf_op jit(solution)/shard_map/ppermute | solution.py:511
  223.5 30.1 %collective-permute-start.24 = (bf16[2,64,3072]{2,1,0:T(8,128)(2,1)S(1)}, bf16[2,64,3072]{2,1,0:T(8,128)(2,1)}, u32[]{:S(2)}, u32[]{:S(2)}) collective-permute-start(bf16[2,64,3072]{2,1,0:T(8,128)(2,1)S(1)} %collective-permute-done.21.refs_2_), channel_id=1, source_target_pairs={{16,24},{20,28},{17,25},{21,29},{18,26},{22,30},{19,27},{23,31}} | collective-permute-start | bytes 2359304 | tf_op jit(solution)/shard_map/ppermute | solution.py:508
  225.0 28.6 %collective-permute-start.25 = (bf16[2,64,3072]{2,1,0:T(8,128)(2,1)}, bf16[2,64,3072]{2,1,0:T(8,128)(2,1)}, u32[]{:S(2)}, u32[]{:S(2)}) collective-permute-start(bf16[2,64,3072]{2,1,0:T(8,128)(2,1)} %collective-permute-done.22.refs_5_), channel_id=1, source_target_pairs={{8,0},{12,4},{9,1},{13,5},{10,2},{14,6},{11,3},{15,7}} | collective-permute-start | bytes 2359304 | tf_op jit(solution)/shard_map/ppermute | solution.py:508
  226.4 18.7 %collective-permute-start.27 = (bf16[128,512]{1,0:T(8,128)(2,1)S(1)}, bf16[128,512]{1,0:T(8,128)(2,1)S(1)}, u32[]{:S(2)}, u32[]{:S(2)}) collective-permute-start(bf16[128,512]{1,0:T(8,128)(2,1)S(1)} %maximum_select_fusion.3), channel_id=1, source_target_pairs={{0,8},{4,12},{8,0},{12,4},{16,24},{20,28},{24,16},{28,20},{1,9},{5... | collective-permute-start | bytes 393224 | tf_op jit(solution)/shard_map/ppermute | solution.py:560
  245.1 6.5 %collective-permute-start.28 = (bf16[256,512]{1,0:T(8,128)(2,1)S(1)}, bf16[256,512]{1,0:T(8,128)(2,1)}, u32[]{:S(2)}, u32[]{:S(2)}) collective-permute-start(bf16[256,512]{1,0:T(8,128)(2,1)S(1)} %maximum_select_fusion.2), channel_id=1, source_target_pairs={{0,2},{1,3},{2,0},{3,1},{4,6},{5,7},{6,4},{7,5},{8,10},{9,11},{10,... | collective-permute-start | bytes 786440 | tf_op jit(solution)/shard_map/ppermute | solution.py:557
  255.8 13.4 %collective-permute-start.29 = (bf16[2,64,3072]{2,1,0:T(8,128)(2,1)}, bf16[2,64,3072]{2,1,0:T(8,128)(2,1)}, u32[]{:S(2)}, u32[]{:S(2)}) collective-permute-start(bf16[2,64,3072]{2,1,0:T(8,128)(2,1)} %select_select_fusion), channel_id=1, source_target_pairs={{0,4},{4,0},{8,12},{12,8},{16,20},{20,16},{24,28},{28,24},{1,5},{5... | collective-permute-start | bytes 2359304 | tf_op jit(solution)/shard_map/ppermute | solution.py:511
  (16 other events, 155.9 us)

commit v10 on v9

--- a/solution.py
+++ b/solution.py
@@ -609,15 +609,14 @@
     )
     for bit in halving:
         term = halved(term, my_class // bit % 2, pat_flip(bit))
-    term = doubled(term.astype(jnp.bfloat16), my_class % 2, pat_flip(1))
+    term = term.astype(jnp.bfloat16)
+    for bit in reversed(halving):
+        term = doubled(term, my_class // bit % 2, pat_flip(bit))
     total = own_near + from_sibling.astype(jnp.float32) + from_across.astype(jnp.float32)
     mine = lax.dynamic_slice_in_dim(object_image, my_class * height, height, 1)
     updated = (mine.astype(jnp.float32) - OBJECT_RATE * total).astype(jnp.bfloat16)
     updated, term = lax.optimization_barrier((updated, term))
-    steps = [
-        functools.partial(doubled, bit=my_class // bit % 2, other=pat_flip(bit)) for bit in reversed(bits[1:])
-    ]
-    steps.append(functools.partial(doubled, bit=line, other=lambda value: flip(value, 2)))
+    steps = [functools.partial(doubled, bit=line, other=lambda value: flip(value, 2))]
     steps.append(lambda part: doubled(part[None], core, lambda value: flip(value, 1)))
     if classes in BY_PERMUTE:
         object_next, term = gather_classes(updated, me, classes, term, steps)

time: 277 us -> 269 us (0.971)
  waiting for transfers between devices: 147 us -> 141 us
  starting transfers between devices: 47.9 us -> 43.7 us
    ppermute x4, waiting for transfers between devices: 24.7 us -> 33 us  [over(): return lax.ppermute(value, 'pat', [(k, k ^ 1) for k in range(classes)])]
    ppermute x9, waiting for transfers between devices: 33.6 us -> 25.6 us  [pat_flip(): lax.ppermute(value, 'pat', [(k, k ^ bit) for k in range(classes)])]
    ppermute x12, waiting for transfers between devices: 43.6 us -> 36.5 us  [flip(): return lax.ppermute(value, 'obj', [(k, k ^ bit) for k in range(owners)])]
    ppermute x9, starting transfers between devices: 12.7 us -> 9.77 us  [pat_flip(): lax.ppermute(value, 'pat', [(k, k ^ bit) for k in range(classes)])]
    unnamed x32 -> x34, local copies, waits for them, and re-layouts: 8.58 us -> 8.6 us
  transfers between devices with their start and end apart: 33 -> 33, of which waited for: 24 -> 25; matrix products, arithmetic and copies ran while one was open for 4% -> 4% of each run, Pallas kernels for 12% -> 15%
where the time goes in v10:
time: 269 us; the launch traced here: 268 us
  waiting for transfers between devices  141 us (52%)
  Pallas kernels  46 us (17%)
  starting transfers between devices  43.7 us (16%)
  other arithmetic  20.6 us (8%)
  local copies, waits for them, and re-layouts  8.95 us (3%)
  blocking collectives  5.99 us (2%)
    ppermute x12, waiting for transfers between devices, flip(): return lax.ppermute(value, 'obj', [(k, k ^ bit) for k in range(owners)])  36.5 us
    ppermute x4, waiting for transfers between devices, over(): return lax.ppermute(value, 'pat', [(k, k ^ 1) for k in range(classes)])  33 us
    ppermute x9, waiting for transfers between devices, pat_flip(): lax.ppermute(value, 'pat', [(k, k ^ bit) for k in range(classes)])  25.6 us
    pallas_call x2, Pallas kernels, wave(): pl.pallas_call(functools.partial(wave_kernel, which), in_specs=[smem, sme...  24.6 us
    ppermute x6, waiting for transfers between devices, along(): return lax.ppermute(value, 'pat', pairs)  23.3 us
    all_to_all x1, waiting for transfers between devices, shards(): lax.all_to_all(grad_0, 'pat', split_axis=0, concat_axis=0, tiled=True)  13 us
    ppermute x6, starting transfers between devices, along(): return lax.ppermute(value, 'pat', pairs)  10.7 us
    ppermute x12, starting transfers between devices, flip(): return lax.ppermute(value, 'obj', [(k, k ^ bit) for k in range(owners)])  9.77 us
  transfers between devices with their start and end apart: 33, of which 25 were waited for; matrix products, arithmetic and copies ran while one was open for 4% of the time, Pallas kernels for 15%

profile of v10, /device:TPU:0, one launch (start us, length us, event | category | flops | bytes accessed | tf_op | source)
XLA Modules:
  0.0 267.6 jit_solution(8456673916462151457)
XLA Ops:
  2.3 6.0 %all-gather = s32[4,2,4]{2,1,0:T(2,128)S(1)} all-gather(s32[1,2,4]{2,1,0:T(2,128)S(1)} %bitcast.11), channel_id=1, replica_groups=mesh['pat'=8,'obj'=4] {'obj'}, dimensions={0}, use_global_device_ids=true | all-gather | bytes 160 | tf_op jit(solution)/shard_map/all_gather | solution.py:574
  8.4 2.8 %copy-done = bf16[2,512,3072]{2,1,0:T(8,128)(2,1)S(1)} copy-done((bf16[2,512,3072]{2,1,0:T(8,128)(2,1)S(1)}, bf16[2,512,3072]{2,1,0:T(8,128)(2,1)}, u32[]{:S(2)}) %copy-start) | copy-done | bytes 6291480
  13.3 6.0 %shard_map.95 = (bf16[1,2,512,512]{3,2,1,0:T(8,128)(2,1)S(1)}, bf16[2,2,512,512]{3,2,1,0:T(8,128)(2,1)}) custom-call(s32[8,4]{1,0:T(8,128)S(1)} %bitcast.6, s32[2]{0:T(128)S(1)} %pad_add_fusion.3.me.spare, bf16[2,512,3072]{2,1,0:T(8,128)(2,1)S(1)} %copy-done, bf16[2,512,3072]{2,1,0:T(8,128)(2,1)S(1)} %copy-done, bf16[2,512,3072]{2,1,0:T(8,128)(2,1)S(1)} %copy-done, ...), custom_call_target="tpu_custom_call" | custom-call | flops 1966080 | bytes 7000000 | tf_op jit(solution)/shard_map/pallas_call | solution.py:195
  33.9 2.3 collective-permute-done.2
  36.3 2.6 collective-permute-start.3
  41.6 6.2 %collective-permute-done.6.across = bf16[2,512,512]{2,1,0:T(8,128)(2,1)} collective-permute-done((bf16[2,512,512]{2,1,0:T(8,128)(2,1)S(1)}, bf16[2,512,512]{2,1,0:T(8,128)(2,1)}, u32[]{:S(2)}, u32[]{:S(2)}) %collective-permute-start.6) | collective-permute-done | bytes 1048608 | tf_op jit(solution)/shard_map/ppermute | solution.py:557
  47.8 12.2 %shard_map.99 = (bf16[8,2,64,512]{3,2,1,0:T(8,128)(2,1)}, f32[2,512,512]{2,1,0:T(8,128)}) custom-call(s32[8,4]{1,0:T(8,128)} %bitcast.9, s32[2]{0:T(128)} %copy-done.7, s32[16,4]{1,0:T(8,128)} %broadcast_select_fusion.2.spare.pos, bf16[2,512,3072]{2,1,0:T(8,128)(2,1)} %band.3, bf16[2,2,512,512]{3,2,1,0:T(8,128)(2,1)} %collective-permute-done.4.sibling, ...), custom_call_target="tpu_custom_call" | custom-call | flops 4294967296 | bytes 100000000 | tf_op jit(solution)/shard_map/pallas_call | solution.py:374
  60.0 9.8 %collective-permute-done.7.across = bf16[2,512,512]{2,1,0:T(8,128)(2,1)S(1)} collective-permute-done((bf16[2,512,512]{2,1,0:T(8,128)(2,1)S(1)}, bf16[2,512,512]{2,1,0:T(8,128)(2,1)S(1)}, u32[]{:S(2)}, u32[]{:S(2)}) %collective-permute-start.7) | collective-permute-done | bytes 1048608 | tf_op jit(solution)/shard_map/ppermute | solution.py:557
  69.8 6.0 %all-to-all-start = ((bf16[8,2,64,512]{3,2,1,0:T(8,128)(2,1)}), bf16[8,2,64,512]{3,2,1,0:T(8,128)(2,1)S(1)}, u32[]{:S(2)}, u32[]{:S(2)}) async-start(bf16[8,2,64,512]{3,2,1,0:T(8,128)(2,1)} %get-tuple-element.54), calls=%async_computation | async-start | bytes 2097152 | tf_op jit(solution)/shard_map/all_to_all | solution.py:590
  75.8 12.5 %shard_map.100 = (bf16[8,2,64,512]{3,2,1,0:T(8,128)(2,1)}, f32[512,512]{1,0:T(8,128)}, bf16[512,512]{1,0:T(8,128)(2,1)}) custom-call(s32[8,4]{1,0:T(8,128)} %bitcast.10, s32[2]{0:T(128)} %copy-done.7, s32[2]{0:T(128)} %copy-done.7, bf16[2,512,3072]{2,1,0:T(8,128)(2,1)} %band.3, bf16[2,2,512,512]{3,2,1,0:T(8,128)(2,1)} %collective-permute-done.4.sibling, ...), custom_call_target="tpu_custom_call" | custom-call | flops 4294967296 | bytes 100000000 | tf_op jit(solution)/shard_map/pallas_call | solution.py:374
  88.3 13.0 %all-to-all-done.first = bf16[8,2,64,512]{3,2,1,0:T(8,128)(2,1)S(1)} async-done(((bf16[8,2,64,512]{3,2,1,0:T(8,128)(2,1)}), bf16[8,2,64,512]{3,2,1,0:T(8,128)(2,1)S(1)}, u32[]{:S(2)}, u32[]{:S(2)}) %all-to-all-start) | async-done | bytes 1048608 | tf_op jit(solution)/shard_map/all_to_all | solution.py:590
  101.3 3.6 %all-to-all-start.1 = ((bf16[8,2,64,512]{3,2,1,0:T(8,128)(2,1)}), bf16[8,2,64,512]{3,2,1,0:T(8,128)(2,1)S(1)}, u32[]{:S(2)}, u32[]{:S(2)}) async-start(bf16[8,2,64,512]{3,2,1,0:T(8,128)(2,1)} %get-tuple-element.56), calls=%async_computation.1 | async-start | bytes 2097152 | tf_op jit(solution)/shard_map/all_to_all | solution.py:595
  111.0 6.8 %collective-permute-done.9 = bf16[256,512]{1,0:T(8,128)(2,1)S(1)} collective-permute-done((bf16[256,512]{1,0:T(8,128)(2,1)S(1)}, bf16[256,512]{1,0:T(8,128)(2,1)S(1)}, u32[]{:S(2)}, u32[]{:S(2)}) %collective-permute-start.9) | collective-permute-done | bytes 262176 | tf_op jit(solution)/shard_map/ppermute | solution.py:557
  120.9 9.7 %all-to-all-done.1.second = bf16[8,2,64,512]{3,2,1,0:T(8,128)(2,1)S(1)} async-done(((bf16[8,2,64,512]{3,2,1,0:T(8,128)(2,1)}), bf16[8,2,64,512]{3,2,1,0:T(8,128)(2,1)S(1)}, u32[]{:S(2)}, u32[]{:S(2)}) %all-to-all-start.1) | async-done | bytes 1048608 | tf_op jit(solution)/shard_map/all_to_all | solution.py:595
  130.7 4.8 %shard_map.101 = (f32[2,64,3072]{2,1,0:T(8,128)S(1)}, f32[2,64,3072]{2,1,0:T(8,128)S(1)}, bf16[2,64,3072]{2,1,0:T(8,128)(2,1)S(1)}, bf16[2,64,3072]{2,1,0:T(8,128)(2,1)}) custom-call(s32[16,4]{1,0:T(8,128)S(1)} %copy-done.9, s32[2]{0:T(128)S(1)} %copy-done.8, bf16[8,2,64,512]{3,2,1,0:T(8,128)(2,1)S(1)} %all-to-all-done.first, ...), custom_call_target="tpu_custom_call" | custom-call | flops 4194304 | bytes 6815744 | tf_op jit(solution)/shard_map/pallas_call | solution.py:446
  138.8 5.9 %collective-permute-done.14 = bf16[64,512]{1,0:T(8,128)(2,1)S(1)} collective-permute-done((bf16[64,512]{1,0:T(8,128)(2,1)S(1)}, bf16[64,512]{1,0:T(8,128)(2,1)S(1)}, u32[]{:S(2)}, u32[]{:S(2)}) %collective-permute-start.14) | collective-permute-done | bytes 65568 | tf_op jit(solution)/shard_map/ppermute | solution.py:560
  146.9 2.8 %add_convert_fusion = bf16[2,64,3072]{2,1,0:T(8,128)(2,1)} fusion(f32[2,64,3072]{2,1,0:T(8,128)} %copy-done.3, bf16[2,64,3072]{2,1,0:T(8,128)(2,1)} %copy-done.15), kind=kLoop, calls=%fused_computation.2 | loop fusion | flops 1179648 | bytes 3145728 | tf_op jit(solution)/shard_map/convert_element_type | solution.py:608
  152.2 3.0 %collective-permute-done.16 = bf16[32,512]{1,0:T(8,128)(2,1)S(1)} collective-permute-done((bf16[32,512]{1,0:T(8,128)(2,1)S(1)}, bf16[32,512]{1,0:T(8,128)(2,1)S(1)}, u32[]{:S(2)}, u32[]{:S(2)}) %collective-permute-start.16) | collective-permute-done | bytes 32800 | tf_op jit(solution)/shard_map/ppermute | solution.py:560
  155.4 5.2 %collective-permute-done.17 = bf16[64,512]{1,0:T(8,128)(2,1)S(1)} collective-permute-done((bf16[64,512]{1,0:T(8,128)(2,1)S(1)}, bf16[64,512]{1,0:T(8,128)(2,1)S(1)}, u32[]{:S(2)}, u32[]{:S(2)}) %collective-permute-start.17) | collective-permute-done | bytes 65568 | tf_op jit(solution)/shard_map/ppermute | solution.py:560
  160.7 5.1 %collective-permute-done.18 = bf16[128,512]{1,0:T(8,128)(2,1)} collective-permute-done((bf16[128,512]{1,0:T(8,128)(2,1)S(1)}, bf16[128,512]{1,0:T(8,128)(2,1)}, u32[]{:S(2)}, u32[]{:S(2)}) %collective-permute-start.18) | collective-permute-done | bytes 131104 | tf_op jit(solution)/shard_map/ppermute | solution.py:560
  166.9 3.0 %collective-permute-done.12 = bf16[2,64,3072]{2,1,0:T(8,128)(2,1)S(1)} collective-permute-done((bf16[2,64,3072]{2,1,0:T(8,128)(2,1)}, bf16[2,64,3072]{2,1,0:T(8,128)(2,1)S(1)}, u32[]{:S(2)}, u32[]{:S(2)}) %collective-permute-start.12) | collective-permute-done | bytes 786464 | tf_op jit(solution)/shard_map/ppermute | solution.py:557
  173.0 4.6 %collective-permute-start.20 = (bf16[2,64,3072]{2,1,0:T(8,128)(2,1)S(1)}, bf16[2,64,3072]{2,1,0:T(8,128)(2,1)S(1)}, u32[]{:S(2)}, u32[]{:S(2)}) collective-permute-start(bf16[2,64,3072]{2,1,0:T(8,128)(2,1)S(1)} %subtract_convert_fusion.refs_0_), channel_id=1, source_target_pairs={{0,8},{4,12},{8,16},{12,20},{16,24},{20,28},{1,9},{5,13},{9,17},{1... | collective-permute-start | bytes 2359304 | tf_op jit(solution)/shard_map/ppermute | solution.py:508
  178.6 14.2 %collective-permute-done.21.refs_4_ = bf16[2,64,3072]{2,1,0:T(8,128)(2,1)S(1)} collective-permute-done((bf16[2,64,3072]{2,1,0:T(8,128)(2,1)S(1)}, bf16[2,64,3072]{2,1,0:T(8,128)(2,1)S(1)}, u32[]{:S(2)}, u32[]{:S(2)}) %collective-permute-start.21) | collective-permute-done | bytes 786464 | tf_op jit(solution)/shard_map/ppermute | solution.py:508
  193.9 2.3 collective-permute-done.19.refs_7_
  200.3 15.1 %collective-permute-done.22.refs_8_ = bf16[2,64,3072]{2,1,0:T(8,128)(2,1)} collective-permute-done((bf16[2,64,3072]{2,1,0:T(8,128)(2,1)}, bf16[2,64,3072]{2,1,0:T(8,128)(2,1)}, u32[]{:S(2)}, u32[]{:S(2)}) %collective-permute-start.22) | collective-permute-done | bytes 786464 | tf_op jit(solution)/shard_map/ppermute | solution.py:511
  215.4 3.3 %collective-permute-done.24.refs_5_ = bf16[2,64,3072]{2,1,0:T(8,128)(2,1)} collective-permute-done((bf16[2,64,3072]{2,1,0:T(8,128)(2,1)S(1)}, bf16[2,64,3072]{2,1,0:T(8,128)(2,1)}, u32[]{:S(2)}, u32[]{:S(2)}) %collective-permute-start.24) | collective-permute-done | bytes 786464 | tf_op jit(solution)/shard_map/ppermute | solution.py:508
  226.7 5.0 %collective-permute-done.28 = bf16[256,512]{1,0:T(8,128)(2,1)} collective-permute-done((bf16[256,512]{1,0:T(8,128)(2,1)S(1)}, bf16[256,512]{1,0:T(8,128)(2,1)}, u32[]{:S(2)}, u32[]{:S(2)}) %collective-permute-start.28) | collective-permute-done | bytes 262176 | tf_op jit(solution)/shard_map/ppermute | solution.py:557
  233.7 4.2 %collective-permute-done.25.refs_9_ = bf16[2,64,3072]{2,1,0:T(8,128)(2,1)} collective-permute-done((bf16[2,64,3072]{2,1,0:T(8,128)(2,1)}, bf16[2,64,3072]{2,1,0:T(8,128)(2,1)}, u32[]{:S(2)}, u32[]{:S(2)}) %collective-permute-start.25) | collective-permute-done | bytes 786464 | tf_op jit(solution)/shard_map/ppermute | solution.py:511
  237.9 4.7 %collective-permute-done.27.refs_6_ = bf16[2,64,3072]{2,1,0:T(8,128)(2,1)} collective-permute-done((bf16[2,64,3072]{2,1,0:T(8,128)(2,1)}, bf16[2,64,3072]{2,1,0:T(8,128)(2,1)}, u32[]{:S(2)}, u32[]{:S(2)}) %collective-permute-start.27) | collective-permute-done | bytes 786464 | tf_op jit(solution)/shard_map/ppermute | solution.py:508
  245.3 2.2 collective-permute-done.30
  249.3 11.3 %collective-permute-done.29.refs_10_ = bf16[2,64,3072]{2,1,0:T(8,128)(2,1)} collective-permute-done((bf16[2,64,3072]{2,1,0:T(8,128)(2,1)}, bf16[2,64,3072]{2,1,0:T(8,128)(2,1)}, u32[]{:S(2)}, u32[]{:S(2)}) %collective-permute-start.29) | collective-permute-done | bytes 786464 | tf_op jit(solution)/shard_map/ppermute | solution.py:511
  262.3 5.1 %shard_map.102 = bf16[2,512,3072]{2,1,0:T(8,128)(2,1)} custom-call(s32[2]{0:T(128)S(1)} %copy-done.8, bf16[2,64,3072]{2,1,0:T(8,128)(2,1)S(1)} %subtract_convert_fusion.refs_0_, bf16[2,64,3072]{2,1,0:T(8,128)(2,1)S(1)} %collective-permute-done.20.refs_1_, bf16[2,64,3072]{2,1,0:T(8,128)(2,1)S(1)} %collective-permute-done.23.refs_2_, ...), custom_call_target="tpu_custom_call" | custom-call | bytes 12582912 | tf_op jit(solution)/shard_map/pallas_call | solution.py:531
  (106 shorter events, 65.0 us)
Async XLA Ops:
  12.9 7.0 %collective-permute-start.5 = (bf16[1,2,512,512]{3,2,1,0:T(8,128)(2,1)S(1)}, bf16[1,2,512,512]{3,2,1,0:T(8,128)(2,1)S(1)}, u32[]{:S(2)}, u32[]{:S(2)}) collective-permute-start(bf16[1,2,512,512]{3,2,1,0:T(8,128)(2,1)S(1)} %shard_map.97), channel_id=1, source_target_pairs={{0,1},{1,0},{2,3},{3,2},{4,5},{5,4},{6,7},{7,6},{8,9},{9,8},{10,11... | collective-permute-start | bytes 3145736 | tf_op jit(solution)/shard_map/ppermute | solution.py:557
  19.4 28.5 %collective-permute-start.4 = (bf16[2,2,512,512]{3,2,1,0:T(8,128)(2,1)}, bf16[2,2,512,512]{3,2,1,0:T(8,128)(2,1)}, u32[]{:S(2)}, u32[]{:S(2)}) collective-permute-start(bf16[2,2,512,512]{3,2,1,0:T(8,128)(2,1)} %get-tuple-element.45), channel_id=1, source_target_pairs={{0,1},{1,0},{2,3},{3,2},{4,5},{5,4},{6,7},{7,6},{8,9},{9,8},{10,11... | collective-permute-start | bytes 6291464 | tf_op jit(solution)/shard_map/ppermute | solution.py:557
  19.6 5.5 %collective-permute-start = (bf16[1,2,512,512]{3,2,1,0:T(8,128)(2,1)S(1)}, bf16[1,2,512,512]{3,2,1,0:T(8,128)(2,1)S(1)}, u32[]{:S(2)}, u32[]{:S(2)}) collective-permute-start(bf16[1,2,512,512]{3,2,1,0:T(8,128)(2,1)S(1)} %get-tuple-element.43), channel_id=1, source_target_pairs={{0,1},{1,0},{2,3},{3,2},{4,5},{5,4},{6,7},{7,6},{8,9},{9,8},{10,11... | collective-permute-start | bytes 3145736 | tf_op jit(solution)/shard_map/ppermute | solution.py:557
  21.7 26.1 %collective-permute-start.6 = (bf16[2,512,512]{2,1,0:T(8,128)(2,1)S(1)}, bf16[2,512,512]{2,1,0:T(8,128)(2,1)}, u32[]{:S(2)}, u32[]{:S(2)}) collective-permute-start(bf16[2,512,512]{2,1,0:T(8,128)(2,1)S(1)} %shard_map.98), channel_id=1, source_target_pairs={{0,2},{1,3},{2,0},{3,1},{4,6},{5,7},{6,4},{7,5},{8,10},{9,11},{10,... | collective-permute-start | bytes 3145736 | tf_op jit(solution)/shard_map/ppermute | solution.py:557
  26.9 42.9 %collective-permute-start.7 = (bf16[2,512,512]{2,1,0:T(8,128)(2,1)S(1)}, bf16[2,512,512]{2,1,0:T(8,128)(2,1)S(1)}, u32[]{:S(2)}, u32[]{:S(2)}) collective-permute-start(bf16[2,512,512]{2,1,0:T(8,128)(2,1)S(1)} %shard_map.96), channel_id=1, source_target_pairs={{0,2},{1,3},{2,0},{3,1},{4,6},{5,7},{6,4},{7,5},{8,10},{9,11},{10,... | collective-permute-start | bytes 3145736 | tf_op jit(solution)/shard_map/ppermute | solution.py:557
  28.9 3.6 %collective-permute-start.1 = (s32[2,4]{0,1:T(4,128)S(1)}, s32[2,4]{0,1:T(4,128)S(1)}, u32[]{:S(2)}, u32[]{:S(2)}) collective-permute-start(s32[2,4]{0,1:T(4,128)S(1)} %pad_add_fusion), channel_id=1, source_target_pairs={{0,4},{4,0},{8,12},{12,8},{16,20},{20,16},{24,28},{28,24},{1,5},{5... | collective-permute-start | bytes 104 | tf_op jit(solution)/shard_map/ppermute | solution.py:560
  32.6 3.6 %collective-permute-start.2 = (s32[4,4]{0,1:T(4,128)S(1)}, s32[4,4]{0,1:T(4,128)S(1)}, u32[]{:S(2)}, u32[]{:S(2)}) collective-permute-start(s32[4,4]{0,1:T(4,128)S(1)} %add_select_fusion), channel_id=1, source_target_pairs={{0,8},{4,12},{8,0},{12,4},{16,24},{20,28},{24,16},{28,20},{1,9},{5... | collective-permute-start | bytes 200 | tf_op jit(solution)/shard_map/ppermute | solution.py:560
  36.3 4.5 %collective-permute-start.3 = (s32[8,4]{0,1:T(4,128)S(1)}, s32[8,4]{0,1:T(4,128)S(1)}, u32[]{:S(2)}, u32[]{:S(2)}) collective-permute-start(s32[8,4]{0,1:T(4,128)S(1)} %add_select_fusion.1), channel_id=1, source_target_pairs={{0,16},{4,20},{8,24},{12,28},{16,0},{20,4},{24,8},{28,12},{1,17},{... | collective-permute-start | bytes 392 | tf_op jit(solution)/shard_map/ppermute | solution.py:560
  69.8 31.5 %all-to-all-start = ((bf16[8,2,64,512]{3,2,1,0:T(8,128)(2,1)}), bf16[8,2,64,512]{3,2,1,0:T(8,128)(2,1)S(1)}, u32[]{:S(2)}, u32[]{:S(2)}) async-start(bf16[8,2,64,512]{3,2,1,0:T(8,128)(2,1)} %get-tuple-element.54), calls=%async_computation | async-start | bytes 2097152 | tf_op jit(solution)/shard_map/all_to_all | solution.py:590
  101.3 29.3 %all-to-all-start.1 = ((bf16[8,2,64,512]{3,2,1,0:T(8,128)(2,1)}), bf16[8,2,64,512]{3,2,1,0:T(8,128)(2,1)S(1)}, u32[]{:S(2)}, u32[]{:S(2)}) async-start(bf16[8,2,64,512]{3,2,1,0:T(8,128)(2,1)} %get-tuple-element.56), calls=%async_computation.1 | async-start | bytes 2097152 | tf_op jit(solution)/shard_map/all_to_all | solution.py:595
  104.9 2.3 collective-permute-start.8
  109.4 8.4 %collective-permute-start.9 = (bf16[256,512]{1,0:T(8,128)(2,1)S(1)}, bf16[256,512]{1,0:T(8,128)(2,1)S(1)}, u32[]{:S(2)}, u32[]{:S(2)}) collective-permute-start(bf16[256,512]{1,0:T(8,128)(2,1)S(1)} %dynamic-slice_convert_fusion), channel_id=1, source_target_pairs={{0,2},{1,3},{2,0},{3,1},{4,6},{5,7},{6,4},{7,5},{8,10},{9,11},{10,... | collective-permute-start | bytes 786440 | tf_op jit(solution)/shard_map/ppermute | solution.py:557
  119.0 18.7 %collective-permute-start.13 = (bf16[128,512]{1,0:T(8,128)(2,1)S(1)}, bf16[128,512]{1,0:T(8,128)(2,1)}, u32[]{:S(2)}, u32[]{:S(2)}) collective-permute-start(bf16[128,512]{1,0:T(8,128)(2,1)S(1)} %dynamic-slice_convert_fusion.1), channel_id=1, source_target_pairs={{0,8},{4,12},{8,0},{12,4},{16,24},{20,28},{24,16},{28,20},{1,9},{5... | collective-permute-start | bytes 393224 | tf_op jit(solution)/shard_map/ppermute | solution.py:560
  137.7 8.3 %collective-permute-start.11 = (bf16[2,64,3072]{2,1,0:T(8,128)(2,1)S(1)}, bf16[2,64,3072]{2,1,0:T(8,128)(2,1)S(1)}, u32[]{:S(2)}, u32[]{:S(2)}) collective-permute-start(bf16[2,64,3072]{2,1,0:T(8,128)(2,1)S(1)} %get-tuple-element.60), channel_id=1, source_target_pairs={{0,1},{1,0},{2,3},{3,2},{4,5},{5,4},{6,7},{7,6},{8,9},{9,8},{10,11... | collective-permute-start | bytes 2359304 | tf_op jit(solution)/shard_map/ppermute | solution.py:557
  138.7 6.0 %collective-permute-start.14 = (bf16[64,512]{1,0:T(8,128)(2,1)S(1)}, bf16[64,512]{1,0:T(8,128)(2,1)S(1)}, u32[]{:S(2)}, u32[]{:S(2)}) collective-permute-start(bf16[64,512]{1,0:T(8,128)(2,1)S(1)} %dynamic-slice_convert_fusion.2), channel_id=1, source_target_pairs={{0,16},{4,20},{8,24},{12,28},{16,0},{20,4},{24,8},{28,12},{1,17},{... | collective-permute-start | bytes 196616 | tf_op jit(solution)/shard_map/ppermute | solution.py:560
  144.8 6.4 %collective-permute-start.15 = (bf16[32,512]{1,0:T(8,128)(2,1)S(1)}, bf16[32,512]{1,0:T(8,128)(2,1)S(1)}, u32[]{:S(2)}, u32[]{:S(2)}) collective-permute-start(bf16[32,512]{1,0:T(8,128)(2,1)S(1)} %dynamic-slice_convert_fusion.3), channel_id=1, source_target_pairs={{0,4},{4,0},{8,12},{12,8},{16,20},{20,16},{24,28},{28,24},{1,5},{5... | collective-permute-start | bytes 98312 | tf_op jit(solution)/shard_map/ppermute | solution.py:560
  146.0 20.8 %collective-permute-start.10 = (bf16[2,64,3072]{2,1,0:T(8,128)(2,1)}, bf16[2,64,3072]{2,1,0:T(8,128)(2,1)S(1)}, u32[]{:S(2)}, u32[]{:S(2)}) collective-permute-start(bf16[2,64,3072]{2,1,0:T(8,128)(2,1)} %get-tuple-element.58), channel_id=1, source_target_pairs={{0,1},{1,0},{2,3},{3,2},{4,5},{5,4},{6,7},{7,6},{8,9},{9,8},{10,11... | collective-permute-start | bytes 2359304 | tf_op jit(solution)/shard_map/ppermute | solution.py:557
  149.7 20.2 %collective-permute-start.12 = (bf16[2,64,3072]{2,1,0:T(8,128)(2,1)}, bf16[2,64,3072]{2,1,0:T(8,128)(2,1)S(1)}, u32[]{:S(2)}, u32[]{:S(2)}) collective-permute-start(bf16[2,64,3072]{2,1,0:T(8,128)(2,1)} %add_convert_fusion), channel_id=1, source_target_pairs={{0,2},{1,3},{2,0},{3,1},{4,6},{5,7},{6,4},{7,5},{8,10},{9,11},{10,... | collective-permute-start | bytes 2359304 | tf_op jit(solution)/shard_map/ppermute | solution.py:557
  151.2 4.0 %collective-permute-start.16 = (bf16[32,512]{1,0:T(8,128)(2,1)S(1)}, bf16[32,512]{1,0:T(8,128)(2,1)S(1)}, u32[]{:S(2)}, u32[]{:S(2)}) collective-permute-start(bf16[32,512]{1,0:T(8,128)(2,1)S(1)} %add_convert_fusion.1), channel_id=1, source_target_pairs={{0,4},{4,0},{8,12},{12,8},{16,20},{20,16},{24,28},{28,24},{1,5},{5... | collective-permute-start | bytes 98312 | tf_op jit(solution)/shard_map/ppermute | solution.py:560
  155.2 5.4 %collective-permute-start.17 = (bf16[64,512]{1,0:T(8,128)(2,1)S(1)}, bf16[64,512]{1,0:T(8,128)(2,1)S(1)}, u32[]{:S(2)}, u32[]{:S(2)}) collective-permute-start(bf16[64,512]{1,0:T(8,128)(2,1)S(1)} %maximum_select_fusion.4), channel_id=1, source_target_pairs={{0,16},{4,20},{8,24},{12,28},{16,0},{20,4},{24,8},{28,12},{1,17},{... | collective-permute-start | bytes 196616 | tf_op jit(solution)/shard_map/ppermute | solution.py:560
  160.6 5.1 %collective-permute-start.18 = (bf16[128,512]{1,0:T(8,128)(2,1)S(1)}, bf16[128,512]{1,0:T(8,128)(2,1)}, u32[]{:S(2)}, u32[]{:S(2)}) collective-permute-start(bf16[128,512]{1,0:T(8,128)(2,1)S(1)} %maximum_select_fusion.3), channel_id=1, source_target_pairs={{0,8},{4,12},{8,0},{12,4},{16,24},{20,28},{24,16},{28,20},{1,9},{5... | collective-permute-start | bytes 393224 | tf_op jit(solution)/shard_map/ppermute | solution.py:560
  171.7 21.1 %collective-permute-start.21 = (bf16[2,64,3072]{2,1,0:T(8,128)(2,1)S(1)}, bf16[2,64,3072]{2,1,0:T(8,128)(2,1)S(1)}, u32[]{:S(2)}, u32[]{:S(2)}) collective-permute-start(bf16[2,64,3072]{2,1,0:T(8,128)(2,1)S(1)} %subtract_convert_fusion.refs_0_), channel_id=1, source_target_pairs={{8,0},{12,4},{16,8},{20,12},{24,16},{28,20},{9,1},{13,5},{17,9},{2... | collective-permute-start | bytes 2359304 | tf_op jit(solution)/shard_map/ppermute | solution.py:508
  173.0 20.9 %collective-permute-start.20 = (bf16[2,64,3072]{2,1,0:T(8,128)(2,1)S(1)}, bf16[2,64,3072]{2,1,0:T(8,128)(2,1)S(1)}, u32[]{:S(2)}, u32[]{:S(2)}) collective-permute-start(bf16[2,64,3072]{2,1,0:T(8,128)(2,1)S(1)} %subtract_convert_fusion.refs_0_), channel_id=1, source_target_pairs={{0,8},{4,12},{8,16},{12,20},{16,24},{20,28},{1,9},{5,13},{9,17},{1... | collective-permute-start | bytes 2359304 | tf_op jit(solution)/shard_map/ppermute | solution.py:508
  177.6 18.7 %collective-permute-start.19 = (bf16[2,64,3072]{2,1,0:T(8,128)(2,1)S(1)}, bf16[2,64,3072]{2,1,0:T(8,128)(2,1)S(1)}, u32[]{:S(2)}, u32[]{:S(2)}) collective-permute-start(bf16[2,64,3072]{2,1,0:T(8,128)(2,1)S(1)} %subtract_convert_fusion.refs_0_), channel_id=1, source_target_pairs={{0,4},{4,0},{8,12},{12,8},{16,20},{20,16},{24,28},{28,24},{1,5},{5... | collective-permute-start | bytes 2359304 | tf_op jit(solution)/shard_map/ppermute | solution.py:511
  197.4 18.0 %collective-permute-start.22 = (bf16[2,64,3072]{2,1,0:T(8,128)(2,1)}, bf16[2,64,3072]{2,1,0:T(8,128)(2,1)}, u32[]{:S(2)}, u32[]{:S(2)}) collective-permute-start(bf16[2,64,3072]{2,1,0:T(8,128)(2,1)} %broadcast_select_fusion.1), channel_id=1, source_target_pairs={{0,4},{4,0},{8,12},{12,8},{16,20},{20,16},{24,28},{28,24},{1,5},{5... | collective-permute-start | bytes 2359304 | tf_op jit(solution)/shard_map/ppermute | solution.py:511
  198.3 17.1 %collective-permute-start.23 = (bf16[2,64,3072]{2,1,0:T(8,128)(2,1)S(1)}, bf16[2,64,3072]{2,1,0:T(8,128)(2,1)S(1)}, u32[]{:S(2)}, u32[]{:S(2)}) collective-permute-start(bf16[2,64,3072]{2,1,0:T(8,128)(2,1)S(1)} %collective-permute-done.20.refs_1_), channel_id=1, source_target_pairs={{8,16},{12,20},{16,24},{20,28},{9,17},{13,21},{17,25},{21,29},{10,... | collective-permute-start | bytes 2359304 | tf_op jit(solution)/shard_map/ppermute | solution.py:508
  199.0 19.7 %collective-permute-start.24 = (bf16[2,64,3072]{2,1,0:T(8,128)(2,1)S(1)}, bf16[2,64,3072]{2,1,0:T(8,128)(2,1)}, u32[]{:S(2)}, u32[]{:S(2)}) collective-permute-start(bf16[2,64,3072]{2,1,0:T(8,128)(2,1)S(1)} %collective-permute-done.21.refs_4_), channel_id=1, source_target_pairs={{8,0},{12,4},{16,8},{20,12},{9,1},{13,5},{17,9},{21,13},{10,2},{14... | collective-permute-start | bytes 2359304 | tf_op jit(solution)/shard_map/ppermute | solution.py:508
  220.8 17.1 %collective-permute-start.25 = (bf16[2,64,3072]{2,1,0:T(8,128)(2,1)}, bf16[2,64,3072]{2,1,0:T(8,128)(2,1)}, u32[]{:S(2)}, u32[]{:S(2)}) collective-permute-start(bf16[2,64,3072]{2,1,0:T(8,128)(2,1)} %broadcast_select_fusion), channel_id=1, source_target_pairs={{0,4},{4,0},{8,12},{12,8},{16,20},{20,16},{24,28},{28,24},{1,5},{5... | collective-permute-start | bytes 2359304 | tf_op jit(solution)/shard_map/ppermute | solution.py:511
  222.3 15.6 %collective-permute-start.26 = (bf16[2,64,3072]{2,1,0:T(8,128)(2,1)S(1)}, bf16[2,64,3072]{2,1,0:T(8,128)(2,1)}, u32[]{:S(2)}, u32[]{:S(2)}) collective-permute-start(bf16[2,64,3072]{2,1,0:T(8,128)(2,1)S(1)} %collective-permute-done.23.refs_2_), channel_id=1, source_target_pairs={{16,24},{20,28},{17,25},{21,29},{18,26},{22,30},{19,27},{23,31}} | collective-permute-start | bytes 2359304 | tf_op jit(solution)/shard_map/ppermute | solution.py:508
  223.9 18.7 %collective-permute-start.27 = (bf16[2,64,3072]{2,1,0:T(8,128)(2,1)}, bf16[2,64,3072]{2,1,0:T(8,128)(2,1)}, u32[]{:S(2)}, u32[]{:S(2)}) collective-permute-start(bf16[2,64,3072]{2,1,0:T(8,128)(2,1)} %collective-permute-done.24.refs_5_), channel_id=1, source_target_pairs={{8,0},{12,4},{9,1},{13,5},{10,2},{14,6},{11,3},{15,7}} | collective-permute-start | bytes 2359304 | tf_op jit(solution)/shard_map/ppermute | solution.py:508
  225.1 6.5 %collective-permute-start.28 = (bf16[256,512]{1,0:T(8,128)(2,1)S(1)}, bf16[256,512]{1,0:T(8,128)(2,1)}, u32[]{:S(2)}, u32[]{:S(2)}) collective-permute-start(bf16[256,512]{1,0:T(8,128)(2,1)S(1)} %maximum_select_fusion.2), channel_id=1, source_target_pairs={{0,2},{1,3},{2,0},{3,1},{4,6},{5,7},{6,4},{7,5},{8,10},{9,11},{10,... | collective-permute-start | bytes 786440 | tf_op jit(solution)/shard_map/ppermute | solution.py:557
  244.8 15.9 %collective-permute-start.29 = (bf16[2,64,3072]{2,1,0:T(8,128)(2,1)}, bf16[2,64,3072]{2,1,0:T(8,128)(2,1)}, u32[]{:S(2)}, u32[]{:S(2)}) collective-permute-start(bf16[2,64,3072]{2,1,0:T(8,128)(2,1)} %select_select_fusion), channel_id=1, source_target_pairs={{0,4},{4,0},{8,12},{12,8},{16,20},{20,16},{24,28},{28,24},{1,5},{5... | collective-permute-start | bytes 2359304 | tf_op jit(solution)/shard_map/ppermute | solution.py:511
  (17 other events, 165.5 us)

commit v11 on v10

--- a/solution.py
+++ b/solution.py
@@ -516,7 +516,7 @@
         ups.append(along(ups[k], range(k, length), 1))
         downs.append(along(downs[k], range(length - k), -1))
         if k == length - 2:
-            for step in term_steps[:-1]:
+            for step in term_steps:
                 term = step(term)
         overs[k], ups[k + 1], downs[k + 1], term = lax.optimization_barrier(
             (overs[k], ups[k + 1], downs[k + 1], term)
@@ -525,8 +525,7 @@
     if length > 2:
         middle = (place > 0) & (place < length - 1)
         end = jnp.where(middle, downs[1], end)
-    last, term = lax.optimization_barrier((over(end), term_steps[-1](term)))
-    overs.append(last)
+    overs.append(over(end))
     operands = [own, *ups[1:], *downs[1:], *overs]
     object_next = pl.pallas_call(
         functools.partial(assemble_kernel, length),

time: 269 us -> 265 us (0.985)
    ppermute x4, waiting for transfers between devices: 33 us -> 40.5 us  [over(): return lax.ppermute(value, 'pat', [(k, k ^ 1) for k in range(classes)])]
    ppermute x12, waiting for transfers between devices: 36.5 us -> 31.6 us  [flip(): return lax.ppermute(value, 'obj', [(k, k ^ bit) for k in range(owners)])]
    ppermute x6, waiting for transfers between devices: 23.3 us -> 18.8 us  [along(): return lax.ppermute(value, 'pat', pairs)]
  transfers between devices with their start and end apart: 33 -> 33, of which waited for: 25 -> 23; matrix products, arithmetic and copies ran while one was open for 4% -> 6% of each run, Pallas kernels for 15% -> 15%
where the time goes in v11:
time: 265 us; the launch traced here: 264 us
  waiting for transfers between devices  140 us (53%)
  Pallas kernels  45.7 us (17%)
  starting transfers between devices  44.1 us (17%)
  other arithmetic  18.8 us (7%)
  local copies, waits for them, and re-layouts  8.95 us (3%)
  blocking collectives  5.99 us (2%)
    ppermute x4, waiting for transfers between devices, over(): return lax.ppermute(value, 'pat', [(k, k ^ 1) for k in range(classes)])  40.5 us
    ppermute x12, waiting for transfers between devices, flip(): return lax.ppermute(value, 'obj', [(k, k ^ bit) for k in range(owners)])  31.6 us
    ppermute x9, waiting for transfers between devices, pat_flip(): lax.ppermute(value, 'pat', [(k, k ^ bit) for k in range(classes)])  25.8 us
    pallas_call x2, Pallas kernels, wave(): pl.pallas_call(functools.partial(wave_kernel, which), in_specs=[smem, sme...  24.6 us
    ppermute x6, waiting for transfers between devices, along(): return lax.ppermute(value, 'pat', pairs)  18.8 us
    all_to_all x1, waiting for transfers between devices, shards(): lax.all_to_all(grad_0, 'pat', split_axis=0, concat_axis=0, tiled=True)  13.2 us
    ppermute x6, starting transfers between devices, along(): return lax.ppermute(value, 'pat', pairs)  10.7 us
    ppermute x12, starting transfers between devices, flip(): return lax.ppermute(value, 'obj', [(k, k ^ bit) for k in range(owners)])  9.81 us
  transfers between devices with their start and end apart: 33, of which 23 were waited for; matrix products, arithmetic and copies ran while one was open for 6% of the time, Pallas kernels for 15%

profile of v11, /device:TPU:0, one launch (start us, length us, event | category | flops | bytes accessed | tf_op | source)
XLA Modules:
  0.0 264.4 jit_solution(14418060507100176202)
XLA Ops:
  2.3 6.0 %all-gather = s32[4,2,4]{2,1,0:T(2,128)S(1)} all-gather(s32[1,2,4]{2,1,0:T(2,128)S(1)} %bitcast.14), channel_id=1, replica_groups=mesh['pat'=8,'obj'=4] {'obj'}, dimensions={0}, use_global_device_ids=true | all-gather | bytes 160 | tf_op jit(solution)/shard_map/all_gather | solution.py:573
  8.4 2.8 %copy-done = bf16[2,512,3072]{2,1,0:T(8,128)(2,1)S(1)} copy-done((bf16[2,512,3072]{2,1,0:T(8,128)(2,1)S(1)}, bf16[2,512,3072]{2,1,0:T(8,128)(2,1)}, u32[]{:S(2)}) %copy-start) | copy-done | bytes 6291480
  13.3 6.0 %shard_map.95 = (bf16[1,2,512,512]{3,2,1,0:T(8,128)(2,1)S(1)}, bf16[2,2,512,512]{3,2,1,0:T(8,128)(2,1)}) custom-call(s32[8,4]{1,0:T(8,128)S(1)} %bitcast.7, s32[2]{0:T(128)S(1)} %pad_add_fusion.3.me.spare, bf16[2,512,3072]{2,1,0:T(8,128)(2,1)S(1)} %copy-done, bf16[2,512,3072]{2,1,0:T(8,128)(2,1)S(1)} %copy-done, bf16[2,512,3072]{2,1,0:T(8,128)(2,1)S(1)} %copy-done, ...), custom_call_target="tpu_custom_call" | custom-call | flops 1966080 | bytes 7000000 | tf_op jit(solution)/shard_map/pallas_call | solution.py:195
  33.9 2.3 collective-permute-done.2
  36.3 2.2 collective-permute-start.3
  38.5 2.2 collective-permute-done.3
  41.6 6.2 %collective-permute-done.6.across = bf16[2,512,512]{2,1,0:T(8,128)(2,1)} collective-permute-done((bf16[2,512,512]{2,1,0:T(8,128)(2,1)S(1)}, bf16[2,512,512]{2,1,0:T(8,128)(2,1)}, u32[]{:S(2)}, u32[]{:S(2)}) %collective-permute-start.6) | collective-permute-done | bytes 1048608 | tf_op jit(solution)/shard_map/ppermute | solution.py:556
  47.8 12.2 %shard_map.99 = (bf16[8,2,64,512]{3,2,1,0:T(8,128)(2,1)}, f32[2,512,512]{2,1,0:T(8,128)}) custom-call(s32[8,4]{1,0:T(8,128)} %bitcast.10, s32[2]{0:T(128)} %copy-done.7, s32[16,4]{1,0:T(8,128)} %broadcast_select_fusion.2.spare.pos, bf16[2,512,3072]{2,1,0:T(8,128)(2,1)} %band.3, bf16[2,2,512,512]{3,2,1,0:T(8,128)(2,1)} %collective-permute-done.4.sibling, ...), custom_call_target="tpu_custom_call" | custom-call | flops 4294967296 | bytes 100000000 | tf_op jit(solution)/shard_map/pallas_call | solution.py:374
  60.0 9.8 %collective-permute-done.7.across = bf16[2,512,512]{2,1,0:T(8,128)(2,1)S(1)} collective-permute-done((bf16[2,512,512]{2,1,0:T(8,128)(2,1)S(1)}, bf16[2,512,512]{2,1,0:T(8,128)(2,1)S(1)}, u32[]{:S(2)}, u32[]{:S(2)}) %collective-permute-start.7) | collective-permute-done | bytes 1048608 | tf_op jit(solution)/shard_map/ppermute | solution.py:556
  69.8 6.0 %all-to-all-start = ((bf16[8,2,64,512]{3,2,1,0:T(8,128)(2,1)}), bf16[8,2,64,512]{3,2,1,0:T(8,128)(2,1)S(1)}, u32[]{:S(2)}, u32[]{:S(2)}) async-start(bf16[8,2,64,512]{3,2,1,0:T(8,128)(2,1)} %get-tuple-element.52), calls=%async_computation | async-start | bytes 2097152 | tf_op jit(solution)/shard_map/all_to_all | solution.py:589
  75.8 12.5 %shard_map.100 = (bf16[8,2,64,512]{3,2,1,0:T(8,128)(2,1)}, f32[512,512]{1,0:T(8,128)}, bf16[512,512]{1,0:T(8,128)(2,1)}) custom-call(s32[8,4]{1,0:T(8,128)} %bitcast.11, s32[2]{0:T(128)} %copy-done.7, s32[2]{0:T(128)} %copy-done.7, bf16[2,512,3072]{2,1,0:T(8,128)(2,1)} %band.3, bf16[2,2,512,512]{3,2,1,0:T(8,128)(2,1)} %collective-permute-done.4.sibling, ...), custom_call_target="tpu_custom_call" | custom-call | flops 4294967296 | bytes 100000000 | tf_op jit(solution)/shard_map/pallas_call | solution.py:374
  88.3 13.2 %all-to-all-done.first = bf16[8,2,64,512]{3,2,1,0:T(8,128)(2,1)S(1)} async-done(((bf16[8,2,64,512]{3,2,1,0:T(8,128)(2,1)}), bf16[8,2,64,512]{3,2,1,0:T(8,128)(2,1)S(1)}, u32[]{:S(2)}, u32[]{:S(2)}) %all-to-all-start) | async-done | bytes 1048608 | tf_op jit(solution)/shard_map/all_to_all | solution.py:589
  101.5 3.6 %all-to-all-start.1 = ((bf16[8,2,64,512]{3,2,1,0:T(8,128)(2,1)}), bf16[8,2,64,512]{3,2,1,0:T(8,128)(2,1)S(1)}, u32[]{:S(2)}, u32[]{:S(2)}) async-start(bf16[8,2,64,512]{3,2,1,0:T(8,128)(2,1)} %get-tuple-element.54), calls=%async_computation.1 | async-start | bytes 2097152 | tf_op jit(solution)/shard_map/all_to_all | solution.py:594
  105.2 2.2 collective-permute-done.8
  111.2 6.8 %collective-permute-done.9 = bf16[256,512]{1,0:T(8,128)(2,1)S(1)} collective-permute-done((bf16[256,512]{1,0:T(8,128)(2,1)S(1)}, bf16[256,512]{1,0:T(8,128)(2,1)S(1)}, u32[]{:S(2)}, u32[]{:S(2)}) %collective-permute-start.9) | collective-permute-done | bytes 262176 | tf_op jit(solution)/shard_map/ppermute | solution.py:556
  121.2 9.8 %all-to-all-done.1.second = bf16[8,2,64,512]{3,2,1,0:T(8,128)(2,1)S(1)} async-done(((bf16[8,2,64,512]{3,2,1,0:T(8,128)(2,1)}), bf16[8,2,64,512]{3,2,1,0:T(8,128)(2,1)S(1)}, u32[]{:S(2)}, u32[]{:S(2)}) %all-to-all-start.1) | async-done | bytes 1048608 | tf_op jit(solution)/shard_map/all_to_all | solution.py:594
  131.0 4.8 %shard_map.101 = (f32[2,64,3072]{2,1,0:T(8,128)S(1)}, f32[2,64,3072]{2,1,0:T(8,128)S(1)}, bf16[2,64,3072]{2,1,0:T(8,128)(2,1)S(1)}, bf16[2,64,3072]{2,1,0:T(8,128)(2,1)}) custom-call(s32[16,4]{1,0:T(8,128)S(1)} %copy-done.9, s32[2]{0:T(128)S(1)} %copy-done.8, bf16[8,2,64,512]{3,2,1,0:T(8,128)(2,1)S(1)} %all-to-all-done.first, ...), custom_call_target="tpu_custom_call" | custom-call | flops 4194304 | bytes 6815744 | tf_op jit(solution)/shard_map/pallas_call | solution.py:446
  139.2 5.9 %collective-permute-done.14 = bf16[64,512]{1,0:T(8,128)(2,1)S(1)} collective-permute-done((bf16[64,512]{1,0:T(8,128)(2,1)S(1)}, bf16[64,512]{1,0:T(8,128)(2,1)S(1)}, u32[]{:S(2)}, u32[]{:S(2)}) %collective-permute-start.14) | collective-permute-done | bytes 65568 | tf_op jit(solution)/shard_map/ppermute | solution.py:559
  147.3 2.8 %add_convert_fusion = bf16[2,64,3072]{2,1,0:T(8,128)(2,1)} fusion(f32[2,64,3072]{2,1,0:T(8,128)} %copy-done.3, bf16[2,64,3072]{2,1,0:T(8,128)(2,1)} %copy-done.15), kind=kLoop, calls=%fused_computation.2 | loop fusion | flops 1179648 | bytes 3145728 | tf_op jit(solution)/shard_map/convert_element_type | solution.py:607
  152.6 3.0 %collective-permute-done.16 = bf16[32,512]{1,0:T(8,128)(2,1)S(1)} collective-permute-done((bf16[32,512]{1,0:T(8,128)(2,1)S(1)}, bf16[32,512]{1,0:T(8,128)(2,1)S(1)}, u32[]{:S(2)}, u32[]{:S(2)}) %collective-permute-start.16) | collective-permute-done | bytes 32800 | tf_op jit(solution)/shard_map/ppermute | solution.py:559
  155.7 5.2 %collective-permute-done.17 = bf16[64,512]{1,0:T(8,128)(2,1)S(1)} collective-permute-done((bf16[64,512]{1,0:T(8,128)(2,1)S(1)}, bf16[64,512]{1,0:T(8,128)(2,1)S(1)}, u32[]{:S(2)}, u32[]{:S(2)}) %collective-permute-start.17) | collective-permute-done | bytes 65568 | tf_op jit(solution)/shard_map/ppermute | solution.py:559
  161.0 5.1 %collective-permute-done.18 = bf16[128,512]{1,0:T(8,128)(2,1)} collective-permute-done((bf16[128,512]{1,0:T(8,128)(2,1)S(1)}, bf16[128,512]{1,0:T(8,128)(2,1)}, u32[]{:S(2)}, u32[]{:S(2)}) %collective-permute-start.18) | collective-permute-done | bytes 131104 | tf_op jit(solution)/shard_map/ppermute | solution.py:559
  167.2 3.0 %collective-permute-done.12 = bf16[2,64,3072]{2,1,0:T(8,128)(2,1)S(1)} collective-permute-done((bf16[2,64,3072]{2,1,0:T(8,128)(2,1)}, bf16[2,64,3072]{2,1,0:T(8,128)(2,1)S(1)}, u32[]{:S(2)}, u32[]{:S(2)}) %collective-permute-start.12) | collective-permute-done | bytes 786464 | tf_op jit(solution)/shard_map/ppermute | solution.py:556
  173.4 4.6 %collective-permute-start.20 = (bf16[2,64,3072]{2,1,0:T(8,128)(2,1)S(1)}, bf16[2,64,3072]{2,1,0:T(8,128)(2,1)S(1)}, u32[]{:S(2)}, u32[]{:S(2)}) collective-permute-start(bf16[2,64,3072]{2,1,0:T(8,128)(2,1)S(1)} %subtract_convert_fusion.refs_0_), channel_id=1, source_target_pairs={{0,8},{4,12},{8,16},{12,20},{16,24},{20,28},{1,9},{5,13},{9,17},{1... | collective-permute-start | bytes 2359304 | tf_op jit(solution)/shard_map/ppermute | solution.py:508
  178.8 14.3 %collective-permute-done.21.refs_4_ = bf16[2,64,3072]{2,1,0:T(8,128)(2,1)S(1)} collective-permute-done((bf16[2,64,3072]{2,1,0:T(8,128)(2,1)S(1)}, bf16[2,64,3072]{2,1,0:T(8,128)(2,1)S(1)}, u32[]{:S(2)}, u32[]{:S(2)}) %collective-permute-start.21) | collective-permute-done | bytes 786464 | tf_op jit(solution)/shard_map/ppermute | solution.py:508
  194.3 2.3 collective-permute-done.19.refs_7_
  200.6 15.2 %collective-permute-done.22.refs_8_ = bf16[2,64,3072]{2,1,0:T(8,128)(2,1)} collective-permute-done((bf16[2,64,3072]{2,1,0:T(8,128)(2,1)}, bf16[2,64,3072]{2,1,0:T(8,128)(2,1)}, u32[]{:S(2)}, u32[]{:S(2)}) %collective-permute-start.22) | collective-permute-done | bytes 786464 | tf_op jit(solution)/shard_map/ppermute | solution.py:511
  215.8 3.3 %collective-permute-done.24.refs_5_ = bf16[2,64,3072]{2,1,0:T(8,128)(2,1)} collective-permute-done((bf16[2,64,3072]{2,1,0:T(8,128)(2,1)S(1)}, bf16[2,64,3072]{2,1,0:T(8,128)(2,1)}, u32[]{:S(2)}, u32[]{:S(2)}) %collective-permute-start.24) | collective-permute-done | bytes 786464 | tf_op jit(solution)/shard_map/ppermute | solution.py:508
  227.9 2.2 collective-permute-done.29
  231.9 10.4 %collective-permute-done.25.refs_9_ = bf16[2,64,3072]{2,1,0:T(8,128)(2,1)} collective-permute-done((bf16[2,64,3072]{2,1,0:T(8,128)(2,1)}, bf16[2,64,3072]{2,1,0:T(8,128)(2,1)}, u32[]{:S(2)}, u32[]{:S(2)}) %collective-permute-start.25) | collective-permute-done | bytes 786464 | tf_op jit(solution)/shard_map/ppermute | solution.py:511
  246.8 12.5 %collective-permute-done.30.refs_10_ = bf16[2,64,3072]{2,1,0:T(8,128)(2,1)S(1)} collective-permute-done((bf16[2,64,3072]{2,1,0:T(8,128)(2,1)S(1)}, bf16[2,64,3072]{2,1,0:T(8,128)(2,1)S(1)}, u32[]{:S(2)}, u32[]{:S(2)}) %collective-permute-start.30) | collective-permute-done | bytes 786464 | tf_op jit(solution)/shard_map/ppermute | solution.py:511
  259.3 4.9 %shard_map.102 = bf16[2,512,3072]{2,1,0:T(8,128)(2,1)} custom-call(s32[2]{0:T(128)S(1)} %copy-done.8, bf16[2,64,3072]{2,1,0:T(8,128)(2,1)S(1)} %subtract_convert_fusion.refs_0_, bf16[2,64,3072]{2,1,0:T(8,128)(2,1)S(1)} %collective-permute-done.20.refs_1_, bf16[2,64,3072]{2,1,0:T(8,128)(2,1)S(1)} %collective-permute-done.23.refs_2_, ...), custom_call_target="tpu_custom_call" | custom-call | bytes 12582912 | tf_op jit(solution)/shard_map/pallas_call | solution.py:530
  (106 shorter events, 59.8 us)
Async XLA Ops:
  12.9 7.0 %collective-permute-start.5 = (bf16[1,2,512,512]{3,2,1,0:T(8,128)(2,1)S(1)}, bf16[1,2,512,512]{3,2,1,0:T(8,128)(2,1)S(1)}, u32[]{:S(2)}, u32[]{:S(2)}) collective-permute-start(bf16[1,2,512,512]{3,2,1,0:T(8,128)(2,1)S(1)} %shard_map.97), channel_id=1, source_target_pairs={{0,1},{1,0},{2,3},{3,2},{4,5},{5,4},{6,7},{7,6},{8,9},{9,8},{10,11... | collective-permute-start | bytes 3145736 | tf_op jit(solution)/shard_map/ppermute | solution.py:556
  19.4 28.5 %collective-permute-start.4 = (bf16[2,2,512,512]{3,2,1,0:T(8,128)(2,1)}, bf16[2,2,512,512]{3,2,1,0:T(8,128)(2,1)}, u32[]{:S(2)}, u32[]{:S(2)}) collective-permute-start(bf16[2,2,512,512]{3,2,1,0:T(8,128)(2,1)} %get-tuple-element.43), channel_id=1, source_target_pairs={{0,1},{1,0},{2,3},{3,2},{4,5},{5,4},{6,7},{7,6},{8,9},{9,8},{10,11... | collective-permute-start | bytes 6291464 | tf_op jit(solution)/shard_map/ppermute | solution.py:556
  19.6 5.5 %collective-permute-start = (bf16[1,2,512,512]{3,2,1,0:T(8,128)(2,1)S(1)}, bf16[1,2,512,512]{3,2,1,0:T(8,128)(2,1)S(1)}, u32[]{:S(2)}, u32[]{:S(2)}) collective-permute-start(bf16[1,2,512,512]{3,2,1,0:T(8,128)(2,1)S(1)} %get-tuple-element.41), channel_id=1, source_target_pairs={{0,1},{1,0},{2,3},{3,2},{4,5},{5,4},{6,7},{7,6},{8,9},{9,8},{10,11... | collective-permute-start | bytes 3145736 | tf_op jit(solution)/shard_map/ppermute | solution.py:556
  21.7 26.1 %collective-permute-start.6 = (bf16[2,512,512]{2,1,0:T(8,128)(2,1)S(1)}, bf16[2,512,512]{2,1,0:T(8,128)(2,1)}, u32[]{:S(2)}, u32[]{:S(2)}) collective-permute-start(bf16[2,512,512]{2,1,0:T(8,128)(2,1)S(1)} %shard_map.98), channel_id=1, source_target_pairs={{0,2},{1,3},{2,0},{3,1},{4,6},{5,7},{6,4},{7,5},{8,10},{9,11},{10,... | collective-permute-start | bytes 3145736 | tf_op jit(solution)/shard_map/ppermute | solution.py:556
  26.9 42.9 %collective-permute-start.7 = (bf16[2,512,512]{2,1,0:T(8,128)(2,1)S(1)}, bf16[2,512,512]{2,1,0:T(8,128)(2,1)S(1)}, u32[]{:S(2)}, u32[]{:S(2)}) collective-permute-start(bf16[2,512,512]{2,1,0:T(8,128)(2,1)S(1)} %shard_map.96), channel_id=1, source_target_pairs={{0,2},{1,3},{2,0},{3,1},{4,6},{5,7},{6,4},{7,5},{8,10},{9,11},{10,... | collective-permute-start | bytes 3145736 | tf_op jit(solution)/shard_map/ppermute | solution.py:556
  28.9 3.6 %collective-permute-start.1 = (s32[2,4]{0,1:T(4,128)S(1)}, s32[2,4]{0,1:T(4,128)S(1)}, u32[]{:S(2)}, u32[]{:S(2)}) collective-permute-start(s32[2,4]{0,1:T(4,128)S(1)} %pad_add_fusion), channel_id=1, source_target_pairs={{0,4},{4,0},{8,12},{12,8},{16,20},{20,16},{24,28},{28,24},{1,5},{5... | collective-permute-start | bytes 104 | tf_op jit(solution)/shard_map/ppermute | solution.py:559
  32.6 3.6 %collective-permute-start.2 = (s32[4,4]{0,1:T(4,128)S(1)}, s32[4,4]{0,1:T(4,128)S(1)}, u32[]{:S(2)}, u32[]{:S(2)}) collective-permute-start(s32[4,4]{0,1:T(4,128)S(1)} %add_select_fusion), channel_id=1, source_target_pairs={{0,8},{4,12},{8,0},{12,4},{16,24},{20,28},{24,16},{28,20},{1,9},{5... | collective-permute-start | bytes 200 | tf_op jit(solution)/shard_map/ppermute | solution.py:559
  36.3 4.5 %collective-permute-start.3 = (s32[8,4]{0,1:T(4,128)S(1)}, s32[8,4]{0,1:T(4,128)S(1)}, u32[]{:S(2)}, u32[]{:S(2)}) collective-permute-start(s32[8,4]{0,1:T(4,128)S(1)} %add_select_fusion.1), channel_id=1, source_target_pairs={{0,16},{4,20},{8,24},{12,28},{16,0},{20,4},{24,8},{28,12},{1,17},{... | collective-permute-start | bytes 392 | tf_op jit(solution)/shard_map/ppermute | solution.py:559
  69.8 31.7 %all-to-all-start = ((bf16[8,2,64,512]{3,2,1,0:T(8,128)(2,1)}), bf16[8,2,64,512]{3,2,1,0:T(8,128)(2,1)S(1)}, u32[]{:S(2)}, u32[]{:S(2)}) async-start(bf16[8,2,64,512]{3,2,1,0:T(8,128)(2,1)} %get-tuple-element.52), calls=%async_computation | async-start | bytes 2097152 | tf_op jit(solution)/shard_map/all_to_all | solution.py:589
  101.5 29.5 %all-to-all-start.1 = ((bf16[8,2,64,512]{3,2,1,0:T(8,128)(2,1)}), bf16[8,2,64,512]{3,2,1,0:T(8,128)(2,1)S(1)}, u32[]{:S(2)}, u32[]{:S(2)}) async-start(bf16[8,2,64,512]{3,2,1,0:T(8,128)(2,1)} %get-tuple-element.54), calls=%async_computation.1 | async-start | bytes 2097152 | tf_op jit(solution)/shard_map/all_to_all | solution.py:594
  105.1 2.3 collective-permute-start.8
  109.6 8.4 %collective-permute-start.9 = (bf16[256,512]{1,0:T(8,128)(2,1)S(1)}, bf16[256,512]{1,0:T(8,128)(2,1)S(1)}, u32[]{:S(2)}, u32[]{:S(2)}) collective-permute-start(bf16[256,512]{1,0:T(8,128)(2,1)S(1)} %dynamic-slice_convert_fusion), channel_id=1, source_target_pairs={{0,2},{1,3},{2,0},{3,1},{4,6},{5,7},{6,4},{7,5},{8,10},{9,11},{10,... | collective-permute-start | bytes 786440 | tf_op jit(solution)/shard_map/ppermute | solution.py:556
  119.2 18.9 %collective-permute-start.13 = (bf16[128,512]{1,0:T(8,128)(2,1)S(1)}, bf16[128,512]{1,0:T(8,128)(2,1)}, u32[]{:S(2)}, u32[]{:S(2)}) collective-permute-start(bf16[128,512]{1,0:T(8,128)(2,1)S(1)} %dynamic-slice_convert_fusion.1), channel_id=1, source_target_pairs={{0,8},{4,12},{8,0},{12,4},{16,24},{20,28},{24,16},{28,20},{1,9},{5... | collective-permute-start | bytes 393224 | tf_op jit(solution)/shard_map/ppermute | solution.py:559
  138.1 8.3 %collective-permute-start.11 = (bf16[2,64,3072]{2,1,0:T(8,128)(2,1)S(1)}, bf16[2,64,3072]{2,1,0:T(8,128)(2,1)S(1)}, u32[]{:S(2)}, u32[]{:S(2)}) collective-permute-start(bf16[2,64,3072]{2,1,0:T(8,128)(2,1)S(1)} %get-tuple-element.58), channel_id=1, source_target_pairs={{0,1},{1,0},{2,3},{3,2},{4,5},{5,4},{6,7},{7,6},{8,9},{9,8},{10,11... | collective-permute-start | bytes 2359304 | tf_op jit(solution)/shard_map/ppermute | solution.py:556
  139.1 6.0 %collective-permute-start.14 = (bf16[64,512]{1,0:T(8,128)(2,1)S(1)}, bf16[64,512]{1,0:T(8,128)(2,1)S(1)}, u32[]{:S(2)}, u32[]{:S(2)}) collective-permute-start(bf16[64,512]{1,0:T(8,128)(2,1)S(1)} %dynamic-slice_convert_fusion.2), channel_id=1, source_target_pairs={{0,16},{4,20},{8,24},{12,28},{16,0},{20,4},{24,8},{28,12},{1,17},{... | collective-permute-start | bytes 196616 | tf_op jit(solution)/shard_map/ppermute | solution.py:559
  145.1 6.5 %collective-permute-start.15 = (bf16[32,512]{1,0:T(8,128)(2,1)S(1)}, bf16[32,512]{1,0:T(8,128)(2,1)S(1)}, u32[]{:S(2)}, u32[]{:S(2)}) collective-permute-start(bf16[32,512]{1,0:T(8,128)(2,1)S(1)} %dynamic-slice_convert_fusion.3), channel_id=1, source_target_pairs={{0,4},{4,0},{8,12},{12,8},{16,20},{20,16},{24,28},{28,24},{1,5},{5... | collective-permute-start | bytes 98312 | tf_op jit(solution)/shard_map/ppermute | solution.py:559
  146.4 20.8 %collective-permute-start.10 = (bf16[2,64,3072]{2,1,0:T(8,128)(2,1)}, bf16[2,64,3072]{2,1,0:T(8,128)(2,1)S(1)}, u32[]{:S(2)}, u32[]{:S(2)}) collective-permute-start(bf16[2,64,3072]{2,1,0:T(8,128)(2,1)} %get-tuple-element.56), channel_id=1, source_target_pairs={{0,1},{1,0},{2,3},{3,2},{4,5},{5,4},{6,7},{7,6},{8,9},{9,8},{10,11... | collective-permute-start | bytes 2359304 | tf_op jit(solution)/shard_map/ppermute | solution.py:556
  150.0 20.2 %collective-permute-start.12 = (bf16[2,64,3072]{2,1,0:T(8,128)(2,1)}, bf16[2,64,3072]{2,1,0:T(8,128)(2,1)S(1)}, u32[]{:S(2)}, u32[]{:S(2)}) collective-permute-start(bf16[2,64,3072]{2,1,0:T(8,128)(2,1)} %add_convert_fusion), channel_id=1, source_target_pairs={{0,2},{1,3},{2,0},{3,1},{4,6},{5,7},{6,4},{7,5},{8,10},{9,11},{10,... | collective-permute-start | bytes 2359304 | tf_op jit(solution)/shard_map/ppermute | solution.py:556
  151.6 4.0 %collective-permute-start.16 = (bf16[32,512]{1,0:T(8,128)(2,1)S(1)}, bf16[32,512]{1,0:T(8,128)(2,1)S(1)}, u32[]{:S(2)}, u32[]{:S(2)}) collective-permute-start(bf16[32,512]{1,0:T(8,128)(2,1)S(1)} %add_convert_fusion.1), channel_id=1, source_target_pairs={{0,4},{4,0},{8,12},{12,8},{16,20},{20,16},{24,28},{28,24},{1,5},{5... | collective-permute-start | bytes 98312 | tf_op jit(solution)/shard_map/ppermute | solution.py:559
  155.6 5.4 %collective-permute-start.17 = (bf16[64,512]{1,0:T(8,128)(2,1)S(1)}, bf16[64,512]{1,0:T(8,128)(2,1)S(1)}, u32[]{:S(2)}, u32[]{:S(2)}) collective-permute-start(bf16[64,512]{1,0:T(8,128)(2,1)S(1)} %maximum_select_fusion.4), channel_id=1, source_target_pairs={{0,16},{4,20},{8,24},{12,28},{16,0},{20,4},{24,8},{28,12},{1,17},{... | collective-permute-start | bytes 196616 | tf_op jit(solution)/shard_map/ppermute | solution.py:559
  160.9 5.1 %collective-permute-start.18 = (bf16[128,512]{1,0:T(8,128)(2,1)S(1)}, bf16[128,512]{1,0:T(8,128)(2,1)}, u32[]{:S(2)}, u32[]{:S(2)}) collective-permute-start(bf16[128,512]{1,0:T(8,128)(2,1)S(1)} %maximum_select_fusion.3), channel_id=1, source_target_pairs={{0,8},{4,12},{8,0},{12,4},{16,24},{20,28},{24,16},{28,20},{1,9},{5... | collective-permute-start | bytes 393224 | tf_op jit(solution)/shard_map/ppermute | solution.py:559
  172.1 21.1 %collective-permute-start.21 = (bf16[2,64,3072]{2,1,0:T(8,128)(2,1)S(1)}, bf16[2,64,3072]{2,1,0:T(8,128)(2,1)S(1)}, u32[]{:S(2)}, u32[]{:S(2)}) collective-permute-start(bf16[2,64,3072]{2,1,0:T(8,128)(2,1)S(1)} %subtract_convert_fusion.refs_0_), channel_id=1, source_target_pairs={{8,0},{12,4},{16,8},{20,12},{24,16},{28,20},{9,1},{13,5},{17,9},{2... | collective-permute-start | bytes 2359304 | tf_op jit(solution)/shard_map/ppermute | solution.py:508
  173.4 20.9 %collective-permute-start.20 = (bf16[2,64,3072]{2,1,0:T(8,128)(2,1)S(1)}, bf16[2,64,3072]{2,1,0:T(8,128)(2,1)S(1)}, u32[]{:S(2)}, u32[]{:S(2)}) collective-permute-start(bf16[2,64,3072]{2,1,0:T(8,128)(2,1)S(1)} %subtract_convert_fusion.refs_0_), channel_id=1, source_target_pairs={{0,8},{4,12},{8,16},{12,20},{16,24},{20,28},{1,9},{5,13},{9,17},{1... | collective-permute-start | bytes 2359304 | tf_op jit(solution)/shard_map/ppermute | solution.py:508
  178.0 18.7 %collective-permute-start.19 = (bf16[2,64,3072]{2,1,0:T(8,128)(2,1)S(1)}, bf16[2,64,3072]{2,1,0:T(8,128)(2,1)S(1)}, u32[]{:S(2)}, u32[]{:S(2)}) collective-permute-start(bf16[2,64,3072]{2,1,0:T(8,128)(2,1)S(1)} %subtract_convert_fusion.refs_0_), channel_id=1, source_target_pairs={{0,4},{4,0},{8,12},{12,8},{16,20},{20,16},{24,28},{28,24},{1,5},{5... | collective-permute-start | bytes 2359304 | tf_op jit(solution)/shard_map/ppermute | solution.py:511
  197.8 18.0 %collective-permute-start.22 = (bf16[2,64,3072]{2,1,0:T(8,128)(2,1)}, bf16[2,64,3072]{2,1,0:T(8,128)(2,1)}, u32[]{:S(2)}, u32[]{:S(2)}) collective-permute-start(bf16[2,64,3072]{2,1,0:T(8,128)(2,1)} %broadcast_select_fusion.1), channel_id=1, source_target_pairs={{0,4},{4,0},{8,12},{12,8},{16,20},{20,16},{24,28},{28,24},{1,5},{5... | collective-permute-start | bytes 2359304 | tf_op jit(solution)/shard_map/ppermute | solution.py:511
  198.5 17.2 %collective-permute-start.23 = (bf16[2,64,3072]{2,1,0:T(8,128)(2,1)S(1)}, bf16[2,64,3072]{2,1,0:T(8,128)(2,1)S(1)}, u32[]{:S(2)}, u32[]{:S(2)}) collective-permute-start(bf16[2,64,3072]{2,1,0:T(8,128)(2,1)S(1)} %collective-permute-done.20.refs_1_), channel_id=1, source_target_pairs={{8,16},{12,20},{16,24},{20,28},{9,17},{13,21},{17,25},{21,29},{10,... | collective-permute-start | bytes 2359304 | tf_op jit(solution)/shard_map/ppermute | solution.py:508
  199.3 19.8 %collective-permute-start.24 = (bf16[2,64,3072]{2,1,0:T(8,128)(2,1)S(1)}, bf16[2,64,3072]{2,1,0:T(8,128)(2,1)}, u32[]{:S(2)}, u32[]{:S(2)}) collective-permute-start(bf16[2,64,3072]{2,1,0:T(8,128)(2,1)S(1)} %collective-permute-done.21.refs_4_), channel_id=1, source_target_pairs={{8,0},{12,4},{16,8},{20,12},{9,1},{13,5},{17,9},{21,13},{10,2},{14... | collective-permute-start | bytes 2359304 | tf_op jit(solution)/shard_map/ppermute | solution.py:508
  219.0 7.9 %collective-permute-start.28 = (bf16[256,512]{1,0:T(8,128)(2,1)S(1)}, bf16[256,512]{1,0:T(8,128)(2,1)S(1)}, u32[]{:S(2)}, u32[]{:S(2)}) collective-permute-start(bf16[256,512]{1,0:T(8,128)(2,1)S(1)} %maximum_select_fusion.2), channel_id=1, source_target_pairs={{0,2},{1,3},{2,0},{3,1},{4,6},{5,7},{6,4},{7,5},{8,10},{9,11},{10,... | collective-permute-start | bytes 786440 | tf_op jit(solution)/shard_map/ppermute | solution.py:556
  220.6 21.7 %collective-permute-start.26 = (bf16[2,64,3072]{2,1,0:T(8,128)(2,1)S(1)}, bf16[2,64,3072]{2,1,0:T(8,128)(2,1)}, u32[]{:S(2)}, u32[]{:S(2)}) collective-permute-start(bf16[2,64,3072]{2,1,0:T(8,128)(2,1)S(1)} %collective-permute-done.23.refs_2_), channel_id=1, source_target_pairs={{16,24},{20,28},{17,25},{21,29},{18,26},{22,30},{19,27},{23,31}} | collective-permute-start | bytes 2359304 | tf_op jit(solution)/shard_map/ppermute | solution.py:508
  222.2 20.2 %collective-permute-start.27 = (bf16[2,64,3072]{2,1,0:T(8,128)(2,1)}, bf16[2,64,3072]{2,1,0:T(8,128)(2,1)}, u32[]{:S(2)}, u32[]{:S(2)}) collective-permute-start(bf16[2,64,3072]{2,1,0:T(8,128)(2,1)} %collective-permute-done.24.refs_5_), channel_id=1, source_target_pairs={{8,0},{12,4},{9,1},{13,5},{10,2},{14,6},{11,3},{15,7}} | collective-permute-start | bytes 2359304 | tf_op jit(solution)/shard_map/ppermute | solution.py:508
  225.6 16.8 %collective-permute-start.25 = (bf16[2,64,3072]{2,1,0:T(8,128)(2,1)}, bf16[2,64,3072]{2,1,0:T(8,128)(2,1)}, u32[]{:S(2)}, u32[]{:S(2)}) collective-permute-start(bf16[2,64,3072]{2,1,0:T(8,128)(2,1)} %broadcast_select_fusion), channel_id=1, source_target_pairs={{0,4},{4,0},{8,12},{12,8},{16,20},{20,16},{24,28},{28,24},{1,5},{5... | collective-permute-start | bytes 2359304 | tf_op jit(solution)/shard_map/ppermute | solution.py:511
  243.7 15.6 %collective-permute-start.30 = (bf16[2,64,3072]{2,1,0:T(8,128)(2,1)S(1)}, bf16[2,64,3072]{2,1,0:T(8,128)(2,1)S(1)}, u32[]{:S(2)}, u32[]{:S(2)}) collective-permute-start(bf16[2,64,3072]{2,1,0:T(8,128)(2,1)S(1)} %select_select_fusion), channel_id=1, source_target_pairs={{0,4},{4,0},{8,12},{12,8},{16,20},{20,16},{24,28},{28,24},{1,5},{5... | collective-permute-start | bytes 2359304 | tf_op jit(solution)/shard_map/ppermute | solution.py:511
  (17 other events, 166.6 us)
